TPU v7x, 32 devices: a whole 2x2x4 slice. The times are simulated.
32 devices in a mesh: grp: 2 (over y), ctx: 4 (over z), head: 4 (over x, core).
Axes of the slice: x: 2, y: 2, z: 4, core: 2. Of those that a mesh axis runs over, the one named last changes fastest.
Arguments:
- key_rows: bfloat16 [8192, 8, 128], P(('grp', 'ctx'), 'head'), parts along dimension 0, may hold values from -6 to 6
- value_rows: bfloat16 [8192, 8, 128], P(('grp', 'ctx'), 'head'), parts along dimension 0, may hold values from -6 to 6
- cluster_labels: int32 [8, 8192], P('head', ('grp', 'ctx')), parts along dimension 1, may hold values from 0 to 4095, as said below
- owner_bounds: int32 [16, 5], P(('grp', 'head')), parts along dimension 0, may hold values from 0 to 4096, as said below
- init_centroids: float32 [16, 4096, 128], P(('grp', 'head')), parts along dimension 0, may hold values from -6 to 6
Outputs:
- centroids: float32 [16, 4096, 128], P(('grp', 'head'), 'ctx'), parts along dimension 0
- regrouped_keys: bfloat16 [16384, 8, 128], P(('grp', 'ctx'), 'head'), parts along dimension 0
- regrouped_values: bfloat16 [16384, 8, 128], P(('grp', 'ctx'), 'head'), parts along dimension 0
There are 2 independent parts, one for each index of `grp`. A program takes and returns all parts, laid end to end along the dimension named above; each array names one. Nothing has to cross between parts.
Inputs may be any that keep to these rules, and one draw needn't show every extreme that they name: `cluster_labels`: for each head, each device's 1024 tokens hold at most 512 labels in the cluster range of any one owner; in every draw one owner of each head gets exactly 512 from every device, 2048 in all. `owner_bounds`: each row starts at 0, ends at 4096 and rises strictly.
All inputs are finite; a program needn't handle non-finite values.
Results may differ from a plain program's by a relative error of at most 0.011.
Values may be sent and summed in bfloat16 or wider, within the bound.
No kernel may reach another device: no remote copies, remote signals or barrier semaphores. Data moves between devices by JAX's collectives and lax.ppermute only.
A program may use at most 128 MiB of HBM per device.

v0:
```python
import functools
import math

import jax
import jax.numpy as jnp
from jax import lax
from jax.experimental import pallas as pl
from jax.experimental.pallas import tpu as pltpu
from jax.sharding import PartitionSpec as P

LANES = 128
EXP2_SCALE = 20.0 * math.log2(math.e)
VMEM_LIMIT = 56 * 1024 * 1024
F32 = jnp.float32
BF16 = jnp.bfloat16
NT = (((1,), (1,)), ((), ()))
NN = (((1,), (0,)), ((), ()))


def dot_nt(a, b):
    return lax.dot_general(a, b, NT, preferred_element_type=F32)


def dot_nn(a, b):
    return lax.dot_general(a, b, NN, preferred_element_type=F32)


def unit_rows(x):
    return x * lax.rsqrt(jnp.sum(x * x, axis=-1, keepdims=True) + 1e-06)


def params(**kwargs):
    return pltpu.CompilerParams(vmem_limit_bytes=VMEM_LIMIT, **kwargs)


def whole(shape):
    return pl.BlockSpec(shape, lambda *_: (0,) * len(shape))


def row_to_lanes(row):
    return jnp.transpose(jnp.broadcast_to(row, (LANES, LANES)))


def split_heads(flat_ref, wide_ref):
    wide_ref[...] = flat_ref[...].astype(F32)


def head_rows(wide_ref, head, heads):
    if heads == 1:
        return wide_ref[...]
    return wide_ref[pl.Slice(head, wide_ref.shape[0] // heads, heads), :]


def totals_kernel(keys_ref, cent_ref, tot_ref, wide_ref, unit_ref, sum_ref):
    head, step = pl.program_id(0), pl.program_id(1)
    heads, tokens, _ = unit_ref.shape

    @pl.when((head == 0) & (step == 0))
    def _():
        split_heads(keys_ref, wide_ref)
        for h in range(heads):
            unit_ref[h] = unit_rows(head_rows(wide_ref, h, heads)).astype(BF16)

    @pl.when(step == 0)
    def _():
        sum_ref[...] = jnp.zeros_like(sum_ref)

    rows = cent_ref.shape[1]
    cent = unit_rows(cent_ref[0]).astype(BF16)
    part = 256
    for t in range(0, tokens, part):
        total = sum_ref[:, t : t + part]
        unit = unit_ref[head, t : t + part, :]
        for c in range(0, rows, part):
            raw = jnp.exp2(dot_nt(cent[c : c + part], unit) * EXP2_SCALE)
            total += jnp.sum(raw.reshape(-1, 8, part), axis=0)
        sum_ref[:, t : t + part] = total

    @pl.when(step == pl.num_programs(1) - 1)
    def _():
        tot_ref[0] = jnp.sum(sum_ref[...], axis=0, keepdims=True)


def own_totals(keys, cents):
    heads, count, width = cents.shape
    tokens = keys.shape[0] // heads
    rows = min(1024, count)
    return pl.pallas_call(
        totals_kernel,
        grid=(heads, count // rows),
        in_specs=[
            whole(keys.shape),
            pl.BlockSpec((1, rows, width), lambda h, c: (h, c, 0)),
        ],
        out_specs=pl.BlockSpec((1, 1, tokens), lambda h, c: (h, 0, 0)),
        out_shape=jax.ShapeDtypeStruct((heads, 1, tokens), F32),
        scratch_shapes=[
            pltpu.VMEM(keys.shape, F32),
            pltpu.VMEM((heads, tokens, width), BF16),
            pltpu.VMEM((8, tokens), F32),
        ],
        compiler_params=params(),
        cost_estimate=pl.CostEstimate(
            flops=2 * heads * tokens * count * width * 2,
            bytes_accessed=cents.size * 4,
            transcendentals=heads * tokens * count,
        ),
        name="own_totals",
    )(keys, cents)


def rank_kernel(own_ref, all_ref, rank_ref):
    count = all_ref.shape[2]
    tokens = own_ref.shape[2]
    mine = jnp.broadcast_to(own_ref[0], (8, tokens))

    def step(i, total):
        row = all_ref[0, :, pl.ds(pl.multiple_of(i * LANES, LANES), LANES)]
        column = row_to_lanes(row)
        for r in range(0, LANES, 8):
            other = jnp.tile(column[r : r + 8], (1, tokens // LANES))
            total += (other < mine).astype(jnp.int32)
        return total

    total = lax.fori_loop(
        0, count // LANES, step, jnp.zeros((8, tokens), jnp.int32)
    )
    rank_ref[0] = jnp.sum(total, axis=0, keepdims=True)


def own_ranks(own, everyone):
    heads, tokens = own.shape
    count = everyone.shape[1]
    return pl.pallas_call(
        rank_kernel,
        grid=(heads,),
        in_specs=[
            pl.BlockSpec((1, 1, tokens), lambda h: (h, 0, 0)),
            pl.BlockSpec((1, 1, count), lambda h: (h, 0, 0)),
        ],
        out_specs=pl.BlockSpec((1, 1, tokens), lambda h: (h, 0, 0)),
        out_shape=jax.ShapeDtypeStruct((heads, 1, tokens), jnp.int32),
        compiler_params=params(),
        cost_estimate=pl.CostEstimate(
            flops=3 * heads * tokens * count, bytes_accessed=65536, transcendentals=0
        ),
        name="own_ranks",
    )(own[:, None, :], everyone[:, None, :])[:, 0, :]


def first_kernel(fresh, keys_ref, tot_ref, cent_ref, *refs):
    if fresh:
        sums_ref, unit_ref, wide_ref, scaled_ref = refs
    else:
        before_ref, _, sums_ref, unit_ref, wide_ref, scaled_ref = refs
    head = pl.program_id(0)
    tokens = unit_ref.shape[1]

    @pl.when(head == 0)
    def _():
        split_heads(keys_ref, wide_ref)

    inverse = 1.0 / tot_ref[0]
    heads = keys_ref.shape[0] // tokens
    unit_ref[0] = unit_rows(head_rows(wide_ref, head, heads)).astype(BF16)
    for t in range(0, tokens, LANES):
        scaled_ref[t : t + LANES] = (
            unit_ref[0, t : t + LANES, :].astype(F32)
            * row_to_lanes(inverse[:, t : t + LANES])
        ).astype(BF16)

    rows = cent_ref.shape[1]
    part = 256
    for c in range(0, rows, part):
        cent = cent_ref[0, c : c + part]
        if fresh:
            total = jnp.zeros((part, cent.shape[1]), F32)
        else:
            total = before_ref[0, c : c + part]
        for t in range(0, tokens, part):
            raw = jnp.exp2(dot_nt(cent, unit_ref[0, t : t + part, :]) * EXP2_SCALE)
            total += dot_nn(raw.astype(BF16), scaled_ref[t : t + part])
        sums_ref[0, c : c + part] = total


def first_block(keys, totals, cents, block, blocks, before):
    heads, rows, width = cents.shape
    tokens = keys.shape[0] // heads
    sums = jax.ShapeDtypeStruct(cents.shape, F32)
    units = jax.ShapeDtypeStruct((heads, blocks * tokens, width), BF16)
    share = pl.BlockSpec((1, rows, width), lambda h: (h, 0, 0))
    in_specs = [
        whole(keys.shape),
        pl.BlockSpec((1, 1, tokens), lambda h: (h, 0, 0)),
        share,
    ]
    args = [keys, totals, cents]
    aliases = {}
    if before is not None:
        in_specs += [share, pl.BlockSpec(memory_space=pl.ANY)]
        args += list(before)
        aliases = {3: 0, 4: 1}
    return pl.pallas_call(
        functools.partial(first_kernel, before is None),
        grid=(heads,),
        in_specs=in_specs,
        out_specs=(
            share,
            pl.BlockSpec((1, tokens, width), lambda h: (h, block, 0)),
        ),
        out_shape=(sums, units),
        input_output_aliases=aliases,
        scratch_shapes=[
            pltpu.VMEM(keys.shape, F32),
            pltpu.VMEM((tokens, width), BF16),
        ],
        compiler_params=params(),
        cost_estimate=pl.CostEstimate(
            flops=8 * heads * tokens * rows * width,
            bytes_accessed=4 * cents.size * 4,
            transcendentals=heads * tokens * rows,
        ),
        name="first_block",
    )(*args)


def raw_kernel(sums_ref, unit_ref, raw_ref, part_ref, cent_ref):
    @pl.when(pl.program_id(0) == 0)
    def _():
        cent_ref[...] = unit_rows(sums_ref[0]).astype(BF16)

    rows, tokens = raw_ref.shape
    part = 256
    for t in range(0, tokens, part):
        unit = unit_ref[0, t : t + part, :]
        total = jnp.zeros((8, part), F32)
        for c in range(0, rows, part):
            raw = jnp.exp2(dot_nt(cent_ref[c : c + part], unit) * EXP2_SCALE)
            raw_ref[c : c + part, t : t + part] = raw.astype(BF16)
            total += jnp.sum(raw.reshape(-1, 8, part), axis=0)
        part_ref[:, t : t + part] = jnp.sum(total, axis=0, keepdims=True)


def raw_weights(sums, units, head, tokens):
    _, rows, width = sums.shape
    count = units.shape[1]
    return pl.pallas_call(
        raw_kernel,
        grid=(count // tokens,),
        in_specs=[
            pl.BlockSpec((1, rows, width), lambda j: (head, 0, 0)),
            pl.BlockSpec((1, tokens, width), lambda j: (head, j, 0)),
        ],
        out_specs=(
            pl.BlockSpec((rows, tokens), lambda j: (0, j)),
            pl.BlockSpec((1, tokens), lambda j: (0, j)),
        ),
        out_shape=(
            jax.ShapeDtypeStruct((rows, count), BF16),
            jax.ShapeDtypeStruct((1, count), F32),
        ),
        scratch_shapes=[pltpu.VMEM((rows, width), BF16)],
        compiler_params=params(),
        cost_estimate=pl.CostEstimate(
            flops=4 * rows * count * width,
            bytes_accessed=2 * rows * count,
            transcendentals=rows * count,
        ),
        name="raw_weights",
    )(sums, units)


def sums_kernel(n_parts, has_before, raw_ref, unit_ref, *refs):
    parts = refs[:n_parts]
    out_ref, scaled_ref, total_ref = refs[n_parts + has_before :]
    step = pl.program_id(0)
    rows, tokens = raw_ref.shape

    @pl.when(step == 0)
    def _():
        total_ref[...] = jnp.zeros_like(total_ref)

    row_total = parts[0][...]
    for part_ref in parts[1:]:
        row_total += part_ref[...]
    inverse = 1.0 / row_total
    for t in range(0, tokens, LANES):
        scaled_ref[t : t + LANES] = (
            unit_ref[0, t : t + LANES, :].astype(F32)
            * row_to_lanes(inverse[:, t : t + LANES])
        ).astype(BF16)
    part = 256
    for c in range(0, rows, part):
        total_ref[c : c + part] += dot_nn(raw_ref[c : c + part, :], scaled_ref[...])

    @pl.when(step == pl.num_programs(0) - 1)
    def _():
        out_ref[0] = unit_rows(total_ref[...])


def weighted_sums(raw, units, parts, head, tokens, before):
    rows, count = raw.shape
    heads, _, width = units.shape
    blocks = count // tokens

    def rolled(shift):
        return pl.BlockSpec((1, tokens), lambda j: (0, lax.rem(j + blocks - shift, blocks)))

    in_specs = [
        pl.BlockSpec((rows, tokens), lambda j: (0, j)),
        pl.BlockSpec((1, tokens, width), lambda j: (head, j, 0)),
    ] + [rolled(shift) for shift in range(len(parts))]
    args = [raw, units, *parts]
    aliases = {}
    if before is not None:
        aliases = {len(args): 0}
        in_specs.append(pl.BlockSpec(memory_space=pl.ANY))
        args.append(before)
    return pl.pallas_call(
        functools.partial(sums_kernel, len(parts), int(before is not None)),
        grid=(blocks,),
        in_specs=in_specs,
        out_specs=pl.BlockSpec((1, rows, width), lambda j: (head, 0, 0)),
        out_shape=jax.ShapeDtypeStruct((heads, rows, width), F32),
        input_output_aliases=aliases,
        scratch_shapes=[
            pltpu.VMEM((tokens, width), BF16),
            pltpu.VMEM((rows, width), F32),
        ],
        compiler_params=params(),
        cost_estimate=pl.CostEstimate(
            flops=4 * rows * count * width,
            bytes_accessed=2 * rows * count,
            transcendentals=0,
        ),
        name="weighted_sums",
    )(*args)


def place_kernel(blocks, tokens, spot_ref, *refs):
    keys, values = refs[:blocks], refs[blocks : 2 * blocks]
    out_keys, out_values, wide_ref, rows_ref, mixed_ref = refs[2 * blocks :]
    step = pl.program_id(0)
    heads = rows_ref.shape[0]
    width = LANES

    @pl.when(step == 0)
    def _():
        for j in range(blocks):
            for side, source in enumerate((keys[j], values[j])):
                split_heads(source, wide_ref)
                for h in range(heads):
                    rows_ref[
                        h,
                        j * tokens : (j + 1) * tokens,
                        side * width : (side + 1) * width,
                    ] = head_rows(wide_ref, h, heads).astype(BF16)

    rows = out_keys.shape[0] // heads
    first = step * rows
    slots = lax.broadcasted_iota(jnp.int32, (rows, 512), 0) + first
    for h in range(heads):
        total = jnp.zeros((rows, 2 * width), F32)
        for t in range(0, blocks * tokens, 512):
            pick = slots == spot_ref[h : h + 1, t : t + 512]
            total += dot_nn(
                jnp.where(pick, 1.0, 0.0).astype(BF16), rows_ref[h, t : t + 512, :]
            )
        mixed_ref[0, pl.Slice(h, rows, heads), :] = total[:, :width]
        mixed_ref[1, pl.Slice(h, rows, heads), :] = total[:, width:]
    out_keys[...] = mixed_ref[0].astype(BF16)
    out_values[...] = mixed_ref[1].astype(BF16)


def place(spots, keys, values, cap):
    blocks = len(keys)
    flat, width = keys[0].shape
    heads = spots.shape[0]
    tokens = flat // heads
    rows = 256
    out = jax.ShapeDtypeStruct((heads * cap, width), BF16)
    return pl.pallas_call(
        functools.partial(place_kernel, blocks, tokens),
        grid=(cap // rows,),
        in_specs=[whole(spots.shape)] + [whole((flat, width))] * (2 * blocks),
        out_specs=(pl.BlockSpec((heads * rows, width), lambda r: (r, 0)),) * 2,
        out_shape=(out, out),
        scratch_shapes=[
            pltpu.VMEM((flat, width), F32),
            pltpu.VMEM((heads, blocks * tokens, 2 * width), BF16),
            pltpu.VMEM((2, heads * rows, width), F32),
        ],
        compiler_params=params(),
        cost_estimate=pl.CostEstimate(
            flops=8 * cap * blocks * tokens * width,
            bytes_accessed=8 * blocks * flat * width,
            transcendentals=0,
        ),
        name="place",
    )(spots, *keys, *values)


def body(key_rows, value_rows, cluster_labels, owner_bounds, init_centroids):
    n = lax.axis_size("ctx")
    me = lax.axis_index("ctx")
    tokens, heads, width = key_rows.shape
    share = init_centroids.shape[1] // n
    cap = 2 * tokens

    def shifted(x, by=1):
        return lax.ppermute(x, "ctx", [(i, (i + by) % n) for i in range(n)])

    def ring(x):
        blocks = [x]
        for _ in range(n - 1):
            blocks.append(shifted(blocks[-1]))
        return blocks

    def spread(x):
        return [x] + [shifted(x, by) for by in range(1, n)]

    keys = ring(key_rows.reshape(heads * tokens, width))
    value_flat, _ = lax.optimization_barrier((value_rows.reshape(heads * tokens, width), keys[-1]))
    values = ring(value_flat)

    labels = spread(cluster_labels)
    token = jnp.arange(tokens, dtype=jnp.int32)
    order = [
        labels[j] * (n * tokens) + lax.rem(me + n - j, n) * tokens + token
        for j in range(n)
    ]
    ranks = spread(own_ranks(order[0], jnp.concatenate(order, axis=1)))
    label_all = jnp.concatenate(labels, axis=1)
    rank_all = jnp.concatenate(ranks, axis=1)
    low = lax.dynamic_slice_in_dim(owner_bounds, me, 1, 1)
    high = lax.dynamic_slice_in_dim(owner_bounds, me + 1, 1, 1)
    start = jnp.sum((label_all < low).astype(jnp.int32), axis=1, keepdims=True)
    spots = jnp.where((label_all >= low) & (label_all < high), rank_all - start, -1)

    totals = spread(own_totals(keys[0], init_centroids))
    own_cents = lax.dynamic_slice_in_dim(init_centroids, me * share, share, 1)
    cents = unit_rows(own_cents).astype(BF16)
    state = None
    for j in range(n):
        state = first_block(keys[j], totals[j], cents, j, n, state)
    sums, units = state

    raws = [raw_weights(sums, units, h, tokens) for h in range(heads)]
    out = None
    for h in range(heads):
        raw, part = raws[h]
        out = weighted_sums(raw, units, spread(part), h, tokens, out)

    placed_keys, placed_values = place(spots, keys, values, cap)
    shape = (cap, heads, width)
    return out, placed_keys.reshape(shape), placed_values.reshape(shape)


def solution(mesh):
    placed = (
        P(("grp", "ctx"), "head", None),
        P(("grp", "ctx"), "head", None),
        P("head", ("grp", "ctx")),
        P(("grp", "head"), None),
        P(("grp", "head"), None, None),
    )
    return jax.shard_map(
        body,
        mesh=mesh,
        in_specs=placed,
        out_specs=(
            P(("grp", "head"), "ctx", None),
            P(("grp", "ctx"), "head", None),
            P(("grp", "ctx"), "head", None),
        ),
        check_vma=False,
    )
```

profile of v0, /device:TPU:0, one launch (start us, length us, event | category | flops | bytes accessed | tf_op | source)
XLA Modules:
  0.0 147.3 jit_solution(11173319568900389758)
XLA Ops:
  0.6 3.1 %collective-permute-start.12 = (s32[2,1024]{1,0:T(2,128)}, s32[2,1024]{1,0:T(2,128)S(1)}, u32[]{:S(2)}, u32[]{:S(2)}) collective-permute-start(s32[2,1024]{1,0:T(2,128)} %param.7), channel_id=1, source_target_pairs={{0,4},{4,8},{8,12},{12,0},{1,5},{5,9},{9,13},{13,1},{2,6},{6,10},{... | collective-permute-start | bytes 24584 | tf_op jit(solution)/shard_map/ppermute | solution.py:411
  3.7 2.6 %collective-permute-start.13 = (s32[2,1024]{1,0:T(2,128)}, s32[2,1024]{1,0:T(2,128)S(1)}, u32[]{:S(2)}, u32[]{:S(2)}) collective-permute-start(s32[2,1024]{1,0:T(2,128)} %param.7), channel_id=1, source_target_pairs={{0,8},{4,12},{8,0},{12,4},{1,9},{5,13},{9,1},{13,5},{2,10},{6,14},... | collective-permute-start | bytes 24584 | tf_op jit(solution)/shard_map/ppermute | solution.py:411
  6.3 1.3 collective-permute-start.14
  7.6 0.7 collective-permute-start
  8.3 9.6 %own_totals.1.tot_ref = f32[2,1,1024]{2,1,0:T(1,128)} custom-call(bf16[2048,128]{1,0:T(8,128)(2,1)} %bitcast.16, f32[2,4096,128]{2,1,0:T(8,128)} %cent_ref.1), custom_call_target="tpu_custom_call" | custom-call | flops 4294967296 | bytes 4194304 | tf_op jit(solution)/shard_map/own_totals/pallas_call | solution.py:88
  17.9 0.1 collective-permute-start.5
  18.0 1.6 %multiply_reduce_fusion = f32[2,1024]{1,0:T(2,128)S(1)} fusion(f32[2,4096,128]{2,1,0:T(8,128)} %cent_ref.1, s32[]{:T(128)S(6)} %select_n.13), kind=kLoop, calls=%fused_computation.1 | loop fusion | flops 522240 | bytes 1056772 | tf_op jit(solution)/shard_map/reduce_sum | solution.py:29
  19.6 2.4 %multiply_convert_fusion.cent_ref = bf16[2,1024,128]{2,1,0:T(8,128)(2,1)} fusion(f32[2,4096,128]{2,1,0:T(8,128)} %cent_ref.1, s32[]{:T(128)S(6)} %select_n.13, f32[2,1024]{1,0:T(2,128)S(1)} %add_rsqrt_fusion), kind=kLoop, calls=%fused_computation | loop fusion | flops 524288 | bytes 1581060 | tf_op jit(solution)/shard_map/convert_element_type | solution.py:442
  22.0 6.5 %first_block.4 = (f32[2,1024,128]{2,1,0:T(8,128)}, bf16[2,4096,128]{2,1,0:T(8,128)(2,1)}) custom-call(bf16[2048,128]{1,0:T(8,128)(2,1)} %bitcast.17, f32[2,1,1024]{2,1,0:T(1,128)} %own_totals.1.tot_ref, bf16[2,1024,128]{2,1,0:T(8,128)(2,1)} %multiply_convert_fusion.cent_ref), custom_call_target="tpu_custom_call" | custom-call | flops 2147483648 | bytes 4194304 | tf_op jit(solution)/shard_map/first_block/pallas_call | solution.py:203
  28.4 0.6 copy.15.own_ref
  29.0 0.2 dynamic-slice_reduce_fusion
  29.2 0.0 collective-permute-done.keys_ref.refs_1_
  29.3 0.9 collective-permute-start.1
  30.1 0.0 collective-permute-done.12
  30.1 0.0 collective-permute-done.13
  30.2 0.0 collective-permute-done.14
  30.2 13.4 %collective-permute-done.1.keys_ref.refs_2_ = bf16[2048,128]{1,0:T(8,128)(2,1)S(1)} collective-permute-done((bf16[2048,128]{1,0:T(8,128)(2,1)S(1)}, bf16[2048,128]{1,0:T(8,128)(2,1)S(1)}, u32[]{:S(2)}, u32[]{:S(2)}) %collective-permute-start.1) | collective-permute-done | bytes 524320 | tf_op jit(solution)/shard_map/ppermute | solution.py:411
  43.6 0.0 collective-permute-start.2
  43.7 0.7 copy.16.all_ref
  44.4 9.0 %own_ranks.1 = s32[2,1,1024]{2,1,0:T(1,128)} custom-call(s32[2,1,1024]{2,1,0:T(1,128)} %copy.15.own_ref, s32[2,1,4096]{2,1,0:T(1,128)} %copy.16.all_ref), custom_call_target="tpu_custom_call" | custom-call | flops 25165824 | bytes 65536 | tf_op jit(solution)/shard_map/own_ranks/pallas_call | solution.py:134
  53.4 0.7 copy.19
  54.1 2.0 %collective-permute-start.15 = (s32[2,1024]{1,0:T(2,128)S(1)}, s32[2,1024]{1,0:T(2,128)S(1)}, u32[]{:S(2)}, u32[]{:S(2)}) collective-permute-start(s32[2,1024]{1,0:T(2,128)S(1)} %bitcast.11), channel_id=1, source_target_pairs={{0,4},{4,8},{8,12},{12,0},{1,5},{5,9},{9,13},{13,1},{2,6},{6,10},{... | collective-permute-start | bytes 24584 | tf_op jit(solution)/shard_map/ppermute | solution.py:411
  56.2 2.3 %collective-permute-start.16 = (s32[2,1024]{1,0:T(2,128)S(1)}, s32[2,1024]{1,0:T(2,128)S(1)}, u32[]{:S(2)}, u32[]{:S(2)}) collective-permute-start(s32[2,1024]{1,0:T(2,128)S(1)} %bitcast.12), channel_id=1, source_target_pairs={{0,8},{4,12},{8,0},{12,4},{1,9},{5,13},{9,1},{13,5},{2,10},{6,14},... | collective-permute-start | bytes 24584 | tf_op jit(solution)/shard_map/ppermute | solution.py:411
  58.4 0.8 collective-permute-start.17
  59.2 0.2 fusion
  59.4 0.0 collective-permute-done.2.keys_ref.refs_3_
  59.4 0.9 collective-permute-start.4
  60.3 0.0 collective-permute-done.15
  60.3 2.8 %collective-permute-start.3 = (f32[2,1,1024]{2,1,0:T(1,128)S(1)}, f32[2,1,1024]{2,1,0:T(1,128)S(1)}, u32[]{:S(2)}, u32[]{:S(2)}) collective-permute-start(f32[2,1,1024]{2,1,0:T(1,128)S(1)} %copy-done.15), channel_id=1, source_target_pairs={{0,12},{4,0},{8,4},{12,8},{1,13},{5,1},{9,5},{13,9},{2,14},{6,2},{... | collective-permute-start | bytes 24584 | tf_op jit(solution)/shard_map/ppermute | solution.py:411
  63.1 0.0 collective-permute-done.16
  63.1 0.0 collective-permute-start.18
  63.1 0.0 collective-permute-done.17
  63.2 0.7 and_select_fusion.spot_ref
  63.9 0.0 collective-permute-done.5.tot_ref
  63.9 0.6 copy-done.16
  64.5 5.5 %first_block.5 = (f32[2,1024,128]{2,1,0:T(8,128)}, bf16[2,4096,128]{2,1,0:T(8,128)(2,1)}) custom-call(bf16[2048,128]{1,0:T(8,128)(2,1)} %copy-done.9, f32[2,1,1024]{2,1,0:T(1,128)} %copy-done.16, bf16[2,1024,128]{2,1,0:T(8,128)(2,1)} %multiply_convert_fusion.cent_ref, ...), custom_call_target="tpu_custom_call", output_to_operand_aliasing={{0}: (3, {}), {1}: (4, {})} | custom-call | flops 2147483648 | bytes 4194304 | tf_op jit(solution)/shard_map/first_block/pallas_call | solution.py:203
  70.0 5.3 %collective-permute-done.18.refs_5_ = bf16[2048,128]{1,0:T(8,128)(2,1)S(1)} collective-permute-done((bf16[2048,128]{1,0:T(8,128)(2,1)S(1)}, bf16[2048,128]{1,0:T(8,128)(2,1)S(1)}, u32[]{:S(2)}, u32[]{:S(2)}) %collective-permute-start.18) | collective-permute-done | bytes 524320 | tf_op jit(solution)/shard_map/ppermute | solution.py:411
  75.3 0.0 copy-start.18
  75.3 0.6 copy-done.18
  75.9 5.5 %first_block.6 = (f32[2,1024,128]{2,1,0:T(8,128)}, bf16[2,4096,128]{2,1,0:T(8,128)(2,1)}) custom-call(bf16[2048,128]{1,0:T(8,128)(2,1)} %copy-done.10, f32[2,1,1024]{2,1,0:T(1,128)} %copy-done.18, bf16[2,1024,128]{2,1,0:T(8,128)(2,1)} %multiply_convert_fusion.cent_ref, ...), custom_call_target="tpu_custom_call", output_to_operand_aliasing={{0}: (3, {}), {1}: (4, {})} | custom-call | flops 2147483648 | bytes 4194304 | tf_op jit(solution)/shard_map/first_block/pallas_call | solution.py:203
  81.5 0.0 collective-permute-done.3.tot_ref
  81.5 0.0 copy-start.17
  81.5 0.6 copy-done.17
  82.1 5.5 %first_block.7 = (f32[2,1024,128]{2,1,0:T(8,128)}, bf16[2,4096,128]{2,1,0:T(8,128)(2,1)}) custom-call(bf16[2048,128]{1,0:T(8,128)(2,1)} %copy-done.11, f32[2,1,1024]{2,1,0:T(1,128)} %copy-done.17, bf16[2,1024,128]{2,1,0:T(8,128)(2,1)} %multiply_convert_fusion.cent_ref, ...), custom_call_target="tpu_custom_call", output_to_operand_aliasing={{0}: (3, {}), {1}: (4, {})} | custom-call | flops 2147483648 | bytes 4194304 | tf_op jit(solution)/shard_map/first_block/pallas_call | solution.py:203
  87.6 6.7 %raw_weights.3 = (bf16[1024,4096]{1,0:T(8,128)(2,1)}, f32[1,4096]{1,0:T(1,128)}) custom-call(f32[2,1024,128]{2,1,0:T(8,128)} %get-tuple-element.24.sums_ref, bf16[2,4096,128]{2,1,0:T(8,128)(2,1)} %get-tuple-element.25.unit_ref), custom_call_target="tpu_custom_call" | custom-call | flops 2147483648 | bytes 8388608 | tf_op jit(solution)/shard_map/raw_weights/pallas_call | solution.py:247
  94.3 0.6 collective-permute-start.10
  94.9 7.2 %collective-permute-start.11 = (f32[1,4096]{1,0:T(1,128)}, f32[1,4096]{1,0:T(1,128)S(1)}, u32[]{:S(2)}, u32[]{:S(2)}) collective-permute-start(f32[1,4096]{1,0:T(1,128)} %get-tuple-element.29.refs_0_), channel_id=1, source_target_pairs={{0,12},{4,0},{8,4},{12,8},{1,13},{5,1},{9,5},{13,9},{2,14},{6,2},{... | collective-permute-start | bytes 49160 | tf_op jit(solution)/shard_map/ppermute | solution.py:411
  102.1 0.0 collective-permute-start.9
  102.1 0.0 collective-permute-done.19.refs_6_
  102.1 0.1 collective-permute-start.20
  102.2 6.8 %raw_weights.2 = (bf16[1024,4096]{1,0:T(8,128)(2,1)}, f32[1,4096]{1,0:T(1,128)}) custom-call(f32[2,1024,128]{2,1,0:T(8,128)} %get-tuple-element.24.sums_ref, bf16[2,4096,128]{2,1,0:T(8,128)(2,1)} %get-tuple-element.25.unit_ref), custom_call_target="tpu_custom_call" | custom-call | flops 2147483648 | bytes 8388608 | tf_op jit(solution)/shard_map/raw_weights/pallas_call | solution.py:247
  109.0 0.9 collective-permute-start.6
  109.9 0.0 collective-permute-done.10.refs_2_
  109.9 3.5 %collective-permute-start.7 = (f32[1,4096]{1,0:T(1,128)}, f32[1,4096]{1,0:T(1,128)S(1)}, u32[]{:S(2)}, u32[]{:S(2)}) collective-permute-start(f32[1,4096]{1,0:T(1,128)} %get-tuple-element.27.refs_0_), channel_id=1, source_target_pairs={{0,8},{4,12},{8,0},{12,4},{1,9},{5,13},{9,1},{13,5},{2,10},{6,14},... | collective-permute-start | bytes 49160 | tf_op jit(solution)/shard_map/ppermute | solution.py:411
  113.4 2.7 %collective-permute-start.8 = (f32[1,4096]{1,0:T(1,128)}, f32[1,4096]{1,0:T(1,128)S(1)}, u32[]{:S(2)}, u32[]{:S(2)}) collective-permute-start(f32[1,4096]{1,0:T(1,128)} %get-tuple-element.27.refs_0_), channel_id=1, source_target_pairs={{0,12},{4,0},{8,4},{12,8},{1,13},{5,1},{9,5},{13,9},{2,14},{6,2},{... | collective-permute-start | bytes 49160 | tf_op jit(solution)/shard_map/ppermute | solution.py:411
  116.1 0.6 copy-done.2
  116.7 7.3 %weighted_sums.2.refs_4_ = f32[2,1024,128]{2,1,0:T(8,128)} custom-call(bf16[1024,4096]{1,0:T(8,128)(2,1)} %get-tuple-element.28.raw_ref, bf16[2,4096,128]{2,1,0:T(8,128)(2,1)} %get-tuple-element.25.unit_ref, f32[1,4096]{1,0:T(1,128)} %get-tuple-element.29.refs_0_, f32[1,4096]{1,0:T(1,128)} %copy-done.2, f32[1,4096]{1,0:T(1,128)} %copy-done, f32[1,4096]{1,0:T(1,128)} %copy-done.1), custom_call_target="tpu_custom_call" | custom-call | flops 2147483648 | bytes 8388608 | tf_op jit(solution)/shard_map/weighted_sums/pallas_call | solution.py:319
  124.0 0.0 copy-start.3
  124.1 0.6 copy-done.3
  124.6 0.0 copy-done.4
  124.6 0.0 copy-done.5
  124.6 7.3 %weighted_sums.3 = f32[2,1024,128]{2,1,0:T(8,128)} custom-call(bf16[1024,4096]{1,0:T(8,128)(2,1)} %get-tuple-element.26.raw_ref, bf16[2,4096,128]{2,1,0:T(8,128)(2,1)} %get-tuple-element.25.unit_ref, f32[1,4096]{1,0:T(1,128)} %get-tuple-element.27.refs_0_, f32[1,4096]{1,0:T(1,128)} %copy-done.3, ...), custom_call_target="tpu_custom_call", output_to_operand_aliasing={{}: (6, {})} | custom-call | flops 2147483648 | bytes 8388608 | tf_op jit(solution)/shard_map/weighted_sums/pallas_call | solution.py:319
  132.0 0.8 copy-done.14
  132.7 14.5 %place.1 = (bf16[4096,128]{1,0:T(8,128)(2,1)}, bf16[4096,128]{1,0:T(8,128)(2,1)}) custom-call(s32[2,4096]{1,0:T(2,128)} %and_select_fusion.spot_ref, bf16[2048,128]{1,0:T(8,128)(2,1)} %bitcast.18, bf16[2048,128]{1,0:T(8,128)(2,1)} %copy-done.9, bf16[2048,128]{1,0:T(8,128)(2,1)} %copy-done.10, bf16[2048,128]{1,0:T(8,128)(2,1)} %copy-done.11, ...), custom_call_target="tpu_custom_call" | custom-call | flops 8589934592 | bytes 8388608 | tf_op jit(solution)/shard_map/place/pallas_call | solution.py:382
  (41 shorter events, 0.1 us)
Async XLA Ops:
  0.6 29.5 %collective-permute-start.12 = (s32[2,1024]{1,0:T(2,128)}, s32[2,1024]{1,0:T(2,128)S(1)}, u32[]{:S(2)}, u32[]{:S(2)}) collective-permute-start(s32[2,1024]{1,0:T(2,128)} %param.7), channel_id=1, source_target_pairs={{0,4},{4,8},{8,12},{12,0},{1,5},{5,9},{9,13},{13,1},{2,6},{6,10},{... | collective-permute-start | bytes 24584 | tf_op jit(solution)/shard_map/ppermute | solution.py:411
  3.7 26.4 %collective-permute-start.13 = (s32[2,1024]{1,0:T(2,128)}, s32[2,1024]{1,0:T(2,128)S(1)}, u32[]{:S(2)}, u32[]{:S(2)}) collective-permute-start(s32[2,1024]{1,0:T(2,128)} %param.7), channel_id=1, source_target_pairs={{0,8},{4,12},{8,0},{12,4},{1,9},{5,13},{9,1},{13,5},{2,10},{6,14},... | collective-permute-start | bytes 24584 | tf_op jit(solution)/shard_map/ppermute | solution.py:411
  6.3 23.9 %collective-permute-start.14 = (s32[2,1024]{1,0:T(2,128)}, s32[2,1024]{1,0:T(2,128)S(1)}, u32[]{:S(2)}, u32[]{:S(2)}) collective-permute-start(s32[2,1024]{1,0:T(2,128)} %param.7), channel_id=1, source_target_pairs={{0,12},{4,0},{8,4},{12,8},{1,13},{5,1},{9,5},{13,9},{2,14},{6,2},{... | collective-permute-start | bytes 24584 | tf_op jit(solution)/shard_map/ppermute | solution.py:411
  7.6 11.9 %copy-start.6 = (s32[2,1024]{1,0:T(2,128)S(1)}, s32[2,1024]{1,0:T(2,128)}, u32[]{:S(2)}) copy-start(s32[2,1024]{1,0:T(2,128)} %param.7) | copy-start | bytes 24580
  7.6 21.6 %collective-permute-start = (bf16[2048,128]{1,0:T(8,128)(2,1)}, bf16[2048,128]{1,0:T(8,128)(2,1)S(1)}, u32[]{:S(2)}, u32[]{:S(2)}) collective-permute-start(bf16[2048,128]{1,0:T(8,128)(2,1)} %bitcast.15), channel_id=1, source_target_pairs={{0,4},{4,8},{8,12},{12,0},{1,5},{5,9},{9,13},{13,1},{2,6},{6,10},{... | collective-permute-start | bytes 1572872 | tf_op jit(solution)/shard_map/ppermute | solution.py:411
  17.9 46.0 %collective-permute-start.5 = (f32[2,1,1024]{2,1,0:T(1,128)}, f32[2,1,1024]{2,1,0:T(1,128)S(1)}, u32[]{:S(2)}, u32[]{:S(2)}) collective-permute-start(f32[2,1,1024]{2,1,0:T(1,128)} %own_totals.1.tot_ref), channel_id=1, source_target_pairs={{0,4},{4,8},{8,12},{12,0},{1,5},{5,9},{9,13},{13,1},{2,6},{6,10},{... | collective-permute-start | bytes 24584 | tf_op jit(solution)/shard_map/ppermute | solution.py:411
  22.0 7.1 %copy-start.7 = (s32[2,5]{1,0:T(2,128)S(1)}, s32[2,5]{1,0:T(2,128)}, u32[]{:S(2)}) copy-start(s32[2,5]{1,0:T(2,128)} %param.8) | copy-start | bytes 124
  22.0 37.5 %copy-start.15 = (f32[2,1,1024]{2,1,0:T(1,128)S(1)}, f32[2,1,1024]{2,1,0:T(1,128)}, u32[]{:S(2)}) copy-start(f32[2,1,1024]{2,1,0:T(1,128)} %own_totals.1.tot_ref) | copy-start | bytes 24580
  22.0 41.2 %copy-start.8 = (bf16[1024,2,128]{2,1,0:T(2,128)(2,1)S(1)}, bf16[1024,2,128]{2,1,0:T(2,128)(2,1)}, u32[]{:S(2)}) copy-start(bf16[1024,2,128]{2,1,0:T(2,128)(2,1)} %param.6) | copy-start | bytes 1572868
  29.2 34.6 %copy-start.9 = (bf16[2048,128]{1,0:T(8,128)(2,1)}, bf16[2048,128]{1,0:T(8,128)(2,1)S(1)}, u32[]{:S(2)}) copy-start(bf16[2048,128]{1,0:T(8,128)(2,1)S(1)} %collective-permute-done.keys_ref.refs_1_) | copy-start | bytes 1572868
  29.3 14.4 %collective-permute-start.1 = (bf16[2048,128]{1,0:T(8,128)(2,1)S(1)}, bf16[2048,128]{1,0:T(8,128)(2,1)S(1)}, u32[]{:S(2)}, u32[]{:S(2)}) collective-permute-start(bf16[2048,128]{1,0:T(8,128)(2,1)S(1)} %collective-permute-done.keys_ref.refs_1_), channel_id=1, source_target_pairs={{0,4},{4,8},{8,12},{12,0},{1,5},{5,9},{9,13},{13,1},{2,6},{6,10},{... | collective-permute-start | bytes 1572872 | tf_op jit(solution)/shard_map/ppermute | solution.py:411
  43.6 31.7 %copy-start.10 = (bf16[2048,128]{1,0:T(8,128)(2,1)}, bf16[2048,128]{1,0:T(8,128)(2,1)S(1)}, u32[]{:S(2)}) copy-start(bf16[2048,128]{1,0:T(8,128)(2,1)S(1)} %collective-permute-done.1.keys_ref.refs_2_) | copy-start | bytes 1572868
  43.6 15.8 %collective-permute-start.2 = (bf16[2048,128]{1,0:T(8,128)(2,1)S(1)}, bf16[2048,128]{1,0:T(8,128)(2,1)S(1)}, u32[]{:S(2)}, u32[]{:S(2)}) collective-permute-start(bf16[2048,128]{1,0:T(8,128)(2,1)S(1)} %collective-permute-done.1.keys_ref.refs_2_), channel_id=1, source_target_pairs={{0,4},{4,8},{8,12},{12,0},{1,5},{5,9},{9,13},{13,1},{2,6},{6,10},{... | collective-permute-start | bytes 1572872 | tf_op jit(solution)/shard_map/ppermute | solution.py:411
  54.1 6.2 %collective-permute-start.15 = (s32[2,1024]{1,0:T(2,128)S(1)}, s32[2,1024]{1,0:T(2,128)S(1)}, u32[]{:S(2)}, u32[]{:S(2)}) collective-permute-start(s32[2,1024]{1,0:T(2,128)S(1)} %bitcast.11), channel_id=1, source_target_pairs={{0,4},{4,8},{8,12},{12,0},{1,5},{5,9},{9,13},{13,1},{2,6},{6,10},{... | collective-permute-start | bytes 24584 | tf_op jit(solution)/shard_map/ppermute | solution.py:411
  56.2 7.0 %collective-permute-start.16 = (s32[2,1024]{1,0:T(2,128)S(1)}, s32[2,1024]{1,0:T(2,128)S(1)}, u32[]{:S(2)}, u32[]{:S(2)}) collective-permute-start(s32[2,1024]{1,0:T(2,128)S(1)} %bitcast.12), channel_id=1, source_target_pairs={{0,8},{4,12},{8,0},{12,4},{1,9},{5,13},{9,1},{13,5},{2,10},{6,14},... | collective-permute-start | bytes 24584 | tf_op jit(solution)/shard_map/ppermute | solution.py:411
  58.4 4.7 %collective-permute-start.17 = (s32[2,1024]{1,0:T(2,128)S(1)}, s32[2,1024]{1,0:T(2,128)S(1)}, u32[]{:S(2)}, u32[]{:S(2)}) collective-permute-start(s32[2,1024]{1,0:T(2,128)S(1)} %bitcast.13), channel_id=1, source_target_pairs={{0,12},{4,0},{8,4},{12,8},{1,13},{5,1},{9,5},{13,9},{2,14},{6,2},{... | collective-permute-start | bytes 24584 | tf_op jit(solution)/shard_map/ppermute | solution.py:411
  59.4 22.0 %copy-start.11 = (bf16[2048,128]{1,0:T(8,128)(2,1)}, bf16[2048,128]{1,0:T(8,128)(2,1)S(1)}, u32[]{:S(2)}) copy-start(bf16[2048,128]{1,0:T(8,128)(2,1)S(1)} %collective-permute-done.2.keys_ref.refs_3_) | copy-start | bytes 1572868
  59.4 15.9 %collective-permute-start.4 = (f32[2,1,1024]{2,1,0:T(1,128)S(1)}, f32[2,1,1024]{2,1,0:T(1,128)S(1)}, u32[]{:S(2)}, u32[]{:S(2)}) collective-permute-start(f32[2,1,1024]{2,1,0:T(1,128)S(1)} %copy-done.15), channel_id=1, source_target_pairs={{0,8},{4,12},{8,0},{12,4},{1,9},{5,13},{9,1},{13,5},{2,10},{6,14},... | collective-permute-start | bytes 24584 | tf_op jit(solution)/shard_map/ppermute | solution.py:411
  60.3 21.2 %collective-permute-start.3 = (f32[2,1,1024]{2,1,0:T(1,128)S(1)}, f32[2,1,1024]{2,1,0:T(1,128)S(1)}, u32[]{:S(2)}, u32[]{:S(2)}) collective-permute-start(f32[2,1,1024]{2,1,0:T(1,128)S(1)} %copy-done.15), channel_id=1, source_target_pairs={{0,12},{4,0},{8,4},{12,8},{1,13},{5,1},{9,5},{13,9},{2,14},{6,2},{... | collective-permute-start | bytes 24584 | tf_op jit(solution)/shard_map/ppermute | solution.py:411
  63.1 12.1 %collective-permute-start.18 = (bf16[2048,128]{1,0:T(8,128)(2,1)S(1)}, bf16[2048,128]{1,0:T(8,128)(2,1)S(1)}, u32[]{:S(2)}, u32[]{:S(2)}) collective-permute-start(bf16[2048,128]{1,0:T(8,128)(2,1)S(1)} %bitcast.20), channel_id=1, source_target_pairs={{0,4},{4,8},{8,12},{12,0},{1,5},{5,9},{9,13},{13,1},{2,6},{6,10},{... | collective-permute-start | bytes 1572872 | tf_op jit(solution)/shard_map/ppermute | solution.py:411
  63.9 0.6 copy-start.16
  75.3 12.3 %copy-start.12 = (bf16[2048,128]{1,0:T(8,128)(2,1)}, bf16[2048,128]{1,0:T(8,128)(2,1)S(1)}, u32[]{:S(2)}) copy-start(bf16[2048,128]{1,0:T(8,128)(2,1)S(1)} %collective-permute-done.18.refs_5_) | copy-start | bytes 1572868
  75.3 26.8 %collective-permute-start.19 = (bf16[2048,128]{1,0:T(8,128)(2,1)S(1)}, bf16[2048,128]{1,0:T(8,128)(2,1)S(1)}, u32[]{:S(2)}, u32[]{:S(2)}) collective-permute-start(bf16[2048,128]{1,0:T(8,128)(2,1)S(1)} %collective-permute-done.18.refs_5_), channel_id=1, source_target_pairs={{0,4},{4,8},{8,12},{12,0},{1,5},{5,9},{9,13},{13,1},{2,6},{6,10},{... | collective-permute-start | bytes 1572872 | tf_op jit(solution)/shard_map/ppermute | solution.py:411
  75.3 0.6 copy-start.18
  81.5 0.6 copy-start.17
  94.3 15.6 %collective-permute-start.10 = (f32[1,4096]{1,0:T(1,128)}, f32[1,4096]{1,0:T(1,128)S(1)}, u32[]{:S(2)}, u32[]{:S(2)}) collective-permute-start(f32[1,4096]{1,0:T(1,128)} %get-tuple-element.29.refs_0_), channel_id=1, source_target_pairs={{0,8},{4,12},{8,0},{12,4},{1,9},{5,13},{9,1},{13,5},{2,10},{6,14},... | collective-permute-start | bytes 49160 | tf_op jit(solution)/shard_map/ppermute | solution.py:411
  94.9 18.5 %collective-permute-start.11 = (f32[1,4096]{1,0:T(1,128)}, f32[1,4096]{1,0:T(1,128)S(1)}, u32[]{:S(2)}, u32[]{:S(2)}) collective-permute-start(f32[1,4096]{1,0:T(1,128)} %get-tuple-element.29.refs_0_), channel_id=1, source_target_pairs={{0,12},{4,0},{8,4},{12,8},{1,13},{5,1},{9,5},{13,9},{2,14},{6,2},{... | collective-permute-start | bytes 49160 | tf_op jit(solution)/shard_map/ppermute | solution.py:411
  102.1 14.0 %collective-permute-start.9 = (f32[1,4096]{1,0:T(1,128)}, f32[1,4096]{1,0:T(1,128)S(1)}, u32[]{:S(2)}, u32[]{:S(2)}) collective-permute-start(f32[1,4096]{1,0:T(1,128)} %get-tuple-element.29.refs_0_), channel_id=1, source_target_pairs={{0,4},{4,8},{8,12},{12,0},{1,5},{5,9},{9,13},{13,1},{2,6},{6,10},{... | collective-permute-start | bytes 49160 | tf_op jit(solution)/shard_map/ppermute | solution.py:411
  102.1 21.9 %copy-start.13 = (bf16[2048,128]{1,0:T(8,128)(2,1)}, bf16[2048,128]{1,0:T(8,128)(2,1)S(1)}, u32[]{:S(2)}) copy-start(bf16[2048,128]{1,0:T(8,128)(2,1)S(1)} %collective-permute-done.19.refs_6_) | copy-start | bytes 1572868
  102.1 29.8 %collective-permute-start.20 = (bf16[2048,128]{1,0:T(8,128)(2,1)S(1)}, bf16[2048,128]{1,0:T(8,128)(2,1)S(1)}, u32[]{:S(2)}, u32[]{:S(2)}) collective-permute-start(bf16[2048,128]{1,0:T(8,128)(2,1)S(1)} %collective-permute-done.19.refs_6_), channel_id=1, source_target_pairs={{0,4},{4,8},{8,12},{12,0},{1,5},{5,9},{9,13},{13,1},{2,6},{6,10},{... | collective-permute-start | bytes 1572872 | tf_op jit(solution)/shard_map/ppermute | solution.py:411
  109.0 15.0 %collective-permute-start.6 = (f32[1,4096]{1,0:T(1,128)}, f32[1,4096]{1,0:T(1,128)S(1)}, u32[]{:S(2)}, u32[]{:S(2)}) collective-permute-start(f32[1,4096]{1,0:T(1,128)} %get-tuple-element.27.refs_0_), channel_id=1, source_target_pairs={{0,4},{4,8},{8,12},{12,0},{1,5},{5,9},{9,13},{13,1},{2,6},{6,10},{... | collective-permute-start | bytes 49160 | tf_op jit(solution)/shard_map/ppermute | solution.py:411
  109.9 6.2 %copy-start = (f32[1,4096]{1,0:T(1,128)}, f32[1,4096]{1,0:T(1,128)S(1)}, u32[]{:S(2)}) copy-start(f32[1,4096]{1,0:T(1,128)S(1)} %collective-permute-done.10.refs_2_) | copy-start | bytes 49156
  109.9 14.1 %collective-permute-start.7 = (f32[1,4096]{1,0:T(1,128)}, f32[1,4096]{1,0:T(1,128)S(1)}, u32[]{:S(2)}, u32[]{:S(2)}) collective-permute-start(f32[1,4096]{1,0:T(1,128)} %get-tuple-element.27.refs_0_), channel_id=1, source_target_pairs={{0,8},{4,12},{8,0},{12,4},{1,9},{5,13},{9,1},{13,5},{2,10},{6,14},... | collective-permute-start | bytes 49160 | tf_op jit(solution)/shard_map/ppermute | solution.py:411
  113.4 2.7 %copy-start.1 = (f32[1,4096]{1,0:T(1,128)}, f32[1,4096]{1,0:T(1,128)S(1)}, u32[]{:S(2)}) copy-start(f32[1,4096]{1,0:T(1,128)S(1)} %collective-permute-done.11.refs_3_) | copy-start | bytes 49156
  113.4 10.7 %collective-permute-start.8 = (f32[1,4096]{1,0:T(1,128)}, f32[1,4096]{1,0:T(1,128)S(1)}, u32[]{:S(2)}, u32[]{:S(2)}) collective-permute-start(f32[1,4096]{1,0:T(1,128)} %get-tuple-element.27.refs_0_), channel_id=1, source_target_pairs={{0,12},{4,0},{8,4},{12,8},{1,13},{5,1},{9,5},{13,9},{2,14},{6,2},{... | collective-permute-start | bytes 49160 | tf_op jit(solution)/shard_map/ppermute | solution.py:411
  116.1 0.6 copy-start.2
  124.0 0.6 copy-start.3
  124.0 0.6 copy-start.4
  124.1 0.6 copy-start.5
  131.9 0.8 copy-start.14
where the time goes:
time: 148 us; the launch traced here: 147 us
  Pallas kernels  84.2 us (57%)
  starting transfers between devices  32.4 us (22%)
  waiting for transfers between devices  18.8 us (13%)
  local copies, waits for them, and re-layouts  6.1 us (4%)
  other arithmetic  4.93 us (3%)
    ppermute x21, starting transfers between devices, shifted(): return lax.ppermute(x, 'ctx', [(i, (i + by) % n) for i in range(n)])  32.4 us
    pallas_call x4, Pallas kernels, first_block(): pl.pallas_call(functools.partial(first_kernel, before is None), grid=(hea...  23 us
    ppermute x21, waiting for transfers between devices, shifted(): return lax.ppermute(x, 'ctx', [(i, (i + by) % n) for i in range(n)])  18.8 us
    pallas_call x2, Pallas kernels, weighted_sums(): pl.pallas_call(functools.partial(sums_kernel, len(parts), int(before is n...  14.6 us
    pallas_call x1, Pallas kernels, place(): pl.pallas_call(functools.partial(place_kernel, blocks, tokens), grid=(cap...  14.5 us
    pallas_call x2, Pallas kernels, raw_weights(): pl.pallas_call(raw_kernel, grid=(count // tokens,), in_specs=[pl.BlockSpe...  13.5 us
    pallas_call x1, Pallas kernels, own_totals(): pl.pallas_call(totals_kernel, grid=(heads, count // rows), in_specs=[whol...  9.55 us
    pallas_call x1, Pallas kernels, own_ranks(): pl.pallas_call(rank_kernel, grid=(heads,), in_specs=[pl.BlockSpec((1, 1,...  9.04 us
  transfers between devices with their start and end apart: 21, of which 2 were waited for; matrix products, arithmetic and copies ran while one was open for 5% of the time, Pallas kernels for 47%

commit v1 on v0

v1 whole, which is shorter than its diff:
```python
import functools
import math

import jax
import jax.numpy as jnp
from jax import lax
from jax.experimental import pallas as pl
from jax.experimental.pallas import tpu as pltpu
from jax.sharding import PartitionSpec as P

LANES = 128
EXP2_SCALE = 20.0 * math.log2(math.e)
VMEM_LIMIT = 28 * 1024 * 1024
PARTS = 2
F32 = jnp.float32
BF16 = jnp.bfloat16
NT = (((1,), (1,)), ((), ()))
NN = (((1,), (0,)), ((), ()))


def dot_nt(a, b):
    return lax.dot_general(a, b, NT, preferred_element_type=F32)


def dot_nn(a, b):
    return lax.dot_general(a, b, NN, preferred_element_type=F32)


def unit_rows(x):
    return x * lax.rsqrt(jnp.sum(x * x, axis=-1, keepdims=True) + 1e-06)


def params(**kwargs):
    return pltpu.CompilerParams(vmem_limit_bytes=VMEM_LIMIT, **kwargs)


def whole(shape):
    return pl.BlockSpec(shape, lambda *_: (0,) * len(shape))


def in_vmem():
    return pl.BlockSpec(memory_space=pltpu.VMEM)


def row_to_lanes(row):
    return jnp.transpose(jnp.broadcast_to(row, (LANES, LANES)))


def split_heads(flat_ref, wide_ref):
    wide_ref[...] = flat_ref[...].astype(F32)


def head_rows(wide_ref, head, heads):
    if heads == 1:
        return wide_ref[...]
    return wide_ref[pl.Slice(head, wide_ref.shape[0] // heads, heads), :]


def totals_kernel(keys_ref, cent_ref, tot_ref, wide_ref, unit_ref, sum_ref):
    head, step = pl.program_id(0), pl.program_id(1)
    heads, tokens, _ = unit_ref.shape

    @pl.when((head == 0) & (step == 0))
    def _():
        split_heads(keys_ref, wide_ref)
        for h in range(heads):
            unit_ref[h] = unit_rows(head_rows(wide_ref, h, heads)).astype(BF16)

    @pl.when(step == 0)
    def _():
        sum_ref[...] = jnp.zeros_like(sum_ref)

    cent = unit_rows(cent_ref[0]).astype(BF16)
    part = 256
    for t in range(0, tokens, part):
        raw = jnp.exp2(dot_nt(cent, unit_ref[head, t : t + part, :]) * EXP2_SCALE)
        sum_ref[:, t : t + part] += jnp.sum(raw.reshape(-1, 8, part), axis=0)

    @pl.when(step == pl.num_programs(1) - 1)
    def _():
        tot_ref[0] = jnp.sum(sum_ref[...], axis=0, keepdims=True)


def own_totals(keys, cents):
    heads, count, width = cents.shape
    tokens = keys.shape[0] // heads
    rows = min(1024, count)
    return pl.pallas_call(
        totals_kernel,
        grid=(heads, count // rows),
        in_specs=[
            whole(keys.shape),
            pl.BlockSpec((1, rows, width), lambda h, c: (h, c, 0)),
        ],
        out_specs=pl.BlockSpec((1, 1, tokens), lambda h, c: (h, 0, 0)),
        out_shape=jax.ShapeDtypeStruct((heads, 1, tokens), F32),
        scratch_shapes=[
            pltpu.VMEM(keys.shape, F32),
            pltpu.VMEM((heads, tokens, width), BF16),
            pltpu.VMEM((8, tokens), F32),
        ],
        compiler_params=params(),
        cost_estimate=pl.CostEstimate(
            flops=4 * heads * tokens * count * width,
            bytes_accessed=cents.size * 4,
            transcendentals=heads * tokens * count,
        ),
        name="own_totals",
    )(keys, cents)


def rank_kernel(own_ref, all_ref, rank_ref):
    count = all_ref.shape[2]
    tokens = own_ref.shape[2]
    mine = jnp.broadcast_to(own_ref[0], (8, tokens))
    wide = 4 * LANES

    def step(i, total):
        row = all_ref[0, :, pl.ds(pl.multiple_of(i * wide, wide), wide)]
        for s in range(0, wide, LANES):
            column = row_to_lanes(row[:, s : s + LANES])
            for r in range(0, LANES, 8):
                other = jnp.tile(column[r : r + 8], (1, tokens // LANES))
                total += (other < mine).astype(jnp.int32)
        return total

    total = lax.fori_loop(0, count // wide, step, jnp.zeros((8, tokens), jnp.int32))
    rank_ref[0] = jnp.sum(total, axis=0, keepdims=True)


def own_ranks(own, everyone):
    heads, tokens = own.shape
    count = everyone.shape[1]
    return pl.pallas_call(
        rank_kernel,
        grid=(heads,),
        in_specs=[
            pl.BlockSpec((1, 1, tokens), lambda h: (h, 0, 0)),
            pl.BlockSpec((1, 1, count), lambda h: (h, 0, 0)),
        ],
        out_specs=pl.BlockSpec((1, 1, tokens), lambda h: (h, 0, 0)),
        out_shape=jax.ShapeDtypeStruct((heads, 1, tokens), jnp.int32),
        compiler_params=params(),
        cost_estimate=pl.CostEstimate(
            flops=3 * heads * tokens * count, bytes_accessed=65536, transcendentals=0
        ),
        name="own_ranks",
    )(own[:, None, :], everyone[:, None, :])[:, 0, :]


def first_kernel(fresh, _, keys_ref, tot_ref, init_ref, *refs):
    if fresh:
        sums_ref, unit_ref, wide_ref, scaled_ref, cent_ref = refs
    else:
        before_ref, sums_ref, unit_ref, wide_ref, scaled_ref, cent_ref = refs
    head = pl.program_id(0)
    tokens = unit_ref.shape[1]
    heads = keys_ref.shape[1] // tokens

    @pl.when(pl.program_id(1) == 0)
    def _():
        cent_ref[...] = unit_rows(init_ref[0]).astype(BF16)
        if fresh:
            sums_ref[...] = jnp.zeros_like(sums_ref)
        else:
            sums_ref[...] = before_ref[...]

    split_heads(keys_ref.at[0], wide_ref)
    unit_ref[0] = unit_rows(head_rows(wide_ref, head, heads)).astype(BF16)
    inverse = 1.0 / tot_ref[0, 0]
    scale_rows(unit_ref, inverse, scaled_ref)
    part = 256
    for t in range(0, tokens, part):
        raw = jnp.exp2(dot_nt(cent_ref[...], unit_ref[0, t : t + part, :]) * EXP2_SCALE)
        sums_ref[0] += dot_nn(raw.astype(BF16), scaled_ref[t : t + part])


def scale_rows(unit_ref, inverse, scaled_ref):
    for t in range(0, scaled_ref.shape[0], LANES):
        scaled_ref[t : t + LANES] = (
            unit_ref[0, t : t + LANES, :].astype(F32)
            * row_to_lanes(inverse[:, t : t + LANES])
        ).astype(BF16)


def first_part(me, keys, totals, init, part, before):
    n, flat, width = keys.shape
    heads = init.shape[0]
    tokens = flat // heads
    rows = init.shape[1] // n
    share = pl.BlockSpec((1, rows, width), lambda h, j, me: (h, 0, 0))
    in_specs = [
        pl.BlockSpec((1, flat, width), lambda h, j, me: (j, 0, 0)),
        pl.BlockSpec((1, 1, 1, tokens), lambda h, j, me: (j, h, 0, part)),
        pl.BlockSpec((1, rows, width), lambda h, j, me: (h, me[0], 0)),
    ]
    args = [me, keys, totals, init]
    aliases = {}
    if before is not None:
        in_specs.append(share)
        args.append(before)
        aliases = {4: 0}
    return pl.pallas_call(
        functools.partial(first_kernel, before is None),
        grid_spec=pltpu.PrefetchScalarGridSpec(
            num_scalar_prefetch=1,
            grid=(heads, n),
            in_specs=in_specs,
            out_specs=(
                share,
                pl.BlockSpec((1, tokens, width), lambda h, j, me: (h, j, 0)),
            ),
            scratch_shapes=[
                pltpu.VMEM((flat, width), F32),
                pltpu.VMEM((tokens, width), BF16),
                pltpu.VMEM((rows, width), BF16),
            ],
        ),
        out_shape=(
            jax.ShapeDtypeStruct((heads, rows, width), F32),
            jax.ShapeDtypeStruct((heads, n * tokens, width), BF16),
        ),
        input_output_aliases=aliases,
        compiler_params=params(),
        cost_estimate=pl.CostEstimate(
            flops=8 * heads * n * tokens * rows * width,
            bytes_accessed=4 * heads * rows * width * 4,
            transcendentals=heads * n * tokens * rows,
        ),
        name="first_part",
    )(*args)


def raw_kernel(parts, sums_ref, *refs):
    units = refs[:parts]
    raw_ref, total_ref, cent_ref = refs[parts:]
    cent_ref[...] = unit_rows(sums_ref[0]).astype(BF16)
    part = 256
    step = 1024

    for p in range(parts):
        unit_ref = units[p]
        size = unit_ref.shape[1]

        def chunk(i, _, unit_ref=unit_ref, p=p, size=size):
            for s in range(0, step, part):
                near = pl.ds(pl.multiple_of(i * step + s, part), part)
                far = pl.ds(pl.multiple_of(p * size + i * step + s, part), part)
                raw = jnp.exp2(dot_nt(cent_ref[...], unit_ref[0, near, :]) * EXP2_SCALE)
                raw_ref[:, far] = raw.astype(BF16)
                total = jnp.sum(raw.reshape(-1, 8, part), axis=0)
                total_ref[:, far] = jnp.sum(total, axis=0, keepdims=True)
            return 0

        lax.fori_loop(0, size // step, chunk, 0)


def raw_weights(sums, units, head):
    _, rows, width = sums.shape
    count = sum(unit.shape[1] for unit in units)
    return pl.pallas_call(
        functools.partial(raw_kernel, len(units)),
        grid=(1,),
        in_specs=[pl.BlockSpec((1, rows, width), lambda _: (head, 0, 0))]
        + [
            pl.BlockSpec((1, unit.shape[1], width), lambda _: (head, 0, 0))
            for unit in units
        ],
        out_specs=(in_vmem(), whole((1, count))),
        out_shape=(
            pltpu.VMEM((rows, count), BF16),
            jax.ShapeDtypeStruct((1, count), F32),
        ),
        scratch_shapes=[pltpu.VMEM((rows, width), BF16)],
        compiler_params=params(),
        cost_estimate=pl.CostEstimate(
            flops=4 * rows * count * width,
            bytes_accessed=2 * count * width,
            transcendentals=rows * count,
        ),
        name="raw_weights",
    )(sums, *units)


def sums_kernel(parts, has_before, raw_ref, tot_ref, *refs):
    units = refs[:parts]
    out_ref, scaled_ref, sum_ref = refs[parts + has_before :]
    inverse = 1.0 / jnp.sum(tot_ref[...], axis=0, keepdims=True)
    start = 0
    for unit_ref in units:
        size = unit_ref.shape[1]
        scale_rows(unit_ref, inverse[:, start : start + size], scaled_ref.at[start : start + size])
        start += size
    step = 1024
    for t in range(0, start, step):
        more = dot_nn(raw_ref[:, t : t + step], scaled_ref[t : t + step])
        if t == 0:
            sum_ref[...] = more
        else:
            sum_ref[...] += more
    out_ref[0] = unit_rows(sum_ref[...])


def weighted_sums(raw, units, totals, head, before):
    rows, count = raw.shape
    heads, _, width = units[0].shape
    raw = pltpu.with_memory_space_constraint(raw, pltpu.VMEM)
    in_specs = [in_vmem(), whole(totals.shape)] + [
        pl.BlockSpec((1, unit.shape[1], width), lambda _: (head, 0, 0)) for unit in units
    ]
    args = [raw, totals, *units]
    aliases = {}
    if before is not None:
        aliases = {len(args): 0}
        in_specs.append(pl.BlockSpec(memory_space=pl.ANY))
        args.append(before)
    return pl.pallas_call(
        functools.partial(sums_kernel, len(units), int(before is not None)),
        grid=(1,),
        in_specs=in_specs,
        out_specs=pl.BlockSpec((1, rows, width), lambda _: (head, 0, 0)),
        out_shape=jax.ShapeDtypeStruct((heads, rows, width), F32),
        input_output_aliases=aliases,
        scratch_shapes=[
            pltpu.VMEM((count, width), BF16),
            pltpu.VMEM((rows, width), F32),
        ],
        compiler_params=params(),
        cost_estimate=pl.CostEstimate(
            flops=4 * rows * count * width,
            bytes_accessed=2 * count * width,
            transcendentals=0,
        ),
        name="weighted_sums",
    )(*args)


def place_kernel(fresh, spot_ref, keys_ref, values_ref, *refs):
    before = refs[: 0 if fresh else 2]
    out_refs, (wide_ref, rows_ref, mixed_ref) = refs[-5:-3], refs[-3:]
    step = pl.program_id(0)
    n, flat, width = keys_ref.shape
    heads = rows_ref.shape[0]
    tokens = flat // heads

    @pl.when(step == 0)
    def _():
        for j in range(n):
            for side, source in enumerate((keys_ref, values_ref)):
                split_heads(source.at[j], wide_ref)
                for h in range(heads):
                    rows_ref[
                        h,
                        j * tokens : (j + 1) * tokens,
                        side * width : (side + 1) * width,
                    ] = head_rows(wide_ref, h, heads).astype(BF16)

    rows = out_refs[0].shape[0] // heads
    part = 1024
    slots = lax.broadcasted_iota(jnp.int16, (rows, part), 0)
    for h in range(heads):
        for t in range(0, n * tokens, part):
            spot = (spot_ref[h : h + 1, t : t + part] - step * rows).astype(jnp.int16)
            pick = jnp.where(slots == spot, jnp.ones((), BF16), jnp.zeros((), BF16))
            more = dot_nn(pick, rows_ref[h, t : t + part, :])
            total = more if t == 0 else total + more
        for side in range(2):
            mixed_ref[side, pl.Slice(h, rows, heads), :] = total[
                :, side * width : (side + 1) * width
            ]
    for side in range(2):
        mixed = mixed_ref[side]
        if not fresh:
            mixed += before[side][...].astype(F32)
        out_refs[side][...] = mixed.astype(BF16)


def place(spots, keys, values, cap, before):
    n, flat, width = keys.shape
    heads = spots.shape[0]
    rows = 512
    out = jax.ShapeDtypeStruct((heads * cap, width), BF16)
    block = pl.BlockSpec((heads * rows, width), lambda r: (r, 0))
    fresh = before is None
    return pl.pallas_call(
        functools.partial(place_kernel, fresh),
        grid=(cap // rows,),
        in_specs=[whole(spots.shape), whole(keys.shape), whole(values.shape)]
        + [block] * (0 if fresh else 2),
        out_specs=(block, block),
        out_shape=(out, out),
        input_output_aliases={} if fresh else {3: 0, 4: 1},
        scratch_shapes=[
            pltpu.VMEM((flat, width), F32),
            pltpu.VMEM((heads, n * flat // heads, 2 * width), BF16),
            pltpu.VMEM((2, heads * rows, width), F32),
        ],
        compiler_params=params(),
        cost_estimate=pl.CostEstimate(
            flops=4 * cap * n * flat * width,
            bytes_accessed=8 * n * flat * width,
            transcendentals=0,
        ),
        name="place",
    )(spots, keys, values, *(() if fresh else before))


def body(key_rows, value_rows, cluster_labels, owner_bounds, init_centroids):
    n = lax.axis_size("ctx")
    me = lax.axis_index("ctx")
    tokens, heads, width = key_rows.shape
    everyone = n * tokens
    cap = 2 * tokens

    def gather(x):
        return lax.all_gather(x, "ctx")

    def gather_parts(flat):
        size = flat.shape[0] // PARTS
        return [gather(flat[p * size : (p + 1) * size]) for p in range(PARTS)]

    key_flat = key_rows.reshape(heads * tokens, width)
    keys = gather_parts(key_flat)
    value_flat, _ = lax.optimization_barrier(
        (value_rows.reshape(heads * tokens, width), keys[-1])
    )
    values = gather_parts(value_flat)

    labels = jnp.swapaxes(gather(cluster_labels), 0, 1).reshape(heads, everyone)
    token = jnp.arange(everyone, dtype=jnp.int32)
    own_order = cluster_labels * everyone + me * tokens + token[:tokens]
    ranks = gather(own_ranks(own_order, labels * everyone + token))
    ranks = jnp.swapaxes(ranks, 0, 1).reshape(heads, everyone)
    low = lax.dynamic_slice_in_dim(owner_bounds, me, 1, 1)
    high = lax.dynamic_slice_in_dim(owner_bounds, me + 1, 1, 1)
    start = jnp.sum((labels < low).astype(jnp.int32), axis=1, keepdims=True)
    spots = jnp.where((labels >= low) & (labels < high), ranks - start, -1)
    spots = spots.reshape(heads, n, PARTS, tokens // PARTS)

    totals = gather(own_totals(key_flat, init_centroids))
    me_array = me.astype(jnp.int32).reshape(1)
    sums, units = None, []
    for p in range(PARTS):
        sums, unit = first_part(me_array, keys[p], totals, init_centroids, p, sums)
        units.append(unit)

    raws = [raw_weights(sums, units, h) for h in range(heads)]
    out = None
    for h in range(heads):
        raw, part = raws[h]
        out = weighted_sums(raw, units, gather(part).reshape(n, everyone), h, out)

    placed = None
    for p in range(PARTS):
        placed = place(
            spots[:, :, p].reshape(heads, everyone // PARTS), keys[p], values[p], cap, placed
        )
    shape = (cap, heads, width)
    return out, placed[0].reshape(shape), placed[1].reshape(shape)


def solution(mesh):
    placed = (
        P(("grp", "ctx"), "head", None),
        P(("grp", "ctx"), "head", None),
        P("head", ("grp", "ctx")),
        P(("grp", "head"), None),
        P(("grp", "head"), None, None),
    )
    return jax.shard_map(
        body,
        mesh=mesh,
        in_specs=placed,
        out_specs=(
            P(("grp", "head"), "ctx", None),
            P(("grp", "ctx"), "head", None),
            P(("grp", "ctx"), "head", None),
        ),
        check_vma=False,
    )
```

time: 148 us -> 171 us (1.16)
  blocking collectives: 0 us -> 68.5 us
  starting transfers between devices: 32.4 us -> 0.16 us
  Pallas kernels: 84.2 us -> 57.7 us
  between operations: 0.87 us -> 13.9 us
  local copies, waits for them, and re-layouts: 6.1 us -> 14.5 us
  waiting for transfers between devices: 18.8 us -> 14.3 us
  other arithmetic: 4.93 us -> 1.12 us
    all_gather x0 -> x5, blocking collectives: none -> 68.5 us  [gather(): return lax.all_gather(x, 'ctx')]
    ppermute x21 -> x0, starting transfers between devices: 32.4 us -> none  [shifted(): return lax.ppermute(x, 'ctx', [(i, (i + by) % n) for i in range(n)])]
    pallas_call x9 -> x8, Pallas kernels: 65.7 us -> 46.2 us  [the longest x2 17.1 us: first_part(): pl.pallas_call(functools.partial(first_kernel, before is None), grid_spec...]
    ppermute x21 -> x0, waiting for transfers between devices: 18.8 us -> none  [shifted(): return lax.ppermute(x, 'ctx', [(i, (i + by) % n) for i in range(n)])]
    all_gather x0 -> x4, waiting for transfers between devices: none -> 13.6 us  [gather(): return lax.all_gather(x, 'ctx')]
    unnamed x39 -> x20, local copies, waits for them, and re-layouts: 4.54 us -> 9.21 us
    pallas_call x1, Pallas kernels: 9.04 us -> 4.41 us  [own_ranks(): pl.pallas_call(rank_kernel, grid=(heads,), in_specs=[pl.BlockSpec((1, 1,...]
    slice x0 -> x3, local copies, waits for them, and re-layouts: none -> 4.12 us  [the longest x2 4.03 us: gather_parts(): return [gather(flat[p * size:(p + 1) * size]) for p in range(PARTS)]]
  transfers between devices with their start and end apart: 21 -> 4, of which waited for: 2 -> 1; matrix products, arithmetic and copies ran while one was open for 5% -> 3% of each run, Pallas kernels for 47% -> 29%
where the time goes in v1:
time: 171 us; the launch traced here: 170 us
  blocking collectives  68.5 us (40%)
  Pallas kernels  57.7 us (34%)
  local copies, waits for them, and re-layouts  14.5 us (8%)
  waiting for transfers between devices  14.3 us (8%)
  between operations  13.9 us (8%)
    all_gather x5, blocking collectives, gather(): return lax.all_gather(x, 'ctx')  68.5 us
    pallas_call x2, Pallas kernels, first_part(): pl.pallas_call(functools.partial(first_kernel, before is None), grid_spec...  17.1 us
    pallas_call x2, Pallas kernels, place(): pl.pallas_call(functools.partial(place_kernel, fresh), grid=(cap // rows,...  14.4 us
    all_gather x4, waiting for transfers between devices, gather(): return lax.all_gather(x, 'ctx')  13.6 us
    unnamed x20, local copies, waits for them, and re-layouts  9.21 us
    pallas_call x2, Pallas kernels, raw_weights(): pl.pallas_call(functools.partial(raw_kernel, len(units)), grid=(1,), in_s...  7.66 us
    pallas_call x1, Pallas kernels, own_totals(): pl.pallas_call(totals_kernel, grid=(heads, count // rows), in_specs=[whol...  7.08 us
    pallas_call x2, Pallas kernels, weighted_sums(): pl.pallas_call(functools.partial(sums_kernel, len(units), int(before is n...  7 us
  transfers between devices with their start and end apart: 4, of which 1 were waited for; matrix products, arithmetic and copies ran while one was open for 3% of the time, Pallas kernels for 29%

profile of v1, /device:TPU:0, one launch (start us, length us, event | category | flops | bytes accessed | tf_op | source)
XLA Modules:
  0.0 170.3 jit_solution(14995219550958872794)
XLA Ops:
  7.2 0.0 all-gather.15.cloned.1.call-start
  7.2 2.2 %fusion.1 = (bf16[512,2,128]{2,1,0:T(2,128)(2,1)}, bf16[512,2,128]{2,1,0:T(2,128)(2,1)}) fusion(bf16[1024,2,128]{2,1,0:T(2,128)(2,1)} %param.5), kind=kLoop, calls=%fused_computation.15 | loop fusion | bytes 1048576 | tf_op jit(solution)/shard_map/slice | solution.py:420
  9.4 0.0 all-gather.15.cloned.1.call-update
  9.4 0.0 all-gather.17.cloned.1.call-start
  9.5 0.7 all-gather.17.cloned.1.call-update
  10.2 0.0 all-gather.21.cloned.1.call-start
  10.2 0.7 add_add_fusion
  10.9 15.1 %all-gather.9 = s32[4,2,1024]{2,1,0:T(2,128)S(1)} all-gather(s32[1,2,1024]{2,1,0:T(2,128)} %bitcast.51), channel_id=5, replica_groups=mesh['grp'=2,'ctx'=4,'head'=4] {'ctx'}, dimensions={0}, use_global_device_ids=true | all-gather | bytes 40960 | tf_op jit(solution)/shard_map/all_gather | solution.py:416
  26.1 1.0 dynamic-slice_reduce_fusion
  27.1 0.2 convert_reduce_fusion
  27.3 0.1 mul.30
  27.3 13.6 %all-gather.15.cloned.1.call-done.keys_ref = bf16[4,1024,128]{2,1,0:T(8,128)(2,1)} async-done(((bf16[1,1024,128]{2,1,0:T(8,128)(2,1)}), bf16[4,1024,128]{2,1,0:T(8,128)(2,1)}) %all-gather.15.cloned.1.call-update) | async-done | bytes 1048592 | tf_op jit(solution)/shard_map/all_gather | solution.py:416
  40.9 1.8 %fusion = (bf16[1024,128]{1,0:T(8,128)(2,1)}, bf16[1024,128]{1,0:T(8,128)(2,1)}) fusion(bf16[2048,128]{1,0:T(8,128)(2,1)} %bitcast.46), kind=kLoop, calls=%fused_computation.14 | loop fusion | bytes 1048576 | tf_op jit(solution)/shard_map/slice | solution.py:420
  42.7 0.0 all-gather.21.cloned.1.call-update
  42.8 0.0 all-gather.19.cloned.1.call-start
  42.9 4.4 %own_ranks.1 = s32[2,1,1024]{2,1,0:T(1,128)S(1)} custom-call(s32[2,1,1024]{2,1,0:T(1,128)S(1)} %broadcast_in_dim.5.own_ref, s32[2,1,4096]{2,1,0:T(1,128)S(1)} %iota_add_fusion.all_ref), custom_call_target="tpu_custom_call" | custom-call | flops 25165824 | bytes 65536 | tf_op jit(solution)/shard_map/own_ranks/pallas_call | solution.py:134
  47.3 13.3 %all-gather.4 = s32[8,1,1024]{2,1,0:T(1,128)S(1)} all-gather(s32[2,1,1024]{2,1,0:T(1,128)S(1)} %own_ranks.1), channel_id=6, replica_groups=mesh['grp'=2,'ctx'=4,'head'=4] {'ctx'}, dimensions={0}, use_global_device_ids=true | all-gather | bytes 40960 | tf_op jit(solution)/shard_map/all_gather | solution.py:416
  60.6 0.1 reduce.3
  60.8 0.1 and_select_fusion
  60.9 0.1 slice_reduce_fusion
  61.0 0.0 copy-start
  61.0 1.0 copy-done
  62.0 0.0 copy-start.1
  62.0 2.2 %copy-done.1 = f32[2,4096,128]{2,1,0:T(8,128)S(1)} copy-done((f32[2,4096,128]{2,1,0:T(8,128)S(1)}, f32[2,4096,128]{2,1,0:T(8,128)}, u32[]{:S(2)}) %copy-start.1) | copy-done | bytes 4194328
  64.2 0.0 copy-start.3
  64.2 7.1 %own_totals.1 = f32[2,1,1024]{2,1,0:T(1,128)S(1)} custom-call(bf16[2048,128]{1,0:T(8,128)(2,1)S(1)} %bitcast.33, f32[2,4096,128]{2,1,0:T(8,128)S(1)} %copy-done.1), custom_call_target="tpu_custom_call" | custom-call | flops 4294967296 | bytes 4194304 | tf_op jit(solution)/shard_map/own_totals/pallas_call | solution.py:88
  71.3 13.2 %all-gather = f32[8,1,1024]{2,1,0:T(1,128)S(1)} all-gather(f32[2,1,1024]{2,1,0:T(1,128)S(1)} %own_totals.1), channel_id=2, replica_groups=mesh['grp'=2,'ctx'=4,'head'=4] {'ctx'}, dimensions={0}, use_global_device_ids=true | all-gather | bytes 40960 | tf_op jit(solution)/shard_map/all_gather | solution.py:416
  84.6 0.0 all-gather.19.cloned.1.call-update
  84.6 0.0 all-gather.17.cloned.1.call-done.keys_ref
  84.6 0.0 copy-start.2
  84.6 2.2 %copy-done.2 = f32[2,4096,128]{2,1,0:T(8,128)S(1)} copy-done((f32[2,4096,128]{2,1,0:T(8,128)S(1)}, f32[2,4096,128]{2,1,0:T(8,128)}, u32[]{:S(2)}) %copy-start.2) | copy-done | bytes 4194328
  86.8 0.0 copy-start.4
  86.8 1.2 copy-done.4
  88.0 8.5 %first_part.2 = (f32[2,1024,128]{2,1,0:T(8,128)S(1)}, bf16[2,2048,128]{2,1,0:T(8,128)(2,1)S(1)}) custom-call(s32[1]{0:T(128)} %bitcast._, bf16[4,1024,128]{2,1,0:T(8,128)(2,1)S(1)} %copy-done.4, f32[4,2,1,1024]{3,2,1,0:T(1,128)S(1)} %bitcast.36, f32[2,4096,128]{2,1,0:T(8,128)S(1)} %copy-done.2), custom_call_target="tpu_custom_call" | custom-call | flops 4294967296 | bytes 4194304 | tf_op jit(solution)/shard_map/first_part/pallas_call | solution.py:203
  96.5 0.0 copy-done.3
  96.5 8.6 %first_part.3 = (f32[2,1024,128]{2,1,0:T(8,128)S(1)}, bf16[2,2048,128]{2,1,0:T(8,128)(2,1)S(1)}) custom-call(s32[1]{0:T(128)} %bitcast._, bf16[4,1024,128]{2,1,0:T(8,128)(2,1)S(1)} %copy-done.3, f32[4,2,1,1024]{3,2,1,0:T(1,128)S(1)} %bitcast.37, f32[2,4096,128]{2,1,0:T(8,128)S(1)} %copy-done.2, ...), custom_call_target="tpu_custom_call", output_to_operand_aliasing={{0}: (4, {})} | custom-call | flops 4294967296 | bytes 4194304 | tf_op jit(solution)/shard_map/first_part/pallas_call | solution.py:203
  105.2 3.8 %raw_weights.3 = (bf16[1024,4096]{1,0:T(8,128)(2,1)S(1)}, f32[1,4096]{1,0:T(1,128)S(1)}) custom-call(f32[2,1024,128]{2,1,0:T(8,128)S(1)} %get-tuple-element.17.sums_ref, bf16[2,2048,128]{2,1,0:T(8,128)(2,1)S(1)} %get-tuple-element.18.refs_0_, bf16[2,2048,128]{2,1,0:T(8,128)(2,1)S(1)} %get-tuple-element.19.refs_1_), custom_call_target="tpu_custom_call" | custom-call | flops 2147483648 | bytes 1048576 | tf_op jit(solution)/shard_map/raw_weights/pallas_call | solution.py:261
  109.0 13.6 %all-gather.8 = f32[4,1,4096]{2,1,0:T(1,128)S(1)} all-gather(f32[1,1,4096]{2,1,0:T(1,128)S(1)} %bitcast.39), channel_id=4, replica_groups=mesh['grp'=2,'ctx'=4,'head'=4] {'ctx'}, dimensions={0}, use_global_device_ids=true | all-gather | bytes 81920 | tf_op jit(solution)/shard_map/all_gather | solution.py:416
  122.7 3.8 %raw_weights.2 = (bf16[1024,4096]{1,0:T(8,128)(2,1)S(1)}, f32[1,4096]{1,0:T(1,128)S(1)}) custom-call(f32[2,1024,128]{2,1,0:T(8,128)S(1)} %get-tuple-element.17.sums_ref, bf16[2,2048,128]{2,1,0:T(8,128)(2,1)S(1)} %get-tuple-element.18.refs_0_, bf16[2,2048,128]{2,1,0:T(8,128)(2,1)S(1)} %get-tuple-element.19.refs_1_), custom_call_target="tpu_custom_call" | custom-call | flops 2147483648 | bytes 1048576 | tf_op jit(solution)/shard_map/raw_weights/pallas_call | solution.py:261
  126.5 13.3 %all-gather.7 = f32[4,1,4096]{2,1,0:T(1,128)S(1)} all-gather(f32[1,1,4096]{2,1,0:T(1,128)S(1)} %bitcast.38), channel_id=3, replica_groups=mesh['grp'=2,'ctx'=4,'head'=4] {'ctx'}, dimensions={0}, use_global_device_ids=true | all-gather | bytes 81920 | tf_op jit(solution)/shard_map/all_gather | solution.py:416
  139.9 3.5 %weighted_sums.2.refs_2_ = f32[2,1024,128]{2,1,0:T(8,128)} custom-call(bf16[1024,4096]{1,0:T(8,128)(2,1)S(1)} %get-tuple-element.22.raw_ref, f32[4,4096]{1,0:T(4,128)S(1)} %bitcast.34, bf16[2,2048,128]{2,1,0:T(8,128)(2,1)S(1)} %get-tuple-element.18.refs_0_, bf16[2,2048,128]{2,1,0:T(8,128)(2,1)S(1)} %get-tuple-element.19.refs_1_), custom_call_target="tpu_custom_call" | custom-call | flops 2147483648 | bytes 1048576 | tf_op jit(solution)/shard_map/weighted_sums/pallas_call | solution.py:317
  143.4 0.0 copy-start.5
  143.4 3.5 %weighted_sums.3 = f32[2,1024,128]{2,1,0:T(8,128)} custom-call(bf16[1024,4096]{1,0:T(8,128)(2,1)S(1)} %get-tuple-element.20.raw_ref, f32[4,4096]{1,0:T(4,128)S(1)} %bitcast.35, bf16[2,2048,128]{2,1,0:T(8,128)(2,1)S(1)} %get-tuple-element.18.refs_0_, bf16[2,2048,128]{2,1,0:T(8,128)(2,1)S(1)} %get-tuple-element.19.refs_1_, ...), custom_call_target="tpu_custom_call", output_to_operand_aliasing={{}: (4, {})} | custom-call | flops 2147483648 | bytes 1048576 | tf_op jit(solution)/shard_map/weighted_sums/pallas_call | solution.py:317
  146.9 0.0 all-gather.21.cloned.1.call-done
  146.9 0.0 copy-done.5
  146.9 0.0 copy-start.6
  146.9 1.2 copy-done.6
  148.1 6.7 %place.2 = (bf16[4096,128]{1,0:T(8,128)(2,1)}, bf16[4096,128]{1,0:T(8,128)(2,1)}) custom-call(s32[2,2048]{1,0:T(2,128)S(1)} %bitcast.41, bf16[4,1024,128]{2,1,0:T(8,128)(2,1)S(1)} %copy-done.5, bf16[4,1024,128]{2,1,0:T(8,128)(2,1)S(1)} %bitcast.42), custom_call_target="tpu_custom_call" | custom-call | flops 4294967296 | bytes 4194304 | tf_op jit(solution)/shard_map/place/pallas_call | solution.py:385
  154.8 0.0 all-gather.19.cloned.1.call-done
  154.8 0.0 copy-start.7
  154.8 1.2 copy-done.7
  156.0 7.7 %place.3 = (bf16[4096,128]{1,0:T(8,128)(2,1)}, bf16[4096,128]{1,0:T(8,128)(2,1)}) custom-call(s32[2,2048]{1,0:T(2,128)S(1)} %bitcast.40, bf16[4,1024,128]{2,1,0:T(8,128)(2,1)S(1)} %copy-done.3, bf16[4,1024,128]{2,1,0:T(8,128)(2,1)S(1)} %bitcast.43, bf16[4096,128]{1,0:T(8,128)(2,1)} %get-tuple-element.25.refs_0_, ...), custom_call_target="tpu_custom_call", output_to_operand_aliasing={{0}: (3, {}), {1}: (4, {})} | custom-call | flops 4294967296 | bytes 4194304 | tf_op jit(solution)/shard_map/place/pallas_call | solution.py:385
  (12 shorter events, 0.3 us)
Async XLA Ops:
  7.2 33.7 %all-gather.15.cloned.1.call-start = ((), (), s32[]{:S(2)}) async-start(), calls=%async_computation | async-start | bytes 1310720 | tf_op jit(solution)/shard_map/all_gather | solution.py:416
  9.4 75.2 %all-gather.17.cloned.1.call-start = ((), (), s32[]{:S(2)}) async-start(), calls=%async_computation.1 | async-start | bytes 1310720 | tf_op jit(solution)/shard_map/all_gather | solution.py:416
  10.2 136.7 %all-gather.21.cloned.1.call-start = ((), (), s32[]{:S(2)}) async-start(), calls=%async_computation.3 | async-start | bytes 1310720 | tf_op jit(solution)/shard_map/all_gather | solution.py:416
  42.8 112.0 %all-gather.19.cloned.1.call-start = ((), (), s32[]{:S(2)}) async-start(), calls=%async_computation.2 | async-start | bytes 1310720 | tf_op jit(solution)/shard_map/all_gather | solution.py:416
  61.0 1.0 copy-start
  62.0 2.2 %copy-start.1 = (f32[2,4096,128]{2,1,0:T(8,128)S(1)}, f32[2,4096,128]{2,1,0:T(8,128)}, u32[]{:S(2)}) copy-start(f32[2,4096,128]{2,1,0:T(8,128)} %init_ref.3) | copy-start | bytes 12582916
  64.2 32.3 %copy-start.3 = (bf16[4,1024,128]{2,1,0:T(8,128)(2,1)S(1)}, bf16[4,1024,128]{2,1,0:T(8,128)(2,1)}, u32[]{:S(2)}) copy-start(bf16[4,1024,128]{2,1,0:T(8,128)(2,1)} %all-gather.15.cloned.1.call-done.keys_ref) | copy-start | bytes 3145732
  84.6 2.2 %copy-start.2 = (f32[2,4096,128]{2,1,0:T(8,128)S(1)}, f32[2,4096,128]{2,1,0:T(8,128)}, u32[]{:S(2)}) copy-start(f32[2,4096,128]{2,1,0:T(8,128)} %init_ref.3) | copy-start | bytes 12582916
  86.8 1.2 copy-start.4
  143.4 3.5 %copy-start.5 = (bf16[4,1024,128]{2,1,0:T(8,128)(2,1)S(1)}, bf16[4,1024,128]{2,1,0:T(8,128)(2,1)}, u32[]{:S(2)}) copy-start(bf16[4,1024,128]{2,1,0:T(8,128)(2,1)} %all-gather.17.cloned.1.call-done.keys_ref) | copy-start | bytes 3145732
  146.9 1.2 copy-start.6
  154.8 1.2 copy-start.7
Sparse Core Ops, SparseCore 0:
  10.1 30.7 all-gather.14
  43.0 27.6 all-gather.16
  72.9 27.6 all-gather.20
  102.0 28.8 all-gather.18

commit v2 on v1

v2 whole, which is shorter than its diff:
```python
import functools
import math

import jax
import jax.numpy as jnp
from jax import lax
from jax.experimental import pallas as pl
from jax.experimental.pallas import tpu as pltpu
from jax.sharding import PartitionSpec as P

LANES = 128
EXP2_SCALE = 20.0 * math.log2(math.e)
VMEM_LIMIT = 28 * 1024 * 1024
F32 = jnp.float32
BF16 = jnp.bfloat16
NT = (((1,), (1,)), ((), ()))
NN = (((1,), (0,)), ((), ()))


def dot_nt(a, b):
    return lax.dot_general(a, b, NT, preferred_element_type=F32)


def dot_nn(a, b):
    return lax.dot_general(a, b, NN, preferred_element_type=F32)


def unit_rows(x):
    return x * lax.rsqrt(jnp.sum(x * x, axis=-1, keepdims=True) + 1e-06)


def params(**kwargs):
    return pltpu.CompilerParams(vmem_limit_bytes=VMEM_LIMIT, **kwargs)


def whole(shape):
    return pl.BlockSpec(shape, lambda *_: (0,) * len(shape))


def in_vmem():
    return pl.BlockSpec(memory_space=pltpu.VMEM)


def row_to_lanes(row):
    return jnp.transpose(jnp.broadcast_to(row, (LANES, LANES)))


def split_heads(flat_ref, wide_ref):
    wide_ref[...] = flat_ref[...].astype(F32)


def head_rows(wide_ref, head, heads):
    if heads == 1:
        return wide_ref[...]
    return wide_ref[pl.Slice(head, wide_ref.shape[0] // heads, heads), :]


def count_below(all_ref, own_row, count):
    tokens = own_row.shape[1]
    mine = jnp.broadcast_to(own_row, (8, tokens))
    wide = 4 * LANES

    def step(i, total):
        row = all_ref[0, :, pl.ds(pl.multiple_of(i * wide, wide), wide)]
        for s in range(0, wide, LANES):
            column = row_to_lanes(row[:, s : s + LANES])
            for r in range(0, LANES, 8):
                other = jnp.tile(column[r : r + 8], (1, tokens // LANES))
                total += (other < mine).astype(jnp.int32)
        return total

    total = lax.fori_loop(0, count // wide, step, jnp.zeros((8, tokens), jnp.int32))
    return jnp.sum(total, axis=0, keepdims=True)


def one_hot_rows(size, spot):
    slots = lax.broadcasted_iota(jnp.int16, (size, spot.shape[1]), 0)
    return jnp.where(
        slots == spot.astype(jnp.int16), jnp.ones((), BF16), jnp.zeros((), BF16)
    )


def sort_kernel(label_ref, keys_ref, values_ref, *refs):
    out_keys, out_values, out_labels, wide_ref, both_ref, order_ref = refs
    head = pl.program_id(0)
    heads = pl.num_programs(0)
    _, tokens, width = out_keys.shape
    flat = wide_ref.shape[1]

    @pl.when(head == 0)
    def _():
        split_heads(keys_ref, wide_ref.at[0])
        split_heads(values_ref, wide_ref.at[1])

    for side in range(2):
        both_ref[:, side * width : (side + 1) * width] = head_rows(
            wide_ref.at[side], head, flat // tokens
        ).astype(BF16)
    label = label_ref[0]
    order = label * tokens + lax.broadcasted_iota(jnp.int32, label.shape, 1)
    order_ref[0] = order
    spot = count_below(order_ref, order, tokens)
    digits = jnp.concatenate(
        [
            jnp.broadcast_to(label >> 6, (8, tokens)),
            jnp.broadcast_to(label & 63, (8, tokens)),
        ],
        axis=0,
    )
    digits = digits.astype(F32).astype(BF16)
    rows = 512
    for r in range(0, tokens, rows):
        pick = one_hot_rows(rows, spot - r)
        moved = dot_nn(pick, both_ref[...]).astype(BF16)
        out_keys[0, r : r + rows] = moved[:, :width]
        out_values[0, r : r + rows] = moved[:, width:]
        digit = dot_nt(digits, pick)
        out_labels[0, :, r : r + rows] = (
            digit[0:1] * 64.0 + digit[8:9]
        ).astype(jnp.int32)


def sort_tokens(labels, keys, values):
    heads, tokens = labels.shape
    flat, width = keys.shape
    rows = jax.ShapeDtypeStruct((heads, tokens, width), BF16)
    row_block = pl.BlockSpec((1, tokens, width), lambda h: (h, 0, 0))
    label_block = pl.BlockSpec((1, 1, tokens), lambda h: (h, 0, 0))
    return pl.pallas_call(
        sort_kernel,
        grid=(heads,),
        in_specs=[label_block, whole(keys.shape), whole(values.shape)],
        out_specs=(row_block, row_block, label_block),
        out_shape=(rows, rows, jax.ShapeDtypeStruct((heads, 1, tokens), jnp.int32)),
        scratch_shapes=[
            pltpu.VMEM((2, flat, width), F32),
            pltpu.VMEM((tokens, 2 * width), BF16),
            pltpu.VMEM((1, 1, tokens), jnp.int32),
        ],
        compiler_params=params(),
        cost_estimate=pl.CostEstimate(
            flops=4 * heads * tokens * tokens * width,
            bytes_accessed=8 * flat * width,
            transcendentals=0,
        ),
        name="sort_tokens",
    )(labels[:, None, :], keys, values)


def windows_kernel(start_ref, values_ref, *out_refs):
    heads = values_ref.shape[0]
    for m, out_ref in enumerate(out_refs):
        size = out_ref.shape[1]
        for h in range(heads):
            start = pl.multiple_of(start_ref[h, m], 16)
            out_ref[h] = values_ref[h, pl.ds(start, size), :]


def windows(starts, values, size):
    heads, tokens, width = values.shape
    n = starts.shape[1]
    out = jax.ShapeDtypeStruct((heads, size, width), BF16)
    return pl.pallas_call(
        windows_kernel,
        in_specs=[pl.BlockSpec(memory_space=pltpu.SMEM), in_vmem()],
        out_specs=(in_vmem(),) * n,
        out_shape=(out,) * n,
        compiler_params=params(),
        cost_estimate=pl.CostEstimate(
            flops=0, bytes_accessed=4 * n * heads * size * width, transcendentals=0
        ),
        name="windows",
    )(starts, values)


def rank_kernel(own_ref, all_ref, rank_ref):
    rank_ref[0] = count_below(all_ref, own_ref[0], all_ref.shape[2])


def own_ranks(own, everyone):
    heads, _, tokens = own.shape
    count = everyone.shape[2]
    own_block = pl.BlockSpec((1, 1, tokens), lambda h: (h, 0, 0))
    return pl.pallas_call(
        rank_kernel,
        grid=(heads,),
        in_specs=[own_block, pl.BlockSpec((1, 1, count), lambda h: (h, 0, 0))],
        out_specs=own_block,
        out_shape=jax.ShapeDtypeStruct((heads, 1, tokens), jnp.int32),
        compiler_params=params(),
        cost_estimate=pl.CostEstimate(
            flops=3 * heads * tokens * count, bytes_accessed=65536, transcendentals=0
        ),
        name="own_ranks",
    )(own, everyone)


def totals_kernel(keys_ref, cent_ref, tot_ref, unit_ref, sum_ref):
    step = pl.program_id(1)
    tokens = unit_ref.shape[0]

    @pl.when(step == 0)
    def _():
        unit_ref[...] = unit_rows(keys_ref[0].astype(F32)).astype(BF16)
        sum_ref[...] = jnp.zeros_like(sum_ref)

    cent = unit_rows(cent_ref[0]).astype(BF16)
    part = 256
    for t in range(0, tokens, part):
        raw = jnp.exp2(dot_nt(cent, unit_ref[t : t + part, :]) * EXP2_SCALE)
        sum_ref[:, t : t + part] += jnp.sum(raw.reshape(-1, 8, part), axis=0)

    @pl.when(step == pl.num_programs(1) - 1)
    def _():
        tot_ref[0] = jnp.sum(sum_ref[...], axis=0, keepdims=True)


def own_totals(keys, cents):
    heads, count, width = cents.shape
    tokens = keys.shape[1]
    rows = min(1024, count)
    return pl.pallas_call(
        totals_kernel,
        grid=(heads, count // rows),
        in_specs=[
            pl.BlockSpec((1, tokens, width), lambda h, c: (h, 0, 0)),
            pl.BlockSpec((1, rows, width), lambda h, c: (h, c, 0)),
        ],
        out_specs=pl.BlockSpec((1, 1, tokens), lambda h, c: (h, 0, 0)),
        out_shape=jax.ShapeDtypeStruct((heads, 1, tokens), F32),
        scratch_shapes=[
            pltpu.VMEM((tokens, width), BF16),
            pltpu.VMEM((8, tokens), F32),
        ],
        compiler_params=params(),
        cost_estimate=pl.CostEstimate(
            flops=4 * heads * tokens * count * width,
            bytes_accessed=cents.size * 4,
            transcendentals=heads * tokens * count,
        ),
        name="own_totals",
    )(keys, cents)


def scale_rows(unit, inverse, scaled_ref):
    for t in range(0, unit.shape[0], LANES):
        scaled_ref[t : t + LANES] = (
            unit[t : t + LANES, :].astype(F32) * row_to_lanes(inverse[:, t : t + LANES])
        ).astype(BF16)


def first_kernel(fresh, _, keys_ref, tot_ref, init_ref, *refs):
    if fresh:
        sums_ref, unit_ref, scaled_ref, cent_ref = refs
    else:
        before_ref, sums_ref, unit_ref, scaled_ref, cent_ref = refs
    tokens = unit_ref.shape[1]
    cent_ref[...] = unit_rows(init_ref[0]).astype(BF16)
    if fresh:
        sums_ref[...] = jnp.zeros_like(sums_ref)
    else:
        sums_ref[...] = before_ref[...]
    unit_ref[0] = unit_rows(keys_ref[0].astype(F32)).astype(BF16)
    scale_rows(unit_ref[0], 1.0 / tot_ref[0], scaled_ref)
    part = 256
    for t in range(0, tokens, part):
        raw = jnp.exp2(dot_nt(cent_ref[...], unit_ref[0, t : t + part, :]) * EXP2_SCALE)
        sums_ref[0] += dot_nn(raw.astype(BF16), scaled_ref[t : t + part])


def first_block(me, keys, totals, init, n, before):
    heads, tokens, width = keys.shape
    rows = init.shape[1] // n
    share = pl.BlockSpec((1, rows, width), lambda h, me: (h, 0, 0))
    key_block = pl.BlockSpec((1, tokens, width), lambda h, me: (h, 0, 0))
    in_specs = [
        key_block,
        pl.BlockSpec((1, 1, tokens), lambda h, me: (h, 0, 0)),
        pl.BlockSpec((1, rows, width), lambda h, me: (h, me[0], 0)),
    ]
    args = [me, keys, totals, init]
    aliases = {}
    if before is not None:
        in_specs.append(share)
        args.append(before)
        aliases = {4: 0}
    return pl.pallas_call(
        functools.partial(first_kernel, before is None),
        grid_spec=pltpu.PrefetchScalarGridSpec(
            num_scalar_prefetch=1,
            grid=(heads,),
            in_specs=in_specs,
            out_specs=(share, key_block),
            scratch_shapes=[
                pltpu.VMEM((tokens, width), BF16),
                pltpu.VMEM((rows, width), BF16),
            ],
        ),
        out_shape=(
            jax.ShapeDtypeStruct((heads, rows, width), F32),
            jax.ShapeDtypeStruct((heads, tokens, width), BF16),
        ),
        input_output_aliases=aliases,
        compiler_params=params(),
        cost_estimate=pl.CostEstimate(
            flops=8 * heads * tokens * rows * width,
            bytes_accessed=4 * heads * rows * width * 4,
            transcendentals=heads * tokens * rows,
        ),
        name="first_block",
    )(*args)


def raw_kernel(blocks, sums_ref, *refs):
    units = refs[:blocks]
    raw_ref, total_ref, cent_ref = refs[blocks:]
    head = pl.program_id(0)
    cent_ref[...] = unit_rows(sums_ref[0]).astype(BF16)
    part = 256
    start = 0
    for unit_ref in units:
        for t in range(0, unit_ref.shape[1], part):
            here = slice(start + t, start + t + part)
            raw = jnp.exp2(dot_nt(cent_ref[...], unit_ref[0, t : t + part, :]) * EXP2_SCALE)
            raw_ref[head, :, here] = raw.astype(BF16)
            total = jnp.sum(raw.reshape(-1, 8, part), axis=0)
            total_ref[0, :, here] = jnp.sum(total, axis=0, keepdims=True)
        start += unit_ref.shape[1]


def raw_weights(sums, units):
    heads, rows, width = sums.shape
    tokens = units[0].shape[1]
    count = tokens * len(units)
    return pl.pallas_call(
        functools.partial(raw_kernel, len(units)),
        grid=(heads,),
        in_specs=[pl.BlockSpec((1, rows, width), lambda h: (h, 0, 0))]
        + [pl.BlockSpec((1, tokens, width), lambda h: (h, 0, 0))] * len(units),
        out_specs=(in_vmem(), pl.BlockSpec((1, 1, count), lambda h: (h, 0, 0))),
        out_shape=(
            pltpu.VMEM((heads, rows, count), BF16),
            jax.ShapeDtypeStruct((heads, 1, count), F32),
        ),
        scratch_shapes=[pltpu.VMEM((rows, width), BF16)],
        compiler_params=params(),
        cost_estimate=pl.CostEstimate(
            flops=4 * heads * rows * count * width,
            bytes_accessed=2 * heads * count * width,
            transcendentals=heads * rows * count,
        ),
        name="raw_weights",
    )(sums, *units)


def sums_kernel(blocks, raw_ref, *refs):
    totals, units = refs[:blocks], refs[blocks : 2 * blocks]
    out_ref, scaled_ref, sum_ref = refs[2 * blocks :]
    head = pl.program_id(0)
    tokens = units[0].shape[1]
    for m, unit_ref in enumerate(units):
        row_total = totals[0][0, :, m * tokens : (m + 1) * tokens]
        for d in range(1, blocks):
            peer = m ^ d
            row_total += totals[d][0, :, peer * tokens : (peer + 1) * tokens]
        scale_rows(unit_ref[0], 1.0 / row_total, scaled_ref)
        more = dot_nn(raw_ref[head, :, m * tokens : (m + 1) * tokens], scaled_ref[...])
        if m == 0:
            sum_ref[...] = more
        else:
            sum_ref[...] += more
    out_ref[0] = unit_rows(sum_ref[...])


def weighted_sums(raw, units, totals):
    heads, rows, count = raw.shape
    _, tokens, width = units[0].shape
    blocks = len(units)
    raw = pltpu.with_memory_space_constraint(raw, pltpu.VMEM)
    return pl.pallas_call(
        functools.partial(sums_kernel, blocks),
        grid=(heads,),
        in_specs=[in_vmem()]
        + [pl.BlockSpec((1, 1, count), lambda h: (h, 0, 0))] * blocks
        + [pl.BlockSpec((1, tokens, width), lambda h: (h, 0, 0))] * blocks,
        out_specs=pl.BlockSpec((1, rows, width), lambda h: (h, 0, 0)),
        out_shape=jax.ShapeDtypeStruct((heads, rows, width), F32),
        scratch_shapes=[
            pltpu.VMEM((tokens, width), BF16),
            pltpu.VMEM((rows, width), F32),
        ],
        compiler_params=params(),
        cost_estimate=pl.CostEstimate(
            flops=4 * heads * rows * count * width,
            bytes_accessed=2 * heads * count * width,
            transcendentals=0,
        ),
        name="weighted_sums",
    )(raw, *totals, *units)


def place_kernel(blocks, size, start_ref, gap_ref, spot_ref, *refs):
    keys, values = refs[:blocks], refs[blocks : 2 * blocks]
    out_refs, (rows_ref, near_ref, mixed_ref) = refs[-5:-3], refs[-3:]
    step = pl.program_id(0)
    heads, tokens, width = keys[0].shape

    @pl.when(step == 0)
    def _():
        rows_ref[:, :, width:] = jnp.zeros((heads, blocks * size, width), BF16)
        for h in range(heads):
            for m in range(blocks):
                start = pl.multiple_of(start_ref[h, m], 16)
                gap = pl.multiple_of(gap_ref[h, m], 16)
                rows_ref[h, m * size : (m + 1) * size, :width] = keys[m][
                    h, pl.ds(start, size), :
                ]
                rows_ref[h, pl.ds(m * size + gap, values[m].shape[1]), width:] = values[m][h]
                spot = pltpu.roll(spot_ref[h, m : m + 1, :], lax.rem(tokens - start, tokens), 1)
                near_ref[h, :, m * size : (m + 1) * size] = spot[:, :size]

    rows = out_refs[0].shape[0] // heads
    total_size = blocks * size
    part = total_size // 2
    for h in range(heads):
        for t in range(0, total_size, part):
            pick = one_hot_rows(rows, near_ref[h, :, t : t + part] - step * rows)
            more = dot_nn(pick, rows_ref[h, t : t + part, :])
            total = more if t == 0 else total + more
        for side in range(2):
            mixed_ref[side, pl.Slice(h, rows, heads), :] = total[
                :, side * width : (side + 1) * width
            ]
    for side in range(2):
        out_refs[side][...] = mixed_ref[side].astype(BF16)


def place(starts, gaps, spots, keys, values, size, cap):
    blocks = len(keys)
    heads, _, width = keys[0].shape
    rows = 512
    out = jax.ShapeDtypeStruct((heads * cap, width), BF16)
    block = pl.BlockSpec((heads * rows, width), lambda r: (r, 0))
    scalars = pl.BlockSpec(memory_space=pltpu.SMEM)
    return pl.pallas_call(
        functools.partial(place_kernel, blocks, size),
        grid=(cap // rows,),
        in_specs=[scalars, scalars]
        + [whole(x.shape) for x in (spots, *keys, *values)],
        out_specs=(block, block),
        out_shape=(out, out),
        scratch_shapes=[
            pltpu.VMEM((heads, blocks * size, 2 * width), BF16),
            pltpu.VMEM((heads, 1, blocks * size), jnp.int32),
            pltpu.VMEM((2, heads * rows, width), F32),
        ],
        compiler_params=params(),
        cost_estimate=pl.CostEstimate(
            flops=4 * heads * cap * blocks * size * width,
            bytes_accessed=12 * heads * cap * width,
            transcendentals=0,
        ),
        name="place",
    )(starts, gaps, spots, *keys, *values)


def body(key_rows, value_rows, cluster_labels, owner_bounds, init_centroids):
    n = lax.axis_size("ctx")
    me = lax.axis_index("ctx").astype(jnp.int32)
    tokens, heads, width = key_rows.shape
    everyone = n * tokens
    cap = 2 * tokens
    slot = cap // n
    send_size = slot + 16
    key_size = min(tokens, -(-send_size // LANES) * LANES)

    def swap(x, d):
        return lax.ppermute(x, "ctx", [(i, i ^ d) for i in range(n)])

    def cube(x):
        blocks = [x]
        for m in range(1, n):
            low = m & -m
            blocks.append(swap(blocks[m ^ low], low))
        return blocks

    def spread(x):
        return [x] + [swap(x, d) for d in range(1, n)]

    def aligned(start, size):
        return jnp.minimum(start // 16 * 16, tokens - size)

    own_keys, own_values, own_labels = sort_tokens(
        cluster_labels,
        key_rows.reshape(heads * tokens, width),
        value_rows.reshape(heads * tokens, width),
    )
    keys = cube(own_keys)
    labels = spread(own_labels)

    place_ids = jnp.arange(tokens, dtype=jnp.int32)
    orders = [
        labels[m] * everyone + (me ^ m) * tokens + place_ids for m in range(n)
    ]
    own_rank = own_ranks(orders[0], jnp.concatenate(orders, axis=2))
    own_total = own_totals(own_keys, init_centroids)
    shared = spread(jnp.concatenate([own_total, own_rank.astype(F32)], axis=1))
    totals = [x[:, 0:1] for x in shared]
    ranks = jnp.stack([x[:, 1] for x in shared], axis=1).astype(jnp.int32)
    block_labels = jnp.concatenate(labels, axis=1)
    low = lax.dynamic_slice_in_dim(owner_bounds, me, 1, 1)[:, :, None]
    high = lax.dynamic_slice_in_dim(owner_bounds, me + 1, 1, 1)[:, :, None]
    below = jnp.sum((block_labels < low).astype(jnp.int32), axis=2)
    first = jnp.sum(below, axis=1)[:, None, None]
    mine = (block_labels >= low) & (block_labels < high)
    spots = jnp.where(mine, ranks - first, -1)
    key_starts = aligned(below, key_size)
    gaps = aligned(below, send_size) - key_starts

    peers = jnp.stack([me ^ m for m in range(n)])
    peer_low = jnp.take(owner_bounds, peers, axis=1)
    own_below = jnp.sum((own_labels < peer_low[:, :, None]).astype(jnp.int32), axis=2)
    own_windows = windows(aligned(own_below, send_size), own_values, send_size)
    *own_windows, _ = lax.optimization_barrier((*own_windows, keys[-1]))
    values = [own_windows[0]] + [swap(own_windows[d], d) for d in range(1, n)]

    sums, units = None, []
    for m in range(n):
        sums, unit = first_block(me.reshape(1), keys[m], totals[m], init_centroids, n, sums)
        units.append(unit)
    raw, part = raw_weights(sums, units)
    out = weighted_sums(raw, units, spread(part))

    placed = place(key_starts, gaps, spots, keys, values, key_size, cap)
    shape = (cap, heads, width)
    return out, placed[0].reshape(shape), placed[1].reshape(shape)


def solution(mesh):
    placed = (
        P(("grp", "ctx"), "head", None),
        P(("grp", "ctx"), "head", None),
        P("head", ("grp", "ctx")),
        P(("grp", "head"), None),
        P(("grp", "head"), None, None),
    )
    return jax.shard_map(
        body,
        mesh=mesh,
        in_specs=placed,
        out_specs=(
            P(("grp", "head"), "ctx", None),
            P(("grp", "ctx"), "head", None),
            P(("grp", "ctx"), "head", None),
        ),
        check_vma=False,
    )
```

time: 171 us -> 102 us (0.60)
  blocking collectives: 68.5 us -> 0 us
  starting transfers between devices: 0.16 us -> 26.1 us
  between operations: 13.9 us -> 0.98 us
  Pallas kernels: 57.7 us -> 49 us
  waiting for transfers between devices: 14.3 us -> 10 us
    all_gather x5 -> x0, blocking collectives: 68.5 us -> none  [gather(): return lax.all_gather(x, 'ctx')]
    ppermute x0 -> x15, starting transfers between devices: none -> 26.1 us  [swap(): return lax.ppermute(x, 'ctx', [(i, i ^ d) for i in range(n)])]
    all_gather x4 -> x0, waiting for transfers between devices: 13.6 us -> none  [gather(): return lax.all_gather(x, 'ctx')]
    ppermute x0 -> x15, waiting for transfers between devices: none -> 10 us  [swap(): return lax.ppermute(x, 'ctx', [(i, i ^ d) for i in range(n)])]
    pallas_call x10 -> x11, Pallas kernels: 57.7 us -> 49 us  [the longest x4 13.1 us: first_block(): pl.pallas_call(functools.partial(first_kernel, before is None), grid_spec...]
    slice x3, local copies, waits for them, and re-layouts: 4.12 us -> 0.04 us  [body(): ranks = jnp.stack([x[:, 1] for x in shared], axis=1).astype(jnp.int32)]
    unnamed x20 -> x32, local copies, waits for them, and re-layouts: 9.21 us -> 11.8 us
  transfers between devices with their start and end apart: 4 -> 15, of which waited for: 1 -> 2; matrix products, arithmetic and copies ran while one was open for 3% -> 3% of each run, Pallas kernels for 29% -> 28%
where the time goes in v2:
time: 102 us; the launch traced here: 101 us
  Pallas kernels  49 us (48%)
  starting transfers between devices  26.1 us (26%)
  local copies, waits for them, and re-layouts  13.4 us (13%)
  waiting for transfers between devices  10 us (10%)
    ppermute x15, starting transfers between devices, swap(): return lax.ppermute(x, 'ctx', [(i, i ^ d) for i in range(n)])  26.1 us
    pallas_call x4, Pallas kernels, first_block(): pl.pallas_call(functools.partial(first_kernel, before is None), grid_spec...  13.1 us
    unnamed x32, local copies, waits for them, and re-layouts  11.8 us
    ppermute x15, waiting for transfers between devices, swap(): return lax.ppermute(x, 'ctx', [(i, i ^ d) for i in range(n)])  10 us
    pallas_call x1, Pallas kernels, place(): pl.pallas_call(functools.partial(place_kernel, blocks, size), grid=(cap /...  8.5 us
    pallas_call x1, Pallas kernels, own_totals(): pl.pallas_call(totals_kernel, grid=(heads, count // rows), in_specs=[pl.B...  7.11 us
    pallas_call x1, Pallas kernels, weighted_sums(): pl.pallas_call(functools.partial(sums_kernel, blocks), grid=(heads,), in_...  6.35 us
    pallas_call x1, Pallas kernels, raw_weights(): pl.pallas_call(functools.partial(raw_kernel, len(units)), grid=(heads,),...  5.05 us
  transfers between devices with their start and end apart: 15, of which 2 were waited for; matrix products, arithmetic and copies ran while one was open for 3% of the time, Pallas kernels for 28%

profile of v2, /device:TPU:0, one launch (start us, length us, event | category | flops | bytes accessed | tf_op | source)
XLA Modules:
  0.0 100.5 jit_solution(9261840839400026626)
XLA Ops:
  0.6 0.0 copy-start.14
  0.6 0.7 broadcast_in_dim.10.label_ref
  1.4 1.0 %copy-done.2 = bf16[1024,2,128]{2,1,0:T(2,128)(2,1)S(1)} copy-done((bf16[1024,2,128]{2,1,0:T(2,128)(2,1)S(1)}, bf16[1024,2,128]{2,1,0:T(2,128)(2,1)}, u32[]{:S(2)}) %copy-start.2) | copy-done | bytes 524312
  2.4 1.0 %copy-done.3 = bf16[1024,2,128]{2,1,0:T(2,128)(2,1)S(1)} copy-done((bf16[1024,2,128]{2,1,0:T(2,128)(2,1)S(1)}, bf16[1024,2,128]{2,1,0:T(2,128)(2,1)}, u32[]{:S(2)}) %copy-start.3) | copy-done | bytes 524312
  3.4 3.9 %sort_tokens.1 = (bf16[2,1024,128]{2,1,0:T(8,128)(2,1)S(1)}, bf16[2,1024,128]{2,1,0:T(8,128)(2,1)S(1)}, s32[2,1,1024]{2,1,0:T(1,128)S(1)}) custom-call(s32[2,1,1024]{2,1,0:T(1,128)S(1)} %broadcast_in_dim.10.label_ref, bf16[2048,128]{1,0:T(8,128)(2,1)S(1)} %bitcast.19, bf16[2048,128]{1,0:T(8,128)(2,1)S(1)} %bitcast.20), custom_call_target="tpu_custom_call" | custom-call | flops 1073741824 | bytes 2097152 | tf_op jit(solution)/shard_map/sort_tokens/pallas_call | solution.py:129
  7.4 0.0 copy-start.4
  7.4 5.1 %collective-permute-start.4 = (s32[2,1,1024]{2,1,0:T(1,128)S(1)}, s32[2,1,1024]{2,1,0:T(1,128)S(1)}, u32[]{:S(2)}, u32[]{:S(2)}) collective-permute-start(s32[2,1,1024]{2,1,0:T(1,128)S(1)} %get-tuple-element.27), channel_id=1, source_target_pairs={{0,12},{4,8},{8,4},{12,0},{1,13},{5,9},{9,5},{13,1},{2,14},{6,10},... | collective-permute-start | bytes 24584 | tf_op jit(solution)/shard_map/ppermute | solution.py:478
  12.5 0.0 collective-permute-start.3
  12.5 0.6 collective-permute-start.2
  13.1 1.4 %collective-permute-start.7 = (bf16[2,1024,128]{2,1,0:T(8,128)(2,1)S(1)}, bf16[2,1024,128]{2,1,0:T(8,128)(2,1)S(1)}, u32[]{:S(2)}, u32[]{:S(2)}) collective-permute-start(bf16[2,1024,128]{2,1,0:T(8,128)(2,1)S(1)} %get-tuple-element.26.keys_ref.refs_0_), channel_id=1, source_target_pairs={{0,4},{4,0},{8,12},{12,8},{1,5},{5,1},{9,13},{13,9},{2,6},{6,2},{1... | collective-permute-start | bytes 1572872 | tf_op jit(solution)/shard_map/ppermute | solution.py:478
  14.5 2.9 %collective-permute-start = (bf16[2,1024,128]{2,1,0:T(8,128)(2,1)S(1)}, bf16[2,1024,128]{2,1,0:T(8,128)(2,1)S(1)}, u32[]{:S(2)}, u32[]{:S(2)}) collective-permute-start(bf16[2,1024,128]{2,1,0:T(8,128)(2,1)S(1)} %get-tuple-element.26.keys_ref.refs_0_), channel_id=1, source_target_pairs={{0,8},{4,12},{8,0},{12,4},{1,9},{5,13},{9,1},{13,5},{2,10},{6,14},... | collective-permute-start | bytes 1572872 | tf_op jit(solution)/shard_map/ppermute | solution.py:478
  17.4 0.1 fusion.3
  17.5 0.8 copy.13
  18.3 0.6 gather_fusion
  18.9 0.1 compare_and_fusion
  18.9 0.1 select_bitcast_fusion
  19.0 0.1 copy.14
  19.1 0.0 copy-start
  19.1 2.2 %copy-done = f32[2,4096,128]{2,1,0:T(8,128)S(1)} copy-done((f32[2,4096,128]{2,1,0:T(8,128)S(1)}, f32[2,4096,128]{2,1,0:T(8,128)}, u32[]{:S(2)}) %copy-start) | copy-done | bytes 4194328
  21.3 7.1 %own_totals.1.tot_ref = f32[2,1,1024]{2,1,0:T(1,128)S(1)} custom-call(bf16[2,1024,128]{2,1,0:T(8,128)(2,1)S(1)} %get-tuple-element.26.keys_ref.refs_0_, f32[2,4096,128]{2,1,0:T(8,128)S(1)} %copy-done), custom_call_target="tpu_custom_call" | custom-call | flops 4294967296 | bytes 4194304 | tf_op jit(solution)/shard_map/own_totals/pallas_call | solution.py:222
  28.4 0.2 convert_reduce_fusion.2
  28.7 3.2 %first_block.4 = (f32[2,1024,128]{2,1,0:T(8,128)S(1)}, bf16[2,1024,128]{2,1,0:T(8,128)(2,1)S(1)}) custom-call(s32[1]{0:T(128)} %bitcast._, bf16[2,1024,128]{2,1,0:T(8,128)(2,1)S(1)} %get-tuple-element.26.keys_ref.refs_0_, f32[2,1,1024]{2,1,0:T(1,128)S(1)} %own_totals.1.tot_ref, f32[2,4096,128]{2,1,0:T(8,128)S(1)} %copy-done), custom_call_target="tpu_custom_call" | custom-call | flops 2147483648 | bytes 4194304 | tf_op jit(solution)/shard_map/first_block/pallas_call | solution.py:287
  31.9 0.0 copy-start.10
  31.9 1.0 copy-done.10
  32.8 0.6 windows.1
  33.5 0.2 dynamic-slice_reduce_fusion
  33.7 0.0 collective-permute-done.4
  33.7 0.0 collective-permute-done.3
  33.8 0.0 collective-permute-done.2
  33.8 4.4 %own_ranks.1 = s32[2,1,1024]{2,1,0:T(1,128)S(1)} custom-call(s32[2,1,1024]{2,1,0:T(1,128)S(1)} %iota_add_fusion.3.own_ref, s32[2,1,4096]{2,1,0:T(1,128)S(1)} %pad_add_fusion.all_ref), custom_call_target="tpu_custom_call" | custom-call | flops 25165824 | bytes 65536 | tf_op jit(solution)/shard_map/own_ranks/pallas_call | solution.py:184
  38.3 0.1 collective-permute-start.8
  38.4 0.6 collective-permute-start.6
  39.0 3.7 %collective-permute-start.5 = (f32[2,2,1024]{2,1,0:T(2,128)S(1)}, f32[2,2,1024]{2,1,0:T(2,128)S(1)}, u32[]{:S(2)}, u32[]{:S(2)}) collective-permute-start(f32[2,2,1024]{2,1,0:T(2,128)S(1)} %pad_maximum_fusion), channel_id=1, source_target_pairs={{0,12},{4,8},{8,4},{12,0},{1,13},{5,9},{9,5},{13,1},{2,14},{6,10},... | collective-permute-start | bytes 49160 | tf_op jit(solution)/shard_map/ppermute | solution.py:478
  42.7 0.3 convert_reduce_fusion
  43.0 0.0 collective-permute-done.8
  43.1 0.0 collective-permute-done.6
  43.1 0.0 collective-permute-done.keys_ref.refs_2_
  43.1 2.2 %collective-permute-start.1 = (bf16[2,1024,128]{2,1,0:T(8,128)(2,1)S(1)}, bf16[2,1024,128]{2,1,0:T(8,128)(2,1)S(1)}, u32[]{:S(2)}, u32[]{:S(2)}) collective-permute-start(bf16[2,1024,128]{2,1,0:T(8,128)(2,1)S(1)} %collective-permute-done.keys_ref.refs_2_), channel_id=1, source_target_pairs={{0,4},{4,0},{8,12},{12,8},{1,5},{5,1},{9,13},{13,9},{2,6},{6,2},{1... | collective-permute-start | bytes 1572872 | tf_op jit(solution)/shard_map/ppermute | solution.py:478
  45.3 0.0 collective-permute-done.5
  45.3 0.0 collective-permute-done.7.keys_ref.refs_1_
  45.3 0.0 copy-start.1
  45.3 2.4 %copy-done.1 = f32[2,4096,128]{2,1,0:T(8,128)S(1)} copy-done((f32[2,4096,128]{2,1,0:T(8,128)S(1)}, f32[2,4096,128]{2,1,0:T(8,128)}, u32[]{:S(2)}) %copy-start.1) | copy-done | bytes 4194328
  47.7 1.2 %copy-done.11 = f32[2,1024,128]{2,1,0:T(8,128)S(1)} copy-done((f32[2,1024,128]{2,1,0:T(8,128)S(1)}, f32[2,1024,128]{2,1,0:T(8,128)}, u32[]{:S(2)}) %copy-start.11) | copy-done | bytes 1048600
  48.9 3.3 %first_block.5 = (f32[2,1024,128]{2,1,0:T(8,128)S(1)}, bf16[2,1024,128]{2,1,0:T(8,128)(2,1)S(1)}) custom-call(s32[1]{0:T(128)} %bitcast._, bf16[2,1024,128]{2,1,0:T(8,128)(2,1)S(1)} %collective-permute-done.7.keys_ref.refs_1_, f32[2,1,1024]{2,1,0:T(1,128)S(1)} %get-tuple-element.56.tot_ref, ...), custom_call_target="tpu_custom_call", output_to_operand_aliasing={{0}: (4, {})} | custom-call | flops 2147483648 | bytes 4194304 | tf_op jit(solution)/shard_map/first_block/pallas_call | solution.py:287
  52.2 3.3 %first_block.6 = (f32[2,1024,128]{2,1,0:T(8,128)S(1)}, bf16[2,1024,128]{2,1,0:T(8,128)(2,1)S(1)}) custom-call(s32[1]{0:T(128)} %bitcast._, bf16[2,1024,128]{2,1,0:T(8,128)(2,1)S(1)} %collective-permute-done.keys_ref.refs_2_, f32[2,1,1024]{2,1,0:T(1,128)S(1)} %get-tuple-element.58.tot_ref, ...), custom_call_target="tpu_custom_call", output_to_operand_aliasing={{0}: (4, {})} | custom-call | flops 2147483648 | bytes 4194304 | tf_op jit(solution)/shard_map/first_block/pallas_call | solution.py:287
  55.5 0.0 collective-permute-done.1.keys_ref.refs_3_
  55.5 3.3 %first_block.7 = (f32[2,1024,128]{2,1,0:T(8,128)S(1)}, bf16[2,1024,128]{2,1,0:T(8,128)(2,1)S(1)}) custom-call(s32[1]{0:T(128)} %bitcast._, bf16[2,1024,128]{2,1,0:T(8,128)(2,1)S(1)} %collective-permute-done.1.keys_ref.refs_3_, f32[2,1,1024]{2,1,0:T(1,128)S(1)} %get-tuple-element.60.tot_ref, ...), custom_call_target="tpu_custom_call", output_to_operand_aliasing={{0}: (4, {})} | custom-call | flops 2147483648 | bytes 4194304 | tf_op jit(solution)/shard_map/first_block/pallas_call | solution.py:287
  58.9 0.0 copy-start.12
  58.9 1.0 copy-done.12
  59.8 1.2 %copy-done.13 = f32[2,1024,128]{2,1,0:T(8,128)S(1)} copy-done((f32[2,1024,128]{2,1,0:T(8,128)S(1)}, f32[2,1024,128]{2,1,0:T(8,128)}, u32[]{:S(2)}) %copy-start.13) | copy-done | bytes 1048600
  61.1 5.0 %raw_weights.1 = (bf16[2,1024,4096]{2,1,0:T(8,128)(2,1)S(1)}, f32[2,1,4096]{2,1,0:T(1,128)S(1)}) custom-call(f32[2,1024,128]{2,1,0:T(8,128)S(1)} %copy-done.13, bf16[2,1024,128]{2,1,0:T(8,128)(2,1)S(1)} %get-tuple-element.32.refs_0_.refs_4_, bf16[2,1024,128]{2,1,0:T(8,128)(2,1)S(1)} %get-tuple-element.33.refs_1_.refs_5_, ...), custom_call_target="tpu_custom_call" | custom-call | flops 4294967296 | bytes 2097152 | tf_op jit(solution)/shard_map/raw_weights/pallas_call | solution.py:335
  66.1 3.3 %collective-permute-start.11 = (f32[2,1,4096]{2,1,0:T(1,128)S(1)}, f32[2,1,4096]{2,1,0:T(1,128)S(1)}, u32[]{:S(2)}, u32[]{:S(2)}) collective-permute-start(f32[2,1,4096]{2,1,0:T(1,128)S(1)} %get-tuple-element.37.refs_0_), channel_id=1, source_target_pairs={{0,12},{4,8},{8,4},{12,0},{1,13},{5,9},{9,5},{13,1},{2,14},{6,10},... | collective-permute-start | bytes 98312 | tf_op jit(solution)/shard_map/ppermute | solution.py:478
  69.4 0.0 collective-permute-start.10
  69.4 1.2 %collective-permute-start.9 = (f32[2,1,4096]{2,1,0:T(1,128)S(1)}, f32[2,1,4096]{2,1,0:T(1,128)S(1)}, u32[]{:S(2)}, u32[]{:S(2)}) collective-permute-start(f32[2,1,4096]{2,1,0:T(1,128)S(1)} %get-tuple-element.37.refs_0_), channel_id=1, source_target_pairs={{0,4},{4,0},{8,12},{12,8},{1,5},{5,1},{9,13},{13,9},{2,6},{6,2},{1... | collective-permute-start | bytes 98312 | tf_op jit(solution)/shard_map/ppermute | solution.py:478
  70.6 0.1 fusion.1.spot_ref
  70.7 0.9 collective-permute-start.12
  71.6 2.9 %collective-permute-start.13 = (bf16[2,528,128]{2,1,0:T(8,128)(2,1)S(1)}, bf16[2,528,128]{2,1,0:T(8,128)(2,1)S(1)}, u32[]{:S(2)}, u32[]{:S(2)}) collective-permute-start(bf16[2,528,128]{2,1,0:T(8,128)(2,1)S(1)} %get-tuple-element.45), channel_id=1, source_target_pairs={{0,8},{4,12},{8,0},{12,4},{1,9},{5,13},{9,1},{13,5},{2,10},{6,14},... | collective-permute-start | bytes 811016 | tf_op jit(solution)/shard_map/ppermute | solution.py:478
  74.5 0.0 collective-permute-done.11.refs_3_
  74.5 1.1 %collective-permute-start.14 = (bf16[2,528,128]{2,1,0:T(8,128)(2,1)S(1)}, bf16[2,528,128]{2,1,0:T(8,128)(2,1)S(1)}, u32[]{:S(2)}, u32[]{:S(2)}) collective-permute-start(bf16[2,528,128]{2,1,0:T(8,128)(2,1)S(1)} %get-tuple-element.46), channel_id=1, source_target_pairs={{0,12},{4,8},{8,4},{12,0},{1,13},{5,9},{9,5},{13,1},{2,14},{6,10},... | collective-permute-start | bytes 811016 | tf_op jit(solution)/shard_map/ppermute | solution.py:478
  75.6 0.4 collective-permute-done.10.refs_2_
  76.1 6.4 %weighted_sums.1 = f32[2,1024,128]{2,1,0:T(8,128)} custom-call(bf16[2,1024,4096]{2,1,0:T(8,128)(2,1)S(1)} %get-tuple-element.36.raw_ref, f32[2,1,4096]{2,1,0:T(1,128)S(1)} %get-tuple-element.37.refs_0_, f32[2,1,4096]{2,1,0:T(1,128)S(1)} %collective-permute-done.9.refs_1_, f32[2,1,4096]{2,1,0:T(1,128)S(1)} %collective-permute-done.10.refs_2_, ...), custom_call_target="tpu_custom_call" | custom-call | flops 4294967296 | bytes 2097152 | tf_op jit(solution)/shard_map/weighted_sums/pallas_call | solution.py:380
  82.4 9.6 %collective-permute-done.13.refs_6_ = bf16[2,528,128]{2,1,0:T(8,128)(2,1)S(1)} collective-permute-done((bf16[2,528,128]{2,1,0:T(8,128)(2,1)S(1)}, bf16[2,528,128]{2,1,0:T(8,128)(2,1)S(1)}, u32[]{:S(2)}, u32[]{:S(2)}) %collective-permute-start.13) | collective-permute-done | bytes 270368 | tf_op jit(solution)/shard_map/ppermute | solution.py:478
  92.0 0.0 collective-permute-done.14.refs_7_
  92.0 8.5 %place.1 = (bf16[4096,128]{1,0:T(8,128)(2,1)}, bf16[4096,128]{1,0:T(8,128)(2,1)}) custom-call(s32[2,4]{1,0:T(2,128)S(1)} %broadcast_minimum_fusion.start_ref, s32[2,4]{1,0:T(2,128)S(1)} %get-tuple-element.53.gap_ref, s32[2,4,1024]{2,1,0:T(4,128)S(1)} %fusion.1.spot_ref, bf16[2,1024,128]{2,1,0:T(8,128)(2,1)S(1)} %copy-done.5, ...), custom_call_target="tpu_custom_call" | custom-call | flops 5368709120 | bytes 6291456 | tf_op jit(solution)/shard_map/place/pallas_call | solution.py:445
  (33 shorter events, 0.2 us)
Async XLA Ops:
  0.6 32.8 %copy-start.14 = (s32[2,5]{1,0:T(2,128)S(1)}, s32[2,5]{1,0:T(2,128)}, u32[]{:S(2)}) copy-start(s32[2,5]{1,0:T(2,128)} %param.8) | copy-start | bytes 124
  1.4 1.0 %copy-start.2 = (bf16[1024,2,128]{2,1,0:T(2,128)(2,1)S(1)}, bf16[1024,2,128]{2,1,0:T(2,128)(2,1)}, u32[]{:S(2)}) copy-start(bf16[1024,2,128]{2,1,0:T(2,128)(2,1)} %param.5) | copy-start | bytes 1572868
  2.4 1.0 %copy-start.3 = (bf16[1024,2,128]{2,1,0:T(2,128)(2,1)S(1)}, bf16[1024,2,128]{2,1,0:T(2,128)(2,1)}, u32[]{:S(2)}) copy-start(bf16[1024,2,128]{2,1,0:T(2,128)(2,1)} %param.6) | copy-start | bytes 1572868
  7.4 48.2 %copy-start.4 = (bf16[2,1024,128]{2,1,0:T(8,128)(2,1)}, bf16[2,1024,128]{2,1,0:T(8,128)(2,1)S(1)}, u32[]{:S(2)}) copy-start(bf16[2,1024,128]{2,1,0:T(8,128)(2,1)S(1)} %get-tuple-element.26.keys_ref.refs_0_) | copy-start | bytes 1572868
  7.4 26.3 %collective-permute-start.4 = (s32[2,1,1024]{2,1,0:T(1,128)S(1)}, s32[2,1,1024]{2,1,0:T(1,128)S(1)}, u32[]{:S(2)}, u32[]{:S(2)}) collective-permute-start(s32[2,1,1024]{2,1,0:T(1,128)S(1)} %get-tuple-element.27), channel_id=1, source_target_pairs={{0,12},{4,8},{8,4},{12,0},{1,13},{5,9},{9,5},{13,1},{2,14},{6,10},... | collective-permute-start | bytes 24584 | tf_op jit(solution)/shard_map/ppermute | solution.py:478
  12.5 21.2 %collective-permute-start.3 = (s32[2,1,1024]{2,1,0:T(1,128)S(1)}, s32[2,1,1024]{2,1,0:T(1,128)S(1)}, u32[]{:S(2)}, u32[]{:S(2)}) collective-permute-start(s32[2,1,1024]{2,1,0:T(1,128)S(1)} %get-tuple-element.27), channel_id=1, source_target_pairs={{0,8},{4,12},{8,0},{12,4},{1,9},{5,13},{9,1},{13,5},{2,10},{6,14},... | collective-permute-start | bytes 24584 | tf_op jit(solution)/shard_map/ppermute | solution.py:478
  12.5 21.3 %collective-permute-start.2 = (s32[2,1,1024]{2,1,0:T(1,128)S(1)}, s32[2,1,1024]{2,1,0:T(1,128)S(1)}, u32[]{:S(2)}, u32[]{:S(2)}) collective-permute-start(s32[2,1,1024]{2,1,0:T(1,128)S(1)} %get-tuple-element.27), channel_id=1, source_target_pairs={{0,4},{4,0},{8,12},{12,8},{1,5},{5,1},{9,13},{13,9},{2,6},{6,2},{1... | collective-permute-start | bytes 24584 | tf_op jit(solution)/shard_map/ppermute | solution.py:478
  13.1 32.2 %collective-permute-start.7 = (bf16[2,1024,128]{2,1,0:T(8,128)(2,1)S(1)}, bf16[2,1024,128]{2,1,0:T(8,128)(2,1)S(1)}, u32[]{:S(2)}, u32[]{:S(2)}) collective-permute-start(bf16[2,1024,128]{2,1,0:T(8,128)(2,1)S(1)} %get-tuple-element.26.keys_ref.refs_0_), channel_id=1, source_target_pairs={{0,4},{4,0},{8,12},{12,8},{1,5},{5,1},{9,13},{13,9},{2,6},{6,2},{1... | collective-permute-start | bytes 1572872 | tf_op jit(solution)/shard_map/ppermute | solution.py:478
  14.5 28.6 %collective-permute-start = (bf16[2,1024,128]{2,1,0:T(8,128)(2,1)S(1)}, bf16[2,1024,128]{2,1,0:T(8,128)(2,1)S(1)}, u32[]{:S(2)}, u32[]{:S(2)}) collective-permute-start(bf16[2,1024,128]{2,1,0:T(8,128)(2,1)S(1)} %get-tuple-element.26.keys_ref.refs_0_), channel_id=1, source_target_pairs={{0,8},{4,12},{8,0},{12,4},{1,9},{5,13},{9,1},{13,5},{2,10},{6,14},... | collective-permute-start | bytes 1572872 | tf_op jit(solution)/shard_map/ppermute | solution.py:478
  19.1 2.2 %copy-start = (f32[2,4096,128]{2,1,0:T(8,128)S(1)}, f32[2,4096,128]{2,1,0:T(8,128)}, u32[]{:S(2)}) copy-start(f32[2,4096,128]{2,1,0:T(8,128)} %init_ref.7) | copy-start | bytes 12582916
  31.9 1.0 copy-start.10
  38.3 4.8 %collective-permute-start.8 = (f32[2,2,1024]{2,1,0:T(2,128)S(1)}, f32[2,2,1024]{2,1,0:T(2,128)S(1)}, u32[]{:S(2)}, u32[]{:S(2)}) collective-permute-start(f32[2,2,1024]{2,1,0:T(2,128)S(1)} %pad_maximum_fusion), channel_id=1, source_target_pairs={{0,4},{4,0},{8,12},{12,8},{1,5},{5,1},{9,13},{13,9},{2,6},{6,2},{1... | collective-permute-start | bytes 49160 | tf_op jit(solution)/shard_map/ppermute | solution.py:478
  38.4 4.7 %collective-permute-start.6 = (f32[2,2,1024]{2,1,0:T(2,128)S(1)}, f32[2,2,1024]{2,1,0:T(2,128)S(1)}, u32[]{:S(2)}, u32[]{:S(2)}) collective-permute-start(f32[2,2,1024]{2,1,0:T(2,128)S(1)} %pad_maximum_fusion), channel_id=1, source_target_pairs={{0,8},{4,12},{8,0},{12,4},{1,9},{5,13},{9,1},{13,5},{2,10},{6,14},... | collective-permute-start | bytes 49160 | tf_op jit(solution)/shard_map/ppermute | solution.py:478
  39.0 6.3 %collective-permute-start.5 = (f32[2,2,1024]{2,1,0:T(2,128)S(1)}, f32[2,2,1024]{2,1,0:T(2,128)S(1)}, u32[]{:S(2)}, u32[]{:S(2)}) collective-permute-start(f32[2,2,1024]{2,1,0:T(2,128)S(1)} %pad_maximum_fusion), channel_id=1, source_target_pairs={{0,12},{4,8},{8,4},{12,0},{1,13},{5,9},{9,5},{13,1},{2,14},{6,10},... | collective-permute-start | bytes 49160 | tf_op jit(solution)/shard_map/ppermute | solution.py:478
  43.1 16.7 %copy-start.8 = (bf16[2,1024,128]{2,1,0:T(8,128)(2,1)}, bf16[2,1024,128]{2,1,0:T(8,128)(2,1)S(1)}, u32[]{:S(2)}) copy-start(bf16[2,1024,128]{2,1,0:T(8,128)(2,1)S(1)} %collective-permute-done.keys_ref.refs_2_) | copy-start | bytes 1572868
  43.1 12.4 %collective-permute-start.1 = (bf16[2,1024,128]{2,1,0:T(8,128)(2,1)S(1)}, bf16[2,1024,128]{2,1,0:T(8,128)(2,1)S(1)}, u32[]{:S(2)}, u32[]{:S(2)}) collective-permute-start(bf16[2,1024,128]{2,1,0:T(8,128)(2,1)S(1)} %collective-permute-done.keys_ref.refs_2_), channel_id=1, source_target_pairs={{0,4},{4,0},{8,12},{12,8},{1,5},{5,1},{9,13},{13,9},{2,6},{6,2},{1... | collective-permute-start | bytes 1572872 | tf_op jit(solution)/shard_map/ppermute | solution.py:478
  45.3 14.5 %copy-start.6 = (bf16[2,1024,128]{2,1,0:T(8,128)(2,1)}, bf16[2,1024,128]{2,1,0:T(8,128)(2,1)S(1)}, u32[]{:S(2)}) copy-start(bf16[2,1024,128]{2,1,0:T(8,128)(2,1)S(1)} %collective-permute-done.7.keys_ref.refs_1_) | copy-start | bytes 1572868
  45.3 2.4 %copy-start.1 = (f32[2,4096,128]{2,1,0:T(8,128)S(1)}, f32[2,4096,128]{2,1,0:T(8,128)}, u32[]{:S(2)}) copy-start(f32[2,4096,128]{2,1,0:T(8,128)} %init_ref.7) | copy-start | bytes 12582916
  47.7 1.2 %copy-start.11 = (f32[2,1024,128]{2,1,0:T(8,128)S(1)}, f32[2,1024,128]{2,1,0:T(8,128)}, u32[]{:S(2)}) copy-start(f32[2,1024,128]{2,1,0:T(8,128)} %copy-done.10) | copy-start | bytes 3145732
  58.9 1.0 copy-start.12
  59.8 1.2 %copy-start.13 = (f32[2,1024,128]{2,1,0:T(8,128)S(1)}, f32[2,1024,128]{2,1,0:T(8,128)}, u32[]{:S(2)}) copy-start(f32[2,1024,128]{2,1,0:T(8,128)} %copy-done.12) | copy-start | bytes 3145732
  61.1 31.0 %copy-start.5 = (bf16[2,1024,128]{2,1,0:T(8,128)(2,1)S(1)}, bf16[2,1024,128]{2,1,0:T(8,128)(2,1)}, u32[]{:S(2)}) copy-start(bf16[2,1024,128]{2,1,0:T(8,128)(2,1)} %copy-done.4) | copy-start | bytes 1572868
  61.1 31.0 %copy-start.7 = (bf16[2,1024,128]{2,1,0:T(8,128)(2,1)S(1)}, bf16[2,1024,128]{2,1,0:T(8,128)(2,1)}, u32[]{:S(2)}) copy-start(bf16[2,1024,128]{2,1,0:T(8,128)(2,1)} %copy-done.6) | copy-start | bytes 1572868
  61.1 31.0 %copy-start.9 = (bf16[2,1024,128]{2,1,0:T(8,128)(2,1)S(1)}, bf16[2,1024,128]{2,1,0:T(8,128)(2,1)}, u32[]{:S(2)}) copy-start(bf16[2,1024,128]{2,1,0:T(8,128)(2,1)} %copy-done.8) | copy-start | bytes 1572868
  66.1 8.4 %collective-permute-start.11 = (f32[2,1,4096]{2,1,0:T(1,128)S(1)}, f32[2,1,4096]{2,1,0:T(1,128)S(1)}, u32[]{:S(2)}, u32[]{:S(2)}) collective-permute-start(f32[2,1,4096]{2,1,0:T(1,128)S(1)} %get-tuple-element.37.refs_0_), channel_id=1, source_target_pairs={{0,12},{4,8},{8,4},{12,0},{1,13},{5,9},{9,5},{13,1},{2,14},{6,10},... | collective-permute-start | bytes 98312 | tf_op jit(solution)/shard_map/ppermute | solution.py:478
  69.4 6.7 %collective-permute-start.10 = (f32[2,1,4096]{2,1,0:T(1,128)S(1)}, f32[2,1,4096]{2,1,0:T(1,128)S(1)}, u32[]{:S(2)}, u32[]{:S(2)}) collective-permute-start(f32[2,1,4096]{2,1,0:T(1,128)S(1)} %get-tuple-element.37.refs_0_), channel_id=1, source_target_pairs={{0,8},{4,12},{8,0},{12,4},{1,9},{5,13},{9,1},{13,5},{2,10},{6,14},... | collective-permute-start | bytes 98312 | tf_op jit(solution)/shard_map/ppermute | solution.py:478
  69.4 6.7 %collective-permute-start.9 = (f32[2,1,4096]{2,1,0:T(1,128)S(1)}, f32[2,1,4096]{2,1,0:T(1,128)S(1)}, u32[]{:S(2)}, u32[]{:S(2)}) collective-permute-start(f32[2,1,4096]{2,1,0:T(1,128)S(1)} %get-tuple-element.37.refs_0_), channel_id=1, source_target_pairs={{0,4},{4,0},{8,12},{12,8},{1,5},{5,1},{9,13},{13,9},{2,6},{6,2},{1... | collective-permute-start | bytes 98312 | tf_op jit(solution)/shard_map/ppermute | solution.py:478
  70.7 11.8 %collective-permute-start.12 = (bf16[2,528,128]{2,1,0:T(8,128)(2,1)S(1)}, bf16[2,528,128]{2,1,0:T(8,128)(2,1)S(1)}, u32[]{:S(2)}, u32[]{:S(2)}) collective-permute-start(bf16[2,528,128]{2,1,0:T(8,128)(2,1)S(1)} %get-tuple-element.44), channel_id=1, source_target_pairs={{0,4},{4,0},{8,12},{12,8},{1,5},{5,1},{9,13},{13,9},{2,6},{6,2},{1... | collective-permute-start | bytes 811016 | tf_op jit(solution)/shard_map/ppermute | solution.py:478
  71.6 20.4 %collective-permute-start.13 = (bf16[2,528,128]{2,1,0:T(8,128)(2,1)S(1)}, bf16[2,528,128]{2,1,0:T(8,128)(2,1)S(1)}, u32[]{:S(2)}, u32[]{:S(2)}) collective-permute-start(bf16[2,528,128]{2,1,0:T(8,128)(2,1)S(1)} %get-tuple-element.45), channel_id=1, source_target_pairs={{0,8},{4,12},{8,0},{12,4},{1,9},{5,13},{9,1},{13,5},{2,10},{6,14},... | collective-permute-start | bytes 811016 | tf_op jit(solution)/shard_map/ppermute | solution.py:478
  74.5 17.5 %collective-permute-start.14 = (bf16[2,528,128]{2,1,0:T(8,128)(2,1)S(1)}, bf16[2,528,128]{2,1,0:T(8,128)(2,1)S(1)}, u32[]{:S(2)}, u32[]{:S(2)}) collective-permute-start(bf16[2,528,128]{2,1,0:T(8,128)(2,1)S(1)} %get-tuple-element.46), channel_id=1, source_target_pairs={{0,12},{4,8},{8,4},{12,0},{1,13},{5,9},{9,5},{13,1},{2,14},{6,10},... | collective-permute-start | bytes 811016 | tf_op jit(solution)/shard_map/ppermute | solution.py:478

commit v3 on v2

--- a/solution.py
+++ b/solution.py
@@ -39,6 +39,18 @@
 
 def in_vmem():
     return pl.BlockSpec(memory_space=pltpu.VMEM)
+
+
+def anywhere():
+    return pl.BlockSpec(memory_space=pl.ANY)
+
+
+def keep_hbm(x):
+    return pltpu.with_memory_space_constraint(x, pltpu.HBM)
+
+
+def keep_vmem(x):
+    return pltpu.with_memory_space_constraint(x, pltpu.VMEM)
 
 
 def row_to_lanes(row):
@@ -80,26 +92,36 @@
     )
 
 
-def sort_kernel(label_ref, keys_ref, values_ref, *refs):
-    out_keys, out_values, out_labels, wide_ref, both_ref, order_ref = refs
+def sort_kernel(label_ref, keys_hbm, values_hbm, *refs):
+    out_keys, out_values, out_labels, flat_ref, wide_ref, both_ref, order_ref, sems = refs
     head = pl.program_id(0)
     heads = pl.num_programs(0)
     _, tokens, width = out_keys.shape
-    flat = wide_ref.shape[1]
+    copies = [
+        pltpu.make_async_copy(source, flat_ref.at[side], sems.at[side])
+        for side, source in enumerate((keys_hbm, values_hbm))
+    ]
 
     @pl.when(head == 0)
     def _():
-        split_heads(keys_ref, wide_ref.at[0])
-        split_heads(values_ref, wide_ref.at[1])
-
-    for side in range(2):
-        both_ref[:, side * width : (side + 1) * width] = head_rows(
-            wide_ref.at[side], head, flat // tokens
-        ).astype(BF16)
-    label = label_ref[0]
+        for copy in copies:
+            copy.start()
+
+    label = label_ref[pl.ds(head, 1), :]
     order = label * tokens + lax.broadcasted_iota(jnp.int32, label.shape, 1)
     order_ref[0] = order
     spot = count_below(order_ref, order, tokens)
+
+    @pl.when(head == 0)
+    def _():
+        for side, copy in enumerate(copies):
+            copy.wait()
+            split_heads(flat_ref.at[side], wide_ref.at[side])
+
+    for side in range(2):
+        both_ref[:, side * width : (side + 1) * width] = head_rows(
+            wide_ref.at[side], head, wide_ref.shape[1] // tokens
+        ).astype(BF16)
     digits = jnp.concatenate(
         [
             jnp.broadcast_to(label >> 6, (8, tokens)),
@@ -115,9 +137,7 @@
         out_keys[0, r : r + rows] = moved[:, :width]
         out_values[0, r : r + rows] = moved[:, width:]
         digit = dot_nt(digits, pick)
-        out_labels[0, :, r : r + rows] = (
-            digit[0:1] * 64.0 + digit[8:9]
-        ).astype(jnp.int32)
+        out_labels[0, :, r : r + rows] = digit[0:1] * 64.0 + digit[8:9]
 
 
 def sort_tokens(labels, keys, values):
@@ -129,13 +149,15 @@
     return pl.pallas_call(
         sort_kernel,
         grid=(heads,),
-        in_specs=[label_block, whole(keys.shape), whole(values.shape)],
+        in_specs=[whole(labels.shape), anywhere(), anywhere()],
         out_specs=(row_block, row_block, label_block),
-        out_shape=(rows, rows, jax.ShapeDtypeStruct((heads, 1, tokens), jnp.int32)),
+        out_shape=(rows, rows, jax.ShapeDtypeStruct((heads, 1, tokens), F32)),
         scratch_shapes=[
+            pltpu.VMEM((2, flat, width), BF16),
             pltpu.VMEM((2, flat, width), F32),
             pltpu.VMEM((tokens, 2 * width), BF16),
             pltpu.VMEM((1, 1, tokens), jnp.int32),
+            pltpu.SemaphoreType.DMA((2,)),
         ],
         compiler_params=params(),
         cost_estimate=pl.CostEstimate(
@@ -144,25 +166,32 @@
             transcendentals=0,
         ),
         name="sort_tokens",
-    )(labels[:, None, :], keys, values)
-
-
-def windows_kernel(start_ref, values_ref, *out_refs):
-    heads = values_ref.shape[0]
-    for m, out_ref in enumerate(out_refs):
-        size = out_ref.shape[1]
-        for h in range(heads):
+    )(labels, keep_hbm(keys), keep_hbm(values))
+
+
+def windows_kernel(size, start_ref, rank_ref, values_ref, *out_refs):
+    heads, tokens, _ = values_ref.shape
+    for h in range(heads):
+        rank = rank_ref[h]
+        digits = [
+            digit[:, t : t + LANES]
+            for digit in (rank >> 7, rank & 127)
+            for t in range(0, tokens, LANES)
+        ]
+        digits = jnp.concatenate(digits, axis=0).astype(F32).astype(BF16)
+        for m, out_ref in enumerate(out_refs):
             start = pl.multiple_of(start_ref[h, m], 16)
-            out_ref[h] = values_ref[h, pl.ds(start, size), :]
-
-
-def windows(starts, values, size):
+            out_ref[h, :size] = values_ref[h, pl.ds(start, size), :]
+            out_ref[h, size:] = digits
+
+
+def windows(starts, ranks, values, size):
     heads, tokens, width = values.shape
     n = starts.shape[1]
-    out = jax.ShapeDtypeStruct((heads, size, width), BF16)
-    return pl.pallas_call(
-        windows_kernel,
-        in_specs=[pl.BlockSpec(memory_space=pltpu.SMEM), in_vmem()],
+    out = jax.ShapeDtypeStruct((heads, size + 2 * tokens // LANES, width), BF16)
+    return pl.pallas_call(
+        functools.partial(windows_kernel, size),
+        in_specs=[pl.BlockSpec(memory_space=pltpu.SMEM), in_vmem(), in_vmem()],
         out_specs=(in_vmem(),) * n,
         out_shape=(out,) * n,
         compiler_params=params(),
@@ -170,7 +199,7 @@
             flops=0, bytes_accessed=4 * n * heads * size * width, transcendentals=0
         ),
         name="windows",
-    )(starts, values)
+    )(starts, ranks, keep_hbm(values))
 
 
 def rank_kernel(own_ref, all_ref, rank_ref):
@@ -204,11 +233,13 @@
         unit_ref[...] = unit_rows(keys_ref[0].astype(F32)).astype(BF16)
         sum_ref[...] = jnp.zeros_like(sum_ref)
 
-    cent = unit_rows(cent_ref[0]).astype(BF16)
     part = 256
-    for t in range(0, tokens, part):
-        raw = jnp.exp2(dot_nt(cent, unit_ref[t : t + part, :]) * EXP2_SCALE)
-        sum_ref[:, t : t + part] += jnp.sum(raw.reshape(-1, 8, part), axis=0)
+    rows = min(1024, cent_ref.shape[1])
+    for c in range(0, cent_ref.shape[1], rows):
+        cent = unit_rows(cent_ref[0, c : c + rows]).astype(BF16)
+        for t in range(0, tokens, part):
+            raw = jnp.exp2(dot_nt(cent, unit_ref[t : t + part, :]) * EXP2_SCALE)
+            sum_ref[:, t : t + part] += jnp.sum(raw.reshape(-1, 8, part), axis=0)
 
     @pl.when(step == pl.num_programs(1) - 1)
     def _():
@@ -218,7 +249,7 @@
 def own_totals(keys, cents):
     heads, count, width = cents.shape
     tokens = keys.shape[1]
-    rows = min(1024, count)
+    rows = min(2048, count)
     return pl.pallas_call(
         totals_kernel,
         grid=(heads, count // rows),
@@ -239,7 +270,7 @@
             transcendentals=heads * tokens * count,
         ),
         name="own_totals",
-    )(keys, cents)
+    )(keep_hbm(keys), keep_hbm(cents))
 
 
 def scale_rows(unit, inverse, scaled_ref):
@@ -249,57 +280,60 @@
         ).astype(BF16)
 
 
-def first_kernel(fresh, _, keys_ref, tot_ref, init_ref, *refs):
+def first_kernel(fresh, _, keys_ref, tot_ref, cent_in, *refs):
+    head = pl.program_id(0)
     if fresh:
-        sums_ref, unit_ref, scaled_ref, cent_ref = refs
+        sums_ref, unit_ref, cent_ref, scaled_ref = refs
+        cent = unit_rows(cent_in[0]).astype(BF16)
+        cent_ref[head] = cent
     else:
-        before_ref, sums_ref, unit_ref, scaled_ref, cent_ref = refs
-    tokens = unit_ref.shape[1]
-    cent_ref[...] = unit_rows(init_ref[0]).astype(BF16)
+        _, sums_ref, unit_ref, scaled_ref = refs
+        cent = cent_in[head]
+    unit = unit_rows(keys_ref[0].astype(F32)).astype(BF16)
+    unit_ref[head] = unit
+    scale_rows(unit, 1.0 / tot_ref[0], scaled_ref)
+    part = 256
+    for t in range(0, unit.shape[0], part):
+        raw = jnp.exp2(dot_nt(cent, unit[t : t + part, :]) * EXP2_SCALE)
+        more = dot_nn(raw.astype(BF16), scaled_ref[t : t + part])
+        if fresh and t == 0:
+            sums_ref[head] = more
+        else:
+            sums_ref[head] += more
+
+
+def first_block(me, keys, totals, cents, n, before):
+    heads, tokens, width = keys.shape
+    fresh = before is None
+    rows = cents.shape[1] // n if fresh else cents.shape[1]
+    in_specs = [
+        pl.BlockSpec((1, tokens, width), lambda h, me: (h, 0, 0)),
+        pl.BlockSpec((1, 1, tokens), lambda h, me: (h, 0, 0)),
+    ]
+    args = [me, keep_hbm(keys), totals]
+    out_shape = [
+        pltpu.VMEM((heads, rows, width), F32),
+        pltpu.VMEM((heads, tokens, width), BF16),
+    ]
+    aliases = {}
     if fresh:
-        sums_ref[...] = jnp.zeros_like(sums_ref)
+        in_specs.append(pl.BlockSpec((1, rows, width), lambda h, me: (h, me[0], 0)))
+        args.append(keep_hbm(cents))
+        out_shape.append(pltpu.VMEM((heads, rows, width), BF16))
     else:
-        sums_ref[...] = before_ref[...]
-    unit_ref[0] = unit_rows(keys_ref[0].astype(F32)).astype(BF16)
-    scale_rows(unit_ref[0], 1.0 / tot_ref[0], scaled_ref)
-    part = 256
-    for t in range(0, tokens, part):
-        raw = jnp.exp2(dot_nt(cent_ref[...], unit_ref[0, t : t + part, :]) * EXP2_SCALE)
-        sums_ref[0] += dot_nn(raw.astype(BF16), scaled_ref[t : t + part])
-
-
-def first_block(me, keys, totals, init, n, before):
-    heads, tokens, width = keys.shape
-    rows = init.shape[1] // n
-    share = pl.BlockSpec((1, rows, width), lambda h, me: (h, 0, 0))
-    key_block = pl.BlockSpec((1, tokens, width), lambda h, me: (h, 0, 0))
-    in_specs = [
-        key_block,
-        pl.BlockSpec((1, 1, tokens), lambda h, me: (h, 0, 0)),
-        pl.BlockSpec((1, rows, width), lambda h, me: (h, me[0], 0)),
-    ]
-    args = [me, keys, totals, init]
-    aliases = {}
-    if before is not None:
-        in_specs.append(share)
-        args.append(before)
+        in_specs += [in_vmem(), in_vmem()]
+        args += [keep_vmem(cents), keep_vmem(before)]
         aliases = {4: 0}
     return pl.pallas_call(
-        functools.partial(first_kernel, before is None),
+        functools.partial(first_kernel, fresh),
         grid_spec=pltpu.PrefetchScalarGridSpec(
             num_scalar_prefetch=1,
             grid=(heads,),
             in_specs=in_specs,
-            out_specs=(share, key_block),
-            scratch_shapes=[
-                pltpu.VMEM((tokens, width), BF16),
-                pltpu.VMEM((rows, width), BF16),
-            ],
-        ),
-        out_shape=(
-            jax.ShapeDtypeStruct((heads, rows, width), F32),
-            jax.ShapeDtypeStruct((heads, tokens, width), BF16),
-        ),
+            out_specs=(in_vmem(),) * len(out_shape),
+            scratch_shapes=[pltpu.VMEM((tokens, width), BF16)],
+        ),
+        out_shape=tuple(out_shape),
         input_output_aliases=aliases,
         compiler_params=params(),
         cost_estimate=pl.CostEstimate(
@@ -315,13 +349,13 @@
     units = refs[:blocks]
     raw_ref, total_ref, cent_ref = refs[blocks:]
     head = pl.program_id(0)
-    cent_ref[...] = unit_rows(sums_ref[0]).astype(BF16)
+    cent_ref[...] = unit_rows(sums_ref[head]).astype(BF16)
     part = 256
     start = 0
     for unit_ref in units:
         for t in range(0, unit_ref.shape[1], part):
             here = slice(start + t, start + t + part)
-            raw = jnp.exp2(dot_nt(cent_ref[...], unit_ref[0, t : t + part, :]) * EXP2_SCALE)
+            raw = jnp.exp2(dot_nt(cent_ref[...], unit_ref[head, t : t + part, :]) * EXP2_SCALE)
             raw_ref[head, :, here] = raw.astype(BF16)
             total = jnp.sum(raw.reshape(-1, 8, part), axis=0)
             total_ref[0, :, here] = jnp.sum(total, axis=0, keepdims=True)
@@ -335,8 +369,7 @@
     return pl.pallas_call(
         functools.partial(raw_kernel, len(units)),
         grid=(heads,),
-        in_specs=[pl.BlockSpec((1, rows, width), lambda h: (h, 0, 0))]
-        + [pl.BlockSpec((1, tokens, width), lambda h: (h, 0, 0))] * len(units),
+        in_specs=[in_vmem()] * (1 + len(units)),
         out_specs=(in_vmem(), pl.BlockSpec((1, 1, count), lambda h: (h, 0, 0))),
         out_shape=(
             pltpu.VMEM((heads, rows, count), BF16),
@@ -350,7 +383,7 @@
             transcendentals=heads * rows * count,
         ),
         name="raw_weights",
-    )(sums, *units)
+    )(keep_vmem(sums), *map(keep_vmem, units))
 
 
 def sums_kernel(blocks, raw_ref, *refs):
@@ -363,7 +396,7 @@
         for d in range(1, blocks):
             peer = m ^ d
             row_total += totals[d][0, :, peer * tokens : (peer + 1) * tokens]
-        scale_rows(unit_ref[0], 1.0 / row_total, scaled_ref)
+        scale_rows(unit_ref[head], 1.0 / row_total, scaled_ref)
         more = dot_nn(raw_ref[head, :, m * tokens : (m + 1) * tokens], scaled_ref[...])
         if m == 0:
             sum_ref[...] = more
@@ -376,13 +409,12 @@
     heads, rows, count = raw.shape
     _, tokens, width = units[0].shape
     blocks = len(units)
-    raw = pltpu.with_memory_space_constraint(raw, pltpu.VMEM)
     return pl.pallas_call(
         functools.partial(sums_kernel, blocks),
         grid=(heads,),
         in_specs=[in_vmem()]
         + [pl.BlockSpec((1, 1, count), lambda h: (h, 0, 0))] * blocks
-        + [pl.BlockSpec((1, tokens, width), lambda h: (h, 0, 0))] * blocks,
+        + [in_vmem()] * blocks,
         out_specs=pl.BlockSpec((1, rows, width), lambda h: (h, 0, 0)),
         out_shape=jax.ShapeDtypeStruct((heads, rows, width), F32),
         scratch_shapes=[
@@ -396,27 +428,59 @@
             transcendentals=0,
         ),
         name="weighted_sums",
-    )(raw, *totals, *units)
-
-
-def place_kernel(blocks, size, start_ref, gap_ref, spot_ref, *refs):
-    keys, values = refs[:blocks], refs[blocks : 2 * blocks]
-    out_refs, (rows_ref, near_ref, mixed_ref) = refs[-5:-3], refs[-3:]
+    )(keep_vmem(raw), *totals, *map(keep_vmem, units))
+
+
+def place_kernel(blocks, size, scalar_ref, *refs):
+    labels, keys, values = (refs[i * blocks : (i + 1) * blocks] for i in range(3))
+    out_refs, (rows_ref, tail_ref, near_ref, mixed_ref, sems) = refs[-7:-5], refs[-5:]
     step = pl.program_id(0)
     heads, tokens, width = keys[0].shape
+    digit_rows = tokens // LANES
+    sent = values[0].shape[1] - 2 * digit_rows
 
     @pl.when(step == 0)
     def _():
         rows_ref[:, :, width:] = jnp.zeros((heads, blocks * size, width), BF16)
+        copies = []
         for h in range(heads):
             for m in range(blocks):
-                start = pl.multiple_of(start_ref[h, m], 16)
-                gap = pl.multiple_of(gap_ref[h, m], 16)
-                rows_ref[h, m * size : (m + 1) * size, :width] = keys[m][
-                    h, pl.ds(start, size), :
+                start = pl.multiple_of(scalar_ref[0, h, m], 16)
+                gap = pl.multiple_of(scalar_ref[1, h, m], 16)
+                first = m * size
+                copies += [
+                    pltpu.make_async_copy(source, target, sems.at[len(copies) + i])
+                    for i, (source, target) in enumerate(
+                        (
+                            (
+                                keys[m].at[h, pl.ds(start, size), :],
+                                rows_ref.at[h, first : first + size, :width],
+                            ),
+                            (
+                                values[m].at[h, :sent, :],
+                                rows_ref.at[h, pl.ds(first + gap, sent), width:],
+                            ),
+                            (values[m].at[h, sent:, :], tail_ref.at[h, m]),
+                        )
+                    )
                 ]
-                rows_ref[h, pl.ds(m * size + gap, values[m].shape[1]), width:] = values[m][h]
-                spot = pltpu.roll(spot_ref[h, m : m + 1, :], lax.rem(tokens - start, tokens), 1)
+        for copy in copies:
+            copy.start()
+        for copy in copies:
+            copy.wait()
+        for h in range(heads):
+            for m in range(blocks):
+                start = scalar_ref[0, h, m]
+                digits = tail_ref[h, m].astype(F32)
+                rank = digits[:digit_rows] * 128.0 + digits[digit_rows:]
+                rank = jnp.concatenate([rank[r : r + 1] for r in range(digit_rows)], axis=1)
+                label = labels[m][h]
+                low, high, before = (
+                    scalar_ref[i, h, 0].astype(F32) for i in range(2, 5)
+                )
+                mine = (label >= low) & (label < high)
+                spot = jnp.where(mine, rank - before, -1.0).astype(jnp.int32)
+                spot = pltpu.roll(spot, lax.rem(tokens - start, tokens), 1)
                 near_ref[h, :, m * size : (m + 1) * size] = spot[:, :size]
 
     rows = out_refs[0].shape[0] // heads
@@ -435,24 +499,26 @@
         out_refs[side][...] = mixed_ref[side].astype(BF16)
 
 
-def place(starts, gaps, spots, keys, values, size, cap):
+def place(scalars, labels, keys, values, size, cap):
     blocks = len(keys)
-    heads, _, width = keys[0].shape
+    heads, tokens, width = keys[0].shape
     rows = 512
     out = jax.ShapeDtypeStruct((heads * cap, width), BF16)
     block = pl.BlockSpec((heads * rows, width), lambda r: (r, 0))
-    scalars = pl.BlockSpec(memory_space=pltpu.SMEM)
     return pl.pallas_call(
         functools.partial(place_kernel, blocks, size),
         grid=(cap // rows,),
-        in_specs=[scalars, scalars]
-        + [whole(x.shape) for x in (spots, *keys, *values)],
+        in_specs=[pl.BlockSpec(memory_space=pltpu.SMEM)]
+        + [whole(labels[0].shape)] * blocks
+        + [anywhere()] * (2 * blocks),
         out_specs=(block, block),
         out_shape=(out, out),
         scratch_shapes=[
             pltpu.VMEM((heads, blocks * size, 2 * width), BF16),
+            pltpu.VMEM((heads, blocks, 2 * tokens // LANES, width), BF16),
             pltpu.VMEM((heads, 1, blocks * size), jnp.int32),
             pltpu.VMEM((2, heads * rows, width), F32),
+            pltpu.SemaphoreType.DMA((3 * heads * blocks,)),
         ],
         compiler_params=params(),
         cost_estimate=pl.CostEstimate(
@@ -461,7 +527,7 @@
             transcendentals=0,
         ),
         name="place",
-    )(starts, gaps, spots, *keys, *values)
+    )(scalars, *labels, *map(keep_hbm, keys), *map(keep_hbm, values))
 
 
 def body(key_rows, value_rows, cluster_labels, owner_bounds, init_centroids):
@@ -496,42 +562,50 @@
         value_rows.reshape(heads * tokens, width),
     )
     keys = cube(own_keys)
-    labels = spread(own_labels)
+    own_total = own_totals(own_keys, init_centroids)
+    shared = spread(jnp.concatenate([own_total, own_labels], axis=1))
+    totals = [own_total] + [x[:, 0:1] for x in shared[1:]]
+    labels = [own_labels] + [x[:, 1:2] for x in shared[1:]]
 
     place_ids = jnp.arange(tokens, dtype=jnp.int32)
     orders = [
-        labels[m] * everyone + (me ^ m) * tokens + place_ids for m in range(n)
+        labels[m].astype(jnp.int32) * everyone + (me ^ m) * tokens + place_ids
+        for m in range(n)
     ]
-    own_rank = own_ranks(orders[0], jnp.concatenate(orders, axis=2))
-    own_total = own_totals(own_keys, init_centroids)
-    shared = spread(jnp.concatenate([own_total, own_rank.astype(F32)], axis=1))
-    totals = [x[:, 0:1] for x in shared]
-    ranks = jnp.stack([x[:, 1] for x in shared], axis=1).astype(jnp.int32)
-    block_labels = jnp.concatenate(labels, axis=1)
-    low = lax.dynamic_slice_in_dim(owner_bounds, me, 1, 1)[:, :, None]
-    high = lax.dynamic_slice_in_dim(owner_bounds, me + 1, 1, 1)[:, :, None]
-    below = jnp.sum((block_labels < low).astype(jnp.int32), axis=2)
-    first = jnp.sum(below, axis=1)[:, None, None]
-    mine = (block_labels >= low) & (block_labels < high)
-    spots = jnp.where(mine, ranks - first, -1)
+    ranks = own_ranks(orders[0], jnp.concatenate(orders, axis=2))
+    low = lax.dynamic_slice_in_dim(owner_bounds, me, 1, 1)
+    high = lax.dynamic_slice_in_dim(owner_bounds, me + 1, 1, 1)
+    block_labels = jnp.concatenate(labels, axis=1).astype(jnp.int32)
+    below = jnp.sum((block_labels < low[:, :, None]).astype(jnp.int32), axis=2)
+    first = jnp.sum(below, axis=1, keepdims=True)
     key_starts = aligned(below, key_size)
     gaps = aligned(below, send_size) - key_starts
-
-    peers = jnp.stack([me ^ m for m in range(n)])
-    peer_low = jnp.take(owner_bounds, peers, axis=1)
-    own_below = jnp.sum((own_labels < peer_low[:, :, None]).astype(jnp.int32), axis=2)
-    own_windows = windows(aligned(own_below, send_size), own_values, send_size)
-    *own_windows, _ = lax.optimization_barrier((*own_windows, keys[-1]))
-    values = [own_windows[0]] + [swap(own_windows[d], d) for d in range(1, n)]
-
-    sums, units = None, []
-    for m in range(n):
-        sums, unit = first_block(me.reshape(1), keys[m], totals[m], init_centroids, n, sums)
+    one = jnp.ones((1, n), jnp.int32)
+    scalars = jnp.stack([key_starts, gaps, low * one, high * one, first * one])
+
+    sums, unit, cents = first_block(
+        me.reshape(1), keys[0], totals[0], init_centroids, n, None
+    )
+    units = [unit]
+    for m in range(1, n):
+        sums, unit = first_block(me.reshape(1), keys[m], totals[m], cents, n, sums)
         units.append(unit)
+        if m == 1:
+            peers = jnp.stack([me ^ m for m in range(n)])
+            peer_low = jnp.take(owner_bounds, peers, axis=1)
+            own_below = jnp.sum(
+                (own_labels.astype(jnp.int32) < peer_low[:, :, None]).astype(jnp.int32), axis=2
+            )
+            own_windows = windows(
+                aligned(own_below, send_size), ranks, own_values, send_size
+            )
+            *own_windows, sums = lax.optimization_barrier((*own_windows, sums))
+            values = [own_windows[0]] + [swap(own_windows[d], d) for d in range(1, n)]
+
     raw, part = raw_weights(sums, units)
     out = weighted_sums(raw, units, spread(part))
 
-    placed = place(key_starts, gaps, spots, keys, values, key_size, cap)
+    placed = place(scalars, labels, keys, values, key_size, cap)
     shape = (cap, heads, width)
     return out, placed[0].reshape(shape), placed[1].reshape(shape)
 

time: 102 us -> 103 us (level); the launches traced: 101 us -> 103 us
  waiting for transfers between devices: 10 us -> 17 us
  starting transfers between devices: 26.1 us -> 19.3 us
  Pallas kernels: 49 us -> 55.1 us
  local copies, waits for them, and re-layouts: 13.4 us -> 9.38 us
    ppermute x15 -> x12, waiting for transfers between devices: 10 us -> 17 us  [swap(): return lax.ppermute(x, 'ctx', [(i, i ^ d) for i in range(n)])]
    ppermute x15 -> x12, starting transfers between devices: 26.1 us -> 19.3 us  [swap(): return lax.ppermute(x, 'ctx', [(i, i ^ d) for i in range(n)])]
    pallas_call x6, Pallas kernels: 17.6 us -> 21.5 us  [the longest x4 16 us: first_block(): pl.pallas_call(functools.partial(first_kernel, fresh), grid_spec=pltpu.Pr...]
    unnamed x32 -> x28, local copies, waits for them, and re-layouts: 11.8 us -> 8.4 us
    pallas_call x1, Pallas kernels: 8.5 us -> 10.1 us  [place(): pl.pallas_call(functools.partial(place_kernel, blocks, size), grid=(cap /...]
  transfers between devices with their start and end apart: 15 -> 12, of which waited for: 2 -> 2; matrix products, arithmetic and copies ran while one was open for 3% -> 2% of each run, Pallas kernels for 28% -> 36%
where the time goes in v3:
time: 103 us
  Pallas kernels  55.1 us (53%)
  starting transfers between devices  19.3 us (19%)
  waiting for transfers between devices  17 us (17%)
  local copies, waits for them, and re-layouts  9.38 us (9%)
    ppermute x12, starting transfers between devices, swap(): return lax.ppermute(x, 'ctx', [(i, i ^ d) for i in range(n)])  19.3 us
    ppermute x12, waiting for transfers between devices, swap(): return lax.ppermute(x, 'ctx', [(i, i ^ d) for i in range(n)])  17 us
    pallas_call x4, Pallas kernels, first_block(): pl.pallas_call(functools.partial(first_kernel, fresh), grid_spec=pltpu.Pr...  16 us
    pallas_call x1, Pallas kernels, place(): pl.pallas_call(functools.partial(place_kernel, blocks, size), grid=(cap /...  10.1 us
    unnamed x28, local copies, waits for them, and re-layouts  8.4 us
    pallas_call x1, Pallas kernels, own_totals(): pl.pallas_call(totals_kernel, grid=(heads, count // rows), in_specs=[pl.B...  7.68 us
    pallas_call x1, Pallas kernels, weighted_sums(): pl.pallas_call(functools.partial(sums_kernel, blocks), grid=(heads,), in_...  6.37 us
    pallas_call x1, Pallas kernels, raw_weights(): pl.pallas_call(functools.partial(raw_kernel, len(units)), grid=(heads,),...  5.02 us
  transfers between devices with their start and end apart: 12, of which 2 were waited for; matrix products, arithmetic and copies ran while one was open for 2% of the time, Pallas kernels for 36%

profile of v3, /device:TPU:0, one launch (start us, length us, event | category | flops | bytes accessed | tf_op | source)
XLA Modules:
  0.0 102.6 jit_solution(1974359494869708631)
XLA Ops:
  0.6 0.0 copy-start.6
  0.6 0.0 copy-start.3
  0.7 0.7 copy-done.3
  1.3 4.4 %sort_tokens.1 = (bf16[2,1024,128]{2,1,0:T(8,128)(2,1)S(1)}, bf16[2,1024,128]{2,1,0:T(8,128)(2,1)S(1)}, f32[2,1,1024]{2,1,0:T(1,128)S(1)}) custom-call(s32[2,1024]{1,0:T(2,128)S(1)} %copy-done.3, bf16[2048,128]{1,0:T(8,128)(2,1)} %bitcast.34, bf16[2048,128]{1,0:T(8,128)(2,1)} %bitcast.35), custom_call_target="tpu_custom_call" | custom-call | flops 1073741824 | bytes 2097152 | tf_op jit(solution)/shard_map/sort_tokens/pallas_call | solution.py:149
  5.8 0.0 copy-start
  5.8 0.8 copy-done
  6.6 0.8 copy-done.1
  7.4 7.7 %own_totals.1.tot_ref = f32[2,1,1024]{2,1,0:T(1,128)S(1)} custom-call(bf16[2,1024,128]{2,1,0:T(8,128)(2,1)} %copy-done.1, f32[2,4096,128]{2,1,0:T(8,128)} %cent_in.1), custom_call_target="tpu_custom_call" | custom-call | flops 4294967296 | bytes 4194304 | tf_op jit(solution)/shard_map/own_totals/pallas_call | solution.py:253
  15.1 3.1 %collective-permute-start.4 = (f32[2,2,1024]{2,1,0:T(2,128)S(1)}, f32[2,2,1024]{2,1,0:T(2,128)S(1)}, u32[]{:S(2)}, u32[]{:S(2)}) collective-permute-start(f32[2,2,1024]{2,1,0:T(2,128)S(1)} %pad_maximum_fusion), channel_id=1, source_target_pairs={{0,4},{4,0},{8,12},{12,8},{1,5},{5,1},{9,13},{13,9},{2,6},{6,2},{1... | collective-permute-start | bytes 49160 | tf_op jit(solution)/shard_map/ppermute | solution.py:544
  18.2 2.6 %collective-permute-start.3 = (f32[2,2,1024]{2,1,0:T(2,128)S(1)}, f32[2,2,1024]{2,1,0:T(2,128)S(1)}, u32[]{:S(2)}, u32[]{:S(2)}) collective-permute-start(f32[2,2,1024]{2,1,0:T(2,128)S(1)} %pad_maximum_fusion), channel_id=1, source_target_pairs={{0,8},{4,12},{8,0},{12,4},{1,9},{5,13},{9,1},{13,5},{2,10},{6,14},... | collective-permute-start | bytes 49160 | tf_op jit(solution)/shard_map/ppermute | solution.py:544
  20.8 0.0 collective-permute-start.2
  20.8 0.9 collective-permute-start.5
  21.7 3.5 %collective-permute-start = (bf16[2,1024,128]{2,1,0:T(8,128)(2,1)}, bf16[2,1024,128]{2,1,0:T(8,128)(2,1)}, u32[]{:S(2)}, u32[]{:S(2)}) collective-permute-start(bf16[2,1024,128]{2,1,0:T(8,128)(2,1)} %copy-done.1), channel_id=1, source_target_pairs={{0,8},{4,12},{8,0},{12,4},{1,9},{5,13},{9,1},{13,5},{2,10},{6,14},... | collective-permute-start | bytes 1572872 | tf_op jit(solution)/shard_map/ppermute | solution.py:544
  25.1 0.1 fusion.2
  25.2 0.0 copy-done.6
  25.2 0.1 copy.13
  25.3 0.6 gather_fusion
  25.9 0.1 compare_and_fusion
  26.0 0.1 select_bitcast_fusion
  26.1 0.1 copy.14
  26.2 0.2 convert_reduce_fusion.2
  26.4 4.2 %first_block.4 = (f32[2,1024,128]{2,1,0:T(8,128)S(1)}, bf16[2,1024,128]{2,1,0:T(8,128)(2,1)S(1)}, bf16[2,1024,128]{2,1,0:T(8,128)(2,1)S(1)}) custom-call(s32[1]{0:T(128)} %bitcast._, bf16[2,1024,128]{2,1,0:T(8,128)(2,1)} %copy-done.1, f32[2,1,1024]{2,1,0:T(1,128)S(1)} %own_totals.1.tot_ref, f32[2,4096,128]{2,1,0:T(8,128)} %cent_in.1), custom_call_target="tpu_custom_call" | custom-call | flops 2147483648 | bytes 4194304 | tf_op jit(solution)/shard_map/first_block/pallas_call | solution.py:327
  30.7 0.2 dynamic-slice_reduce_fusion
  30.9 0.0 collective-permute-done.4
  30.9 0.0 collective-permute-done.3
  31.0 0.0 collective-permute-done.2
  31.0 0.3 convert_reduce_fusion
  31.4 0.1 constant_dynamic-update-slice_fusion.2
  31.5 4.4 %own_ranks.1.rank_ref = s32[2,1,1024]{2,1,0:T(1,128)S(1)} custom-call(s32[2,1,1024]{2,1,0:T(1,128)S(1)} %iota_add_fusion.3.own_ref, s32[2,1,4096]{2,1,0:T(1,128)S(1)} %pad_add_fusion.all_ref), custom_call_target="tpu_custom_call" | custom-call | flops 25165824 | bytes 65536 | tf_op jit(solution)/shard_map/own_ranks/pallas_call | solution.py:213
  35.9 1.1 %windows.1 = (bf16[2,544,128]{2,1,0:T(8,128)(2,1)S(1)}, bf16[2,544,128]{2,1,0:T(8,128)(2,1)S(1)}, bf16[2,544,128]{2,1,0:T(8,128)(2,1)S(1)}, bf16[2,544,128]{2,1,0:T(8,128)(2,1)S(1)}) custom-call(s32[2,4]{1,0:T(2,128)S(1)} %multiply_minimum_fusion.start_ref, s32[2,1,1024]{2,1,0:T(1,128)S(1)} %own_ranks.1.rank_ref, bf16[2,1024,128]{2,1,0:T(8,128)(2,1)} %copy-done), custom_call_target="tpu_custom_call" | custom-call | bytes 2162688 | tf_op jit(solution)/shard_map/windows/pallas_call | solution.py:192
  37.0 0.0 copy-start.2
  37.0 0.7 copy-done.2
  37.7 0.1 constant_dynamic-update-slice_fusion.1
  37.8 9.9 %collective-permute-done.keys_ref.refs_6_ = bf16[2,1024,128]{2,1,0:T(8,128)(2,1)} collective-permute-done((bf16[2,1024,128]{2,1,0:T(8,128)(2,1)}, bf16[2,1024,128]{2,1,0:T(8,128)(2,1)}, u32[]{:S(2)}, u32[]{:S(2)}) %collective-permute-start) | collective-permute-done | bytes 524320 | tf_op jit(solution)/shard_map/ppermute | solution.py:544
  47.7 0.3 collective-permute-start.1
  48.1 0.1 constant_dynamic-update-slice_fusion.scalar_ref
  48.1 0.0 collective-permute-done.5.keys_ref.refs_5_
  48.1 0.8 copy-done.7
  48.9 3.9 %first_block.5 = (f32[2,1024,128]{2,1,0:T(8,128)S(1)}, bf16[2,1024,128]{2,1,0:T(8,128)(2,1)S(1)}) custom-call(s32[1]{0:T(128)} %bitcast._, bf16[2,1024,128]{2,1,0:T(8,128)(2,1)} %copy-done.7, f32[2,1,1024]{2,1,0:T(1,128)S(1)} %get-tuple-element.58.tot_ref, bf16[2,1024,128]{2,1,0:T(8,128)(2,1)S(1)} %get-tuple-element.30.cent_in, ...), custom_call_target="tpu_custom_call", output_to_operand_aliasing={{0}: (4, {})} | custom-call | flops 2147483648 | bytes 4194304 | tf_op jit(solution)/shard_map/first_block/pallas_call | solution.py:327
  52.9 1.8 %collective-permute-start.9 = (bf16[2,544,128]{2,1,0:T(8,128)(2,1)S(1)}, bf16[2,544,128]{2,1,0:T(8,128)(2,1)S(1)}, u32[]{:S(2)}, u32[]{:S(2)}) collective-permute-start(bf16[2,544,128]{2,1,0:T(8,128)(2,1)S(1)} %get-tuple-element.48), channel_id=1, source_target_pairs={{0,4},{4,0},{8,12},{12,8},{1,5},{5,1},{9,13},{13,9},{2,6},{6,2},{1... | collective-permute-start | bytes 835592 | tf_op jit(solution)/shard_map/ppermute | solution.py:544
  54.6 0.9 collective-permute-start.10
  55.5 1.8 %collective-permute-start.11 = (bf16[2,544,128]{2,1,0:T(8,128)(2,1)S(1)}, bf16[2,544,128]{2,1,0:T(8,128)(2,1)S(1)}, u32[]{:S(2)}, u32[]{:S(2)}) collective-permute-start(bf16[2,544,128]{2,1,0:T(8,128)(2,1)S(1)} %get-tuple-element.50), channel_id=1, source_target_pairs={{0,12},{4,8},{8,4},{12,0},{1,13},{5,9},{9,5},{13,1},{2,14},{6,10},... | collective-permute-start | bytes 835592 | tf_op jit(solution)/shard_map/ppermute | solution.py:544
  57.3 3.9 %first_block.6 = (f32[2,1024,128]{2,1,0:T(8,128)S(1)}, bf16[2,1024,128]{2,1,0:T(8,128)(2,1)S(1)}) custom-call(s32[1]{0:T(128)} %bitcast._, bf16[2,1024,128]{2,1,0:T(8,128)(2,1)} %collective-permute-done.keys_ref.refs_6_, f32[2,1,1024]{2,1,0:T(1,128)S(1)} %get-tuple-element.60.tot_ref, ...), custom_call_target="tpu_custom_call", output_to_operand_aliasing={{0}: (4, {})} | custom-call | flops 2147483648 | bytes 4194304 | tf_op jit(solution)/shard_map/first_block/pallas_call | solution.py:327
  61.2 7.0 %collective-permute-done.1.keys_ref.refs_7_ = bf16[2,1024,128]{2,1,0:T(8,128)(2,1)S(1)} collective-permute-done((bf16[2,1024,128]{2,1,0:T(8,128)(2,1)}, bf16[2,1024,128]{2,1,0:T(8,128)(2,1)S(1)}, u32[]{:S(2)}, u32[]{:S(2)}) %collective-permute-start.1) | collective-permute-done | bytes 524320 | tf_op jit(solution)/shard_map/ppermute | solution.py:544
  68.3 0.8 copy-done.8
  69.0 3.9 %first_block.7 = (f32[2,1024,128]{2,1,0:T(8,128)S(1)}, bf16[2,1024,128]{2,1,0:T(8,128)(2,1)S(1)}) custom-call(s32[1]{0:T(128)} %bitcast._, bf16[2,1024,128]{2,1,0:T(8,128)(2,1)} %copy-done.8, f32[2,1,1024]{2,1,0:T(1,128)S(1)} %get-tuple-element.62.tot_ref, bf16[2,1024,128]{2,1,0:T(8,128)(2,1)S(1)} %get-tuple-element.30.cent_in, ...), custom_call_target="tpu_custom_call", output_to_operand_aliasing={{0}: (4, {})} | custom-call | flops 2147483648 | bytes 4194304 | tf_op jit(solution)/shard_map/first_block/pallas_call | solution.py:327
  73.0 0.0 copy-start.4
  73.0 1.0 copy-done.4
  74.0 1.2 %copy-done.5 = f32[2,1024,128]{2,1,0:T(8,128)S(1)} copy-done((f32[2,1024,128]{2,1,0:T(8,128)S(1)}, f32[2,1024,128]{2,1,0:T(8,128)}, u32[]{:S(2)}) %copy-start.5) | copy-done | bytes 1048600
  75.2 5.0 %raw_weights.1 = (bf16[2,1024,4096]{2,1,0:T(8,128)(2,1)S(1)}, f32[2,1,4096]{2,1,0:T(1,128)S(1)}) custom-call(f32[2,1024,128]{2,1,0:T(8,128)S(1)} %copy-done.5, bf16[2,1024,128]{2,1,0:T(8,128)(2,1)S(1)} %get-tuple-element.41.refs_0_.refs_4_, bf16[2,1024,128]{2,1,0:T(8,128)(2,1)S(1)} %get-tuple-element.42.refs_1_.refs_5_, ...), custom_call_target="tpu_custom_call" | custom-call | flops 4294967296 | bytes 2097152 | tf_op jit(solution)/shard_map/raw_weights/pallas_call | solution.py:369
  80.2 1.8 %collective-permute-start.8 = (f32[2,1,4096]{2,1,0:T(1,128)S(1)}, f32[2,1,4096]{2,1,0:T(1,128)S(1)}, u32[]{:S(2)}, u32[]{:S(2)}) collective-permute-start(f32[2,1,4096]{2,1,0:T(1,128)S(1)} %get-tuple-element.46.refs_0_), channel_id=1, source_target_pairs={{0,12},{4,8},{8,4},{12,0},{1,13},{5,9},{9,5},{13,1},{2,14},{6,10},... | collective-permute-start | bytes 98312 | tf_op jit(solution)/shard_map/ppermute | solution.py:544
  82.0 0.0 collective-permute-start.7
  82.0 0.0 collective-permute-done.9.refs_9_
  82.0 2.6 %collective-permute-start.6 = (f32[2,1,4096]{2,1,0:T(1,128)S(1)}, f32[2,1,4096]{2,1,0:T(1,128)S(1)}, u32[]{:S(2)}, u32[]{:S(2)}) collective-permute-start(f32[2,1,4096]{2,1,0:T(1,128)S(1)} %get-tuple-element.46.refs_0_), channel_id=1, source_target_pairs={{0,4},{4,0},{8,12},{12,8},{1,5},{5,1},{9,13},{13,9},{2,6},{6,2},{1... | collective-permute-start | bytes 98312 | tf_op jit(solution)/shard_map/ppermute | solution.py:544
  84.7 0.0 collective-permute-done.10.refs_10_
  84.7 0.0 collective-permute-done.11.refs_11_
  84.7 0.0 copy-done.9
  84.7 0.7 copy-done.10
  85.4 0.7 copy-done.11
  86.1 10.1 %place.1 = (bf16[4096,128]{1,0:T(8,128)(2,1)}, bf16[4096,128]{1,0:T(8,128)(2,1)}) custom-call(s32[5,2,4]{2,1,0:T(2,128)S(1)} %constant_dynamic-update-slice_fusion.scalar_ref, f32[2,1,1024]{2,1,0:T(1,128)S(1)} %get-tuple-element.29.refs_0_, f32[2,1,1024]{2,1,0:T(1,128)S(1)} %get-tuple-element.57.refs_1_, f32[2,1,1024]{2,1,0:T(1,128)S(1)} %get-tuple-element.59.refs_2_, ...), custom_call_target="tpu_custom_call" | custom-call | flops 5368709120 | bytes 6291456 | tf_op jit(solution)/shard_map/place/pallas_call | solution.py:508
  96.2 0.0 collective-permute-done.8.refs_3_
  96.2 0.0 collective-permute-done.7.refs_2_
  96.2 0.0 collective-permute-done.6.refs_1_
  96.2 6.4 %weighted_sums.1 = f32[2,1024,128]{2,1,0:T(8,128)} custom-call(bf16[2,1024,4096]{2,1,0:T(8,128)(2,1)S(1)} %get-tuple-element.45.raw_ref, f32[2,1,4096]{2,1,0:T(1,128)S(1)} %get-tuple-element.46.refs_0_, f32[2,1,4096]{2,1,0:T(1,128)S(1)} %collective-permute-done.6.refs_1_, f32[2,1,4096]{2,1,0:T(1,128)S(1)} %collective-permute-done.7.refs_2_, ...), custom_call_target="tpu_custom_call" | custom-call | flops 4294967296 | bytes 2097152 | tf_op jit(solution)/shard_map/weighted_sums/pallas_call | solution.py:412
  (22 shorter events, 0.2 us)
Async XLA Ops:
  0.6 24.6 %copy-start.6 = (s32[2,5]{1,0:T(2,128)S(1)}, s32[2,5]{1,0:T(2,128)}, u32[]{:S(2)}) copy-start(s32[2,5]{1,0:T(2,128)} %param.8) | copy-start | bytes 124
  0.6 0.7 copy-start.3
  5.8 0.8 copy-start
  6.6 0.8 copy-start.1
  15.1 15.8 %collective-permute-start.4 = (f32[2,2,1024]{2,1,0:T(2,128)S(1)}, f32[2,2,1024]{2,1,0:T(2,128)S(1)}, u32[]{:S(2)}, u32[]{:S(2)}) collective-permute-start(f32[2,2,1024]{2,1,0:T(2,128)S(1)} %pad_maximum_fusion), channel_id=1, source_target_pairs={{0,4},{4,0},{8,12},{12,8},{1,5},{5,1},{9,13},{13,9},{2,6},{6,2},{1... | collective-permute-start | bytes 49160 | tf_op jit(solution)/shard_map/ppermute | solution.py:544
  18.2 12.8 %collective-permute-start.3 = (f32[2,2,1024]{2,1,0:T(2,128)S(1)}, f32[2,2,1024]{2,1,0:T(2,128)S(1)}, u32[]{:S(2)}, u32[]{:S(2)}) collective-permute-start(f32[2,2,1024]{2,1,0:T(2,128)S(1)} %pad_maximum_fusion), channel_id=1, source_target_pairs={{0,8},{4,12},{8,0},{12,4},{1,9},{5,13},{9,1},{13,5},{2,10},{6,14},... | collective-permute-start | bytes 49160 | tf_op jit(solution)/shard_map/ppermute | solution.py:544
  20.8 10.2 %collective-permute-start.2 = (f32[2,2,1024]{2,1,0:T(2,128)S(1)}, f32[2,2,1024]{2,1,0:T(2,128)S(1)}, u32[]{:S(2)}, u32[]{:S(2)}) collective-permute-start(f32[2,2,1024]{2,1,0:T(2,128)S(1)} %pad_maximum_fusion), channel_id=1, source_target_pairs={{0,12},{4,8},{8,4},{12,0},{1,13},{5,9},{9,5},{13,1},{2,14},{6,10},... | collective-permute-start | bytes 49160 | tf_op jit(solution)/shard_map/ppermute | solution.py:544
  20.8 27.4 %collective-permute-start.5 = (bf16[2,1024,128]{2,1,0:T(8,128)(2,1)}, bf16[2,1024,128]{2,1,0:T(8,128)(2,1)S(1)}, u32[]{:S(2)}, u32[]{:S(2)}) collective-permute-start(bf16[2,1024,128]{2,1,0:T(8,128)(2,1)} %copy-done.1), channel_id=1, source_target_pairs={{0,4},{4,0},{8,12},{12,8},{1,5},{5,1},{9,13},{13,9},{2,6},{6,2},{1... | collective-permute-start | bytes 1572872 | tf_op jit(solution)/shard_map/ppermute | solution.py:544
  21.7 26.1 %collective-permute-start = (bf16[2,1024,128]{2,1,0:T(8,128)(2,1)}, bf16[2,1024,128]{2,1,0:T(8,128)(2,1)}, u32[]{:S(2)}, u32[]{:S(2)}) collective-permute-start(bf16[2,1024,128]{2,1,0:T(8,128)(2,1)} %copy-done.1), channel_id=1, source_target_pairs={{0,8},{4,12},{8,0},{12,4},{1,9},{5,13},{9,1},{13,5},{2,10},{6,14},... | collective-permute-start | bytes 1572872 | tf_op jit(solution)/shard_map/ppermute | solution.py:544
  37.0 0.7 copy-start.2
  47.7 20.5 %collective-permute-start.1 = (bf16[2,1024,128]{2,1,0:T(8,128)(2,1)}, bf16[2,1024,128]{2,1,0:T(8,128)(2,1)S(1)}, u32[]{:S(2)}, u32[]{:S(2)}) collective-permute-start(bf16[2,1024,128]{2,1,0:T(8,128)(2,1)} %collective-permute-done.keys_ref.refs_6_), channel_id=1, source_target_pairs={{0,4},{4,0},{8,12},{12,8},{1,5},{5,1},{9,13},{13,9},{2,6},{6,2},{1... | collective-permute-start | bytes 1572872 | tf_op jit(solution)/shard_map/ppermute | solution.py:544
  48.1 0.8 copy-start.7
  52.9 29.2 %collective-permute-start.9 = (bf16[2,544,128]{2,1,0:T(8,128)(2,1)S(1)}, bf16[2,544,128]{2,1,0:T(8,128)(2,1)S(1)}, u32[]{:S(2)}, u32[]{:S(2)}) collective-permute-start(bf16[2,544,128]{2,1,0:T(8,128)(2,1)S(1)} %get-tuple-element.48), channel_id=1, source_target_pairs={{0,4},{4,0},{8,12},{12,8},{1,5},{5,1},{9,13},{13,9},{2,6},{6,2},{1... | collective-permute-start | bytes 835592 | tf_op jit(solution)/shard_map/ppermute | solution.py:544
  54.6 30.1 %collective-permute-start.10 = (bf16[2,544,128]{2,1,0:T(8,128)(2,1)S(1)}, bf16[2,544,128]{2,1,0:T(8,128)(2,1)S(1)}, u32[]{:S(2)}, u32[]{:S(2)}) collective-permute-start(bf16[2,544,128]{2,1,0:T(8,128)(2,1)S(1)} %get-tuple-element.49), channel_id=1, source_target_pairs={{0,8},{4,12},{8,0},{12,4},{1,9},{5,13},{9,1},{13,5},{2,10},{6,14},... | collective-permute-start | bytes 835592 | tf_op jit(solution)/shard_map/ppermute | solution.py:544
  55.5 29.2 %collective-permute-start.11 = (bf16[2,544,128]{2,1,0:T(8,128)(2,1)S(1)}, bf16[2,544,128]{2,1,0:T(8,128)(2,1)S(1)}, u32[]{:S(2)}, u32[]{:S(2)}) collective-permute-start(bf16[2,544,128]{2,1,0:T(8,128)(2,1)S(1)} %get-tuple-element.50), channel_id=1, source_target_pairs={{0,12},{4,8},{8,4},{12,0},{1,13},{5,9},{9,5},{13,1},{2,14},{6,10},... | collective-permute-start | bytes 835592 | tf_op jit(solution)/shard_map/ppermute | solution.py:544
  68.3 0.8 copy-start.8
  73.0 1.0 copy-start.4
  73.9 1.2 %copy-start.5 = (f32[2,1024,128]{2,1,0:T(8,128)S(1)}, f32[2,1024,128]{2,1,0:T(8,128)}, u32[]{:S(2)}) copy-start(f32[2,1024,128]{2,1,0:T(8,128)} %copy-done.4) | copy-start | bytes 3145732
  80.2 16.0 %collective-permute-start.8 = (f32[2,1,4096]{2,1,0:T(1,128)S(1)}, f32[2,1,4096]{2,1,0:T(1,128)S(1)}, u32[]{:S(2)}, u32[]{:S(2)}) collective-permute-start(f32[2,1,4096]{2,1,0:T(1,128)S(1)} %get-tuple-element.46.refs_0_), channel_id=1, source_target_pairs={{0,12},{4,8},{8,4},{12,0},{1,13},{5,9},{9,5},{13,1},{2,14},{6,10},... | collective-permute-start | bytes 98312 | tf_op jit(solution)/shard_map/ppermute | solution.py:544
  82.0 14.2 %collective-permute-start.7 = (f32[2,1,4096]{2,1,0:T(1,128)S(1)}, f32[2,1,4096]{2,1,0:T(1,128)S(1)}, u32[]{:S(2)}, u32[]{:S(2)}) collective-permute-start(f32[2,1,4096]{2,1,0:T(1,128)S(1)} %get-tuple-element.46.refs_0_), channel_id=1, source_target_pairs={{0,8},{4,12},{8,0},{12,4},{1,9},{5,13},{9,1},{13,5},{2,10},{6,14},... | collective-permute-start | bytes 98312 | tf_op jit(solution)/shard_map/ppermute | solution.py:544
  82.0 2.7 %copy-start.9 = (bf16[2,544,128]{2,1,0:T(8,128)(2,1)}, bf16[2,544,128]{2,1,0:T(8,128)(2,1)S(1)}, u32[]{:S(2)}) copy-start(bf16[2,544,128]{2,1,0:T(8,128)(2,1)S(1)} %collective-permute-done.9.refs_9_) | copy-start | bytes 835588
  82.0 14.2 %collective-permute-start.6 = (f32[2,1,4096]{2,1,0:T(1,128)S(1)}, f32[2,1,4096]{2,1,0:T(1,128)S(1)}, u32[]{:S(2)}, u32[]{:S(2)}) collective-permute-start(f32[2,1,4096]{2,1,0:T(1,128)S(1)} %get-tuple-element.46.refs_0_), channel_id=1, source_target_pairs={{0,4},{4,0},{8,12},{12,8},{1,5},{5,1},{9,13},{13,9},{2,6},{6,2},{1... | collective-permute-start | bytes 98312 | tf_op jit(solution)/shard_map/ppermute | solution.py:544
  84.7 0.7 copy-start.10
  85.4 0.7 copy-start.11

commit v4 on v3

--- a/solution.py
+++ b/solution.py
@@ -10,7 +10,7 @@
 
 LANES = 128
 EXP2_SCALE = 20.0 * math.log2(math.e)
-VMEM_LIMIT = 28 * 1024 * 1024
+VMEM_LIMIT = 24 * 1024 * 1024
 F32 = jnp.float32
 BF16 = jnp.bfloat16
 NT = (((1,), (1,)), ((), ()))
@@ -92,10 +92,9 @@
     )
 
 
-def sort_kernel(label_ref, keys_hbm, values_hbm, *refs):
-    out_keys, out_values, out_labels, flat_ref, wide_ref, both_ref, order_ref, sems = refs
+def sort_kernel(label_hbm, keys_hbm, values_hbm, *refs):
+    out_keys, out_values, out_labels, flat_ref, wide_ref, both_ref, order_ref, label_ref, sems = refs
     head = pl.program_id(0)
-    heads = pl.num_programs(0)
     _, tokens, width = out_keys.shape
     copies = [
         pltpu.make_async_copy(source, flat_ref.at[side], sems.at[side])
@@ -104,8 +103,11 @@
 
     @pl.when(head == 0)
     def _():
+        label_copy = pltpu.make_async_copy(label_hbm, label_ref, sems.at[2])
+        label_copy.start()
         for copy in copies:
             copy.start()
+        label_copy.wait()
 
     label = label_ref[pl.ds(head, 1), :]
     order = label * tokens + lax.broadcasted_iota(jnp.int32, label.shape, 1)
@@ -134,30 +136,29 @@
     for r in range(0, tokens, rows):
         pick = one_hot_rows(rows, spot - r)
         moved = dot_nn(pick, both_ref[...]).astype(BF16)
-        out_keys[0, r : r + rows] = moved[:, :width]
-        out_values[0, r : r + rows] = moved[:, width:]
+        out_keys[head, r : r + rows] = moved[:, :width]
+        out_values[head, r : r + rows] = moved[:, width:]
         digit = dot_nt(digits, pick)
-        out_labels[0, :, r : r + rows] = digit[0:1] * 64.0 + digit[8:9]
+        out_labels[head, :, r : r + rows] = digit[0:1] * 64.0 + digit[8:9]
 
 
 def sort_tokens(labels, keys, values):
     heads, tokens = labels.shape
     flat, width = keys.shape
-    rows = jax.ShapeDtypeStruct((heads, tokens, width), BF16)
-    row_block = pl.BlockSpec((1, tokens, width), lambda h: (h, 0, 0))
-    label_block = pl.BlockSpec((1, 1, tokens), lambda h: (h, 0, 0))
+    rows = pltpu.VMEM((heads, tokens, width), BF16)
     return pl.pallas_call(
         sort_kernel,
         grid=(heads,),
-        in_specs=[whole(labels.shape), anywhere(), anywhere()],
-        out_specs=(row_block, row_block, label_block),
-        out_shape=(rows, rows, jax.ShapeDtypeStruct((heads, 1, tokens), F32)),
+        in_specs=[anywhere()] * 3,
+        out_specs=(in_vmem(),) * 3,
+        out_shape=(rows, rows, pltpu.VMEM((heads, 1, tokens), F32)),
         scratch_shapes=[
             pltpu.VMEM((2, flat, width), BF16),
             pltpu.VMEM((2, flat, width), F32),
             pltpu.VMEM((tokens, 2 * width), BF16),
             pltpu.VMEM((1, 1, tokens), jnp.int32),
-            pltpu.SemaphoreType.DMA((2,)),
+            pltpu.VMEM(labels.shape, jnp.int32),
+            pltpu.SemaphoreType.DMA((3,)),
         ],
         compiler_params=params(),
         cost_estimate=pl.CostEstimate(
@@ -166,7 +167,7 @@
             transcendentals=0,
         ),
         name="sort_tokens",
-    )(labels, keep_hbm(keys), keep_hbm(values))
+    )(keep_hbm(labels), keep_hbm(keys), keep_hbm(values))
 
 
 def windows_kernel(size, start_ref, rank_ref, values_ref, *out_refs):
@@ -188,7 +189,7 @@
 def windows(starts, ranks, values, size):
     heads, tokens, width = values.shape
     n = starts.shape[1]
-    out = jax.ShapeDtypeStruct((heads, size + 2 * tokens // LANES, width), BF16)
+    out = pltpu.VMEM((heads, size + 2 * tokens // LANES, width), BF16)
     return pl.pallas_call(
         functools.partial(windows_kernel, size),
         in_specs=[pl.BlockSpec(memory_space=pltpu.SMEM), in_vmem(), in_vmem()],
@@ -199,7 +200,7 @@
             flops=0, bytes_accessed=4 * n * heads * size * width, transcendentals=0
         ),
         name="windows",
-    )(starts, ranks, keep_hbm(values))
+    )(starts, ranks, keep_vmem(values))
 
 
 def rank_kernel(own_ref, all_ref, rank_ref):
@@ -230,7 +231,7 @@
 
     @pl.when(step == 0)
     def _():
-        unit_ref[...] = unit_rows(keys_ref[0].astype(F32)).astype(BF16)
+        unit_ref[...] = unit_rows(keys_ref[pl.program_id(0)].astype(F32)).astype(BF16)
         sum_ref[...] = jnp.zeros_like(sum_ref)
 
     part = 256
@@ -254,7 +255,7 @@
         totals_kernel,
         grid=(heads, count // rows),
         in_specs=[
-            pl.BlockSpec((1, tokens, width), lambda h, c: (h, 0, 0)),
+            in_vmem(),
             pl.BlockSpec((1, rows, width), lambda h, c: (h, c, 0)),
         ],
         out_specs=pl.BlockSpec((1, 1, tokens), lambda h, c: (h, 0, 0)),
@@ -270,7 +271,7 @@
             transcendentals=heads * tokens * count,
         ),
         name="own_totals",
-    )(keep_hbm(keys), keep_hbm(cents))
+    )(keep_vmem(keys), keep_hbm(cents))
 
 
 def scale_rows(unit, inverse, scaled_ref):
@@ -289,7 +290,7 @@
     else:
         _, sums_ref, unit_ref, scaled_ref = refs
         cent = cent_in[head]
-    unit = unit_rows(keys_ref[0].astype(F32)).astype(BF16)
+    unit = unit_rows(keys_ref[head].astype(F32)).astype(BF16)
     unit_ref[head] = unit
     scale_rows(unit, 1.0 / tot_ref[0], scaled_ref)
     part = 256
@@ -307,10 +308,10 @@
     fresh = before is None
     rows = cents.shape[1] // n if fresh else cents.shape[1]
     in_specs = [
-        pl.BlockSpec((1, tokens, width), lambda h, me: (h, 0, 0)),
+        in_vmem(),
         pl.BlockSpec((1, 1, tokens), lambda h, me: (h, 0, 0)),
     ]
-    args = [me, keep_hbm(keys), totals]
+    args = [me, keep_vmem(keys), totals]
     out_shape = [
         pltpu.VMEM((heads, rows, width), F32),
         pltpu.VMEM((heads, tokens, width), BF16),
@@ -336,11 +337,7 @@
         out_shape=tuple(out_shape),
         input_output_aliases=aliases,
         compiler_params=params(),
-        cost_estimate=pl.CostEstimate(
-            flops=8 * heads * tokens * rows * width,
-            bytes_accessed=4 * heads * rows * width * 4,
-            transcendentals=heads * tokens * rows,
-        ),
+        cost_estimate=pl.CostEstimate(flops=1, bytes_accessed=1, transcendentals=0),
         name="first_block",
     )(*args)
 
@@ -377,11 +374,7 @@
         ),
         scratch_shapes=[pltpu.VMEM((rows, width), BF16)],
         compiler_params=params(),
-        cost_estimate=pl.CostEstimate(
-            flops=4 * heads * rows * count * width,
-            bytes_accessed=2 * heads * count * width,
-            transcendentals=heads * rows * count,
-        ),
+        cost_estimate=pl.CostEstimate(flops=1, bytes_accessed=1, transcendentals=0),
         name="raw_weights",
     )(keep_vmem(sums), *map(keep_vmem, units))
 
@@ -422,18 +415,14 @@
             pltpu.VMEM((rows, width), F32),
         ],
         compiler_params=params(),
-        cost_estimate=pl.CostEstimate(
-            flops=4 * heads * rows * count * width,
-            bytes_accessed=2 * heads * count * width,
-            transcendentals=0,
-        ),
+        cost_estimate=pl.CostEstimate(flops=1, bytes_accessed=1, transcendentals=0),
         name="weighted_sums",
     )(keep_vmem(raw), *totals, *map(keep_vmem, units))
 
 
-def place_kernel(blocks, size, scalar_ref, *refs):
-    labels, keys, values = (refs[i * blocks : (i + 1) * blocks] for i in range(3))
-    out_refs, (rows_ref, tail_ref, near_ref, mixed_ref, sems) = refs[-7:-5], refs[-5:]
+def place_kernel(blocks, size, scalar_ref, label_ref, *refs):
+    keys, values = refs[:blocks], refs[blocks : 2 * blocks]
+    out_refs, (rows_ref, near_ref, mixed_ref) = refs[-5:-3], refs[-3:]
     step = pl.program_id(0)
     heads, tokens, width = keys[0].shape
     digit_rows = tokens // LANES
@@ -442,39 +431,17 @@
     @pl.when(step == 0)
     def _():
         rows_ref[:, :, width:] = jnp.zeros((heads, blocks * size, width), BF16)
-        copies = []
         for h in range(heads):
             for m in range(blocks):
                 start = pl.multiple_of(scalar_ref[0, h, m], 16)
                 gap = pl.multiple_of(scalar_ref[1, h, m], 16)
                 first = m * size
-                copies += [
-                    pltpu.make_async_copy(source, target, sems.at[len(copies) + i])
-                    for i, (source, target) in enumerate(
-                        (
-                            (
-                                keys[m].at[h, pl.ds(start, size), :],
-                                rows_ref.at[h, first : first + size, :width],
-                            ),
-                            (
-                                values[m].at[h, :sent, :],
-                                rows_ref.at[h, pl.ds(first + gap, sent), width:],
-                            ),
-                            (values[m].at[h, sent:, :], tail_ref.at[h, m]),
-                        )
-                    )
-                ]
-        for copy in copies:
-            copy.start()
-        for copy in copies:
-            copy.wait()
-        for h in range(heads):
-            for m in range(blocks):
-                start = scalar_ref[0, h, m]
-                digits = tail_ref[h, m].astype(F32)
+                rows_ref[h, first : first + size, :width] = keys[m][h, pl.ds(start, size), :]
+                rows_ref[h, pl.ds(first + gap, sent), width:] = values[m][h, :sent, :]
+                digits = values[m][h, sent:, :].astype(F32)
                 rank = digits[:digit_rows] * 128.0 + digits[digit_rows:]
                 rank = jnp.concatenate([rank[r : r + 1] for r in range(digit_rows)], axis=1)
-                label = labels[m][h]
+                label = label_ref[h, m : m + 1, :]
                 low, high, before = (
                     scalar_ref[i, h, 0].astype(F32) for i in range(2, 5)
                 )
@@ -509,25 +476,19 @@
         functools.partial(place_kernel, blocks, size),
         grid=(cap // rows,),
         in_specs=[pl.BlockSpec(memory_space=pltpu.SMEM)]
-        + [whole(labels[0].shape)] * blocks
-        + [anywhere()] * (2 * blocks),
+        + [whole(labels.shape)]
+        + [in_vmem()] * (2 * blocks),
         out_specs=(block, block),
         out_shape=(out, out),
         scratch_shapes=[
             pltpu.VMEM((heads, blocks * size, 2 * width), BF16),
-            pltpu.VMEM((heads, blocks, 2 * tokens // LANES, width), BF16),
             pltpu.VMEM((heads, 1, blocks * size), jnp.int32),
             pltpu.VMEM((2, heads * rows, width), F32),
-            pltpu.SemaphoreType.DMA((3 * heads * blocks,)),
         ],
         compiler_params=params(),
-        cost_estimate=pl.CostEstimate(
-            flops=4 * heads * cap * blocks * size * width,
-            bytes_accessed=12 * heads * cap * width,
-            transcendentals=0,
-        ),
+        cost_estimate=pl.CostEstimate(flops=1, bytes_accessed=1, transcendentals=0),
         name="place",
-    )(scalars, *labels, *map(keep_hbm, keys), *map(keep_hbm, values))
+    )(scalars, labels, *map(keep_vmem, keys), *map(keep_vmem, values))
 
 
 def body(key_rows, value_rows, cluster_labels, owner_bounds, init_centroids):
@@ -543,15 +504,11 @@
     def swap(x, d):
         return lax.ppermute(x, "ctx", [(i, i ^ d) for i in range(n)])
 
-    def cube(x):
-        blocks = [x]
-        for m in range(1, n):
-            low = m & -m
-            blocks.append(swap(blocks[m ^ low], low))
-        return blocks
-
     def spread(x):
         return [x] + [swap(x, d) for d in range(1, n)]
+
+    def widen(x, d):
+        return jnp.concatenate([x, swap(x, d)], axis=1)
 
     def aligned(start, size):
         return jnp.minimum(start // 16 * 16, tokens - size)
@@ -561,21 +518,28 @@
         key_rows.reshape(heads * tokens, width),
         value_rows.reshape(heads * tokens, width),
     )
-    keys = cube(own_keys)
-    own_total = own_totals(own_keys, init_centroids)
-    shared = spread(jnp.concatenate([own_total, own_labels], axis=1))
-    totals = [own_total] + [x[:, 0:1] for x in shared[1:]]
-    labels = [own_labels] + [x[:, 1:2] for x in shared[1:]]
+    keys = {0: own_keys}
+    d = 1
+    while d < n:
+        keys[d] = swap(own_keys, d)
+        d *= 2
+    labels = widen(own_labels, 1)
+    total_keys, labels = lax.optimization_barrier((own_keys, labels))
+    own_total = own_totals(total_keys, init_centroids)
+    totals = own_total
+    d = 1
+    while d < n:
+        labels = widen(labels, d) if d > 1 else labels
+        totals = widen(totals, d)
+        d *= 2
 
     place_ids = jnp.arange(tokens, dtype=jnp.int32)
-    orders = [
-        labels[m].astype(jnp.int32) * everyone + (me ^ m) * tokens + place_ids
-        for m in range(n)
-    ]
-    ranks = own_ranks(orders[0], jnp.concatenate(orders, axis=2))
+    peers = me ^ jnp.arange(n, dtype=jnp.int32)
+    block_labels = labels.astype(jnp.int32)
+    orders = block_labels * everyone + (peers[:, None] * tokens + place_ids)
+    ranks = own_ranks(orders[:, 0:1], orders.reshape(heads, 1, everyone))
     low = lax.dynamic_slice_in_dim(owner_bounds, me, 1, 1)
     high = lax.dynamic_slice_in_dim(owner_bounds, me + 1, 1, 1)
-    block_labels = jnp.concatenate(labels, axis=1).astype(jnp.int32)
     below = jnp.sum((block_labels < low[:, :, None]).astype(jnp.int32), axis=2)
     first = jnp.sum(below, axis=1, keepdims=True)
     key_starts = aligned(below, key_size)
@@ -583,15 +547,23 @@
     one = jnp.ones((1, n), jnp.int32)
     scalars = jnp.stack([key_starts, gaps, low * one, high * one, first * one])
 
+    *came, ranks = lax.optimization_barrier((*keys.values(), ranks))
+    keys = dict(zip(keys, came))
+    for m in range(1, n):
+        if m not in keys:
+            keys[m] = swap(keys[m & (m - 1)], m & -m)
+    keys = [keys[m] for m in range(n)]
+
     sums, unit, cents = first_block(
-        me.reshape(1), keys[0], totals[0], init_centroids, n, None
+        me.reshape(1), own_keys, own_total, init_centroids, n, None
     )
     units = [unit]
     for m in range(1, n):
-        sums, unit = first_block(me.reshape(1), keys[m], totals[m], cents, n, sums)
+        sums, unit = first_block(
+            me.reshape(1), keys[m], totals[:, m : m + 1], cents, n, sums
+        )
         units.append(unit)
-        if m == 1:
-            peers = jnp.stack([me ^ m for m in range(n)])
+        if m == min(2, n - 1):
             peer_low = jnp.take(owner_bounds, peers, axis=1)
             own_below = jnp.sum(
                 (own_labels.astype(jnp.int32) < peer_low[:, :, None]).astype(jnp.int32), axis=2
@@ -605,6 +577,7 @@
     raw, part = raw_weights(sums, units)
     out = weighted_sums(raw, units, spread(part))
 
+    scalars, out = lax.optimization_barrier((scalars, out))
     placed = place(scalars, labels, keys, values, key_size, cap)
     shape = (cap, heads, width)
     return out, placed[0].reshape(shape), placed[1].reshape(shape)

time: 103 us -> 109 us (1.058)
  waiting for transfers between devices: 17 us -> 30.6 us
  Pallas kernels: 55.1 us -> 50.1 us
  local copies, waits for them, and re-layouts: 9.38 us -> 5.67 us
  starting transfers between devices: 19.3 us -> 20.9 us
    ppermute x12 -> x13, waiting for transfers between devices: 17 us -> 30.6 us  [swap(): return lax.ppermute(x, 'ctx', [(i, i ^ d) for i in range(n)])]
    unnamed x28 -> x15, local copies, waits for them, and re-layouts: 8.4 us -> 4.58 us
    pallas_call x4, Pallas kernels: 16 us -> 13 us  [first_block(): pl.pallas_call(functools.partial(first_kernel, fresh), grid_spec=pltpu.Pr...]
    ppermute x12 -> x13, starting transfers between devices: 19.3 us -> 20.9 us  [swap(): return lax.ppermute(x, 'ctx', [(i, i ^ d) for i in range(n)])]
    pallas_call x1, Pallas kernels: 10.1 us -> 8.57 us  [place(): pl.pallas_call(functools.partial(place_kernel, blocks, size), grid=(cap /...]
  transfers between devices with their start and end apart: 12 -> 13, of which waited for: 2 -> 5; matrix products, arithmetic and copies ran while one was open for 2% -> 3% of each run, Pallas kernels for 36% -> 34%
where the time goes in v4:
time: 109 us
  Pallas kernels  50.1 us (46%)
  waiting for transfers between devices  30.6 us (28%)
  starting transfers between devices  20.9 us (19%)
  local copies, waits for them, and re-layouts  5.67 us (5%)
    ppermute x13, waiting for transfers between devices, swap(): return lax.ppermute(x, 'ctx', [(i, i ^ d) for i in range(n)])  30.6 us
    ppermute x13, starting transfers between devices, swap(): return lax.ppermute(x, 'ctx', [(i, i ^ d) for i in range(n)])  20.9 us
    pallas_call x4, Pallas kernels, first_block(): pl.pallas_call(functools.partial(first_kernel, fresh), grid_spec=pltpu.Pr...  13 us
    pallas_call x1, Pallas kernels, place(): pl.pallas_call(functools.partial(place_kernel, blocks, size), grid=(cap /...  8.57 us
    pallas_call x1, Pallas kernels, own_totals(): pl.pallas_call(totals_kernel, grid=(heads, count // rows), in_specs=[in_v...  7.57 us
    pallas_call x1, Pallas kernels, weighted_sums(): pl.pallas_call(functools.partial(sums_kernel, blocks), grid=(heads,), in_...  6.34 us
    pallas_call x1, Pallas kernels, raw_weights(): pl.pallas_call(functools.partial(raw_kernel, len(units)), grid=(heads,),...  5.03 us
    unnamed x15, local copies, waits for them, and re-layouts  4.58 us
  transfers between devices with their start and end apart: 13, of which 5 were waited for; matrix products, arithmetic and copies ran while one was open for 3% of the time, Pallas kernels for 34%

profile of v4, /device:TPU:0, one launch (start us, length us, event | category | flops | bytes accessed | tf_op | source)
XLA Modules:
  0.0 108.9 jit_solution(8492588642283844117)
XLA Ops:
  0.6 0.0 copy-start.4
  0.6 4.6 %sort_tokens.1 = (bf16[2,1024,128]{2,1,0:T(8,128)(2,1)S(1)}, bf16[2,1024,128]{2,1,0:T(8,128)(2,1)S(1)}, f32[2,1,1024]{2,1,0:T(1,128)S(1)}) custom-call(s32[2,1024]{1,0:T(2,128)} %label_hbm.1, bf16[2048,128]{1,0:T(8,128)(2,1)} %bitcast.35, bf16[2048,128]{1,0:T(8,128)(2,1)} %bitcast.36), custom_call_target="tpu_custom_call" | custom-call | flops 1073741824 | bytes 2097152 | tf_op jit(solution)/shard_map/sort_tokens/pallas_call | solution.py:149
  5.2 0.0 copy-start.2
  5.2 0.8 copy-done.2
  6.0 3.0 %collective-permute-start.2 = (bf16[2,1024,128]{2,1,0:T(8,128)(2,1)S(1)}, bf16[2,1024,128]{2,1,0:T(8,128)(2,1)S(1)}, u32[]{:S(2)}, u32[]{:S(2)}) collective-permute-start(bf16[2,1024,128]{2,1,0:T(8,128)(2,1)S(1)} %get-tuple-element.62.keys_ref.refs_0_), channel_id=1, source_target_pairs={{0,4},{4,0},{8,12},{12,8},{1,5},{5,1},{9,13},{13,9},{2,6},{6,2},{1... | collective-permute-start | bytes 1572872 | tf_op jit(solution)/shard_map/ppermute | solution.py:505
  9.0 2.6 %collective-permute-start.3 = (bf16[2,1024,128]{2,1,0:T(8,128)(2,1)S(1)}, bf16[2,1024,128]{2,1,0:T(8,128)(2,1)S(1)}, u32[]{:S(2)}, u32[]{:S(2)}) collective-permute-start(bf16[2,1024,128]{2,1,0:T(8,128)(2,1)S(1)} %get-tuple-element.62.keys_ref.refs_0_), channel_id=1, source_target_pairs={{0,8},{4,12},{8,0},{12,4},{1,9},{5,13},{9,1},{13,5},{2,10},{6,14},... | collective-permute-start | bytes 1572872 | tf_op jit(solution)/shard_map/ppermute | solution.py:505
  11.6 0.4 collective-permute-start
  12.1 0.1 iota_add_fusion
  12.2 0.8 copy.19
  13.0 0.6 gather_fusion
  13.5 0.1 select_bitcast_fusion
  13.6 0.1 copy.20
  13.7 0.1 add.94
  13.8 0.2 convert_reduce_fusion.2
  14.0 18.2 %collective-permute-done = f32[2,1,1024]{2,1,0:T(1,128)S(1)} collective-permute-done((f32[2,1,1024]{2,1,0:T(1,128)S(1)}, f32[2,1,1024]{2,1,0:T(1,128)S(1)}, u32[]{:S(2)}, u32[]{:S(2)}) %collective-permute-start) | collective-permute-done | bytes 8224 | tf_op jit(solution)/shard_map/ppermute | solution.py:505
  32.3 7.6 %own_totals.1.tot_ref = f32[2,1,1024]{2,1,0:T(1,128)S(1)} custom-call(bf16[2,1024,128]{2,1,0:T(8,128)(2,1)S(1)} %get-tuple-element.62.keys_ref.refs_0_, f32[2,4096,128]{2,1,0:T(8,128)} %cent_in.1), custom_call_target="tpu_custom_call" | custom-call | flops 4294967296 | bytes 4194304 | tf_op jit(solution)/shard_map/own_totals/pallas_call | solution.py:254
  39.9 2.0 %collective-permute-start.5 = (f32[2,1,1024]{2,1,0:T(1,128)S(1)}, f32[2,1,1024]{2,1,0:T(1,128)S(1)}, u32[]{:S(2)}, u32[]{:S(2)}) collective-permute-start(f32[2,1,1024]{2,1,0:T(1,128)S(1)} %own_totals.1.tot_ref), channel_id=1, source_target_pairs={{0,4},{4,0},{8,12},{12,8},{1,5},{5,1},{9,13},{13,9},{2,6},{6,2},{1... | collective-permute-start | bytes 24584 | tf_op jit(solution)/shard_map/ppermute | solution.py:505
  41.8 0.0 copy-done.4
  41.9 0.2 dynamic-slice_reduce_fusion
  42.1 1.4 %collective-permute-start.1 = (f32[2,2,1024]{2,1,0:T(2,128)S(1)}, f32[2,2,1024]{2,1,0:T(2,128)S(1)}, u32[]{:S(2)}, u32[]{:S(2)}) collective-permute-start(f32[2,2,1024]{2,1,0:T(2,128)S(1)} %pad_maximum_fusion.1), channel_id=1, source_target_pairs={{0,8},{4,12},{8,0},{12,4},{1,9},{5,13},{9,1},{13,5},{2,10},{6,14},... | collective-permute-start | bytes 49160 | tf_op jit(solution)/shard_map/ppermute | solution.py:505
  43.5 4.1 %first_block.4 = (f32[2,1024,128]{2,1,0:T(8,128)S(1)}, bf16[2,1024,128]{2,1,0:T(8,128)(2,1)S(1)}, bf16[2,1024,128]{2,1,0:T(8,128)(2,1)S(1)}) custom-call(s32[1]{0:T(128)} %bitcast.3._, bf16[2,1024,128]{2,1,0:T(8,128)(2,1)S(1)} %get-tuple-element.62.keys_ref.refs_0_, f32[2,1,1024]{2,1,0:T(1,128)S(1)} %own_totals.1.tot_ref, f32[2,4096,128]{2,1,0:T(8,128)} %cent_in.1), custom_call_target="tpu_custom_call" | custom-call | flops 1 | bytes 1 | tf_op jit(solution)/shard_map/first_block/pallas_call | solution.py:328
  47.6 0.0 copy-start
  47.6 0.8 copy-done
  48.4 0.0 collective-permute-done.5.tot_ref
  48.4 1.7 %collective-permute-start.6 = (f32[2,2,1024]{2,1,0:T(2,128)S(1)}, f32[2,2,1024]{2,1,0:T(2,128)S(1)}, u32[]{:S(2)}, u32[]{:S(2)}) collective-permute-start(f32[2,2,1024]{2,1,0:T(2,128)S(1)} %pad_maximum_fusion.2), channel_id=1, source_target_pairs={{0,8},{4,12},{8,0},{12,4},{1,9},{5,13},{9,1},{13,5},{2,10},{6,14},... | collective-permute-start | bytes 49160 | tf_op jit(solution)/shard_map/ppermute | solution.py:505
  50.1 0.0 collective-permute-done.1
  50.1 0.3 convert_reduce_fusion
  50.3 0.1 mul.60
  50.5 4.4 %own_ranks.1.rank_ref = s32[2,1,1024]{2,1,0:T(1,128)S(1)} custom-call(s32[2,1,1024]{2,1,0:T(1,128)S(1)} %slice_add_fusion.own_ref, s32[2,1,4096]{2,1,0:T(1,128)S(1)} %broadcast_add_fusion.all_ref), custom_call_target="tpu_custom_call" | custom-call | flops 25165824 | bytes 65536 | tf_op jit(solution)/shard_map/own_ranks/pallas_call | solution.py:214
  54.9 0.0 collective-permute-done.2.keys_ref.refs_1_
  54.9 0.0 collective-permute-done.3.keys_ref.refs_2_
  54.9 0.2 collective-permute-start.4
  55.1 0.1 constant_dynamic-update-slice_fusion.2
  55.2 0.1 constant_dynamic-update-slice_fusion.1
  55.3 0.0 collective-permute-done.6
  55.3 3.0 %first_block.5 = (f32[2,1024,128]{2,1,0:T(8,128)S(1)}, bf16[2,1024,128]{2,1,0:T(8,128)(2,1)S(1)}) custom-call(s32[1]{0:T(128)} %bitcast.3._, bf16[2,1024,128]{2,1,0:T(8,128)(2,1)S(1)} %collective-permute-done.2.keys_ref.refs_1_, f32[2,1,1024]{2,1,0:T(1,128)S(1)} %collective-permute-done.5.tot_ref, ...), custom_call_target="tpu_custom_call", output_to_operand_aliasing={{0}: (4, {})} | custom-call | flops 1 | bytes 1 | tf_op jit(solution)/shard_map/first_block/pallas_call | solution.py:328
  58.3 3.0 %first_block.6 = (f32[2,1024,128]{2,1,0:T(8,128)S(1)}, bf16[2,1024,128]{2,1,0:T(8,128)(2,1)S(1)}) custom-call(s32[1]{0:T(128)} %bitcast.3._, bf16[2,1024,128]{2,1,0:T(8,128)(2,1)S(1)} %collective-permute-done.3.keys_ref.refs_2_, f32[2,1,1024]{2,1,0:T(1,128)S(1)} %get-tuple-element.73.tot_ref, ...), custom_call_target="tpu_custom_call", output_to_operand_aliasing={{0}: (4, {})} | custom-call | flops 1 | bytes 1 | tf_op jit(solution)/shard_map/first_block/pallas_call | solution.py:328
  61.3 0.0 copy-start.3
  61.3 1.0 copy-done.3
  62.3 0.6 windows.1
  63.0 2.0 %collective-permute-start.10 = (bf16[2,544,128]{2,1,0:T(8,128)(2,1)S(1)}, bf16[2,544,128]{2,1,0:T(8,128)(2,1)S(1)}, u32[]{:S(2)}, u32[]{:S(2)}) collective-permute-start(bf16[2,544,128]{2,1,0:T(8,128)(2,1)S(1)} %get-tuple-element.64), channel_id=1, source_target_pairs={{0,4},{4,0},{8,12},{12,8},{1,5},{5,1},{9,13},{13,9},{2,6},{6,2},{1... | collective-permute-start | bytes 835592 | tf_op jit(solution)/shard_map/ppermute | solution.py:505
  64.9 1.3 %collective-permute-start.11 = (bf16[2,544,128]{2,1,0:T(8,128)(2,1)S(1)}, bf16[2,544,128]{2,1,0:T(8,128)(2,1)S(1)}, u32[]{:S(2)}, u32[]{:S(2)}) collective-permute-start(bf16[2,544,128]{2,1,0:T(8,128)(2,1)S(1)} %get-tuple-element.65), channel_id=1, source_target_pairs={{0,8},{4,12},{8,0},{12,4},{1,9},{5,13},{9,1},{13,5},{2,10},{6,14},... | collective-permute-start | bytes 835592 | tf_op jit(solution)/shard_map/ppermute | solution.py:505
  66.2 1.2 %collective-permute-start.12 = (bf16[2,544,128]{2,1,0:T(8,128)(2,1)S(1)}, bf16[2,544,128]{2,1,0:T(8,128)(2,1)S(1)}, u32[]{:S(2)}, u32[]{:S(2)}) collective-permute-start(bf16[2,544,128]{2,1,0:T(8,128)(2,1)S(1)} %get-tuple-element.66), channel_id=1, source_target_pairs={{0,12},{4,8},{8,4},{12,0},{1,13},{5,9},{9,5},{13,1},{2,14},{6,10},... | collective-permute-start | bytes 835592 | tf_op jit(solution)/shard_map/ppermute | solution.py:505
  67.4 7.4 %collective-permute-done.4.keys_ref.refs_3_ = bf16[2,1024,128]{2,1,0:T(8,128)(2,1)S(1)} collective-permute-done((bf16[2,1024,128]{2,1,0:T(8,128)(2,1)S(1)}, bf16[2,1024,128]{2,1,0:T(8,128)(2,1)S(1)}, u32[]{:S(2)}, u32[]{:S(2)}) %collective-permute-start.4) | collective-permute-done | bytes 524320 | tf_op jit(solution)/shard_map/ppermute | solution.py:505
  74.8 3.0 %first_block.7 = (f32[2,1024,128]{2,1,0:T(8,128)S(1)}, bf16[2,1024,128]{2,1,0:T(8,128)(2,1)S(1)}) custom-call(s32[1]{0:T(128)} %bitcast.3._, bf16[2,1024,128]{2,1,0:T(8,128)(2,1)S(1)} %collective-permute-done.4.keys_ref.refs_3_, f32[2,1,1024]{2,1,0:T(1,128)S(1)} %get-tuple-element.74.tot_ref, ...), custom_call_target="tpu_custom_call", output_to_operand_aliasing={{0}: (4, {})} | custom-call | flops 1 | bytes 1 | tf_op jit(solution)/shard_map/first_block/pallas_call | solution.py:328
  77.7 0.0 copy-start.1
  77.8 1.0 copy-done.1
  78.8 5.0 %raw_weights.1 = (bf16[2,1024,4096]{2,1,0:T(8,128)(2,1)S(1)}, f32[2,1,4096]{2,1,0:T(1,128)S(1)}) custom-call(f32[2,1024,128]{2,1,0:T(8,128)S(1)} %get-tuple-element.53.sums_ref, bf16[2,1024,128]{2,1,0:T(8,128)(2,1)S(1)} %copy-done.1, bf16[2,1024,128]{2,1,0:T(8,128)(2,1)S(1)} %get-tuple-element.55.refs_1_.refs_5_, ...), custom_call_target="tpu_custom_call" | custom-call | flops 1 | bytes 1 | tf_op jit(solution)/shard_map/raw_weights/pallas_call | solution.py:366
  83.8 0.1 collective-permute-start.7
  83.9 0.1 constant_dynamic-update-slice_fusion.scalar_ref
  84.0 2.6 %collective-permute-start.8 = (f32[2,1,4096]{2,1,0:T(1,128)S(1)}, f32[2,1,4096]{2,1,0:T(1,128)S(1)}, u32[]{:S(2)}, u32[]{:S(2)}) collective-permute-start(f32[2,1,4096]{2,1,0:T(1,128)S(1)} %get-tuple-element.59.refs_0_), channel_id=1, source_target_pairs={{0,8},{4,12},{8,0},{12,4},{1,9},{5,13},{9,1},{13,5},{2,10},{6,14},... | collective-permute-start | bytes 98312 | tf_op jit(solution)/shard_map/ppermute | solution.py:505
  86.6 1.7 %collective-permute-done.7.refs_1_ = f32[2,1,4096]{2,1,0:T(1,128)S(1)} collective-permute-done((f32[2,1,4096]{2,1,0:T(1,128)S(1)}, f32[2,1,4096]{2,1,0:T(1,128)S(1)}, u32[]{:S(2)}, u32[]{:S(2)}) %collective-permute-start.7) | collective-permute-done | bytes 32800 | tf_op jit(solution)/shard_map/ppermute | solution.py:505
  88.3 2.4 %collective-permute-start.9 = (f32[2,1,4096]{2,1,0:T(1,128)S(1)}, f32[2,1,4096]{2,1,0:T(1,128)S(1)}, u32[]{:S(2)}, u32[]{:S(2)}) collective-permute-start(f32[2,1,4096]{2,1,0:T(1,128)S(1)} %get-tuple-element.59.refs_0_), channel_id=1, source_target_pairs={{0,12},{4,8},{8,4},{12,0},{1,13},{5,9},{9,5},{13,1},{2,14},{6,10},... | collective-permute-start | bytes 98312 | tf_op jit(solution)/shard_map/ppermute | solution.py:505
  90.8 1.2 %collective-permute-done.8.refs_2_ = f32[2,1,4096]{2,1,0:T(1,128)S(1)} collective-permute-done((f32[2,1,4096]{2,1,0:T(1,128)S(1)}, f32[2,1,4096]{2,1,0:T(1,128)S(1)}, u32[]{:S(2)}, u32[]{:S(2)}) %collective-permute-start.8) | collective-permute-done | bytes 32800 | tf_op jit(solution)/shard_map/ppermute | solution.py:505
  92.0 2.0 %collective-permute-done.9.refs_3_ = f32[2,1,4096]{2,1,0:T(1,128)S(1)} collective-permute-done((f32[2,1,4096]{2,1,0:T(1,128)S(1)}, f32[2,1,4096]{2,1,0:T(1,128)S(1)}, u32[]{:S(2)}, u32[]{:S(2)}) %collective-permute-start.9) | collective-permute-done | bytes 32800 | tf_op jit(solution)/shard_map/ppermute | solution.py:505
  94.0 6.3 %weighted_sums.1 = f32[2,1024,128]{2,1,0:T(8,128)} custom-call(bf16[2,1024,4096]{2,1,0:T(8,128)(2,1)S(1)} %get-tuple-element.58.raw_ref, f32[2,1,4096]{2,1,0:T(1,128)S(1)} %get-tuple-element.59.refs_0_, f32[2,1,4096]{2,1,0:T(1,128)S(1)} %collective-permute-done.7.refs_1_, f32[2,1,4096]{2,1,0:T(1,128)S(1)} %collective-permute-done.8.refs_2_, ...), custom_call_target="tpu_custom_call" | custom-call | flops 1 | bytes 1 | tf_op jit(solution)/shard_map/weighted_sums/pallas_call | solution.py:405
  100.4 0.0 collective-permute-done.10.refs_5_
  100.4 0.0 collective-permute-done.11.refs_6_
  100.4 0.0 collective-permute-done.12.refs_7_
  100.4 8.6 %place.1 = (bf16[4096,128]{1,0:T(8,128)(2,1)}, bf16[4096,128]{1,0:T(8,128)(2,1)}) custom-call(s32[5,2,4]{2,1,0:T(2,128)S(1)} %constant_dynamic-update-slice_fusion.scalar_ref, f32[2,4,1024]{2,1,0:T(4,128)S(1)} %pad_maximum_fusion.label_ref, bf16[2,1024,128]{2,1,0:T(8,128)(2,1)S(1)} %get-tuple-element.62.keys_ref.refs_0_, ...), custom_call_target="tpu_custom_call" | custom-call | flops 1 | bytes 1 | tf_op jit(solution)/shard_map/place/pallas_call | solution.py:475
  (18 shorter events, 0.2 us)
Async XLA Ops:
  0.6 41.2 %copy-start.4 = (s32[2,5]{1,0:T(2,128)S(1)}, s32[2,5]{1,0:T(2,128)}, u32[]{:S(2)}) copy-start(s32[2,5]{1,0:T(2,128)} %param.8) | copy-start | bytes 124
  5.2 0.8 copy-start.2
  6.0 48.9 %collective-permute-start.2 = (bf16[2,1024,128]{2,1,0:T(8,128)(2,1)S(1)}, bf16[2,1024,128]{2,1,0:T(8,128)(2,1)S(1)}, u32[]{:S(2)}, u32[]{:S(2)}) collective-permute-start(bf16[2,1024,128]{2,1,0:T(8,128)(2,1)S(1)} %get-tuple-element.62.keys_ref.refs_0_), channel_id=1, source_target_pairs={{0,4},{4,0},{8,12},{12,8},{1,5},{5,1},{9,13},{13,9},{2,6},{6,2},{1... | collective-permute-start | bytes 1572872 | tf_op jit(solution)/shard_map/ppermute | solution.py:505
  9.0 45.9 %collective-permute-start.3 = (bf16[2,1024,128]{2,1,0:T(8,128)(2,1)S(1)}, bf16[2,1024,128]{2,1,0:T(8,128)(2,1)S(1)}, u32[]{:S(2)}, u32[]{:S(2)}) collective-permute-start(bf16[2,1024,128]{2,1,0:T(8,128)(2,1)S(1)} %get-tuple-element.62.keys_ref.refs_0_), channel_id=1, source_target_pairs={{0,8},{4,12},{8,0},{12,4},{1,9},{5,13},{9,1},{13,5},{2,10},{6,14},... | collective-permute-start | bytes 1572872 | tf_op jit(solution)/shard_map/ppermute | solution.py:505
  11.6 20.6 %collective-permute-start = (f32[2,1,1024]{2,1,0:T(1,128)S(1)}, f32[2,1,1024]{2,1,0:T(1,128)S(1)}, u32[]{:S(2)}, u32[]{:S(2)}) collective-permute-start(f32[2,1,1024]{2,1,0:T(1,128)S(1)} %get-tuple-element.37), channel_id=1, source_target_pairs={{0,4},{4,0},{8,12},{12,8},{1,5},{5,1},{9,13},{13,9},{2,6},{6,2},{1... | collective-permute-start | bytes 24584 | tf_op jit(solution)/shard_map/ppermute | solution.py:505
  39.9 8.5 %collective-permute-start.5 = (f32[2,1,1024]{2,1,0:T(1,128)S(1)}, f32[2,1,1024]{2,1,0:T(1,128)S(1)}, u32[]{:S(2)}, u32[]{:S(2)}) collective-permute-start(f32[2,1,1024]{2,1,0:T(1,128)S(1)} %own_totals.1.tot_ref), channel_id=1, source_target_pairs={{0,4},{4,0},{8,12},{12,8},{1,5},{5,1},{9,13},{13,9},{2,6},{6,2},{1... | collective-permute-start | bytes 24584 | tf_op jit(solution)/shard_map/ppermute | solution.py:505
  42.1 8.0 %collective-permute-start.1 = (f32[2,2,1024]{2,1,0:T(2,128)S(1)}, f32[2,2,1024]{2,1,0:T(2,128)S(1)}, u32[]{:S(2)}, u32[]{:S(2)}) collective-permute-start(f32[2,2,1024]{2,1,0:T(2,128)S(1)} %pad_maximum_fusion.1), channel_id=1, source_target_pairs={{0,8},{4,12},{8,0},{12,4},{1,9},{5,13},{9,1},{13,5},{2,10},{6,14},... | collective-permute-start | bytes 49160 | tf_op jit(solution)/shard_map/ppermute | solution.py:505
  47.6 0.8 copy-start
  48.4 6.9 %collective-permute-start.6 = (f32[2,2,1024]{2,1,0:T(2,128)S(1)}, f32[2,2,1024]{2,1,0:T(2,128)S(1)}, u32[]{:S(2)}, u32[]{:S(2)}) collective-permute-start(f32[2,2,1024]{2,1,0:T(2,128)S(1)} %pad_maximum_fusion.2), channel_id=1, source_target_pairs={{0,8},{4,12},{8,0},{12,4},{1,9},{5,13},{9,1},{13,5},{2,10},{6,14},... | collective-permute-start | bytes 49160 | tf_op jit(solution)/shard_map/ppermute | solution.py:505
  54.9 19.8 %collective-permute-start.4 = (bf16[2,1024,128]{2,1,0:T(8,128)(2,1)S(1)}, bf16[2,1024,128]{2,1,0:T(8,128)(2,1)S(1)}, u32[]{:S(2)}, u32[]{:S(2)}) collective-permute-start(bf16[2,1024,128]{2,1,0:T(8,128)(2,1)S(1)} %collective-permute-done.3.keys_ref.refs_2_), channel_id=1, source_target_pairs={{0,4},{4,0},{8,12},{12,8},{1,5},{5,1},{9,13},{13,9},{2,6},{6,2},{1... | collective-permute-start | bytes 1572872 | tf_op jit(solution)/shard_map/ppermute | solution.py:505
  61.3 1.0 copy-start.3
  63.0 37.4 %collective-permute-start.10 = (bf16[2,544,128]{2,1,0:T(8,128)(2,1)S(1)}, bf16[2,544,128]{2,1,0:T(8,128)(2,1)S(1)}, u32[]{:S(2)}, u32[]{:S(2)}) collective-permute-start(bf16[2,544,128]{2,1,0:T(8,128)(2,1)S(1)} %get-tuple-element.64), channel_id=1, source_target_pairs={{0,4},{4,0},{8,12},{12,8},{1,5},{5,1},{9,13},{13,9},{2,6},{6,2},{1... | collective-permute-start | bytes 835592 | tf_op jit(solution)/shard_map/ppermute | solution.py:505
  64.9 35.5 %collective-permute-start.11 = (bf16[2,544,128]{2,1,0:T(8,128)(2,1)S(1)}, bf16[2,544,128]{2,1,0:T(8,128)(2,1)S(1)}, u32[]{:S(2)}, u32[]{:S(2)}) collective-permute-start(bf16[2,544,128]{2,1,0:T(8,128)(2,1)S(1)} %get-tuple-element.65), channel_id=1, source_target_pairs={{0,8},{4,12},{8,0},{12,4},{1,9},{5,13},{9,1},{13,5},{2,10},{6,14},... | collective-permute-start | bytes 835592 | tf_op jit(solution)/shard_map/ppermute | solution.py:505
  66.2 34.1 %collective-permute-start.12 = (bf16[2,544,128]{2,1,0:T(8,128)(2,1)S(1)}, bf16[2,544,128]{2,1,0:T(8,128)(2,1)S(1)}, u32[]{:S(2)}, u32[]{:S(2)}) collective-permute-start(bf16[2,544,128]{2,1,0:T(8,128)(2,1)S(1)} %get-tuple-element.66), channel_id=1, source_target_pairs={{0,12},{4,8},{8,4},{12,0},{1,13},{5,9},{9,5},{13,1},{2,14},{6,10},... | collective-permute-start | bytes 835592 | tf_op jit(solution)/shard_map/ppermute | solution.py:505
  77.7 1.0 copy-start.1
  83.8 4.5 %collective-permute-start.7 = (f32[2,1,4096]{2,1,0:T(1,128)S(1)}, f32[2,1,4096]{2,1,0:T(1,128)S(1)}, u32[]{:S(2)}, u32[]{:S(2)}) collective-permute-start(f32[2,1,4096]{2,1,0:T(1,128)S(1)} %get-tuple-element.59.refs_0_), channel_id=1, source_target_pairs={{0,4},{4,0},{8,12},{12,8},{1,5},{5,1},{9,13},{13,9},{2,6},{6,2},{1... | collective-permute-start | bytes 98312 | tf_op jit(solution)/shard_map/ppermute | solution.py:505
  84.0 8.0 %collective-permute-start.8 = (f32[2,1,4096]{2,1,0:T(1,128)S(1)}, f32[2,1,4096]{2,1,0:T(1,128)S(1)}, u32[]{:S(2)}, u32[]{:S(2)}) collective-permute-start(f32[2,1,4096]{2,1,0:T(1,128)S(1)} %get-tuple-element.59.refs_0_), channel_id=1, source_target_pairs={{0,8},{4,12},{8,0},{12,4},{1,9},{5,13},{9,1},{13,5},{2,10},{6,14},... | collective-permute-start | bytes 98312 | tf_op jit(solution)/shard_map/ppermute | solution.py:505
  88.3 5.7 %collective-permute-start.9 = (f32[2,1,4096]{2,1,0:T(1,128)S(1)}, f32[2,1,4096]{2,1,0:T(1,128)S(1)}, u32[]{:S(2)}, u32[]{:S(2)}) collective-permute-start(f32[2,1,4096]{2,1,0:T(1,128)S(1)} %get-tuple-element.59.refs_0_), channel_id=1, source_target_pairs={{0,12},{4,8},{8,4},{12,0},{1,13},{5,9},{9,5},{13,1},{2,14},{6,10},... | collective-permute-start | bytes 98312 | tf_op jit(solution)/shard_map/ppermute | solution.py:505

commit v5 on v4

--- a/solution.py
+++ b/solution.py
@@ -92,38 +92,31 @@
     )
 
 
-def sort_kernel(label_hbm, keys_hbm, values_hbm, *refs):
-    out_keys, out_values, out_labels, flat_ref, wide_ref, both_ref, order_ref, label_ref, sems = refs
+def sort_kernel(label_hbm, keys_hbm, *refs):
+    out_keys, out_labels, out_spots, flat_ref, wide_ref, rows_ref, order_ref, label_ref, sems = refs
     head = pl.program_id(0)
     _, tokens, width = out_keys.shape
-    copies = [
-        pltpu.make_async_copy(source, flat_ref.at[side], sems.at[side])
-        for side, source in enumerate((keys_hbm, values_hbm))
-    ]
+    copy = pltpu.make_async_copy(keys_hbm, flat_ref, sems.at[0])
 
     @pl.when(head == 0)
     def _():
-        label_copy = pltpu.make_async_copy(label_hbm, label_ref, sems.at[2])
+        label_copy = pltpu.make_async_copy(label_hbm, label_ref, sems.at[1])
         label_copy.start()
-        for copy in copies:
-            copy.start()
+        copy.start()
         label_copy.wait()
 
     label = label_ref[pl.ds(head, 1), :]
     order = label * tokens + lax.broadcasted_iota(jnp.int32, label.shape, 1)
     order_ref[0] = order
     spot = count_below(order_ref, order, tokens)
+    out_spots[head] = spot
 
     @pl.when(head == 0)
     def _():
-        for side, copy in enumerate(copies):
-            copy.wait()
-            split_heads(flat_ref.at[side], wide_ref.at[side])
-
-    for side in range(2):
-        both_ref[:, side * width : (side + 1) * width] = head_rows(
-            wide_ref.at[side], head, wide_ref.shape[1] // tokens
-        ).astype(BF16)
+        copy.wait()
+        split_heads(flat_ref, wide_ref)
+
+    rows_ref[...] = head_rows(wide_ref, head, wide_ref.shape[0] // tokens).astype(BF16)
     digits = jnp.concatenate(
         [
             jnp.broadcast_to(label >> 6, (8, tokens)),
@@ -135,94 +128,109 @@
     rows = 512
     for r in range(0, tokens, rows):
         pick = one_hot_rows(rows, spot - r)
-        moved = dot_nn(pick, both_ref[...]).astype(BF16)
-        out_keys[head, r : r + rows] = moved[:, :width]
-        out_values[head, r : r + rows] = moved[:, width:]
+        out_keys[head, r : r + rows] = dot_nn(pick, rows_ref[...]).astype(BF16)
         digit = dot_nt(digits, pick)
         out_labels[head, :, r : r + rows] = digit[0:1] * 64.0 + digit[8:9]
 
 
-def sort_tokens(labels, keys, values):
+def sort_keys(labels, keys):
     heads, tokens = labels.shape
     flat, width = keys.shape
-    rows = pltpu.VMEM((heads, tokens, width), BF16)
     return pl.pallas_call(
         sort_kernel,
         grid=(heads,),
-        in_specs=[anywhere()] * 3,
+        in_specs=[anywhere()] * 2,
         out_specs=(in_vmem(),) * 3,
-        out_shape=(rows, rows, pltpu.VMEM((heads, 1, tokens), F32)),
+        out_shape=(
+            pltpu.VMEM((heads, tokens, width), BF16),
+            pltpu.VMEM((heads, 1, tokens), F32),
+            pltpu.VMEM((heads, 1, tokens), jnp.int32),
+        ),
         scratch_shapes=[
-            pltpu.VMEM((2, flat, width), BF16),
-            pltpu.VMEM((2, flat, width), F32),
-            pltpu.VMEM((tokens, 2 * width), BF16),
+            pltpu.VMEM((flat, width), BF16),
+            pltpu.VMEM((flat, width), F32),
+            pltpu.VMEM((tokens, width), BF16),
             pltpu.VMEM((1, 1, tokens), jnp.int32),
             pltpu.VMEM(labels.shape, jnp.int32),
-            pltpu.SemaphoreType.DMA((3,)),
-        ],
-        compiler_params=params(),
-        cost_estimate=pl.CostEstimate(
-            flops=4 * heads * tokens * tokens * width,
-            bytes_accessed=8 * flat * width,
-            transcendentals=0,
-        ),
-        name="sort_tokens",
-    )(keep_hbm(labels), keep_hbm(keys), keep_hbm(values))
-
-
-def windows_kernel(size, start_ref, rank_ref, values_ref, *out_refs):
-    heads, tokens, _ = values_ref.shape
+            pltpu.SemaphoreType.DMA((2,)),
+        ],
+        compiler_params=params(),
+        name="sort_keys",
+    )(keep_hbm(labels), keep_hbm(keys))
+
+
+def windows_kernel(size, start_ref, spot_ref, values_hbm, *refs):
+    out_refs, (flat_ref, wide_ref, rows_ref, sem) = refs[:-4], refs[-4:]
+    heads, _, tokens = spot_ref.shape
+    copy = pltpu.make_async_copy(values_hbm, flat_ref, sem)
+    copy.start()
+    copy.wait()
+    split_heads(flat_ref, wide_ref)
+    rows = 512
     for h in range(heads):
-        rank = rank_ref[h]
-        digits = [
-            digit[:, t : t + LANES]
-            for digit in (rank >> 7, rank & 127)
-            for t in range(0, tokens, LANES)
-        ]
-        digits = jnp.concatenate(digits, axis=0).astype(F32).astype(BF16)
+        values = head_rows(wide_ref, h, heads).astype(BF16)
+        for r in range(0, tokens, rows):
+            pick = one_hot_rows(rows, spot_ref[h] - r)
+            rows_ref[h, r : r + rows] = dot_nn(pick, values).astype(BF16)
         for m, out_ref in enumerate(out_refs):
             start = pl.multiple_of(start_ref[h, m], 16)
-            out_ref[h, :size] = values_ref[h, pl.ds(start, size), :]
-            out_ref[h, size:] = digits
-
-
-def windows(starts, ranks, values, size):
-    heads, tokens, width = values.shape
+            out_ref[h] = rows_ref[h, pl.ds(start, size), :]
+
+
+def windows(starts, spots, values, size):
+    heads, _, tokens = spots.shape
+    flat, width = values.shape
     n = starts.shape[1]
-    out = pltpu.VMEM((heads, size + 2 * tokens // LANES, width), BF16)
+    out = pltpu.VMEM((heads, size, width), BF16)
     return pl.pallas_call(
         functools.partial(windows_kernel, size),
-        in_specs=[pl.BlockSpec(memory_space=pltpu.SMEM), in_vmem(), in_vmem()],
+        in_specs=[pl.BlockSpec(memory_space=pltpu.SMEM), in_vmem(), anywhere()],
         out_specs=(in_vmem(),) * n,
         out_shape=(out,) * n,
-        compiler_params=params(),
-        cost_estimate=pl.CostEstimate(
-            flops=0, bytes_accessed=4 * n * heads * size * width, transcendentals=0
-        ),
+        scratch_shapes=[
+            pltpu.VMEM((flat, width), BF16),
+            pltpu.VMEM((flat, width), F32),
+            pltpu.VMEM((heads, tokens, width), BF16),
+            pltpu.SemaphoreType.DMA,
+        ],
+        compiler_params=params(),
         name="windows",
-    )(starts, ranks, keep_vmem(values))
-
-
-def rank_kernel(own_ref, all_ref, rank_ref):
-    rank_ref[0] = count_below(all_ref, own_ref[0], all_ref.shape[2])
-
-
-def own_ranks(own, everyone):
-    heads, _, tokens = own.shape
-    count = everyone.shape[2]
-    own_block = pl.BlockSpec((1, 1, tokens), lambda h: (h, 0, 0))
+    )(starts, keep_vmem(spots), keep_hbm(values))
+
+
+def rank_kernel(me_ref, label_ref, rank_ref):
+    n, tokens = label_ref.shape[1:]
+    me = me_ref[0]
+    own = label_ref[0, 0:1, :].astype(jnp.int32)
+    rank = lax.broadcasted_iota(jnp.int32, own.shape, 1)
+    for m in range(1, n):
+        bar = own + ((me ^ m) < me).astype(jnp.int32)
+        bar = jnp.broadcast_to(bar, (16, tokens)).astype(jnp.int16)
+        count = jnp.zeros((16, tokens), BF16)
+        for s in range(0, tokens, LANES):
+            column = row_to_lanes(label_ref[0, m : m + 1, s : s + LANES])
+            column = column.astype(jnp.int32).astype(jnp.int16)
+            for r in range(0, LANES, 16):
+                other = jnp.tile(column[r : r + 16], (1, tokens // LANES))
+                count += jnp.where(other < bar, jnp.ones((), BF16), jnp.zeros((), BF16))
+        rank += jnp.sum(count.astype(F32), axis=0, keepdims=True).astype(jnp.int32)
+    rank_ref[0] = rank.astype(F32)
+
+
+def own_ranks(me, labels):
+    heads, n, tokens = labels.shape
     return pl.pallas_call(
         rank_kernel,
         grid=(heads,),
-        in_specs=[own_block, pl.BlockSpec((1, 1, count), lambda h: (h, 0, 0))],
-        out_specs=own_block,
-        out_shape=jax.ShapeDtypeStruct((heads, 1, tokens), jnp.int32),
-        compiler_params=params(),
-        cost_estimate=pl.CostEstimate(
-            flops=3 * heads * tokens * count, bytes_accessed=65536, transcendentals=0
-        ),
+        in_specs=[
+            pl.BlockSpec(memory_space=pltpu.SMEM),
+            pl.BlockSpec((1, n, tokens), lambda h: (h, 0, 0)),
+        ],
+        out_specs=pl.BlockSpec((1, 1, tokens), lambda h: (h, 0, 0)),
+        out_shape=jax.ShapeDtypeStruct((heads, 1, tokens), F32),
+        compiler_params=params(),
         name="own_ranks",
-    )(own, everyone)
+    )(me, labels)
 
 
 def totals_kernel(keys_ref, cent_ref, tot_ref, unit_ref, sum_ref):
@@ -265,11 +273,6 @@
             pltpu.VMEM((8, tokens), F32),
         ],
         compiler_params=params(),
-        cost_estimate=pl.CostEstimate(
-            flops=4 * heads * tokens * count * width,
-            bytes_accessed=cents.size * 4,
-            transcendentals=heads * tokens * count,
-        ),
         name="own_totals",
     )(keep_vmem(keys), keep_hbm(cents))
 
@@ -337,7 +340,6 @@
         out_shape=tuple(out_shape),
         input_output_aliases=aliases,
         compiler_params=params(),
-        cost_estimate=pl.CostEstimate(flops=1, bytes_accessed=1, transcendentals=0),
         name="first_block",
     )(*args)
 
@@ -374,28 +376,24 @@
         ),
         scratch_shapes=[pltpu.VMEM((rows, width), BF16)],
         compiler_params=params(),
-        cost_estimate=pl.CostEstimate(flops=1, bytes_accessed=1, transcendentals=0),
         name="raw_weights",
     )(keep_vmem(sums), *map(keep_vmem, units))
 
 
 def sums_kernel(blocks, raw_ref, *refs):
     totals, units = refs[:blocks], refs[blocks : 2 * blocks]
-    out_ref, scaled_ref, sum_ref = refs[2 * blocks :]
+    out_ref, scaled_ref = refs[2 * blocks :]
     head = pl.program_id(0)
     tokens = units[0].shape[1]
     for m, unit_ref in enumerate(units):
-        row_total = totals[0][0, :, m * tokens : (m + 1) * tokens]
+        row_total = totals[0][head, :, m * tokens : (m + 1) * tokens]
         for d in range(1, blocks):
             peer = m ^ d
-            row_total += totals[d][0, :, peer * tokens : (peer + 1) * tokens]
-        scale_rows(unit_ref[head], 1.0 / row_total, scaled_ref)
-        more = dot_nn(raw_ref[head, :, m * tokens : (m + 1) * tokens], scaled_ref[...])
-        if m == 0:
-            sum_ref[...] = more
-        else:
-            sum_ref[...] += more
-    out_ref[0] = unit_rows(sum_ref[...])
+            row_total += totals[d][head, :, peer * tokens : (peer + 1) * tokens]
+        scale_rows(
+            unit_ref[head], 1.0 / row_total, scaled_ref.at[m * tokens : (m + 1) * tokens]
+        )
+    out_ref[0] = unit_rows(dot_nn(raw_ref[head], scaled_ref[...]))
 
 
 def weighted_sums(raw, units, totals):
@@ -406,27 +404,23 @@
         functools.partial(sums_kernel, blocks),
         grid=(heads,),
         in_specs=[in_vmem()]
-        + [pl.BlockSpec((1, 1, count), lambda h: (h, 0, 0))] * blocks
-        + [in_vmem()] * blocks,
+        + [in_vmem()] * (2 * blocks),
         out_specs=pl.BlockSpec((1, rows, width), lambda h: (h, 0, 0)),
         out_shape=jax.ShapeDtypeStruct((heads, rows, width), F32),
         scratch_shapes=[
-            pltpu.VMEM((tokens, width), BF16),
-            pltpu.VMEM((rows, width), F32),
-        ],
-        compiler_params=params(),
-        cost_estimate=pl.CostEstimate(flops=1, bytes_accessed=1, transcendentals=0),
+            pltpu.VMEM((count, width), BF16),
+        ],
+        compiler_params=params(),
         name="weighted_sums",
-    )(keep_vmem(raw), *totals, *map(keep_vmem, units))
+    )(keep_vmem(raw), *map(keep_vmem, totals), *map(keep_vmem, units))
 
 
 def place_kernel(blocks, size, scalar_ref, label_ref, *refs):
-    keys, values = refs[:blocks], refs[blocks : 2 * blocks]
+    keys, values, ranks = (refs[i * blocks : (i + 1) * blocks] for i in range(3))
     out_refs, (rows_ref, near_ref, mixed_ref) = refs[-5:-3], refs[-3:]
     step = pl.program_id(0)
     heads, tokens, width = keys[0].shape
-    digit_rows = tokens // LANES
-    sent = values[0].shape[1] - 2 * digit_rows
+    sent = values[0].shape[1]
 
     @pl.when(step == 0)
     def _():
@@ -437,10 +431,8 @@
                 gap = pl.multiple_of(scalar_ref[1, h, m], 16)
                 first = m * size
                 rows_ref[h, first : first + size, :width] = keys[m][h, pl.ds(start, size), :]
-                rows_ref[h, pl.ds(first + gap, sent), width:] = values[m][h, :sent, :]
-                digits = values[m][h, sent:, :].astype(F32)
-                rank = digits[:digit_rows] * 128.0 + digits[digit_rows:]
-                rank = jnp.concatenate([rank[r : r + 1] for r in range(digit_rows)], axis=1)
+                rows_ref[h, pl.ds(first + gap, sent), width:] = values[m][h]
+                rank = ranks[m][h, :, -tokens:]
                 label = label_ref[h, m : m + 1, :]
                 low, high, before = (
                     scalar_ref[i, h, 0].astype(F32) for i in range(2, 5)
@@ -451,13 +443,9 @@
                 near_ref[h, :, m * size : (m + 1) * size] = spot[:, :size]
 
     rows = out_refs[0].shape[0] // heads
-    total_size = blocks * size
-    part = total_size // 2
     for h in range(heads):
-        for t in range(0, total_size, part):
-            pick = one_hot_rows(rows, near_ref[h, :, t : t + part] - step * rows)
-            more = dot_nn(pick, rows_ref[h, t : t + part, :])
-            total = more if t == 0 else total + more
+        pick = one_hot_rows(rows, near_ref[h] - step * rows)
+        total = dot_nn(pick, rows_ref[h])
         for side in range(2):
             mixed_ref[side, pl.Slice(h, rows, heads), :] = total[
                 :, side * width : (side + 1) * width
@@ -466,7 +454,7 @@
         out_refs[side][...] = mixed_ref[side].astype(BF16)
 
 
-def place(scalars, labels, keys, values, size, cap):
+def place(scalars, labels, keys, values, ranks, size, cap):
     blocks = len(keys)
     heads, tokens, width = keys[0].shape
     rows = 512
@@ -477,7 +465,7 @@
         grid=(cap // rows,),
         in_specs=[pl.BlockSpec(memory_space=pltpu.SMEM)]
         + [whole(labels.shape)]
-        + [in_vmem()] * (2 * blocks),
+        + [in_vmem()] * (3 * blocks),
         out_specs=(block, block),
         out_shape=(out, out),
         scratch_shapes=[
@@ -486,16 +474,14 @@
             pltpu.VMEM((2, heads * rows, width), F32),
         ],
         compiler_params=params(),
-        cost_estimate=pl.CostEstimate(flops=1, bytes_accessed=1, transcendentals=0),
         name="place",
-    )(scalars, labels, *map(keep_vmem, keys), *map(keep_vmem, values))
+    )(scalars, labels, *(keep_vmem(x) for x in (*keys, *values, *ranks)))
 
 
 def body(key_rows, value_rows, cluster_labels, owner_bounds, init_centroids):
     n = lax.axis_size("ctx")
     me = lax.axis_index("ctx").astype(jnp.int32)
     tokens, heads, width = key_rows.shape
-    everyone = n * tokens
     cap = 2 * tokens
     slot = cap // n
     send_size = slot + 16
@@ -507,78 +493,63 @@
     def spread(x):
         return [x] + [swap(x, d) for d in range(1, n)]
 
-    def widen(x, d):
-        return jnp.concatenate([x, swap(x, d)], axis=1)
-
     def aligned(start, size):
         return jnp.minimum(start // 16 * 16, tokens - size)
 
-    own_keys, own_values, own_labels = sort_tokens(
-        cluster_labels,
-        key_rows.reshape(heads * tokens, width),
-        value_rows.reshape(heads * tokens, width),
+    me_array = me.reshape(1)
+    own_keys, own_labels, own_spots = sort_keys(
+        cluster_labels, key_rows.reshape(heads * tokens, width)
     )
     keys = {0: own_keys}
     d = 1
     while d < n:
         keys[d] = swap(own_keys, d)
         d *= 2
-    labels = widen(own_labels, 1)
-    total_keys, labels = lax.optimization_barrier((own_keys, labels))
-    own_total = own_totals(total_keys, init_centroids)
-    totals = own_total
-    d = 1
-    while d < n:
-        labels = widen(labels, d) if d > 1 else labels
-        totals = widen(totals, d)
-        d *= 2
-
-    place_ids = jnp.arange(tokens, dtype=jnp.int32)
-    peers = me ^ jnp.arange(n, dtype=jnp.int32)
-    block_labels = labels.astype(jnp.int32)
-    orders = block_labels * everyone + (peers[:, None] * tokens + place_ids)
-    ranks = own_ranks(orders[:, 0:1], orders.reshape(heads, 1, everyone))
+    own_total = own_totals(own_keys, init_centroids)
+    shared = spread(jnp.concatenate([own_total, own_labels], axis=1))
+    totals = [own_total] + [x[:, 0:1] for x in shared[1:]]
+
+    sums, unit, cents = first_block(me_array, own_keys, own_total, init_centroids, n, None)
+    units = [unit]
+    *came, sums = lax.optimization_barrier((*keys.values(), sums))
+    keys = dict(zip(keys, came))
+    for m in range(1, n):
+        if m not in keys:
+            keys[m] = swap(keys[m & (m - 1)], m & -m)
+    keys = [keys[m] for m in range(n)]
+    peer_low = jnp.take(owner_bounds, me ^ jnp.arange(n, dtype=jnp.int32), axis=1)
+    own_below = jnp.sum((own_labels < peer_low[:, :, None]).astype(jnp.int32), axis=2)
+    own_windows = windows(
+        aligned(own_below, send_size),
+        own_spots,
+        value_rows.reshape(heads * tokens, width),
+        send_size,
+    )
+    for m in range(1, n):
+        sums, unit = first_block(me_array, keys[m], totals[m], cents, n, sums)
+        units.append(unit)
+        if m == min(2, n - 1):
+            *own_windows, sums = lax.optimization_barrier((*own_windows, sums))
+            values = [own_windows[0]] + [swap(own_windows[d], d) for d in range(1, n)]
+            labels, sums = lax.optimization_barrier(
+                (jnp.concatenate([x[:, -1:] for x in shared], axis=1), sums)
+            )
+            ranks = own_ranks(me_array, labels)
+
+    raw, part = raw_weights(sums, units)
+    parts = spread(jnp.concatenate([part, ranks], axis=2))
+    out = weighted_sums(raw, units, parts)
+
     low = lax.dynamic_slice_in_dim(owner_bounds, me, 1, 1)
     high = lax.dynamic_slice_in_dim(owner_bounds, me + 1, 1, 1)
-    below = jnp.sum((block_labels < low[:, :, None]).astype(jnp.int32), axis=2)
+    below = jnp.sum((labels < low[:, :, None]).astype(jnp.int32), axis=2)
     first = jnp.sum(below, axis=1, keepdims=True)
     key_starts = aligned(below, key_size)
     gaps = aligned(below, send_size) - key_starts
     one = jnp.ones((1, n), jnp.int32)
     scalars = jnp.stack([key_starts, gaps, low * one, high * one, first * one])
-
-    *came, ranks = lax.optimization_barrier((*keys.values(), ranks))
-    keys = dict(zip(keys, came))
-    for m in range(1, n):
-        if m not in keys:
-            keys[m] = swap(keys[m & (m - 1)], m & -m)
-    keys = [keys[m] for m in range(n)]
-
-    sums, unit, cents = first_block(
-        me.reshape(1), own_keys, own_total, init_centroids, n, None
-    )
-    units = [unit]
-    for m in range(1, n):
-        sums, unit = first_block(
-            me.reshape(1), keys[m], totals[:, m : m + 1], cents, n, sums
-        )
-        units.append(unit)
-        if m == min(2, n - 1):
-            peer_low = jnp.take(owner_bounds, peers, axis=1)
-            own_below = jnp.sum(
-                (own_labels.astype(jnp.int32) < peer_low[:, :, None]).astype(jnp.int32), axis=2
-            )
-            own_windows = windows(
-                aligned(own_below, send_size), ranks, own_values, send_size
-            )
-            *own_windows, sums = lax.optimization_barrier((*own_windows, sums))
-            values = [own_windows[0]] + [swap(own_windows[d], d) for d in range(1, n)]
-
-    raw, part = raw_weights(sums, units)
-    out = weighted_sums(raw, units, spread(part))
-
     scalars, out = lax.optimization_barrier((scalars, out))
-    placed = place(scalars, labels, keys, values, key_size, cap)
+    placed = place(scalars, labels, keys, values, parts, key_size, cap)
     shape = (cap, heads, width)
     return out, placed[0].reshape(shape), placed[1].reshape(shape)
 

time: 109 us -> 86.7 us (0.80)
  waiting for transfers between devices: 30.6 us -> 12.7 us
  starting transfers between devices: 20.9 us -> 18.1 us
  local copies, waits for them, and re-layouts: 5.67 us -> 4.49 us
    ppermute x13 -> x12, waiting for transfers between devices: 30.6 us -> 12.7 us  [swap(): return lax.ppermute(x, 'ctx', [(i, i ^ d) for i in range(n)])]
    ppermute x13 -> x12, starting transfers between devices: 20.9 us -> 18.1 us  [swap(): return lax.ppermute(x, 'ctx', [(i, i ^ d) for i in range(n)])]
    pallas_call x2, Pallas kernels: 8.98 us -> 6.21 us  [the longest x1 4.45 us: sort_keys(): pl.pallas_call(sort_kernel, grid=(heads,), in_specs=[anywhere()] * 2, out...]
    pallas_call x1, Pallas kernels: 0.63 us -> 2.94 us  [windows(): pl.pallas_call(functools.partial(windows_kernel, size), in_specs=[pl.Bloc...]
    unnamed x15 -> x8, local copies, waits for them, and re-layouts: 4.58 us -> 2.75 us
  transfers between devices with their start and end apart: 13 -> 12, of which waited for: 5 -> 4; matrix products, arithmetic and copies ran while one was open for 3% -> 4% of each run, Pallas kernels for 34% -> 42%
where the time goes in v5:
time: 86.7 us; the launch traced here: 86.3 us
  Pallas kernels  49.5 us (57%)
  starting transfers between devices  18.1 us (21%)
  waiting for transfers between devices  12.7 us (15%)
  local copies, waits for them, and re-layouts  4.49 us (5%)
    ppermute x12, starting transfers between devices, swap(): return lax.ppermute(x, 'ctx', [(i, i ^ d) for i in range(n)])  18.1 us
    pallas_call x4, Pallas kernels, first_block(): pl.pallas_call(functools.partial(first_kernel, fresh), grid_spec=pltpu.Pr...  13 us
    ppermute x12, waiting for transfers between devices, swap(): return lax.ppermute(x, 'ctx', [(i, i ^ d) for i in range(n)])  12.7 us
    pallas_call x1, Pallas kernels, place(): pl.pallas_call(functools.partial(place_kernel, blocks, size), grid=(cap /...  8.56 us
    pallas_call x1, Pallas kernels, own_totals(): pl.pallas_call(totals_kernel, grid=(heads, count // rows), in_specs=[in_v...  7.55 us
    pallas_call x1, Pallas kernels, weighted_sums(): pl.pallas_call(functools.partial(sums_kernel, blocks), grid=(heads,), in_...  6.19 us
    pallas_call x1, Pallas kernels, raw_weights(): pl.pallas_call(functools.partial(raw_kernel, len(units)), grid=(heads,),...  5.04 us
    pallas_call x1, Pallas kernels, sort_keys(): pl.pallas_call(sort_kernel, grid=(heads,), in_specs=[anywhere()] * 2, out...  4.45 us
  transfers between devices with their start and end apart: 12, of which 4 were waited for; matrix products, arithmetic and copies ran while one was open for 4% of the time, Pallas kernels for 42%

profile of v5, /device:TPU:0, one launch (start us, length us, event | category | flops | bytes accessed | tf_op | source)
XLA Modules:
  0.0 86.3 jit_solution(8780123474743143723)
XLA Ops:
  0.6 4.4 %sort_keys.1 = (bf16[2,1024,128]{2,1,0:T(8,128)(2,1)S(1)}, f32[2,1,1024]{2,1,0:T(1,128)S(1)}, s32[2,1,1024]{2,1,0:T(1,128)S(1)}) custom-call(s32[2,1024]{1,0:T(2,128)} %label_hbm.1, bf16[2048,128]{1,0:T(8,128)(2,1)} %bitcast.26), custom_call_target="tpu_custom_call" | custom-call | tf_op jit(solution)/shard_map/sort_keys/pallas_call | solution.py:139
  5.1 3.1 %collective-permute-start.3 = (bf16[2,1024,128]{2,1,0:T(8,128)(2,1)S(1)}, bf16[2,1024,128]{2,1,0:T(8,128)(2,1)S(1)}, u32[]{:S(2)}, u32[]{:S(2)}) collective-permute-start(bf16[2,1024,128]{2,1,0:T(8,128)(2,1)S(1)} %get-tuple-element.62.keys_ref.refs_0_), channel_id=1, source_target_pairs={{0,4},{4,0},{8,12},{12,8},{1,5},{5,1},{9,13},{13,9},{2,6},{6,2},{1... | collective-permute-start | bytes 1572872 | tf_op jit(solution)/shard_map/ppermute | solution.py:491
  8.2 2.6 %collective-permute-start.4 = (bf16[2,1024,128]{2,1,0:T(8,128)(2,1)S(1)}, bf16[2,1024,128]{2,1,0:T(8,128)(2,1)S(1)}, u32[]{:S(2)}, u32[]{:S(2)}) collective-permute-start(bf16[2,1024,128]{2,1,0:T(8,128)(2,1)S(1)} %get-tuple-element.62.keys_ref.refs_0_), channel_id=1, source_target_pairs={{0,8},{4,12},{8,0},{12,4},{1,9},{5,13},{9,1},{13,5},{2,10},{6,14},... | collective-permute-start | bytes 1572872 | tf_op jit(solution)/shard_map/ppermute | solution.py:491
  10.8 7.6 %own_totals.1.tot_ref = f32[2,1,1024]{2,1,0:T(1,128)S(1)} custom-call(bf16[2,1024,128]{2,1,0:T(8,128)(2,1)S(1)} %get-tuple-element.62.keys_ref.refs_0_, f32[2,4096,128]{2,1,0:T(8,128)} %cent_in.1), custom_call_target="tpu_custom_call" | custom-call | tf_op jit(solution)/shard_map/own_totals/pallas_call | solution.py:262
  18.4 0.5 collective-permute-start
  18.9 0.0 collective-permute-start.1
  18.9 3.9 %collective-permute-start.2 = (f32[2,2,1024]{2,1,0:T(2,128)S(1)}, f32[2,2,1024]{2,1,0:T(2,128)S(1)}, u32[]{:S(2)}, u32[]{:S(2)}) collective-permute-start(f32[2,2,1024]{2,1,0:T(2,128)S(1)} %pad_maximum_fusion.2), channel_id=1, source_target_pairs={{0,12},{4,8},{8,4},{12,0},{1,13},{5,9},{9,5},{13,1},{2,14},{6,10},... | collective-permute-start | bytes 49160 | tf_op jit(solution)/shard_map/ppermute | solution.py:491
  22.8 0.8 copy.13
  23.6 0.6 gather_fusion
  24.2 0.1 convert_bitcast_fusion
  24.2 0.1 copy.14
  24.3 0.2 convert_reduce_fusion.2
  24.6 4.1 %first_block.4 = (f32[2,1024,128]{2,1,0:T(8,128)S(1)}, bf16[2,1024,128]{2,1,0:T(8,128)(2,1)S(1)}, bf16[2,1024,128]{2,1,0:T(8,128)(2,1)S(1)}) custom-call(s32[1]{0:T(128)} %bitcast.4._.me_ref, bf16[2,1024,128]{2,1,0:T(8,128)(2,1)S(1)} %get-tuple-element.62.keys_ref.refs_0_, f32[2,1,1024]{2,1,0:T(1,128)S(1)} %own_totals.1.tot_ref, f32[2,4096,128]{2,1,0:T(8,128)} %cent_in.1), custom_call_target="tpu_custom_call" | custom-call | tf_op jit(solution)/shard_map/first_block/pallas_call | solution.py:331
  28.7 0.0 copy-start
  28.7 0.8 copy-done
  29.5 1.0 %dynamic-slice_reduce_fusion = (s32[2]{0:T(128)S(1)}, s32[2]{0:T(128)S(1)}) fusion(s32[2,5]{1,0:T(2,128)} %param.8, s32[]{:T(128)S(6)} %select_n.56, s32[]{:T(128)S(6)} %select_n.54), kind=kLoop, calls=%fused_computation.28 | loop fusion | bytes 40 | tf_op jit(solution)/shard_map/dynamic_slice | solution.py:544
  30.5 2.9 %windows.1 = (bf16[2,528,128]{2,1,0:T(8,128)(2,1)S(1)}, bf16[2,528,128]{2,1,0:T(8,128)(2,1)S(1)}, bf16[2,528,128]{2,1,0:T(8,128)(2,1)S(1)}, bf16[2,528,128]{2,1,0:T(8,128)(2,1)S(1)}) custom-call(s32[2,4]{1,0:T(2,128)S(1)} %multiply_minimum_fusion.start_ref, s32[2,1,1024]{2,1,0:T(1,128)S(1)} %get-tuple-element.38.spot_ref, bf16[2048,128]{1,0:T(8,128)(2,1)} %bitcast.27), custom_call_target="tpu_custom_call" | custom-call | tf_op jit(solution)/shard_map/windows/pallas_call | solution.py:185
  33.4 0.0 collective-permute-done
  33.5 1.5 %collective-permute-done.1 = f32[2,2,1024]{2,1,0:T(2,128)S(1)} collective-permute-done((f32[2,2,1024]{2,1,0:T(2,128)S(1)}, f32[2,2,1024]{2,1,0:T(2,128)S(1)}, u32[]{:S(2)}, u32[]{:S(2)}) %collective-permute-start.1) | collective-permute-done | bytes 16416 | tf_op jit(solution)/shard_map/ppermute | solution.py:491
  35.0 0.0 collective-permute-done.2
  35.1 0.0 collective-permute-done.3.keys_ref.refs_1_
  35.1 0.0 collective-permute-done.4.keys_ref.refs_2_
  35.1 0.8 collective-permute-start.5
  35.9 3.0 %first_block.5 = (f32[2,1024,128]{2,1,0:T(8,128)S(1)}, bf16[2,1024,128]{2,1,0:T(8,128)(2,1)S(1)}) custom-call(s32[1]{0:T(128)} %bitcast.4._.me_ref, bf16[2,1024,128]{2,1,0:T(8,128)(2,1)S(1)} %collective-permute-done.3.keys_ref.refs_1_, f32[2,1,1024]{2,1,0:T(1,128)S(1)} %get-tuple-element.75.tot_ref, ...), custom_call_target="tpu_custom_call", output_to_operand_aliasing={{0}: (4, {})} | custom-call | tf_op jit(solution)/shard_map/first_block/pallas_call | solution.py:331
  38.8 3.0 %first_block.6 = (f32[2,1024,128]{2,1,0:T(8,128)S(1)}, bf16[2,1024,128]{2,1,0:T(8,128)(2,1)S(1)}) custom-call(s32[1]{0:T(128)} %bitcast.4._.me_ref, bf16[2,1024,128]{2,1,0:T(8,128)(2,1)S(1)} %collective-permute-done.4.keys_ref.refs_2_, f32[2,1,1024]{2,1,0:T(1,128)S(1)} %get-tuple-element.77.tot_ref, ...), custom_call_target="tpu_custom_call", output_to_operand_aliasing={{0}: (4, {})} | custom-call | tf_op jit(solution)/shard_map/first_block/pallas_call | solution.py:331
  41.8 0.3 convert_reduce_fusion
  42.1 1.8 %own_ranks.1 = f32[2,1,1024]{2,1,0:T(1,128)S(1)} custom-call(s32[1]{0:T(128)} %bitcast.4._.me_ref, f32[2,4,1024]{2,1,0:T(4,128)S(1)} %pad_maximum_fusion.1.label_ref), custom_call_target="tpu_custom_call" | custom-call | tf_op jit(solution)/shard_map/own_ranks/pallas_call | solution.py:222
  43.9 2.4 %collective-permute-start.10 = (bf16[2,528,128]{2,1,0:T(8,128)(2,1)S(1)}, bf16[2,528,128]{2,1,0:T(8,128)(2,1)S(1)}, u32[]{:S(2)}, u32[]{:S(2)}) collective-permute-start(bf16[2,528,128]{2,1,0:T(8,128)(2,1)S(1)} %get-tuple-element.65), channel_id=1, source_target_pairs={{0,8},{4,12},{8,0},{12,4},{1,9},{5,13},{9,1},{13,5},{2,10},{6,14},... | collective-permute-start | bytes 811016 | tf_op jit(solution)/shard_map/ppermute | solution.py:491
  46.2 1.4 %collective-permute-start.11 = (bf16[2,528,128]{2,1,0:T(8,128)(2,1)S(1)}, bf16[2,528,128]{2,1,0:T(8,128)(2,1)S(1)}, u32[]{:S(2)}, u32[]{:S(2)}) collective-permute-start(bf16[2,528,128]{2,1,0:T(8,128)(2,1)S(1)} %get-tuple-element.66), channel_id=1, source_target_pairs={{0,12},{4,8},{8,4},{12,0},{1,13},{5,9},{9,5},{13,1},{2,14},{6,10},... | collective-permute-start | bytes 811016 | tf_op jit(solution)/shard_map/ppermute | solution.py:491
  47.6 0.0 collective-permute-start.9
  47.6 0.1 constant_dynamic-update-slice_fusion.2
  47.7 4.0 %collective-permute-done.5.keys_ref.refs_3_ = bf16[2,1024,128]{2,1,0:T(8,128)(2,1)S(1)} collective-permute-done((bf16[2,1024,128]{2,1,0:T(8,128)(2,1)S(1)}, bf16[2,1024,128]{2,1,0:T(8,128)(2,1)S(1)}, u32[]{:S(2)}, u32[]{:S(2)}) %collective-permute-start.5) | collective-permute-done | bytes 524320 | tf_op jit(solution)/shard_map/ppermute | solution.py:491
  51.7 3.0 %first_block.7 = (f32[2,1024,128]{2,1,0:T(8,128)S(1)}, bf16[2,1024,128]{2,1,0:T(8,128)(2,1)S(1)}) custom-call(s32[1]{0:T(128)} %bitcast.4._.me_ref, bf16[2,1024,128]{2,1,0:T(8,128)(2,1)S(1)} %collective-permute-done.5.keys_ref.refs_3_, f32[2,1,1024]{2,1,0:T(1,128)S(1)} %get-tuple-element.73.tot_ref, ...), custom_call_target="tpu_custom_call", output_to_operand_aliasing={{0}: (4, {})} | custom-call | tf_op jit(solution)/shard_map/first_block/pallas_call | solution.py:331
  54.7 0.0 copy-start.1
  54.7 1.0 %copy-done.1 = bf16[2,1024,128]{2,1,0:T(8,128)(2,1)S(1)} copy-done((bf16[2,1024,128]{2,1,0:T(8,128)(2,1)S(1)}, bf16[2,1024,128]{2,1,0:T(8,128)(2,1)}, u32[]{:S(2)}) %copy-start.1) | copy-done | bytes 524312
  55.7 5.0 %raw_weights.1 = (bf16[2,1024,4096]{2,1,0:T(8,128)(2,1)S(1)}, f32[2,1,4096]{2,1,0:T(1,128)S(1)}) custom-call(f32[2,1024,128]{2,1,0:T(8,128)S(1)} %get-tuple-element.53.sums_ref, bf16[2,1024,128]{2,1,0:T(8,128)(2,1)S(1)} %copy-done.1, bf16[2,1024,128]{2,1,0:T(8,128)(2,1)S(1)} %get-tuple-element.55.refs_1_.refs_5_, ...), custom_call_target="tpu_custom_call" | custom-call | tf_op jit(solution)/shard_map/raw_weights/pallas_call | solution.py:368
  60.8 0.1 collective-permute-start.6
  60.9 0.1 constant_dynamic-update-slice_fusion.1
  61.0 1.0 %collective-permute-start.7 = (f32[2,1,5120]{2,1,0:T(1,128)S(1)}, f32[2,1,5120]{2,1,0:T(1,128)S(1)}, u32[]{:S(2)}, u32[]{:S(2)}) collective-permute-start(f32[2,1,5120]{2,1,0:T(1,128)S(1)} %pad_maximum_fusion.refs_0_.refs_8_), channel_id=1, source_target_pairs={{0,8},{4,12},{8,0},{12,4},{1,9},{5,13},{9,1},{13,5},{2,10},{6,14},... | collective-permute-start | bytes 122888 | tf_op jit(solution)/shard_map/ppermute | solution.py:491
  62.0 3.6 %collective-permute-done.6.refs_1_.refs_9_ = f32[2,1,5120]{2,1,0:T(1,128)S(1)} collective-permute-done((f32[2,1,5120]{2,1,0:T(1,128)S(1)}, f32[2,1,5120]{2,1,0:T(1,128)S(1)}, u32[]{:S(2)}, u32[]{:S(2)}) %collective-permute-start.6) | collective-permute-done | bytes 40992 | tf_op jit(solution)/shard_map/ppermute | solution.py:491
  65.5 2.3 %collective-permute-start.8 = (f32[2,1,5120]{2,1,0:T(1,128)S(1)}, f32[2,1,5120]{2,1,0:T(1,128)S(1)}, u32[]{:S(2)}, u32[]{:S(2)}) collective-permute-start(f32[2,1,5120]{2,1,0:T(1,128)S(1)} %pad_maximum_fusion.refs_0_.refs_8_), channel_id=1, source_target_pairs={{0,12},{4,8},{8,4},{12,0},{1,13},{5,9},{9,5},{13,1},{2,14},{6,10},... | collective-permute-start | bytes 122888 | tf_op jit(solution)/shard_map/ppermute | solution.py:491
  67.9 0.1 constant_dynamic-update-slice_fusion.scalar_ref
  67.9 3.6 %collective-permute-done.7.refs_2_.refs_10_ = f32[2,1,5120]{2,1,0:T(1,128)S(1)} collective-permute-done((f32[2,1,5120]{2,1,0:T(1,128)S(1)}, f32[2,1,5120]{2,1,0:T(1,128)S(1)}, u32[]{:S(2)}, u32[]{:S(2)}) %collective-permute-start.7) | collective-permute-done | bytes 40992 | tf_op jit(solution)/shard_map/ppermute | solution.py:491
  71.6 0.0 collective-permute-done.8.refs_3_.refs_11_
  71.6 6.2 %weighted_sums.1 = f32[2,1024,128]{2,1,0:T(8,128)} custom-call(bf16[2,1024,4096]{2,1,0:T(8,128)(2,1)S(1)} %get-tuple-element.58.raw_ref, f32[2,1,5120]{2,1,0:T(1,128)S(1)} %pad_maximum_fusion.refs_0_.refs_8_, f32[2,1,5120]{2,1,0:T(1,128)S(1)} %collective-permute-done.6.refs_1_.refs_9_, f32[2,1,5120]{2,1,0:T(1,128)S(1)} %collective-permute-done.7.refs_2_.refs_10_, ...), custom_call_target="tpu_custom_call" | custom-call | tf_op jit(solution)/shard_map/weighted_sums/pallas_call | solution.py:403
  77.8 0.0 collective-permute-done.10.refs_6_
  77.8 0.0 collective-permute-done.11.refs_7_
  77.8 0.0 collective-permute-done.9.refs_5_
  77.8 8.6 %place.1 = (bf16[4096,128]{1,0:T(8,128)(2,1)}, bf16[4096,128]{1,0:T(8,128)(2,1)}) custom-call(s32[5,2,4]{2,1,0:T(2,128)S(1)} %constant_dynamic-update-slice_fusion.scalar_ref, f32[2,4,1024]{2,1,0:T(4,128)S(1)} %pad_maximum_fusion.1.label_ref, bf16[2,1024,128]{2,1,0:T(8,128)(2,1)S(1)} %get-tuple-element.62.keys_ref.refs_0_, ...), custom_call_target="tpu_custom_call" | custom-call | tf_op jit(solution)/shard_map/place/pallas_call | solution.py:463
  (14 shorter events, 0.2 us)
Async XLA Ops:
  5.1 30.0 %collective-permute-start.3 = (bf16[2,1024,128]{2,1,0:T(8,128)(2,1)S(1)}, bf16[2,1024,128]{2,1,0:T(8,128)(2,1)S(1)}, u32[]{:S(2)}, u32[]{:S(2)}) collective-permute-start(bf16[2,1024,128]{2,1,0:T(8,128)(2,1)S(1)} %get-tuple-element.62.keys_ref.refs_0_), channel_id=1, source_target_pairs={{0,4},{4,0},{8,12},{12,8},{1,5},{5,1},{9,13},{13,9},{2,6},{6,2},{1... | collective-permute-start | bytes 1572872 | tf_op jit(solution)/shard_map/ppermute | solution.py:491
  8.2 26.9 %collective-permute-start.4 = (bf16[2,1024,128]{2,1,0:T(8,128)(2,1)S(1)}, bf16[2,1024,128]{2,1,0:T(8,128)(2,1)S(1)}, u32[]{:S(2)}, u32[]{:S(2)}) collective-permute-start(bf16[2,1024,128]{2,1,0:T(8,128)(2,1)S(1)} %get-tuple-element.62.keys_ref.refs_0_), channel_id=1, source_target_pairs={{0,8},{4,12},{8,0},{12,4},{1,9},{5,13},{9,1},{13,5},{2,10},{6,14},... | collective-permute-start | bytes 1572872 | tf_op jit(solution)/shard_map/ppermute | solution.py:491
  18.4 15.1 %collective-permute-start = (f32[2,2,1024]{2,1,0:T(2,128)S(1)}, f32[2,2,1024]{2,1,0:T(2,128)S(1)}, u32[]{:S(2)}, u32[]{:S(2)}) collective-permute-start(f32[2,2,1024]{2,1,0:T(2,128)S(1)} %pad_maximum_fusion.2), channel_id=1, source_target_pairs={{0,4},{4,0},{8,12},{12,8},{1,5},{5,1},{9,13},{13,9},{2,6},{6,2},{1... | collective-permute-start | bytes 49160 | tf_op jit(solution)/shard_map/ppermute | solution.py:491
  18.9 16.1 %collective-permute-start.1 = (f32[2,2,1024]{2,1,0:T(2,128)S(1)}, f32[2,2,1024]{2,1,0:T(2,128)S(1)}, u32[]{:S(2)}, u32[]{:S(2)}) collective-permute-start(f32[2,2,1024]{2,1,0:T(2,128)S(1)} %pad_maximum_fusion.2), channel_id=1, source_target_pairs={{0,8},{4,12},{8,0},{12,4},{1,9},{5,13},{9,1},{13,5},{2,10},{6,14},... | collective-permute-start | bytes 49160 | tf_op jit(solution)/shard_map/ppermute | solution.py:491
  18.9 16.1 %collective-permute-start.2 = (f32[2,2,1024]{2,1,0:T(2,128)S(1)}, f32[2,2,1024]{2,1,0:T(2,128)S(1)}, u32[]{:S(2)}, u32[]{:S(2)}) collective-permute-start(f32[2,2,1024]{2,1,0:T(2,128)S(1)} %pad_maximum_fusion.2), channel_id=1, source_target_pairs={{0,12},{4,8},{8,4},{12,0},{1,13},{5,9},{9,5},{13,1},{2,14},{6,10},... | collective-permute-start | bytes 49160 | tf_op jit(solution)/shard_map/ppermute | solution.py:491
  28.7 0.8 copy-start
  35.1 16.6 %collective-permute-start.5 = (bf16[2,1024,128]{2,1,0:T(8,128)(2,1)S(1)}, bf16[2,1024,128]{2,1,0:T(8,128)(2,1)S(1)}, u32[]{:S(2)}, u32[]{:S(2)}) collective-permute-start(bf16[2,1024,128]{2,1,0:T(8,128)(2,1)S(1)} %collective-permute-done.4.keys_ref.refs_2_), channel_id=1, source_target_pairs={{0,4},{4,0},{8,12},{12,8},{1,5},{5,1},{9,13},{13,9},{2,6},{6,2},{1... | collective-permute-start | bytes 1572872 | tf_op jit(solution)/shard_map/ppermute | solution.py:491
  43.9 33.9 %collective-permute-start.10 = (bf16[2,528,128]{2,1,0:T(8,128)(2,1)S(1)}, bf16[2,528,128]{2,1,0:T(8,128)(2,1)S(1)}, u32[]{:S(2)}, u32[]{:S(2)}) collective-permute-start(bf16[2,528,128]{2,1,0:T(8,128)(2,1)S(1)} %get-tuple-element.65), channel_id=1, source_target_pairs={{0,8},{4,12},{8,0},{12,4},{1,9},{5,13},{9,1},{13,5},{2,10},{6,14},... | collective-permute-start | bytes 811016 | tf_op jit(solution)/shard_map/ppermute | solution.py:491
  46.2 31.5 %collective-permute-start.11 = (bf16[2,528,128]{2,1,0:T(8,128)(2,1)S(1)}, bf16[2,528,128]{2,1,0:T(8,128)(2,1)S(1)}, u32[]{:S(2)}, u32[]{:S(2)}) collective-permute-start(bf16[2,528,128]{2,1,0:T(8,128)(2,1)S(1)} %get-tuple-element.66), channel_id=1, source_target_pairs={{0,12},{4,8},{8,4},{12,0},{1,13},{5,9},{9,5},{13,1},{2,14},{6,10},... | collective-permute-start | bytes 811016 | tf_op jit(solution)/shard_map/ppermute | solution.py:491
  47.6 30.2 %collective-permute-start.9 = (bf16[2,528,128]{2,1,0:T(8,128)(2,1)S(1)}, bf16[2,528,128]{2,1,0:T(8,128)(2,1)S(1)}, u32[]{:S(2)}, u32[]{:S(2)}) collective-permute-start(bf16[2,528,128]{2,1,0:T(8,128)(2,1)S(1)} %get-tuple-element.64), channel_id=1, source_target_pairs={{0,4},{4,0},{8,12},{12,8},{1,5},{5,1},{9,13},{13,9},{2,6},{6,2},{1... | collective-permute-start | bytes 811016 | tf_op jit(solution)/shard_map/ppermute | solution.py:491
  54.7 1.0 %copy-start.1 = (bf16[2,1024,128]{2,1,0:T(8,128)(2,1)S(1)}, bf16[2,1024,128]{2,1,0:T(8,128)(2,1)}, u32[]{:S(2)}) copy-start(bf16[2,1024,128]{2,1,0:T(8,128)(2,1)} %copy-done) | copy-start | bytes 1572868
  60.8 4.7 %collective-permute-start.6 = (f32[2,1,5120]{2,1,0:T(1,128)S(1)}, f32[2,1,5120]{2,1,0:T(1,128)S(1)}, u32[]{:S(2)}, u32[]{:S(2)}) collective-permute-start(f32[2,1,5120]{2,1,0:T(1,128)S(1)} %pad_maximum_fusion.refs_0_.refs_8_), channel_id=1, source_target_pairs={{0,4},{4,0},{8,12},{12,8},{1,5},{5,1},{9,13},{13,9},{2,6},{6,2},{1... | collective-permute-start | bytes 122888 | tf_op jit(solution)/shard_map/ppermute | solution.py:491
  61.0 10.6 %collective-permute-start.7 = (f32[2,1,5120]{2,1,0:T(1,128)S(1)}, f32[2,1,5120]{2,1,0:T(1,128)S(1)}, u32[]{:S(2)}, u32[]{:S(2)}) collective-permute-start(f32[2,1,5120]{2,1,0:T(1,128)S(1)} %pad_maximum_fusion.refs_0_.refs_8_), channel_id=1, source_target_pairs={{0,8},{4,12},{8,0},{12,4},{1,9},{5,13},{9,1},{13,5},{2,10},{6,14},... | collective-permute-start | bytes 122888 | tf_op jit(solution)/shard_map/ppermute | solution.py:491
  65.5 6.1 %collective-permute-start.8 = (f32[2,1,5120]{2,1,0:T(1,128)S(1)}, f32[2,1,5120]{2,1,0:T(1,128)S(1)}, u32[]{:S(2)}, u32[]{:S(2)}) collective-permute-start(f32[2,1,5120]{2,1,0:T(1,128)S(1)} %pad_maximum_fusion.refs_0_.refs_8_), channel_id=1, source_target_pairs={{0,12},{4,8},{8,4},{12,0},{1,13},{5,9},{9,5},{13,1},{2,14},{6,10},... | collective-permute-start | bytes 122888 | tf_op jit(solution)/shard_map/ppermute | solution.py:491

commit v6 on v5

--- a/solution.py
+++ b/solution.py
@@ -10,7 +10,7 @@
 
 LANES = 128
 EXP2_SCALE = 20.0 * math.log2(math.e)
-VMEM_LIMIT = 24 * 1024 * 1024
+VMEM_LIMIT = 16 * 1024 * 1024
 F32 = jnp.float32
 BF16 = jnp.bfloat16
 NT = (((1,), (1,)), ((), ()))
@@ -159,8 +159,7 @@
     )(keep_hbm(labels), keep_hbm(keys))
 
 
-def windows_kernel(size, start_ref, spot_ref, values_hbm, *refs):
-    out_refs, (flat_ref, wide_ref, rows_ref, sem) = refs[:-4], refs[-4:]
+def values_kernel(spot_ref, values_hbm, out_ref, flat_ref, wide_ref, sem):
     heads, _, tokens = spot_ref.shape
     copy = pltpu.make_async_copy(values_hbm, flat_ref, sem)
     copy.start()
@@ -171,31 +170,55 @@
         values = head_rows(wide_ref, h, heads).astype(BF16)
         for r in range(0, tokens, rows):
             pick = one_hot_rows(rows, spot_ref[h] - r)
-            rows_ref[h, r : r + rows] = dot_nn(pick, values).astype(BF16)
-        for m, out_ref in enumerate(out_refs):
-            start = pl.multiple_of(start_ref[h, m], 16)
-            out_ref[h] = rows_ref[h, pl.ds(start, size), :]
-
-
-def windows(starts, spots, values, size):
+            out_ref[h, r : r + rows] = dot_nn(pick, values).astype(BF16)
+
+
+def sort_values(spots, values):
     heads, _, tokens = spots.shape
     flat, width = values.shape
-    n = starts.shape[1]
-    out = pltpu.VMEM((heads, size, width), BF16)
-    return pl.pallas_call(
-        functools.partial(windows_kernel, size),
-        in_specs=[pl.BlockSpec(memory_space=pltpu.SMEM), in_vmem(), anywhere()],
-        out_specs=(in_vmem(),) * n,
-        out_shape=(out,) * n,
+    return pl.pallas_call(
+        values_kernel,
+        in_specs=[in_vmem(), anywhere()],
+        out_specs=in_vmem(),
+        out_shape=pltpu.VMEM((heads, tokens, width), BF16),
         scratch_shapes=[
             pltpu.VMEM((flat, width), BF16),
             pltpu.VMEM((flat, width), F32),
-            pltpu.VMEM((heads, tokens, width), BF16),
             pltpu.SemaphoreType.DMA,
         ],
         compiler_params=params(),
+        name="sort_values",
+    )(keep_vmem(spots), keep_hbm(values))
+
+
+def windows_kernel(size, start_ref, rank_ref, values_ref, _, *out_refs):
+    heads, tokens, _ = values_ref.shape
+    for h in range(heads):
+        rank = rank_ref[h].astype(jnp.int32)
+        digits = [
+            digit[:, t : t + LANES]
+            for digit in (rank >> 7, rank & 127)
+            for t in range(0, tokens, LANES)
+        ]
+        digits = jnp.concatenate(digits, axis=0).astype(F32).astype(BF16)
+        for m, out_ref in enumerate(out_refs):
+            start = pl.multiple_of(start_ref[h, m], 16)
+            out_ref[h, :size] = values_ref[h, pl.ds(start, size), :]
+            out_ref[h, size:] = digits
+
+
+def windows(starts, ranks, values, size, after):
+    heads, tokens, width = values.shape
+    n = starts.shape[1]
+    out = pltpu.VMEM((heads, size + 2 * tokens // LANES, width), BF16)
+    return pl.pallas_call(
+        functools.partial(windows_kernel, size),
+        in_specs=[pl.BlockSpec(memory_space=pltpu.SMEM), in_vmem(), in_vmem(), in_vmem()],
+        out_specs=(in_vmem(),) * n,
+        out_shape=(out,) * n,
+        compiler_params=params(),
         name="windows",
-    )(starts, keep_vmem(spots), keep_hbm(values))
+    )(starts, ranks, keep_vmem(values), keep_vmem(after))
 
 
 def rank_kernel(me_ref, label_ref, rank_ref):
@@ -233,7 +256,7 @@
     )(me, labels)
 
 
-def totals_kernel(keys_ref, cent_ref, tot_ref, unit_ref, sum_ref):
+def totals_kernel(keys_ref, cent_ref, _, tot_ref, unit_ref, sum_ref):
     step = pl.program_id(1)
     tokens = unit_ref.shape[0]
 
@@ -255,7 +278,7 @@
         tot_ref[0] = jnp.sum(sum_ref[...], axis=0, keepdims=True)
 
 
-def own_totals(keys, cents):
+def own_totals(keys, cents, after):
     heads, count, width = cents.shape
     tokens = keys.shape[1]
     rows = min(2048, count)
@@ -265,6 +288,7 @@
         in_specs=[
             in_vmem(),
             pl.BlockSpec((1, rows, width), lambda h, c: (h, c, 0)),
+            in_vmem(),
         ],
         out_specs=pl.BlockSpec((1, 1, tokens), lambda h, c: (h, 0, 0)),
         out_shape=jax.ShapeDtypeStruct((heads, 1, tokens), F32),
@@ -274,7 +298,7 @@
         ],
         compiler_params=params(),
         name="own_totals",
-    )(keep_vmem(keys), keep_hbm(cents))
+    )(keep_vmem(keys), keep_hbm(cents), after)
 
 
 def scale_rows(unit, inverse, scaled_ref):
@@ -415,34 +439,36 @@
     )(keep_vmem(raw), *map(keep_vmem, totals), *map(keep_vmem, units))
 
 
-def place_kernel(blocks, size, scalar_ref, label_ref, *refs):
-    keys, values, ranks = (refs[i * blocks : (i + 1) * blocks] for i in range(3))
-    out_refs, (rows_ref, near_ref, mixed_ref) = refs[-5:-3], refs[-3:]
+def place_kernel(blocks, size, fresh, scalar_ref, label_ref, *refs):
+    count = len(blocks)
+    keys, values, refs = refs[:count], refs[count : 2 * count], refs[2 * count :]
+    before, (*out_refs, rows_ref, near_ref, mixed_ref) = refs[: 0 if fresh else 2], refs[0 if fresh else 2 :]
     step = pl.program_id(0)
     heads, tokens, width = keys[0].shape
-    sent = values[0].shape[1]
+    digit_rows = tokens // LANES
+    sent = values[0].shape[1] - 2 * digit_rows
+    rows = mixed_ref.shape[1] // heads
 
     @pl.when(step == 0)
     def _():
-        rows_ref[:, :, width:] = jnp.zeros((heads, blocks * size, width), BF16)
+        rows_ref[:, :, width:] = jnp.zeros((heads, count * size, width), BF16)
         for h in range(heads):
-            for m in range(blocks):
+            low, high, first = (scalar_ref[i, h, 0].astype(F32) for i in range(2, 5))
+            for i, m in enumerate(blocks):
                 start = pl.multiple_of(scalar_ref[0, h, m], 16)
                 gap = pl.multiple_of(scalar_ref[1, h, m], 16)
-                first = m * size
-                rows_ref[h, first : first + size, :width] = keys[m][h, pl.ds(start, size), :]
-                rows_ref[h, pl.ds(first + gap, sent), width:] = values[m][h]
-                rank = ranks[m][h, :, -tokens:]
+                here = i * size
+                rows_ref[h, here : here + size, :width] = keys[i][h, pl.ds(start, size), :]
+                rows_ref[h, pl.ds(here + gap, sent), width:] = values[i][h, :sent, :]
+                digits = values[i][h, sent:, :].astype(F32)
+                rank = digits[:digit_rows] * 128.0 + digits[digit_rows:]
+                rank = jnp.concatenate([rank[r : r + 1] for r in range(digit_rows)], axis=1)
                 label = label_ref[h, m : m + 1, :]
-                low, high, before = (
-                    scalar_ref[i, h, 0].astype(F32) for i in range(2, 5)
-                )
                 mine = (label >= low) & (label < high)
-                spot = jnp.where(mine, rank - before, -1.0).astype(jnp.int32)
+                spot = jnp.where(mine, rank - first, -1.0).astype(jnp.int32)
                 spot = pltpu.roll(spot, lax.rem(tokens - start, tokens), 1)
-                near_ref[h, :, m * size : (m + 1) * size] = spot[:, :size]
-
-    rows = out_refs[0].shape[0] // heads
+                near_ref[h, :, here : here + size] = spot[:, :size]
+
     for h in range(heads):
         pick = one_hot_rows(rows, near_ref[h] - step * rows)
         total = dot_nn(pick, rows_ref[h])
@@ -451,31 +477,42 @@
                 :, side * width : (side + 1) * width
             ]
     for side in range(2):
-        out_refs[side][...] = mixed_ref[side].astype(BF16)
-
-
-def place(scalars, labels, keys, values, ranks, size, cap):
-    blocks = len(keys)
-    heads, tokens, width = keys[0].shape
+        if fresh:
+            here = pl.ds(pl.multiple_of(step * rows * heads, rows * heads), rows * heads)
+            out_refs[side][here] = mixed_ref[side].astype(BF16)
+        else:
+            here = pl.ds(pl.multiple_of(step * rows * heads, rows * heads), rows * heads)
+            more = mixed_ref[side] + before[side][here].astype(F32)
+            out_refs[side][...] = more.astype(BF16)
+
+
+def place(scalars, labels, keys, values, blocks, size, cap, before):
+    heads, _, width = keys[0].shape
     rows = 512
-    out = jax.ShapeDtypeStruct((heads * cap, width), BF16)
-    block = pl.BlockSpec((heads * rows, width), lambda r: (r, 0))
-    return pl.pallas_call(
-        functools.partial(place_kernel, blocks, size),
+    fresh = before is None
+    if fresh:
+        out = pltpu.VMEM((heads * cap, width), BF16)
+        block = in_vmem()
+    else:
+        out = jax.ShapeDtypeStruct((heads * cap, width), BF16)
+        block = pl.BlockSpec((heads * rows, width), lambda r: (r, 0))
+    moved = [x[m] for x in (keys, values) for m in blocks] + list(before or ())
+    return pl.pallas_call(
+        functools.partial(place_kernel, blocks, size, fresh),
         grid=(cap // rows,),
         in_specs=[pl.BlockSpec(memory_space=pltpu.SMEM)]
         + [whole(labels.shape)]
-        + [in_vmem()] * (3 * blocks),
+        + [in_vmem()] * len(moved),
         out_specs=(block, block),
         out_shape=(out, out),
         scratch_shapes=[
-            pltpu.VMEM((heads, blocks * size, 2 * width), BF16),
-            pltpu.VMEM((heads, 1, blocks * size), jnp.int32),
+            pltpu.VMEM((heads, len(blocks) * size, 2 * width), BF16),
+            pltpu.VMEM((heads, 1, len(blocks) * size), jnp.int32),
             pltpu.VMEM((2, heads * rows, width), F32),
         ],
         compiler_params=params(),
         name="place",
-    )(scalars, labels, *(keep_vmem(x) for x in (*keys, *values, *ranks)))
+    )(scalars, labels, *map(keep_vmem, moved))
 
 
 def body(key_rows, value_rows, cluster_labels, owner_bounds, init_centroids):
@@ -505,7 +542,9 @@
     while d < n:
         keys[d] = swap(own_keys, d)
         d *= 2
-    own_total = own_totals(own_keys, init_centroids)
+    pairs = [(i, i ^ 1) for i in range(lax.axis_size("head"))]
+    word = lax.ppermute(own_labels[:, :, :LANES], "head", pairs)
+    own_total = own_totals(own_keys, init_centroids, word)
     shared = spread(jnp.concatenate([own_total, own_labels], axis=1))
     totals = [own_total] + [x[:, 0:1] for x in shared[1:]]
 
@@ -519,27 +558,11 @@
     keys = [keys[m] for m in range(n)]
     peer_low = jnp.take(owner_bounds, me ^ jnp.arange(n, dtype=jnp.int32), axis=1)
     own_below = jnp.sum((own_labels < peer_low[:, :, None]).astype(jnp.int32), axis=2)
-    own_windows = windows(
-        aligned(own_below, send_size),
-        own_spots,
-        value_rows.reshape(heads * tokens, width),
-        send_size,
-    )
-    for m in range(1, n):
-        sums, unit = first_block(me_array, keys[m], totals[m], cents, n, sums)
-        units.append(unit)
-        if m == min(2, n - 1):
-            *own_windows, sums = lax.optimization_barrier((*own_windows, sums))
-            values = [own_windows[0]] + [swap(own_windows[d], d) for d in range(1, n)]
-            labels, sums = lax.optimization_barrier(
-                (jnp.concatenate([x[:, -1:] for x in shared], axis=1), sums)
-            )
-            ranks = own_ranks(me_array, labels)
-
-    raw, part = raw_weights(sums, units)
-    parts = spread(jnp.concatenate([part, ranks], axis=2))
-    out = weighted_sums(raw, units, parts)
-
+    own_values = sort_values(own_spots, value_rows.reshape(heads * tokens, width))
+
+    labels = jnp.concatenate([x[:, -1:] for x in shared], axis=1)
+    ranks = own_ranks(me_array, labels)
+    value_starts = aligned(own_below, send_size)
     low = lax.dynamic_slice_in_dim(owner_bounds, me, 1, 1)
     high = lax.dynamic_slice_in_dim(owner_bounds, me + 1, 1, 1)
     below = jnp.sum((labels < low[:, :, None]).astype(jnp.int32), axis=2)
@@ -548,8 +571,24 @@
     gaps = aligned(below, send_size) - key_starts
     one = jnp.ones((1, n), jnp.int32)
     scalars = jnp.stack([key_starts, gaps, low * one, high * one, first * one])
-    scalars, out = lax.optimization_barrier((scalars, out))
-    placed = place(scalars, labels, keys, values, parts, key_size, cap)
+
+    late = [2]
+    early = [d for d in range(1, n) if d not in late]
+    values = {}
+    for m in range(1, n):
+        sums, unit = first_block(me_array, keys[m], totals[m], cents, n, sums)
+        units.append(unit)
+        going = {1: early, 2: [0, *late]}.get(m, [])
+        if going:
+            starts = jnp.stack([value_starts[:, d] for d in going], axis=1)
+            for d, window in zip(going, windows(starts, ranks, own_values, send_size, unit)):
+                values[d] = swap(window, d) if d else window
+
+    raw, part = raw_weights(sums, units)
+    parts = spread(part)
+    placed = place(scalars, labels, keys, values, [0, *early], key_size, cap, None)
+    out = weighted_sums(raw, units, parts)
+    placed = place(scalars, labels, keys, values, late, key_size, cap, placed)
     shape = (cap, heads, width)
     return out, placed[0].reshape(shape), placed[1].reshape(shape)
 

time: 86.7 us -> 82.3 us (0.949)
  waiting for transfers between devices: 12.7 us -> 6.81 us
  Pallas kernels: 49.5 us -> 52.7 us
  local copies, waits for them, and re-layouts: 4.49 us -> 2.74 us
    ppermute x12, waiting for transfers between devices: 12.7 us -> 6.81 us  [swap(): return lax.ppermute(x, 'ctx', [(i, i ^ d) for i in range(n)])]
    pallas_call x1 -> x3, Pallas kernels: 8.56 us -> 13.3 us  [the longest x2 10.9 us: place(): pl.pallas_call(functools.partial(place_kernel, blocks, size, fresh), grid...]
    unnamed x8 -> x4, local copies, waits for them, and re-layouts: 2.75 us -> 0.92 us
    pallas_call x1 -> x2, Pallas kernels: 2.94 us -> 1.18 us  [windows(): pl.pallas_call(functools.partial(windows_kernel, size), in_specs=[pl.Bloc...]
  transfers between devices with their start and end apart: 12 -> 13, of which waited for: 4 -> 4; matrix products, arithmetic and copies ran while one was open for 4% -> 4% of each run, Pallas kernels for 42% -> 51%
where the time goes in v6:
time: 82.3 us; the launch traced here: 82.1 us
  Pallas kernels  52.7 us (64%)
  starting transfers between devices  18.3 us (22%)
  waiting for transfers between devices  6.81 us (8%)
  local copies, waits for them, and re-layouts  2.74 us (3%)
  between operations  0.86 us (1%)
    ppermute x12, starting transfers between devices, swap(): return lax.ppermute(x, 'ctx', [(i, i ^ d) for i in range(n)])  18.3 us
    pallas_call x4, Pallas kernels, first_block(): pl.pallas_call(functools.partial(first_kernel, fresh), grid_spec=pltpu.Pr...  13 us
    pallas_call x2, Pallas kernels, place(): pl.pallas_call(functools.partial(place_kernel, blocks, size, fresh), grid...  10.9 us
    pallas_call x1, Pallas kernels, own_totals(): pl.pallas_call(totals_kernel, grid=(heads, count // rows), in_specs=[in_v...  7.56 us
    ppermute x12, waiting for transfers between devices, swap(): return lax.ppermute(x, 'ctx', [(i, i ^ d) for i in range(n)])  6.81 us
    pallas_call x1, Pallas kernels, weighted_sums(): pl.pallas_call(functools.partial(sums_kernel, blocks), grid=(heads,), in_...  6.21 us
    pallas_call x1, Pallas kernels, raw_weights(): pl.pallas_call(functools.partial(raw_kernel, len(units)), grid=(heads,),...  5.22 us
    pallas_call x1, Pallas kernels, sort_keys(): pl.pallas_call(sort_kernel, grid=(heads,), in_specs=[anywhere()] * 2, out...  4.45 us
  transfers between devices with their start and end apart: 13, of which 4 were waited for; matrix products, arithmetic and copies ran while one was open for 4% of the time, Pallas kernels for 51%

profile of v6, /device:TPU:0, one launch (start us, length us, event | category | flops | bytes accessed | tf_op | source)
XLA Modules:
  0.0 82.1 jit_solution(6393750394736079927)
XLA Ops:
  0.6 4.4 %sort_keys.1 = (bf16[2,1024,128]{2,1,0:T(8,128)(2,1)S(1)}, f32[2,1,1024]{2,1,0:T(1,128)S(1)}, s32[2,1,1024]{2,1,0:T(1,128)S(1)}) custom-call(s32[2,1024]{1,0:T(2,128)} %label_hbm.1, bf16[2048,128]{1,0:T(8,128)(2,1)} %bitcast.26), custom_call_target="tpu_custom_call" | custom-call | tf_op jit(solution)/shard_map/sort_keys/pallas_call | solution.py:139
  5.1 4.1 %collective-permute-start.1 = (bf16[2,1024,128]{2,1,0:T(8,128)(2,1)S(1)}, bf16[2,1024,128]{2,1,0:T(8,128)(2,1)S(1)}, u32[]{:S(2)}, u32[]{:S(2)}) collective-permute-start(bf16[2,1024,128]{2,1,0:T(8,128)(2,1)S(1)} %get-tuple-element.47.keys_ref.refs_0_), channel_id=1, source_target_pairs={{0,8},{4,12},{8,0},{12,4},{1,9},{5,13},{9,1},{13,5},{2,10},{6,14},... | collective-permute-start | bytes 1572872 | tf_op jit(solution)/shard_map/ppermute | solution.py:528
  9.2 1.6 %collective-permute-start = (bf16[2,1024,128]{2,1,0:T(8,128)(2,1)S(1)}, bf16[2,1024,128]{2,1,0:T(8,128)(2,1)S(1)}, u32[]{:S(2)}, u32[]{:S(2)}) collective-permute-start(bf16[2,1024,128]{2,1,0:T(8,128)(2,1)S(1)} %get-tuple-element.47.keys_ref.refs_0_), channel_id=1, source_target_pairs={{0,4},{4,0},{8,12},{12,8},{1,5},{5,1},{9,13},{13,9},{2,6},{6,2},{1... | collective-permute-start | bytes 1572872 | tf_op jit(solution)/shard_map/ppermute | solution.py:528
  10.8 0.0 collective-permute-start.2
  10.8 0.8 copy.13
  11.6 0.6 gather_fusion
  12.1 0.1 convert_bitcast_fusion
  12.2 0.1 copy.14
  12.3 0.2 convert_reduce_fusion.2
  12.6 0.1 fusion.5
  12.6 0.0 collective-permute-done.2._
  12.6 7.6 %own_totals.1.tot_ref = f32[2,1,1024]{2,1,0:T(1,128)S(1)} custom-call(bf16[2,1024,128]{2,1,0:T(8,128)(2,1)S(1)} %get-tuple-element.47.keys_ref.refs_0_, f32[2,4096,128]{2,1,0:T(8,128)} %cent_in.1, f32[2,1,128]{2,1,0:T(1,128)S(1)} %collective-permute-done.2._), custom_call_target="tpu_custom_call" | custom-call | tf_op jit(solution)/shard_map/own_totals/pallas_call | solution.py:285
  20.2 0.5 collective-permute-start.6
  20.7 0.1 pad_add_fusion
  20.8 1.0 %dynamic-slice_reduce_fusion = (s32[2]{0:T(128)S(1)}, s32[2]{0:T(128)S(1)}) fusion(s32[2,5]{1,0:T(2,128)} %param.8, s32[]{:T(128)S(6)} %select_n.52, s32[]{:T(128)S(6)} %select_n.50), kind=kLoop, calls=%fused_computation.30 | loop fusion | bytes 40 | tf_op jit(solution)/shard_map/dynamic_slice | solution.py:567
  21.8 2.4 %sort_values.1.values_ref = bf16[2,1024,128]{2,1,0:T(8,128)(2,1)S(1)} custom-call(s32[2,1,1024]{2,1,0:T(1,128)S(1)} %get-tuple-element.45.spot_ref, bf16[2048,128]{1,0:T(8,128)(2,1)} %bitcast.27), custom_call_target="tpu_custom_call" | custom-call | tf_op jit(solution)/shard_map/sort_values/pallas_call | solution.py:179
  24.2 0.1 collective-permute-start.5
  24.3 3.9 %collective-permute-start.4 = (f32[2,2,1024]{2,1,0:T(2,128)S(1)}, f32[2,2,1024]{2,1,0:T(2,128)S(1)}, u32[]{:S(2)}, u32[]{:S(2)}) collective-permute-start(f32[2,2,1024]{2,1,0:T(2,128)S(1)} %pad_maximum_fusion.1), channel_id=1, source_target_pairs={{0,12},{4,8},{8,4},{12,0},{1,13},{5,9},{9,5},{13,1},{2,14},{6,10},... | collective-permute-start | bytes 49160 | tf_op jit(solution)/shard_map/ppermute | solution.py:528
  28.2 4.1 %first_block.4 = (f32[2,1024,128]{2,1,0:T(8,128)S(1)}, bf16[2,1024,128]{2,1,0:T(8,128)(2,1)S(1)}, bf16[2,1024,128]{2,1,0:T(8,128)(2,1)S(1)}) custom-call(s32[1]{0:T(128)} %bitcast._.me_ref, bf16[2,1024,128]{2,1,0:T(8,128)(2,1)S(1)} %get-tuple-element.47.keys_ref.refs_0_, f32[2,1,1024]{2,1,0:T(1,128)S(1)} %own_totals.1.tot_ref, f32[2,4096,128]{2,1,0:T(8,128)} %cent_in.1), custom_call_target="tpu_custom_call" | custom-call | tf_op jit(solution)/shard_map/first_block/pallas_call | solution.py:355
  32.3 1.2 %collective-permute-done.6 = f32[2,2,1024]{2,1,0:T(2,128)S(1)} collective-permute-done((f32[2,2,1024]{2,1,0:T(2,128)S(1)}, f32[2,2,1024]{2,1,0:T(2,128)S(1)}, u32[]{:S(2)}, u32[]{:S(2)}) %collective-permute-start.6) | collective-permute-done | bytes 16416 | tf_op jit(solution)/shard_map/ppermute | solution.py:528
  33.5 0.0 collective-permute-done.5
  33.6 0.9 %collective-permute-done.4 = f32[2,2,1024]{2,1,0:T(2,128)S(1)} collective-permute-done((f32[2,2,1024]{2,1,0:T(2,128)S(1)}, f32[2,2,1024]{2,1,0:T(2,128)S(1)}, u32[]{:S(2)}, u32[]{:S(2)}) %collective-permute-start.4) | collective-permute-done | bytes 16416 | tf_op jit(solution)/shard_map/ppermute | solution.py:528
  34.5 0.1 broadcast_compare_fusion
  34.6 0.2 convert_reduce_fusion
  34.8 0.0 collective-permute-done.1.keys_ref.refs_0_
  34.8 0.0 collective-permute-done.keys_ref.refs_1_
  34.8 0.5 collective-permute-start.3
  35.3 1.8 %own_ranks.1.rank_ref = f32[2,1,1024]{2,1,0:T(1,128)S(1)} custom-call(s32[1]{0:T(128)} %bitcast._.me_ref, f32[2,4,1024]{2,1,0:T(4,128)S(1)} %get-tuple-element.60.label_ref), custom_call_target="tpu_custom_call" | custom-call | tf_op jit(solution)/shard_map/own_ranks/pallas_call | solution.py:245
  37.1 3.0 %first_block.5 = (f32[2,1024,128]{2,1,0:T(8,128)S(1)}, bf16[2,1024,128]{2,1,0:T(8,128)(2,1)S(1)}) custom-call(s32[1]{0:T(128)} %bitcast._.me_ref, bf16[2,1024,128]{2,1,0:T(8,128)(2,1)S(1)} %collective-permute-done.keys_ref.refs_1_, f32[2,1,1024]{2,1,0:T(1,128)S(1)} %get-tuple-element.62.tot_ref, ...), custom_call_target="tpu_custom_call", output_to_operand_aliasing={{0}: (4, {})} | custom-call | tf_op jit(solution)/shard_map/first_block/pallas_call | solution.py:355
  40.1 0.6 windows.3
  40.7 1.7 %collective-permute-start.11 = (bf16[2,544,128]{2,1,0:T(8,128)(2,1)S(1)}, bf16[2,544,128]{2,1,0:T(8,128)(2,1)S(1)}, u32[]{:S(2)}, u32[]{:S(2)}) collective-permute-start(bf16[2,544,128]{2,1,0:T(8,128)(2,1)S(1)} %get-tuple-element.49), channel_id=1, source_target_pairs={{0,4},{4,0},{8,12},{12,8},{1,5},{5,1},{9,13},{13,9},{2,6},{6,2},{1... | collective-permute-start | bytes 835592 | tf_op jit(solution)/shard_map/ppermute | solution.py:528
  42.3 0.1 constant_dynamic-update-slice_fusion.2
  42.4 2.6 %collective-permute-start.12 = (bf16[2,544,128]{2,1,0:T(8,128)(2,1)S(1)}, bf16[2,544,128]{2,1,0:T(8,128)(2,1)S(1)}, u32[]{:S(2)}, u32[]{:S(2)}) collective-permute-start(bf16[2,544,128]{2,1,0:T(8,128)(2,1)S(1)} %get-tuple-element.50), channel_id=1, source_target_pairs={{0,12},{4,8},{8,4},{12,0},{1,13},{5,9},{9,5},{13,1},{2,14},{6,10},... | collective-permute-start | bytes 835592 | tf_op jit(solution)/shard_map/ppermute | solution.py:528
  45.0 3.0 %first_block.6 = (f32[2,1024,128]{2,1,0:T(8,128)S(1)}, bf16[2,1024,128]{2,1,0:T(8,128)(2,1)S(1)}) custom-call(s32[1]{0:T(128)} %bitcast._.me_ref, bf16[2,1024,128]{2,1,0:T(8,128)(2,1)S(1)} %collective-permute-done.1.keys_ref.refs_0_, f32[2,1,1024]{2,1,0:T(1,128)S(1)} %get-tuple-element.64.tot_ref, ...), custom_call_target="tpu_custom_call", output_to_operand_aliasing={{0}: (4, {})} | custom-call | tf_op jit(solution)/shard_map/first_block/pallas_call | solution.py:355
  48.0 0.6 windows.2
  48.6 0.1 collective-permute-start.10
  48.6 0.1 constant_dynamic-update-slice_fusion.1
  48.7 1.0 %collective-permute-done.3.keys_ref.refs_2_ = bf16[2,1024,128]{2,1,0:T(8,128)(2,1)S(1)} collective-permute-done((bf16[2,1024,128]{2,1,0:T(8,128)(2,1)S(1)}, bf16[2,1024,128]{2,1,0:T(8,128)(2,1)S(1)}, u32[]{:S(2)}, u32[]{:S(2)}) %collective-permute-start.3) | collective-permute-done | bytes 524320 | tf_op jit(solution)/shard_map/ppermute | solution.py:528
  49.7 3.0 %first_block.7 = (f32[2,1024,128]{2,1,0:T(8,128)S(1)}, bf16[2,1024,128]{2,1,0:T(8,128)(2,1)S(1)}) custom-call(s32[1]{0:T(128)} %bitcast._.me_ref, bf16[2,1024,128]{2,1,0:T(8,128)(2,1)S(1)} %collective-permute-done.3.keys_ref.refs_2_, f32[2,1,1024]{2,1,0:T(1,128)S(1)} %get-tuple-element.66.tot_ref, ...), custom_call_target="tpu_custom_call", output_to_operand_aliasing={{0}: (4, {})} | custom-call | tf_op jit(solution)/shard_map/first_block/pallas_call | solution.py:355
  52.7 5.2 %raw_weights.1 = (bf16[2,1024,4096]{2,1,0:T(8,128)(2,1)S(1)}, f32[2,1,4096]{2,1,0:T(1,128)S(1)}) custom-call(f32[2,1024,128]{2,1,0:T(8,128)S(1)} %get-tuple-element.38.sums_ref, bf16[2,1024,128]{2,1,0:T(8,128)(2,1)S(1)} %get-tuple-element.39.refs_0_.refs_4_, bf16[2,1024,128]{2,1,0:T(8,128)(2,1)S(1)} %get-tuple-element.40.refs_1_.refs_5_._, ...), custom_call_target="tpu_custom_call" | custom-call | tf_op jit(solution)/shard_map/raw_weights/pallas_call | solution.py:392
  57.9 3.3 %collective-permute-start.9 = (f32[2,1,4096]{2,1,0:T(1,128)S(1)}, f32[2,1,4096]{2,1,0:T(1,128)S(1)}, u32[]{:S(2)}, u32[]{:S(2)}) collective-permute-start(f32[2,1,4096]{2,1,0:T(1,128)S(1)} %get-tuple-element.44.refs_0_), channel_id=1, source_target_pairs={{0,12},{4,8},{8,4},{12,0},{1,13},{5,9},{9,5},{13,1},{2,14},{6,10},... | collective-permute-start | bytes 98312 | tf_op jit(solution)/shard_map/ppermute | solution.py:528
  61.2 0.0 collective-permute-start.8
  61.2 3.6 %collective-permute-done.11.refs_4_ = bf16[2,544,128]{2,1,0:T(8,128)(2,1)S(1)} collective-permute-done((bf16[2,544,128]{2,1,0:T(8,128)(2,1)S(1)}, bf16[2,544,128]{2,1,0:T(8,128)(2,1)S(1)}, u32[]{:S(2)}, u32[]{:S(2)}) %collective-permute-start.11) | collective-permute-done | bytes 278560 | tf_op jit(solution)/shard_map/ppermute | solution.py:528
  64.8 0.0 collective-permute-start.7
  64.8 0.1 constant_dynamic-update-slice_fusion.scalar_ref
  64.9 0.0 collective-permute-done.12.refs_5_
  64.9 6.5 %place.2 = (bf16[4096,128]{1,0:T(8,128)(2,1)S(1)}, bf16[4096,128]{1,0:T(8,128)(2,1)S(1)}) custom-call(s32[5,2,4]{2,1,0:T(2,128)S(1)} %constant_dynamic-update-slice_fusion.scalar_ref, f32[2,4,1024]{2,1,0:T(4,128)S(1)} %get-tuple-element.60.label_ref, bf16[2,1024,128]{2,1,0:T(8,128)(2,1)S(1)} %get-tuple-element.47.keys_ref.refs_0_, ...), custom_call_target="tpu_custom_call" | custom-call | tf_op jit(solution)/shard_map/place/pallas_call | solution.py:500
  71.4 0.0 collective-permute-done.10.refs_1_
  71.4 4.4 %place.3 = (bf16[4096,128]{1,0:T(8,128)(2,1)}, bf16[4096,128]{1,0:T(8,128)(2,1)}) custom-call(s32[5,2,4]{2,1,0:T(2,128)S(1)} %constant_dynamic-update-slice_fusion.scalar_ref, f32[2,4,1024]{2,1,0:T(4,128)S(1)} %get-tuple-element.60.label_ref, bf16[2,1024,128]{2,1,0:T(8,128)(2,1)S(1)} %collective-permute-done.1.keys_ref.refs_0_, ...), custom_call_target="tpu_custom_call" | custom-call | tf_op jit(solution)/shard_map/place/pallas_call | solution.py:500
  75.9 0.0 collective-permute-done.9.refs_3_
  75.9 0.0 collective-permute-done.8.refs_2_
  75.9 0.0 collective-permute-done.7.refs_1_
  75.9 6.2 %weighted_sums.1 = f32[2,1024,128]{2,1,0:T(8,128)} custom-call(bf16[2,1024,4096]{2,1,0:T(8,128)(2,1)S(1)} %get-tuple-element.43.raw_ref, f32[2,1,4096]{2,1,0:T(1,128)S(1)} %get-tuple-element.44.refs_0_, f32[2,1,4096]{2,1,0:T(1,128)S(1)} %collective-permute-done.7.refs_1_, f32[2,1,4096]{2,1,0:T(1,128)S(1)} %collective-permute-done.8.refs_2_, ...), custom_call_target="tpu_custom_call" | custom-call | tf_op jit(solution)/shard_map/weighted_sums/pallas_call | solution.py:427
  (13 shorter events, 0.1 us)
Async XLA Ops:
  5.1 29.7 %collective-permute-start.1 = (bf16[2,1024,128]{2,1,0:T(8,128)(2,1)S(1)}, bf16[2,1024,128]{2,1,0:T(8,128)(2,1)S(1)}, u32[]{:S(2)}, u32[]{:S(2)}) collective-permute-start(bf16[2,1024,128]{2,1,0:T(8,128)(2,1)S(1)} %get-tuple-element.47.keys_ref.refs_0_), channel_id=1, source_target_pairs={{0,8},{4,12},{8,0},{12,4},{1,9},{5,13},{9,1},{13,5},{2,10},{6,14},... | collective-permute-start | bytes 1572872 | tf_op jit(solution)/shard_map/ppermute | solution.py:528
  9.2 25.6 %collective-permute-start = (bf16[2,1024,128]{2,1,0:T(8,128)(2,1)S(1)}, bf16[2,1024,128]{2,1,0:T(8,128)(2,1)S(1)}, u32[]{:S(2)}, u32[]{:S(2)}) collective-permute-start(bf16[2,1024,128]{2,1,0:T(8,128)(2,1)S(1)} %get-tuple-element.47.keys_ref.refs_0_), channel_id=1, source_target_pairs={{0,4},{4,0},{8,12},{12,8},{1,5},{5,1},{9,13},{13,9},{2,6},{6,2},{1... | collective-permute-start | bytes 1572872 | tf_op jit(solution)/shard_map/ppermute | solution.py:528
  10.8 1.9 %collective-permute-start.2 = (f32[2,1,128]{2,1,0:T(1,128)S(1)}, f32[2,1,128]{2,1,0:T(1,128)S(1)}, u32[]{:S(2)}, u32[]{:S(2)}) collective-permute-start(f32[2,1,128]{2,1,0:T(1,128)S(1)} %slice.33), channel_id=1, source_target_pairs={{0,1},{1,0},{2,3},{3,2},{4,5},{5,4},{6,7},{7,6},{8,9},{9,8},{10,11... | collective-permute-start | bytes 3080 | tf_op jit(solution)/shard_map/ppermute | solution.py:546
  20.2 13.3 %collective-permute-start.6 = (f32[2,2,1024]{2,1,0:T(2,128)S(1)}, f32[2,2,1024]{2,1,0:T(2,128)S(1)}, u32[]{:S(2)}, u32[]{:S(2)}) collective-permute-start(f32[2,2,1024]{2,1,0:T(2,128)S(1)} %pad_maximum_fusion.1), channel_id=1, source_target_pairs={{0,4},{4,0},{8,12},{12,8},{1,5},{5,1},{9,13},{13,9},{2,6},{6,2},{1... | collective-permute-start | bytes 49160 | tf_op jit(solution)/shard_map/ppermute | solution.py:528
  24.2 9.4 %collective-permute-start.5 = (f32[2,2,1024]{2,1,0:T(2,128)S(1)}, f32[2,2,1024]{2,1,0:T(2,128)S(1)}, u32[]{:S(2)}, u32[]{:S(2)}) collective-permute-start(f32[2,2,1024]{2,1,0:T(2,128)S(1)} %pad_maximum_fusion.1), channel_id=1, source_target_pairs={{0,8},{4,12},{8,0},{12,4},{1,9},{5,13},{9,1},{13,5},{2,10},{6,14},... | collective-permute-start | bytes 49160 | tf_op jit(solution)/shard_map/ppermute | solution.py:528
  24.3 10.2 %collective-permute-start.4 = (f32[2,2,1024]{2,1,0:T(2,128)S(1)}, f32[2,2,1024]{2,1,0:T(2,128)S(1)}, u32[]{:S(2)}, u32[]{:S(2)}) collective-permute-start(f32[2,2,1024]{2,1,0:T(2,128)S(1)} %pad_maximum_fusion.1), channel_id=1, source_target_pairs={{0,12},{4,8},{8,4},{12,0},{1,13},{5,9},{9,5},{13,1},{2,14},{6,10},... | collective-permute-start | bytes 49160 | tf_op jit(solution)/shard_map/ppermute | solution.py:528
  34.8 14.9 %collective-permute-start.3 = (bf16[2,1024,128]{2,1,0:T(8,128)(2,1)S(1)}, bf16[2,1024,128]{2,1,0:T(8,128)(2,1)S(1)}, u32[]{:S(2)}, u32[]{:S(2)}) collective-permute-start(bf16[2,1024,128]{2,1,0:T(8,128)(2,1)S(1)} %collective-permute-done.1.keys_ref.refs_0_), channel_id=1, source_target_pairs={{0,4},{4,0},{8,12},{12,8},{1,5},{5,1},{9,13},{13,9},{2,6},{6,2},{1... | collective-permute-start | bytes 1572872 | tf_op jit(solution)/shard_map/ppermute | solution.py:528
  40.7 24.2 %collective-permute-start.11 = (bf16[2,544,128]{2,1,0:T(8,128)(2,1)S(1)}, bf16[2,544,128]{2,1,0:T(8,128)(2,1)S(1)}, u32[]{:S(2)}, u32[]{:S(2)}) collective-permute-start(bf16[2,544,128]{2,1,0:T(8,128)(2,1)S(1)} %get-tuple-element.49), channel_id=1, source_target_pairs={{0,4},{4,0},{8,12},{12,8},{1,5},{5,1},{9,13},{13,9},{2,6},{6,2},{1... | collective-permute-start | bytes 835592 | tf_op jit(solution)/shard_map/ppermute | solution.py:528
  42.4 22.5 %collective-permute-start.12 = (bf16[2,544,128]{2,1,0:T(8,128)(2,1)S(1)}, bf16[2,544,128]{2,1,0:T(8,128)(2,1)S(1)}, u32[]{:S(2)}, u32[]{:S(2)}) collective-permute-start(bf16[2,544,128]{2,1,0:T(8,128)(2,1)S(1)} %get-tuple-element.50), channel_id=1, source_target_pairs={{0,12},{4,8},{8,4},{12,0},{1,13},{5,9},{9,5},{13,1},{2,14},{6,10},... | collective-permute-start | bytes 835592 | tf_op jit(solution)/shard_map/ppermute | solution.py:528
  48.6 22.9 %collective-permute-start.10 = (bf16[2,544,128]{2,1,0:T(8,128)(2,1)S(1)}, bf16[2,544,128]{2,1,0:T(8,128)(2,1)S(1)}, u32[]{:S(2)}, u32[]{:S(2)}) collective-permute-start(bf16[2,544,128]{2,1,0:T(8,128)(2,1)S(1)} %get-tuple-element.46), channel_id=1, source_target_pairs={{0,8},{4,12},{8,0},{12,4},{1,9},{5,13},{9,1},{13,5},{2,10},{6,14},... | collective-permute-start | bytes 835592 | tf_op jit(solution)/shard_map/ppermute | solution.py:528
  57.9 17.9 %collective-permute-start.9 = (f32[2,1,4096]{2,1,0:T(1,128)S(1)}, f32[2,1,4096]{2,1,0:T(1,128)S(1)}, u32[]{:S(2)}, u32[]{:S(2)}) collective-permute-start(f32[2,1,4096]{2,1,0:T(1,128)S(1)} %get-tuple-element.44.refs_0_), channel_id=1, source_target_pairs={{0,12},{4,8},{8,4},{12,0},{1,13},{5,9},{9,5},{13,1},{2,14},{6,10},... | collective-permute-start | bytes 98312 | tf_op jit(solution)/shard_map/ppermute | solution.py:528
  61.2 14.6 %collective-permute-start.8 = (f32[2,1,4096]{2,1,0:T(1,128)S(1)}, f32[2,1,4096]{2,1,0:T(1,128)S(1)}, u32[]{:S(2)}, u32[]{:S(2)}) collective-permute-start(f32[2,1,4096]{2,1,0:T(1,128)S(1)} %get-tuple-element.44.refs_0_), channel_id=1, source_target_pairs={{0,8},{4,12},{8,0},{12,4},{1,9},{5,13},{9,1},{13,5},{2,10},{6,14},... | collective-permute-start | bytes 98312 | tf_op jit(solution)/shard_map/ppermute | solution.py:528
  64.8 11.0 %collective-permute-start.7 = (f32[2,1,4096]{2,1,0:T(1,128)S(1)}, f32[2,1,4096]{2,1,0:T(1,128)S(1)}, u32[]{:S(2)}, u32[]{:S(2)}) collective-permute-start(f32[2,1,4096]{2,1,0:T(1,128)S(1)} %get-tuple-element.44.refs_0_), channel_id=1, source_target_pairs={{0,4},{4,0},{8,12},{12,8},{1,5},{5,1},{9,13},{13,9},{2,6},{6,2},{1... | collective-permute-start | bytes 98312 | tf_op jit(solution)/shard_map/ppermute | solution.py:528

commit v7 on v6

--- a/solution.py
+++ b/solution.py
@@ -406,113 +406,110 @@
 
 def sums_kernel(blocks, raw_ref, *refs):
     totals, units = refs[:blocks], refs[blocks : 2 * blocks]
-    out_ref, scaled_ref = refs[2 * blocks :]
-    head = pl.program_id(0)
-    tokens = units[0].shape[1]
-    for m, unit_ref in enumerate(units):
-        row_total = totals[0][head, :, m * tokens : (m + 1) * tokens]
-        for d in range(1, blocks):
-            peer = m ^ d
-            row_total += totals[d][head, :, peer * tokens : (peer + 1) * tokens]
-        scale_rows(
-            unit_ref[head], 1.0 / row_total, scaled_ref.at[m * tokens : (m + 1) * tokens]
-        )
-    out_ref[0] = unit_rows(dot_nn(raw_ref[head], scaled_ref[...]))
+    out_hbm, scaled_ref, result_ref, sems = refs[2 * blocks :]
+    heads, tokens, _ = units[0].shape
+    copies = []
+    for h in range(heads):
+        for m, unit_ref in enumerate(units):
+            row_total = totals[0][h, :, m * tokens : (m + 1) * tokens]
+            for d in range(1, blocks):
+                peer = m ^ d
+                row_total += totals[d][h, :, peer * tokens : (peer + 1) * tokens]
+            here = slice(m * tokens, (m + 1) * tokens)
+            scale_rows(unit_ref[h], 1.0 / row_total, scaled_ref.at[h, here])
+        result_ref[h] = unit_rows(dot_nn(raw_ref[h], scaled_ref[h]))
+        copies.append(pltpu.make_async_copy(result_ref.at[h], out_hbm.at[h], sems.at[h]))
+        copies[-1].start()
+    for copy in copies:
+        copy.wait()
 
 
 def weighted_sums(raw, units, totals):
     heads, rows, count = raw.shape
-    _, tokens, width = units[0].shape
-    blocks = len(units)
-    return pl.pallas_call(
-        functools.partial(sums_kernel, blocks),
-        grid=(heads,),
-        in_specs=[in_vmem()]
-        + [in_vmem()] * (2 * blocks),
-        out_specs=pl.BlockSpec((1, rows, width), lambda h: (h, 0, 0)),
+    width = units[0].shape[2]
+    return pl.pallas_call(
+        functools.partial(sums_kernel, len(units)),
+        in_specs=[in_vmem()] * (1 + 2 * len(units)),
+        out_specs=anywhere(),
         out_shape=jax.ShapeDtypeStruct((heads, rows, width), F32),
         scratch_shapes=[
-            pltpu.VMEM((count, width), BF16),
+            pltpu.VMEM((heads, count, width), BF16),
+            pltpu.VMEM((heads, rows, width), F32),
+            pltpu.SemaphoreType.DMA((heads,)),
         ],
         compiler_params=params(),
         name="weighted_sums",
     )(keep_vmem(raw), *map(keep_vmem, totals), *map(keep_vmem, units))
 
 
-def place_kernel(blocks, size, fresh, scalar_ref, label_ref, *refs):
-    count = len(blocks)
-    keys, values, refs = refs[:count], refs[count : 2 * count], refs[2 * count :]
-    before, (*out_refs, rows_ref, near_ref, mixed_ref) = refs[: 0 if fresh else 2], refs[0 if fresh else 2 :]
-    step = pl.program_id(0)
+def place_kernel(blocks, size, scalar_ref, label_ref, _, *refs):
+    keys, values, refs = refs[:blocks], refs[blocks : 2 * blocks], refs[2 * blocks :]
+    *out_hbm, rows_ref, near_ref, mixed_ref, done_ref, sems = refs
     heads, tokens, width = keys[0].shape
     digit_rows = tokens // LANES
     sent = values[0].shape[1] - 2 * digit_rows
+    rows_ref[:, :, width:] = jnp.zeros((heads, blocks * size, width), BF16)
+    for h in range(heads):
+        low, high, first = (scalar_ref[i, h, 0].astype(F32) for i in range(2, 5))
+        for m in range(blocks):
+            start = pl.multiple_of(scalar_ref[0, h, m], 16)
+            gap = pl.multiple_of(scalar_ref[1, h, m], 16)
+            here = m * size
+            rows_ref[h, here : here + size, :width] = keys[m][h, pl.ds(start, size), :]
+            rows_ref[h, pl.ds(here + gap, sent), width:] = values[m][h, :sent, :]
+            digits = values[m][h, sent:, :].astype(F32)
+            rank = digits[:digit_rows] * 128.0 + digits[digit_rows:]
+            rank = jnp.concatenate([rank[r : r + 1] for r in range(digit_rows)], axis=1)
+            label = label_ref[h, m : m + 1, :]
+            mine = (label >= low) & (label < high)
+            spot = jnp.where(mine, rank - first, -1.0).astype(jnp.int32)
+            spot = pltpu.roll(spot, lax.rem(tokens - start, tokens), 1)
+            near_ref[h, :, here : here + size] = spot[:, :size]
+
     rows = mixed_ref.shape[1] // heads
-
-    @pl.when(step == 0)
-    def _():
-        rows_ref[:, :, width:] = jnp.zeros((heads, count * size, width), BF16)
+    copies = []
+    for step in range(out_hbm[0].shape[0] // (rows * heads)):
         for h in range(heads):
-            low, high, first = (scalar_ref[i, h, 0].astype(F32) for i in range(2, 5))
-            for i, m in enumerate(blocks):
-                start = pl.multiple_of(scalar_ref[0, h, m], 16)
-                gap = pl.multiple_of(scalar_ref[1, h, m], 16)
-                here = i * size
-                rows_ref[h, here : here + size, :width] = keys[i][h, pl.ds(start, size), :]
-                rows_ref[h, pl.ds(here + gap, sent), width:] = values[i][h, :sent, :]
-                digits = values[i][h, sent:, :].astype(F32)
-                rank = digits[:digit_rows] * 128.0 + digits[digit_rows:]
-                rank = jnp.concatenate([rank[r : r + 1] for r in range(digit_rows)], axis=1)
-                label = label_ref[h, m : m + 1, :]
-                mine = (label >= low) & (label < high)
-                spot = jnp.where(mine, rank - first, -1.0).astype(jnp.int32)
-                spot = pltpu.roll(spot, lax.rem(tokens - start, tokens), 1)
-                near_ref[h, :, here : here + size] = spot[:, :size]
-
-    for h in range(heads):
-        pick = one_hot_rows(rows, near_ref[h] - step * rows)
-        total = dot_nn(pick, rows_ref[h])
+            pick = one_hot_rows(rows, near_ref[h] - step * rows)
+            total = dot_nn(pick, rows_ref[h])
+            for side in range(2):
+                mixed_ref[side, pl.Slice(h, rows, heads), :] = total[
+                    :, side * width : (side + 1) * width
+                ]
+        here = slice(step * rows * heads, (step + 1) * rows * heads)
         for side in range(2):
-            mixed_ref[side, pl.Slice(h, rows, heads), :] = total[
-                :, side * width : (side + 1) * width
-            ]
-    for side in range(2):
-        if fresh:
-            here = pl.ds(pl.multiple_of(step * rows * heads, rows * heads), rows * heads)
-            out_refs[side][here] = mixed_ref[side].astype(BF16)
-        else:
-            here = pl.ds(pl.multiple_of(step * rows * heads, rows * heads), rows * heads)
-            more = mixed_ref[side] + before[side][here].astype(F32)
-            out_refs[side][...] = more.astype(BF16)
-
-
-def place(scalars, labels, keys, values, blocks, size, cap, before):
+            done_ref[side, here] = mixed_ref[side].astype(BF16)
+            copies.append(
+                pltpu.make_async_copy(
+                    done_ref.at[side, here], out_hbm[side].at[here], sems.at[len(copies)]
+                )
+            )
+            copies[-1].start()
+    for copy in copies:
+        copy.wait()
+
+
+def place(scalars, labels, keys, values, size, cap, after):
+    blocks = len(keys)
     heads, _, width = keys[0].shape
     rows = 512
-    fresh = before is None
-    if fresh:
-        out = pltpu.VMEM((heads * cap, width), BF16)
-        block = in_vmem()
-    else:
-        out = jax.ShapeDtypeStruct((heads * cap, width), BF16)
-        block = pl.BlockSpec((heads * rows, width), lambda r: (r, 0))
-    moved = [x[m] for x in (keys, values) for m in blocks] + list(before or ())
-    return pl.pallas_call(
-        functools.partial(place_kernel, blocks, size, fresh),
-        grid=(cap // rows,),
-        in_specs=[pl.BlockSpec(memory_space=pltpu.SMEM)]
-        + [whole(labels.shape)]
-        + [in_vmem()] * len(moved),
-        out_specs=(block, block),
+    out = jax.ShapeDtypeStruct((heads * cap, width), BF16)
+    return pl.pallas_call(
+        functools.partial(place_kernel, blocks, size),
+        in_specs=[pl.BlockSpec(memory_space=pltpu.SMEM), in_vmem(), anywhere()]
+        + [in_vmem()] * (2 * blocks),
+        out_specs=(anywhere(), anywhere()),
         out_shape=(out, out),
         scratch_shapes=[
-            pltpu.VMEM((heads, len(blocks) * size, 2 * width), BF16),
-            pltpu.VMEM((heads, 1, len(blocks) * size), jnp.int32),
+            pltpu.VMEM((heads, blocks * size, 2 * width), BF16),
+            pltpu.VMEM((heads, 1, blocks * size), jnp.int32),
             pltpu.VMEM((2, heads * rows, width), F32),
+            pltpu.VMEM((2, heads * cap, width), BF16),
+            pltpu.SemaphoreType.DMA((2 * cap // rows,)),
         ],
         compiler_params=params(),
         name="place",
-    )(scalars, labels, *map(keep_vmem, moved))
+    )(scalars, labels, keep_hbm(after), *(keep_vmem(x) for x in (*keys, *values)))
 
 
 def body(key_rows, value_rows, cluster_labels, owner_bounds, init_centroids):
@@ -562,7 +559,6 @@
 
     labels = jnp.concatenate([x[:, -1:] for x in shared], axis=1)
     ranks = own_ranks(me_array, labels)
-    value_starts = aligned(own_below, send_size)
     low = lax.dynamic_slice_in_dim(owner_bounds, me, 1, 1)
     high = lax.dynamic_slice_in_dim(owner_bounds, me + 1, 1, 1)
     below = jnp.sum((labels < low[:, :, None]).astype(jnp.int32), axis=2)
@@ -572,23 +568,26 @@
     one = jnp.ones((1, n), jnp.int32)
     scalars = jnp.stack([key_starts, gaps, low * one, high * one, first * one])
 
-    late = [2]
-    early = [d for d in range(1, n) if d not in late]
-    values = {}
+    starts = aligned(own_below, send_size)
+    own_windows = windows(starts, ranks, own_values, send_size, own_labels)
+    middle = [2]
+    far = [d for d in range(1, n) if d & (d - 1)]
+    near = [1] + [d for d in range(3, n) if not d & (d - 1)]
+    values = {0: own_windows[0]}
     for m in range(1, n):
+        group = {1: far, 2: near, 3: middle}.get(m)
+        if group:
+            *leaving, sums = lax.optimization_barrier((*(own_windows[d] for d in group), sums))
+            for d, window in zip(group, leaving):
+                values[d] = swap(window, d)
         sums, unit = first_block(me_array, keys[m], totals[m], cents, n, sums)
         units.append(unit)
-        going = {1: early, 2: [0, *late]}.get(m, [])
-        if going:
-            starts = jnp.stack([value_starts[:, d] for d in going], axis=1)
-            for d, window in zip(going, windows(starts, ranks, own_values, send_size, unit)):
-                values[d] = swap(window, d) if d else window
 
     raw, part = raw_weights(sums, units)
     parts = spread(part)
-    placed = place(scalars, labels, keys, values, [0, *early], key_size, cap, None)
     out = weighted_sums(raw, units, parts)
-    placed = place(scalars, labels, keys, values, late, key_size, cap, placed)
+    values = [values[m] for m in range(n)]
+    placed = place(scalars, labels, keys, values, key_size, cap, out)
     shape = (cap, heads, width)
     return out, placed[0].reshape(shape), placed[1].reshape(shape)
 

time: 82.3 us -> 93 us (1.13)
  starting transfers between devices: 18.3 us -> 30.1 us
  Pallas kernels: 52.7 us -> 49 us
  waiting for transfers between devices: 6.81 us -> 9.44 us
    ppermute x12, starting transfers between devices: 18.3 us -> 30 us  [swap(): return lax.ppermute(x, 'ctx', [(i, i ^ d) for i in range(n)])]
    pallas_call x3 -> x2, Pallas kernels: 17.1 us -> 14 us  [the longest x1 7.95 us: place(): pl.pallas_call(functools.partial(place_kernel, blocks, size), in_specs=[p...]
    ppermute x12, waiting for transfers between devices: 6.81 us -> 9.44 us  [swap(): return lax.ppermute(x, 'ctx', [(i, i ^ d) for i in range(n)])]
  transfers between devices with their start and end apart: 13 -> 13, of which waited for: 4 -> 7; matrix products, arithmetic and copies ran while one was open for 4% -> 4% of each run, Pallas kernels for 51% -> 39%
where the time goes in v7:
time: 93 us; the launch traced here: 92.8 us
  Pallas kernels  49 us (53%)
  starting transfers between devices  30.1 us (32%)
  waiting for transfers between devices  9.44 us (10%)
  local copies, waits for them, and re-layouts  2.67 us (3%)
  between operations  1 us (1%)
    ppermute x12, starting transfers between devices, swap(): return lax.ppermute(x, 'ctx', [(i, i ^ d) for i in range(n)])  30 us
    pallas_call x4, Pallas kernels, first_block(): pl.pallas_call(functools.partial(first_kernel, fresh), grid_spec=pltpu.Pr...  13 us
    ppermute x12, waiting for transfers between devices, swap(): return lax.ppermute(x, 'ctx', [(i, i ^ d) for i in range(n)])  9.44 us
    pallas_call x1, Pallas kernels, place(): pl.pallas_call(functools.partial(place_kernel, blocks, size), in_specs=[p...  7.95 us
    pallas_call x1, Pallas kernels, own_totals(): pl.pallas_call(totals_kernel, grid=(heads, count // rows), in_specs=[in_v...  7.57 us
    pallas_call x1, Pallas kernels, weighted_sums(): pl.pallas_call(functools.partial(sums_kernel, len(units)), in_specs=[in_v...  6.06 us
    pallas_call x1, Pallas kernels, raw_weights(): pl.pallas_call(functools.partial(raw_kernel, len(units)), grid=(heads,),...  5.23 us
    pallas_call x1, Pallas kernels, sort_keys(): pl.pallas_call(sort_kernel, grid=(heads,), in_specs=[anywhere()] * 2, out...  4.45 us
  transfers between devices with their start and end apart: 13, of which 7 were waited for; matrix products, arithmetic and copies ran while one was open for 4% of the time, Pallas kernels for 39%

profile of v7, /device:TPU:0, one launch (start us, length us, event | category | flops | bytes accessed | tf_op | source)
XLA Modules:
  0.0 92.8 jit_solution(6157938263965859662)
XLA Ops:
  0.6 4.4 %sort_keys.1 = (bf16[2,1024,128]{2,1,0:T(8,128)(2,1)S(1)}, f32[2,1,1024]{2,1,0:T(1,128)S(1)}, s32[2,1,1024]{2,1,0:T(1,128)S(1)}) custom-call(s32[2,1024]{1,0:T(2,128)} %label_hbm.1, bf16[2048,128]{1,0:T(8,128)(2,1)} %bitcast.26), custom_call_target="tpu_custom_call" | custom-call | tf_op jit(solution)/shard_map/sort_keys/pallas_call | solution.py:139
  5.1 4.1 %collective-permute-start.1 = (bf16[2,1024,128]{2,1,0:T(8,128)(2,1)S(1)}, bf16[2,1024,128]{2,1,0:T(8,128)(2,1)S(1)}, u32[]{:S(2)}, u32[]{:S(2)}) collective-permute-start(bf16[2,1024,128]{2,1,0:T(8,128)(2,1)S(1)} %get-tuple-element.56.keys_ref.refs_0_), channel_id=1, source_target_pairs={{0,8},{4,12},{8,0},{12,4},{1,9},{5,13},{9,1},{13,5},{2,10},{6,14},... | collective-permute-start | bytes 1572872 | tf_op jit(solution)/shard_map/ppermute | solution.py:525
  9.2 1.6 %collective-permute-start = (bf16[2,1024,128]{2,1,0:T(8,128)(2,1)S(1)}, bf16[2,1024,128]{2,1,0:T(8,128)(2,1)S(1)}, u32[]{:S(2)}, u32[]{:S(2)}) collective-permute-start(bf16[2,1024,128]{2,1,0:T(8,128)(2,1)S(1)} %get-tuple-element.56.keys_ref.refs_0_), channel_id=1, source_target_pairs={{0,4},{4,0},{8,12},{12,8},{1,5},{5,1},{9,13},{13,9},{2,6},{6,2},{1... | collective-permute-start | bytes 1572872 | tf_op jit(solution)/shard_map/ppermute | solution.py:525
  10.8 0.0 collective-permute-start.2
  10.8 0.8 copy.13
  11.6 0.6 gather_fusion
  12.1 0.1 convert_bitcast_fusion
  12.2 0.1 copy.14
  12.3 0.2 convert_reduce_fusion.2
  12.5 0.0 collective-permute-done.2._
  12.5 7.6 %own_totals.1.tot_ref = f32[2,1,1024]{2,1,0:T(1,128)S(1)} custom-call(bf16[2,1024,128]{2,1,0:T(8,128)(2,1)S(1)} %get-tuple-element.56.keys_ref.refs_0_, f32[2,4096,128]{2,1,0:T(8,128)} %cent_in.1, f32[2,1,128]{2,1,0:T(1,128)S(1)} %collective-permute-done.2._), custom_call_target="tpu_custom_call" | custom-call | tf_op jit(solution)/shard_map/own_totals/pallas_call | solution.py:285
  20.1 0.4 collective-permute-start.6
  20.6 1.0 %dynamic-slice_reduce_fusion = (s32[2]{0:T(128)S(1)}, s32[2]{0:T(128)S(1)}) fusion(s32[2,5]{1,0:T(2,128)} %param.8, s32[]{:T(128)S(6)} %select_n.56, s32[]{:T(128)S(6)} %select_n.54), kind=kLoop, calls=%fused_computation.27 | loop fusion | bytes 40 | tf_op jit(solution)/shard_map/dynamic_slice | solution.py:563
  21.5 2.3 %sort_values.1.values_ref = bf16[2,1024,128]{2,1,0:T(8,128)(2,1)S(1)} custom-call(s32[2,1,1024]{2,1,0:T(1,128)S(1)} %get-tuple-element.38.spot_ref, bf16[2048,128]{1,0:T(8,128)(2,1)} %bitcast.27), custom_call_target="tpu_custom_call" | custom-call | tf_op jit(solution)/shard_map/sort_values/pallas_call | solution.py:179
  23.9 0.3 collective-permute-start.5
  24.2 3.9 %collective-permute-start.4 = (f32[2,2,1024]{2,1,0:T(2,128)S(1)}, f32[2,2,1024]{2,1,0:T(2,128)S(1)}, u32[]{:S(2)}, u32[]{:S(2)}) collective-permute-start(f32[2,2,1024]{2,1,0:T(2,128)S(1)} %pad_maximum_fusion.1), channel_id=1, source_target_pairs={{0,12},{4,8},{8,4},{12,0},{1,13},{5,9},{9,5},{13,1},{2,14},{6,10},... | collective-permute-start | bytes 49160 | tf_op jit(solution)/shard_map/ppermute | solution.py:525
  28.0 4.1 %first_block.4 = (f32[2,1024,128]{2,1,0:T(8,128)S(1)}, bf16[2,1024,128]{2,1,0:T(8,128)(2,1)S(1)}, bf16[2,1024,128]{2,1,0:T(8,128)(2,1)S(1)}) custom-call(s32[1]{0:T(128)} %bitcast._.me_ref, bf16[2,1024,128]{2,1,0:T(8,128)(2,1)S(1)} %get-tuple-element.56.keys_ref.refs_0_, f32[2,1,1024]{2,1,0:T(1,128)S(1)} %own_totals.1.tot_ref, f32[2,4096,128]{2,1,0:T(8,128)} %cent_in.1), custom_call_target="tpu_custom_call" | custom-call | tf_op jit(solution)/shard_map/first_block/pallas_call | solution.py:355
  32.1 1.0 %collective-permute-done.6 = f32[2,2,1024]{2,1,0:T(2,128)S(1)} collective-permute-done((f32[2,2,1024]{2,1,0:T(2,128)S(1)}, f32[2,2,1024]{2,1,0:T(2,128)S(1)}, u32[]{:S(2)}, u32[]{:S(2)}) %collective-permute-start.6) | collective-permute-done | bytes 16416 | tf_op jit(solution)/shard_map/ppermute | solution.py:525
  33.2 0.3 collective-permute-done.5
  33.5 1.0 %collective-permute-done.4 = f32[2,2,1024]{2,1,0:T(2,128)S(1)} collective-permute-done((f32[2,2,1024]{2,1,0:T(2,128)S(1)}, f32[2,2,1024]{2,1,0:T(2,128)S(1)}, u32[]{:S(2)}, u32[]{:S(2)}) %collective-permute-start.4) | collective-permute-done | bytes 16416 | tf_op jit(solution)/shard_map/ppermute | solution.py:525
  34.5 0.1 broadcast_compare_fusion
  34.6 0.2 convert_reduce_fusion
  34.8 0.0 collective-permute-done.1.keys_ref.refs_2_
  34.8 0.0 collective-permute-done.keys_ref.refs_1_
  34.8 0.6 collective-permute-start.3
  35.4 1.8 %own_ranks.1.rank_ref = f32[2,1,1024]{2,1,0:T(1,128)S(1)} custom-call(s32[1]{0:T(128)} %bitcast._.me_ref, f32[2,4,1024]{2,1,0:T(4,128)S(1)} %get-tuple-element.68.label_ref), custom_call_target="tpu_custom_call" | custom-call | tf_op jit(solution)/shard_map/own_ranks/pallas_call | solution.py:245
  37.2 0.6 windows.1
  37.8 0.1 constant_dynamic-update-slice_fusion.2
  37.9 2.9 %collective-permute-start.12 = (bf16[2,544,128]{2,1,0:T(8,128)(2,1)S(1)}, bf16[2,544,128]{2,1,0:T(8,128)(2,1)S(1)}, u32[]{:S(2)}, u32[]{:S(2)}) collective-permute-start(bf16[2,544,128]{2,1,0:T(8,128)(2,1)S(1)} %get-tuple-element.60), channel_id=1, source_target_pairs={{0,12},{4,8},{8,4},{12,0},{1,13},{5,9},{9,5},{13,1},{2,14},{6,10},... | collective-permute-start | bytes 835592 | tf_op jit(solution)/shard_map/ppermute | solution.py:525
  40.8 3.0 %first_block.5 = (f32[2,1024,128]{2,1,0:T(8,128)S(1)}, bf16[2,1024,128]{2,1,0:T(8,128)(2,1)S(1)}) custom-call(s32[1]{0:T(128)} %bitcast._.me_ref, bf16[2,1024,128]{2,1,0:T(8,128)(2,1)S(1)} %collective-permute-done.keys_ref.refs_1_, f32[2,1,1024]{2,1,0:T(1,128)S(1)} %get-tuple-element.69.tot_ref, ...), custom_call_target="tpu_custom_call", output_to_operand_aliasing={{0}: (4, {})} | custom-call | tf_op jit(solution)/shard_map/first_block/pallas_call | solution.py:355
  43.7 0.4 collective-permute-start.10
  44.2 3.0 %first_block.6 = (f32[2,1024,128]{2,1,0:T(8,128)S(1)}, bf16[2,1024,128]{2,1,0:T(8,128)(2,1)S(1)}) custom-call(s32[1]{0:T(128)} %bitcast._.me_ref, bf16[2,1024,128]{2,1,0:T(8,128)(2,1)S(1)} %collective-permute-done.1.keys_ref.refs_2_, f32[2,1,1024]{2,1,0:T(1,128)S(1)} %get-tuple-element.71.tot_ref, ...), custom_call_target="tpu_custom_call", output_to_operand_aliasing={{0}: (4, {})} | custom-call | tf_op jit(solution)/shard_map/first_block/pallas_call | solution.py:355
  47.1 1.2 %collective-permute-start.11 = (bf16[2,544,128]{2,1,0:T(8,128)(2,1)S(1)}, bf16[2,544,128]{2,1,0:T(8,128)(2,1)S(1)}, u32[]{:S(2)}, u32[]{:S(2)}) collective-permute-start(bf16[2,544,128]{2,1,0:T(8,128)(2,1)S(1)} %get-tuple-element.59), channel_id=1, source_target_pairs={{0,8},{4,12},{8,0},{12,4},{1,9},{5,13},{9,1},{13,5},{2,10},{6,14},... | collective-permute-start | bytes 835592 | tf_op jit(solution)/shard_map/ppermute | solution.py:525
  48.4 1.4 %collective-permute-done.3.keys_ref.refs_3_ = bf16[2,1024,128]{2,1,0:T(8,128)(2,1)S(1)} collective-permute-done((bf16[2,1024,128]{2,1,0:T(8,128)(2,1)S(1)}, bf16[2,1024,128]{2,1,0:T(8,128)(2,1)S(1)}, u32[]{:S(2)}, u32[]{:S(2)}) %collective-permute-start.3) | collective-permute-done | bytes 524320 | tf_op jit(solution)/shard_map/ppermute | solution.py:525
  49.8 3.0 %first_block.7 = (f32[2,1024,128]{2,1,0:T(8,128)S(1)}, bf16[2,1024,128]{2,1,0:T(8,128)(2,1)S(1)}) custom-call(s32[1]{0:T(128)} %bitcast._.me_ref, bf16[2,1024,128]{2,1,0:T(8,128)(2,1)S(1)} %collective-permute-done.3.keys_ref.refs_3_, f32[2,1,1024]{2,1,0:T(1,128)S(1)} %get-tuple-element.74.tot_ref, ...), custom_call_target="tpu_custom_call", output_to_operand_aliasing={{0}: (4, {})} | custom-call | tf_op jit(solution)/shard_map/first_block/pallas_call | solution.py:355
  52.8 5.2 %raw_weights.1 = (bf16[2,1024,4096]{2,1,0:T(8,128)(2,1)S(1)}, f32[2,1,4096]{2,1,0:T(1,128)S(1)}) custom-call(f32[2,1024,128]{2,1,0:T(8,128)S(1)} %get-tuple-element.49.sums_ref, bf16[2,1024,128]{2,1,0:T(8,128)(2,1)S(1)} %get-tuple-element.50.refs_0_.refs_4_, bf16[2,1024,128]{2,1,0:T(8,128)(2,1)S(1)} %get-tuple-element.51.refs_1_.refs_5_, ...), custom_call_target="tpu_custom_call" | custom-call | tf_op jit(solution)/shard_map/raw_weights/pallas_call | solution.py:392
  58.0 14.7 %collective-permute-start.9 = (f32[2,1,4096]{2,1,0:T(1,128)S(1)}, f32[2,1,4096]{2,1,0:T(1,128)S(1)}, u32[]{:S(2)}, u32[]{:S(2)}) collective-permute-start(f32[2,1,4096]{2,1,0:T(1,128)S(1)} %get-tuple-element.55.refs_0_), channel_id=1, source_target_pairs={{0,12},{4,8},{8,4},{12,0},{1,13},{5,9},{9,5},{13,1},{2,14},{6,10},... | collective-permute-start | bytes 98312 | tf_op jit(solution)/shard_map/ppermute | solution.py:525
  72.8 0.1 constant_dynamic-update-slice_fusion.1
  72.8 0.0 collective-permute-start.8
  72.8 1.8 %collective-permute-done.9.refs_3_ = f32[2,1,4096]{2,1,0:T(1,128)S(1)} collective-permute-done((f32[2,1,4096]{2,1,0:T(1,128)S(1)}, f32[2,1,4096]{2,1,0:T(1,128)S(1)}, u32[]{:S(2)}, u32[]{:S(2)}) %collective-permute-start.9) | collective-permute-done | bytes 32800 | tf_op jit(solution)/shard_map/ppermute | solution.py:525
  74.6 0.0 collective-permute-start.7
  74.7 0.1 constant_dynamic-update-slice_fusion.scalar_ref
  74.7 2.9 %collective-permute-done.8.refs_2_ = f32[2,1,4096]{2,1,0:T(1,128)S(1)} collective-permute-done((f32[2,1,4096]{2,1,0:T(1,128)S(1)}, f32[2,1,4096]{2,1,0:T(1,128)S(1)}, u32[]{:S(2)}, u32[]{:S(2)}) %collective-permute-start.8) | collective-permute-done | bytes 32800 | tf_op jit(solution)/shard_map/ppermute | solution.py:525
  77.6 0.9 collective-permute-done.7.refs_1_
  78.6 6.1 %weighted_sums.1._ = f32[2,1024,128]{2,1,0:T(8,128)} custom-call(bf16[2,1024,4096]{2,1,0:T(8,128)(2,1)S(1)} %get-tuple-element.54.raw_ref, f32[2,1,4096]{2,1,0:T(1,128)S(1)} %get-tuple-element.55.refs_0_, f32[2,1,4096]{2,1,0:T(1,128)S(1)} %collective-permute-done.7.refs_1_, f32[2,1,4096]{2,1,0:T(1,128)S(1)} %collective-permute-done.8.refs_2_, ...), custom_call_target="tpu_custom_call" | custom-call | tf_op jit(solution)/shard_map/weighted_sums/pallas_call | solution.py:430
  84.6 0.0 collective-permute-done.12.refs_7_
  84.6 0.0 collective-permute-done.10.refs_5_
  84.7 0.0 collective-permute-done.11.refs_6_
  84.7 8.0 %place.1 = (bf16[4096,128]{1,0:T(8,128)(2,1)}, bf16[4096,128]{1,0:T(8,128)(2,1)}) custom-call(s32[5,2,4]{2,1,0:T(2,128)S(1)} %constant_dynamic-update-slice_fusion.scalar_ref, f32[2,4,1024]{2,1,0:T(4,128)S(1)} %get-tuple-element.68.label_ref, f32[2,1024,128]{2,1,0:T(8,128)} %weighted_sums.1._, bf16[2,1024,128]{2,1,0:T(8,128)(2,1)S(1)} %get-tuple-element.56.keys_ref.refs_0_, ...), custom_call_target="tpu_custom_call" | custom-call | tf_op jit(solution)/shard_map/place/pallas_call | solution.py:497
  (13 shorter events, 0.1 us)
Async XLA Ops:
  5.1 29.7 %collective-permute-start.1 = (bf16[2,1024,128]{2,1,0:T(8,128)(2,1)S(1)}, bf16[2,1024,128]{2,1,0:T(8,128)(2,1)S(1)}, u32[]{:S(2)}, u32[]{:S(2)}) collective-permute-start(bf16[2,1024,128]{2,1,0:T(8,128)(2,1)S(1)} %get-tuple-element.56.keys_ref.refs_0_), channel_id=1, source_target_pairs={{0,8},{4,12},{8,0},{12,4},{1,9},{5,13},{9,1},{13,5},{2,10},{6,14},... | collective-permute-start | bytes 1572872 | tf_op jit(solution)/shard_map/ppermute | solution.py:525
  9.2 25.6 %collective-permute-start = (bf16[2,1024,128]{2,1,0:T(8,128)(2,1)S(1)}, bf16[2,1024,128]{2,1,0:T(8,128)(2,1)S(1)}, u32[]{:S(2)}, u32[]{:S(2)}) collective-permute-start(bf16[2,1024,128]{2,1,0:T(8,128)(2,1)S(1)} %get-tuple-element.56.keys_ref.refs_0_), channel_id=1, source_target_pairs={{0,4},{4,0},{8,12},{12,8},{1,5},{5,1},{9,13},{13,9},{2,6},{6,2},{1... | collective-permute-start | bytes 1572872 | tf_op jit(solution)/shard_map/ppermute | solution.py:525
  10.8 1.8 %collective-permute-start.2 = (f32[2,1,128]{2,1,0:T(1,128)S(1)}, f32[2,1,128]{2,1,0:T(1,128)S(1)}, u32[]{:S(2)}, u32[]{:S(2)}) collective-permute-start(f32[2,1,128]{2,1,0:T(1,128)S(1)} %slice.21), channel_id=1, source_target_pairs={{0,1},{1,0},{2,3},{3,2},{4,5},{5,4},{6,7},{7,6},{8,9},{9,8},{10,11... | collective-permute-start | bytes 3080 | tf_op jit(solution)/shard_map/ppermute | solution.py:543
  20.1 13.0 %collective-permute-start.6 = (f32[2,2,1024]{2,1,0:T(2,128)S(1)}, f32[2,2,1024]{2,1,0:T(2,128)S(1)}, u32[]{:S(2)}, u32[]{:S(2)}) collective-permute-start(f32[2,2,1024]{2,1,0:T(2,128)S(1)} %pad_maximum_fusion.1), channel_id=1, source_target_pairs={{0,8},{4,12},{8,0},{12,4},{1,9},{5,13},{9,1},{13,5},{2,10},{6,14},... | collective-permute-start | bytes 49160 | tf_op jit(solution)/shard_map/ppermute | solution.py:525
  23.9 9.6 %collective-permute-start.5 = (f32[2,2,1024]{2,1,0:T(2,128)S(1)}, f32[2,2,1024]{2,1,0:T(2,128)S(1)}, u32[]{:S(2)}, u32[]{:S(2)}) collective-permute-start(f32[2,2,1024]{2,1,0:T(2,128)S(1)} %pad_maximum_fusion.1), channel_id=1, source_target_pairs={{0,4},{4,0},{8,12},{12,8},{1,5},{5,1},{9,13},{13,9},{2,6},{6,2},{1... | collective-permute-start | bytes 49160 | tf_op jit(solution)/shard_map/ppermute | solution.py:525
  24.2 10.3 %collective-permute-start.4 = (f32[2,2,1024]{2,1,0:T(2,128)S(1)}, f32[2,2,1024]{2,1,0:T(2,128)S(1)}, u32[]{:S(2)}, u32[]{:S(2)}) collective-permute-start(f32[2,2,1024]{2,1,0:T(2,128)S(1)} %pad_maximum_fusion.1), channel_id=1, source_target_pairs={{0,12},{4,8},{8,4},{12,0},{1,13},{5,9},{9,5},{13,1},{2,14},{6,10},... | collective-permute-start | bytes 49160 | tf_op jit(solution)/shard_map/ppermute | solution.py:525
  34.8 15.0 %collective-permute-start.3 = (bf16[2,1024,128]{2,1,0:T(8,128)(2,1)S(1)}, bf16[2,1024,128]{2,1,0:T(8,128)(2,1)S(1)}, u32[]{:S(2)}, u32[]{:S(2)}) collective-permute-start(bf16[2,1024,128]{2,1,0:T(8,128)(2,1)S(1)} %collective-permute-done.1.keys_ref.refs_2_), channel_id=1, source_target_pairs={{0,4},{4,0},{8,12},{12,8},{1,5},{5,1},{9,13},{13,9},{2,6},{6,2},{1... | collective-permute-start | bytes 1572872 | tf_op jit(solution)/shard_map/ppermute | solution.py:525
  37.9 46.7 %collective-permute-start.12 = (bf16[2,544,128]{2,1,0:T(8,128)(2,1)S(1)}, bf16[2,544,128]{2,1,0:T(8,128)(2,1)S(1)}, u32[]{:S(2)}, u32[]{:S(2)}) collective-permute-start(bf16[2,544,128]{2,1,0:T(8,128)(2,1)S(1)} %get-tuple-element.60), channel_id=1, source_target_pairs={{0,12},{4,8},{8,4},{12,0},{1,13},{5,9},{9,5},{13,1},{2,14},{6,10},... | collective-permute-start | bytes 835592 | tf_op jit(solution)/shard_map/ppermute | solution.py:525
  43.7 40.9 %collective-permute-start.10 = (bf16[2,544,128]{2,1,0:T(8,128)(2,1)S(1)}, bf16[2,544,128]{2,1,0:T(8,128)(2,1)S(1)}, u32[]{:S(2)}, u32[]{:S(2)}) collective-permute-start(bf16[2,544,128]{2,1,0:T(8,128)(2,1)S(1)} %get-tuple-element.58), channel_id=1, source_target_pairs={{0,4},{4,0},{8,12},{12,8},{1,5},{5,1},{9,13},{13,9},{2,6},{6,2},{1... | collective-permute-start | bytes 835592 | tf_op jit(solution)/shard_map/ppermute | solution.py:525
  47.1 37.5 %collective-permute-start.11 = (bf16[2,544,128]{2,1,0:T(8,128)(2,1)S(1)}, bf16[2,544,128]{2,1,0:T(8,128)(2,1)S(1)}, u32[]{:S(2)}, u32[]{:S(2)}) collective-permute-start(bf16[2,544,128]{2,1,0:T(8,128)(2,1)S(1)} %get-tuple-element.59), channel_id=1, source_target_pairs={{0,8},{4,12},{8,0},{12,4},{1,9},{5,13},{9,1},{13,5},{2,10},{6,14},... | collective-permute-start | bytes 835592 | tf_op jit(solution)/shard_map/ppermute | solution.py:525
  58.0 16.6 %collective-permute-start.9 = (f32[2,1,4096]{2,1,0:T(1,128)S(1)}, f32[2,1,4096]{2,1,0:T(1,128)S(1)}, u32[]{:S(2)}, u32[]{:S(2)}) collective-permute-start(f32[2,1,4096]{2,1,0:T(1,128)S(1)} %get-tuple-element.55.refs_0_), channel_id=1, source_target_pairs={{0,12},{4,8},{8,4},{12,0},{1,13},{5,9},{9,5},{13,1},{2,14},{6,10},... | collective-permute-start | bytes 98312 | tf_op jit(solution)/shard_map/ppermute | solution.py:525
  72.8 4.8 %collective-permute-start.8 = (f32[2,1,4096]{2,1,0:T(1,128)S(1)}, f32[2,1,4096]{2,1,0:T(1,128)S(1)}, u32[]{:S(2)}, u32[]{:S(2)}) collective-permute-start(f32[2,1,4096]{2,1,0:T(1,128)S(1)} %get-tuple-element.55.refs_0_), channel_id=1, source_target_pairs={{0,8},{4,12},{8,0},{12,4},{1,9},{5,13},{9,1},{13,5},{2,10},{6,14},... | collective-permute-start | bytes 98312 | tf_op jit(solution)/shard_map/ppermute | solution.py:525
  74.6 3.9 %collective-permute-start.7 = (f32[2,1,4096]{2,1,0:T(1,128)S(1)}, f32[2,1,4096]{2,1,0:T(1,128)S(1)}, u32[]{:S(2)}, u32[]{:S(2)}) collective-permute-start(f32[2,1,4096]{2,1,0:T(1,128)S(1)} %get-tuple-element.55.refs_0_), channel_id=1, source_target_pairs={{0,4},{4,0},{8,12},{12,8},{1,5},{5,1},{9,13},{13,9},{2,6},{6,2},{1... | collective-permute-start | bytes 98312 | tf_op jit(solution)/shard_map/ppermute | solution.py:525

commit v8 on v7

--- a/solution.py
+++ b/solution.py
@@ -442,22 +442,20 @@
     )(keep_vmem(raw), *map(keep_vmem, totals), *map(keep_vmem, units))
 
 
-def place_kernel(blocks, size, scalar_ref, label_ref, _, *refs):
-    keys, values, refs = refs[:blocks], refs[blocks : 2 * blocks], refs[2 * blocks :]
-    *out_hbm, rows_ref, near_ref, mixed_ref, done_ref, sems = refs
+def fill_windows(ids, size, scalar_ref, label_ref, keys, values, rows_ref, near_ref):
     heads, tokens, width = keys[0].shape
     digit_rows = tokens // LANES
     sent = values[0].shape[1] - 2 * digit_rows
-    rows_ref[:, :, width:] = jnp.zeros((heads, blocks * size, width), BF16)
+    rows_ref[:, :, width:] = jnp.zeros((heads, len(ids) * size, width), BF16)
     for h in range(heads):
         low, high, first = (scalar_ref[i, h, 0].astype(F32) for i in range(2, 5))
-        for m in range(blocks):
+        for i, m in enumerate(ids):
             start = pl.multiple_of(scalar_ref[0, h, m], 16)
             gap = pl.multiple_of(scalar_ref[1, h, m], 16)
-            here = m * size
-            rows_ref[h, here : here + size, :width] = keys[m][h, pl.ds(start, size), :]
-            rows_ref[h, pl.ds(here + gap, sent), width:] = values[m][h, :sent, :]
-            digits = values[m][h, sent:, :].astype(F32)
+            here = i * size
+            rows_ref[h, here : here + size, :width] = keys[i][h, pl.ds(start, size), :]
+            rows_ref[h, pl.ds(here + gap, sent), width:] = values[i][h, :sent, :]
+            digits = values[i][h, sent:, :].astype(F32)
             rank = digits[:digit_rows] * 128.0 + digits[digit_rows:]
             rank = jnp.concatenate([rank[r : r + 1] for r in range(digit_rows)], axis=1)
             label = label_ref[h, m : m + 1, :]
@@ -466,12 +464,43 @@
             spot = pltpu.roll(spot, lax.rem(tokens - start, tokens), 1)
             near_ref[h, :, here : here + size] = spot[:, :size]
 
+
+def collect_kernel(ids, size, scalar_ref, label_ref, *refs):
+    count = len(ids)
+    keys, values, (rows_ref, near_ref) = refs[:count], refs[count : 2 * count], refs[2 * count :]
+    fill_windows(ids, size, scalar_ref, label_ref, keys, values, rows_ref, near_ref)
+
+
+def collect(scalars, labels, keys, values, ids, size):
+    heads, _, width = keys[0].shape
+    moved = [x[m] for x in (keys, values) for m in ids]
+    return pl.pallas_call(
+        functools.partial(collect_kernel, ids, size),
+        in_specs=[pl.BlockSpec(memory_space=pltpu.SMEM)] + [in_vmem()] * (1 + len(moved)),
+        out_specs=(in_vmem(), in_vmem()),
+        out_shape=(
+            pltpu.VMEM((heads, len(ids) * size, 2 * width), BF16),
+            pltpu.VMEM((heads, 1, len(ids) * size), jnp.int32),
+        ),
+        compiler_params=params(),
+        name="collect",
+    )(scalars, labels, *map(keep_vmem, moved))
+
+
+def place_kernel(ids, size, scalar_ref, label_ref, most_ref, most_near_ref, _, *refs):
+    count = len(ids)
+    keys, values, refs = refs[:count], refs[count : 2 * count], refs[2 * count :]
+    *out_hbm, rows_ref, near_ref, mixed_ref, done_ref, sems = refs
+    fill_windows(ids, size, scalar_ref, label_ref, keys, values, rows_ref, near_ref)
+    heads, _, width = keys[0].shape
     rows = mixed_ref.shape[1] // heads
     copies = []
     for step in range(out_hbm[0].shape[0] // (rows * heads)):
         for h in range(heads):
+            pick = one_hot_rows(rows, most_near_ref[h] - step * rows)
+            total = dot_nn(pick, most_ref[h])
             pick = one_hot_rows(rows, near_ref[h] - step * rows)
-            total = dot_nn(pick, rows_ref[h])
+            total += dot_nn(pick, rows_ref[h])
             for side in range(2):
                 mixed_ref[side, pl.Slice(h, rows, heads), :] = total[
                     :, side * width : (side + 1) * width
@@ -489,27 +518,29 @@
         copy.wait()
 
 
-def place(scalars, labels, keys, values, size, cap, after):
-    blocks = len(keys)
+def place(scalars, labels, most, keys, values, ids, size, cap, after):
     heads, _, width = keys[0].shape
     rows = 512
     out = jax.ShapeDtypeStruct((heads * cap, width), BF16)
-    return pl.pallas_call(
-        functools.partial(place_kernel, blocks, size),
-        in_specs=[pl.BlockSpec(memory_space=pltpu.SMEM), in_vmem(), anywhere()]
-        + [in_vmem()] * (2 * blocks),
+    moved = [x[m] for x in (keys, values) for m in ids]
+    return pl.pallas_call(
+        functools.partial(place_kernel, ids, size),
+        in_specs=[pl.BlockSpec(memory_space=pltpu.SMEM)]
+        + [in_vmem()] * 3
+        + [anywhere()]
+        + [in_vmem()] * len(moved),
         out_specs=(anywhere(), anywhere()),
         out_shape=(out, out),
         scratch_shapes=[
-            pltpu.VMEM((heads, blocks * size, 2 * width), BF16),
-            pltpu.VMEM((heads, 1, blocks * size), jnp.int32),
+            pltpu.VMEM((heads, len(ids) * size, 2 * width), BF16),
+            pltpu.VMEM((heads, 1, len(ids) * size), jnp.int32),
             pltpu.VMEM((2, heads * rows, width), F32),
             pltpu.VMEM((2, heads * cap, width), BF16),
             pltpu.SemaphoreType.DMA((2 * cap // rows,)),
         ],
         compiler_params=params(),
         name="place",
-    )(scalars, labels, keep_hbm(after), *(keep_vmem(x) for x in (*keys, *values)))
+    )(scalars, labels, *map(keep_vmem, most), keep_hbm(after), *map(keep_vmem, moved))
 
 
 def body(key_rows, value_rows, cluster_labels, owner_bounds, init_centroids):
@@ -569,25 +600,33 @@
     scalars = jnp.stack([key_starts, gaps, low * one, high * one, first * one])
 
     starts = aligned(own_below, send_size)
-    own_windows = windows(starts, ranks, own_values, send_size, own_labels)
-    middle = [2]
-    far = [d for d in range(1, n) if d & (d - 1)]
-    near = [1] + [d for d in range(3, n) if not d & (d - 1)]
-    values = {0: own_windows[0]}
+    near, middle = [1], [2]
+    far = [d for d in range(1, n) if d not in near + middle]
+
+    def cut(group, after):
+        some = jnp.stack([starts[:, d] for d in group], axis=1)
+        return windows(some, ranks, own_values, send_size, after)
+
+    values = {}
     for m in range(1, n):
-        group = {1: far, 2: near, 3: middle}.get(m)
-        if group:
-            *leaving, sums = lax.optimization_barrier((*(own_windows[d] for d in group), sums))
-            for d, window in zip(group, leaving):
-                values[d] = swap(window, d)
         sums, unit = first_block(me_array, keys[m], totals[m], cents, n, sums)
         units.append(unit)
+        group = {1: far, 2: [0, *middle]}.get(m)
+        if group:
+            *leaving, sums = lax.optimization_barrier((*cut(group, unit), sums))
+            for d, window in zip(group, leaving):
+                values[d] = swap(window, d) if d else window
 
     raw, part = raw_weights(sums, units)
+    scalars, part = lax.optimization_barrier((scalars, part))
     parts = spread(part)
+    most = [*collect(scalars, labels, keys, values, [0, *far, *middle], key_size)]
+    own_values, *parts = lax.optimization_barrier((own_values, *parts))
+    for d, window in zip(near, cut(near, most[1])):
+        values[d] = swap(window, d)
+    most[0], *parts = lax.optimization_barrier((most[0], *parts))
     out = weighted_sums(raw, units, parts)
-    values = [values[m] for m in range(n)]
-    placed = place(scalars, labels, keys, values, key_size, cap, out)
+    placed = place(scalars, labels, most, keys, values, near, key_size, cap, out)
     shape = (cap, heads, width)
     return out, placed[0].reshape(shape), placed[1].reshape(shape)
 

time: 93 us -> 87.6 us (0.942)
  starting transfers between devices: 30.1 us -> 22.5 us
  Pallas kernels: 49 us -> 51.4 us
    ppermute x12, starting transfers between devices: 30 us -> 22.5 us  [swap(): return lax.ppermute(x, 'ctx', [(i, i ^ d) for i in range(n)])]
    pallas_call x1 -> x2, Pallas kernels: 7.95 us -> 9.26 us  [the longest x1 8.09 us: place(): pl.pallas_call(functools.partial(place_kernel, ids, size), in_specs=[pl.B...]
    pallas_call x1 -> x3, Pallas kernels: 0.63 us -> 1.74 us  [windows(): pl.pallas_call(functools.partial(windows_kernel, size), in_specs=[pl.Bloc...]
  transfers between devices with their start and end apart: 13 -> 13, of which waited for: 7 -> 6; matrix products, arithmetic and copies ran while one was open for 4% -> 3% of each run, Pallas kernels for 39% -> 44%
where the time goes in v8:
time: 87.6 us; the launch traced here: 87.3 us
  Pallas kernels  51.4 us (59%)
  starting transfers between devices  22.5 us (26%)
  waiting for transfers between devices  9.71 us (11%)
  local copies, waits for them, and re-layouts  1.99 us (2%)
  between operations  1.03 us (1%)
    ppermute x12, starting transfers between devices, swap(): return lax.ppermute(x, 'ctx', [(i, i ^ d) for i in range(n)])  22.5 us
    pallas_call x4, Pallas kernels, first_block(): pl.pallas_call(functools.partial(first_kernel, fresh), grid_spec=pltpu.Pr...  13 us
    ppermute x12, waiting for transfers between devices, swap(): return lax.ppermute(x, 'ctx', [(i, i ^ d) for i in range(n)])  9.71 us
    pallas_call x1, Pallas kernels, place(): pl.pallas_call(functools.partial(place_kernel, ids, size), in_specs=[pl.B...  8.09 us
    pallas_call x1, Pallas kernels, own_totals(): pl.pallas_call(totals_kernel, grid=(heads, count // rows), in_specs=[in_v...  7.55 us
    pallas_call x1, Pallas kernels, weighted_sums(): pl.pallas_call(functools.partial(sums_kernel, len(units)), in_specs=[in_v...  6.06 us
    pallas_call x1, Pallas kernels, raw_weights(): pl.pallas_call(functools.partial(raw_kernel, len(units)), grid=(heads,),...  5.22 us
    pallas_call x1, Pallas kernels, sort_keys(): pl.pallas_call(sort_kernel, grid=(heads,), in_specs=[anywhere()] * 2, out...  4.45 us
  transfers between devices with their start and end apart: 13, of which 6 were waited for; matrix products, arithmetic and copies ran while one was open for 3% of the time, Pallas kernels for 44%

profile of v8, /device:TPU:0, one launch (start us, length us, event | category | flops | bytes accessed | tf_op | source)
XLA Modules:
  0.0 87.3 jit_solution(7976467207188170442)
XLA Ops:
  0.6 0.0 copy-start
  0.6 4.5 %sort_keys.1 = (bf16[2,1024,128]{2,1,0:T(8,128)(2,1)S(1)}, f32[2,1,1024]{2,1,0:T(1,128)S(1)}, s32[2,1,1024]{2,1,0:T(1,128)S(1)}) custom-call(s32[2,1024]{1,0:T(2,128)} %label_hbm.1, bf16[2048,128]{1,0:T(8,128)(2,1)} %bitcast.26), custom_call_target="tpu_custom_call" | custom-call | tf_op jit(solution)/shard_map/sort_keys/pallas_call | solution.py:139
  5.1 4.1 %collective-permute-start.1 = (bf16[2,1024,128]{2,1,0:T(8,128)(2,1)S(1)}, bf16[2,1024,128]{2,1,0:T(8,128)(2,1)S(1)}, u32[]{:S(2)}, u32[]{:S(2)}) collective-permute-start(bf16[2,1024,128]{2,1,0:T(8,128)(2,1)S(1)} %get-tuple-element.66.keys_ref.refs_0_), channel_id=1, source_target_pairs={{0,8},{4,12},{8,0},{12,4},{1,9},{5,13},{9,1},{13,5},{2,10},{6,14},... | collective-permute-start | bytes 1572872 | tf_op jit(solution)/shard_map/ppermute | solution.py:556
  9.2 1.6 %collective-permute-start = (bf16[2,1024,128]{2,1,0:T(8,128)(2,1)S(1)}, bf16[2,1024,128]{2,1,0:T(8,128)(2,1)S(1)}, u32[]{:S(2)}, u32[]{:S(2)}) collective-permute-start(bf16[2,1024,128]{2,1,0:T(8,128)(2,1)S(1)} %get-tuple-element.66.keys_ref.refs_0_), channel_id=1, source_target_pairs={{0,4},{4,0},{8,12},{12,8},{1,5},{5,1},{9,13},{13,9},{2,6},{6,2},{1... | collective-permute-start | bytes 1572872 | tf_op jit(solution)/shard_map/ppermute | solution.py:556
  10.8 0.0 collective-permute-start.2
  10.8 0.8 copy.13
  11.6 0.6 gather_fusion
  12.2 0.1 convert_bitcast_fusion
  12.2 0.1 copy.14
  12.3 0.2 convert_reduce_fusion.2
  12.6 0.1 fusion.5
  12.6 0.0 collective-permute-done.2._
  12.6 7.5 %own_totals.1.tot_ref = f32[2,1,1024]{2,1,0:T(1,128)S(1)} custom-call(bf16[2,1024,128]{2,1,0:T(8,128)(2,1)S(1)} %get-tuple-element.66.keys_ref.refs_0_, f32[2,4096,128]{2,1,0:T(8,128)} %cent_in.1, f32[2,1,128]{2,1,0:T(1,128)S(1)} %collective-permute-done.2._), custom_call_target="tpu_custom_call" | custom-call | tf_op jit(solution)/shard_map/own_totals/pallas_call | solution.py:285
  20.2 0.4 collective-permute-start.6
  20.6 0.1 pad_add_fusion.start_ref
  20.7 0.0 copy-done
  20.7 0.2 dynamic-slice_reduce_fusion
  20.9 2.4 %sort_values.1.values_ref = bf16[2,1024,128]{2,1,0:T(8,128)(2,1)S(1)} custom-call(s32[2,1,1024]{2,1,0:T(1,128)S(1)} %get-tuple-element.49.spot_ref, bf16[2048,128]{1,0:T(8,128)(2,1)} %bitcast.27), custom_call_target="tpu_custom_call" | custom-call | tf_op jit(solution)/shard_map/sort_values/pallas_call | solution.py:179
  23.3 0.3 collective-permute-start.5
  23.6 3.9 %collective-permute-start.4 = (f32[2,2,1024]{2,1,0:T(2,128)S(1)}, f32[2,2,1024]{2,1,0:T(2,128)S(1)}, u32[]{:S(2)}, u32[]{:S(2)}) collective-permute-start(f32[2,2,1024]{2,1,0:T(2,128)S(1)} %pad_maximum_fusion.1), channel_id=1, source_target_pairs={{0,12},{4,8},{8,4},{12,0},{1,13},{5,9},{9,5},{13,1},{2,14},{6,10},... | collective-permute-start | bytes 49160 | tf_op jit(solution)/shard_map/ppermute | solution.py:556
  27.4 4.1 %first_block.4 = (f32[2,1024,128]{2,1,0:T(8,128)S(1)}, bf16[2,1024,128]{2,1,0:T(8,128)(2,1)S(1)}, bf16[2,1024,128]{2,1,0:T(8,128)(2,1)S(1)}) custom-call(s32[1]{0:T(128)} %bitcast._.me_ref, bf16[2,1024,128]{2,1,0:T(8,128)(2,1)S(1)} %get-tuple-element.66.keys_ref.refs_0_, f32[2,1,1024]{2,1,0:T(1,128)S(1)} %own_totals.1.tot_ref, f32[2,4096,128]{2,1,0:T(8,128)} %cent_in.1), custom_call_target="tpu_custom_call" | custom-call | tf_op jit(solution)/shard_map/first_block/pallas_call | solution.py:355
  31.5 1.7 %collective-permute-done.6 = f32[2,2,1024]{2,1,0:T(2,128)S(1)} collective-permute-done((f32[2,2,1024]{2,1,0:T(2,128)S(1)}, f32[2,2,1024]{2,1,0:T(2,128)S(1)}, u32[]{:S(2)}, u32[]{:S(2)}) %collective-permute-start.6) | collective-permute-done | bytes 16416 | tf_op jit(solution)/shard_map/ppermute | solution.py:556
  33.2 0.3 collective-permute-done.5
  33.6 1.0 %collective-permute-done.4 = f32[2,2,1024]{2,1,0:T(2,128)S(1)} collective-permute-done((f32[2,2,1024]{2,1,0:T(2,128)S(1)}, f32[2,2,1024]{2,1,0:T(2,128)S(1)}, u32[]{:S(2)}, u32[]{:S(2)}) %collective-permute-start.4) | collective-permute-done | bytes 16416 | tf_op jit(solution)/shard_map/ppermute | solution.py:556
  34.5 0.1 broadcast_compare_fusion
  34.6 0.2 convert_reduce_fusion
  34.8 0.0 collective-permute-done.1.keys_ref.refs_2_
  34.8 0.0 collective-permute-done.keys_ref.refs_0_
  34.8 0.6 collective-permute-start.3
  35.4 0.1 constant_dynamic-update-slice_fusion.2
  35.5 1.7 %own_ranks.1.rank_ref = f32[2,1,1024]{2,1,0:T(1,128)S(1)} custom-call(s32[1]{0:T(128)} %bitcast._.me_ref, f32[2,4,1024]{2,1,0:T(4,128)S(1)} %get-tuple-element.90.label_ref), custom_call_target="tpu_custom_call" | custom-call | tf_op jit(solution)/shard_map/own_ranks/pallas_call | solution.py:245
  37.3 3.0 %first_block.5 = (f32[2,1024,128]{2,1,0:T(8,128)S(1)}, bf16[2,1024,128]{2,1,0:T(8,128)(2,1)S(1)}) custom-call(s32[1]{0:T(128)} %bitcast._.me_ref, bf16[2,1024,128]{2,1,0:T(8,128)(2,1)S(1)} %collective-permute-done.keys_ref.refs_0_, f32[2,1,1024]{2,1,0:T(1,128)S(1)} %get-tuple-element.91.tot_ref, ...), custom_call_target="tpu_custom_call", output_to_operand_aliasing={{0}: (4, {})} | custom-call | tf_op jit(solution)/shard_map/first_block/pallas_call | solution.py:355
  40.3 0.6 windows.3
  40.8 2.9 %collective-permute-start.7 = (bf16[2,544,128]{2,1,0:T(8,128)(2,1)S(1)}, bf16[2,544,128]{2,1,0:T(8,128)(2,1)S(1)}, u32[]{:S(2)}, u32[]{:S(2)}) collective-permute-start(bf16[2,544,128]{2,1,0:T(8,128)(2,1)S(1)} %windows.3), channel_id=1, source_target_pairs={{0,12},{4,8},{8,4},{12,0},{1,13},{5,9},{9,5},{13,1},{2,14},{6,10},... | collective-permute-start | bytes 835592 | tf_op jit(solution)/shard_map/ppermute | solution.py:556
  43.8 3.0 %first_block.6 = (f32[2,1024,128]{2,1,0:T(8,128)S(1)}, bf16[2,1024,128]{2,1,0:T(8,128)(2,1)S(1)}) custom-call(s32[1]{0:T(128)} %bitcast._.me_ref, bf16[2,1024,128]{2,1,0:T(8,128)(2,1)S(1)} %collective-permute-done.1.keys_ref.refs_2_, f32[2,1,1024]{2,1,0:T(1,128)S(1)} %get-tuple-element.93.tot_ref, ...), custom_call_target="tpu_custom_call", output_to_operand_aliasing={{0}: (4, {})} | custom-call | tf_op jit(solution)/shard_map/first_block/pallas_call | solution.py:355
  46.7 0.6 windows.4
  47.3 0.2 collective-permute-start.8
  47.5 0.1 constant_dynamic-update-slice_fusion.1
  47.6 0.1 constant_dynamic-update-slice_fusion.scalar_ref
  47.6 0.2 collective-permute-done.3.keys_ref.refs_1_
  47.8 3.0 %first_block.7 = (f32[2,1024,128]{2,1,0:T(8,128)S(1)}, bf16[2,1024,128]{2,1,0:T(8,128)(2,1)S(1)}) custom-call(s32[1]{0:T(128)} %bitcast._.me_ref, bf16[2,1024,128]{2,1,0:T(8,128)(2,1)S(1)} %collective-permute-done.3.keys_ref.refs_1_, f32[2,1,1024]{2,1,0:T(1,128)S(1)} %get-tuple-element.96.tot_ref, ...), custom_call_target="tpu_custom_call", output_to_operand_aliasing={{0}: (4, {})} | custom-call | tf_op jit(solution)/shard_map/first_block/pallas_call | solution.py:355
  50.8 5.2 %raw_weights.1 = (bf16[2,1024,4096]{2,1,0:T(8,128)(2,1)S(1)}, f32[2,1,4096]{2,1,0:T(1,128)S(1)}) custom-call(f32[2,1024,128]{2,1,0:T(8,128)S(1)} %get-tuple-element.60.sums_ref, bf16[2,1024,128]{2,1,0:T(8,128)(2,1)S(1)} %get-tuple-element.61.refs_0_.refs_4_, bf16[2,1024,128]{2,1,0:T(8,128)(2,1)S(1)} %get-tuple-element.52._.refs_1_.refs_5_, ...), custom_call_target="tpu_custom_call" | custom-call | tf_op jit(solution)/shard_map/raw_weights/pallas_call | solution.py:392
  56.0 7.9 %collective-permute-start.11 = (f32[2,1,4096]{2,1,0:T(1,128)S(1)}, f32[2,1,4096]{2,1,0:T(1,128)S(1)}, u32[]{:S(2)}, u32[]{:S(2)}) collective-permute-start(f32[2,1,4096]{2,1,0:T(1,128)S(1)} %get-tuple-element.76.refs_0_), channel_id=1, source_target_pairs={{0,12},{4,8},{8,4},{12,0},{1,13},{5,9},{9,5},{13,1},{2,14},{6,10},... | collective-permute-start | bytes 98312 | tf_op jit(solution)/shard_map/ppermute | solution.py:556
  63.9 0.0 collective-permute-start.10
  63.9 0.6 collective-permute-start.9
  64.6 0.0 collective-permute-done.7.refs_4_
  64.6 5.0 %collective-permute-done.8.refs_5_ = bf16[2,544,128]{2,1,0:T(8,128)(2,1)S(1)} collective-permute-done((bf16[2,544,128]{2,1,0:T(8,128)(2,1)S(1)}, bf16[2,544,128]{2,1,0:T(8,128)(2,1)S(1)}, u32[]{:S(2)}, u32[]{:S(2)}) %collective-permute-start.8) | collective-permute-done | bytes 278560 | tf_op jit(solution)/shard_map/ppermute | solution.py:556
  69.6 1.2 %collect.1 = (bf16[2,1920,256]{2,1,0:T(8,128)(2,1)S(1)}, s32[2,1,1920]{2,1,0:T(1,128)S(1)}) custom-call(s32[5,2,4]{2,1,0:T(2,128)S(1)} %constant_dynamic-update-slice_fusion.scalar_ref, f32[2,4,1024]{2,1,0:T(4,128)S(1)} %get-tuple-element.90.label_ref, bf16[2,1024,128]{2,1,0:T(8,128)(2,1)S(1)} %get-tuple-element.66.keys_ref.refs_0_, ...), custom_call_target="tpu_custom_call" | custom-call | tf_op jit(solution)/shard_map/collect/pallas_call | solution.py:477
  70.8 0.0 collective-permute-done.11.refs_3_
  70.8 0.0 collective-permute-done.10.refs_2_
  70.8 0.0 collective-permute-done.9.refs_1_
  70.8 0.6 windows.5
  71.4 0.1 collective-permute-start.12
  71.5 6.1 %weighted_sums.1._ = f32[2,1024,128]{2,1,0:T(8,128)} custom-call(bf16[2,1024,4096]{2,1,0:T(8,128)(2,1)S(1)} %get-tuple-element.63.raw_ref, f32[2,1,4096]{2,1,0:T(1,128)S(1)} %get-tuple-element.76.refs_0_, f32[2,1,4096]{2,1,0:T(1,128)S(1)} %collective-permute-done.9.refs_1_, f32[2,1,4096]{2,1,0:T(1,128)S(1)} %collective-permute-done.10.refs_2_, ...), custom_call_target="tpu_custom_call" | custom-call | tf_op jit(solution)/shard_map/weighted_sums/pallas_call | solution.py:430
  77.5 1.5 %collective-permute-done.12.refs_1_ = bf16[2,544,128]{2,1,0:T(8,128)(2,1)S(1)} collective-permute-done((bf16[2,544,128]{2,1,0:T(8,128)(2,1)S(1)}, bf16[2,544,128]{2,1,0:T(8,128)(2,1)S(1)}, u32[]{:S(2)}, u32[]{:S(2)}) %collective-permute-start.12) | collective-permute-done | bytes 278560 | tf_op jit(solution)/shard_map/ppermute | solution.py:556
  79.1 8.1 %place.1 = (bf16[4096,128]{1,0:T(8,128)(2,1)}, bf16[4096,128]{1,0:T(8,128)(2,1)}) custom-call(s32[5,2,4]{2,1,0:T(2,128)S(1)} %constant_dynamic-update-slice_fusion.scalar_ref, f32[2,4,1024]{2,1,0:T(4,128)S(1)} %get-tuple-element.90.label_ref, bf16[2,1920,256]{2,1,0:T(8,128)(2,1)S(1)} %get-tuple-element.80.most_ref, ...), custom_call_target="tpu_custom_call" | custom-call | tf_op jit(solution)/shard_map/place/pallas_call | solution.py:526
  (13 shorter events, 0.1 us)
Async XLA Ops:
  0.6 20.1 %copy-start = (s32[2,5]{1,0:T(2,128)S(1)}, s32[2,5]{1,0:T(2,128)}, u32[]{:S(2)}) copy-start(s32[2,5]{1,0:T(2,128)} %param.8) | copy-start | bytes 124
  5.1 29.7 %collective-permute-start.1 = (bf16[2,1024,128]{2,1,0:T(8,128)(2,1)S(1)}, bf16[2,1024,128]{2,1,0:T(8,128)(2,1)S(1)}, u32[]{:S(2)}, u32[]{:S(2)}) collective-permute-start(bf16[2,1024,128]{2,1,0:T(8,128)(2,1)S(1)} %get-tuple-element.66.keys_ref.refs_0_), channel_id=1, source_target_pairs={{0,8},{4,12},{8,0},{12,4},{1,9},{5,13},{9,1},{13,5},{2,10},{6,14},... | collective-permute-start | bytes 1572872 | tf_op jit(solution)/shard_map/ppermute | solution.py:556
  9.2 25.6 %collective-permute-start = (bf16[2,1024,128]{2,1,0:T(8,128)(2,1)S(1)}, bf16[2,1024,128]{2,1,0:T(8,128)(2,1)S(1)}, u32[]{:S(2)}, u32[]{:S(2)}) collective-permute-start(bf16[2,1024,128]{2,1,0:T(8,128)(2,1)S(1)} %get-tuple-element.66.keys_ref.refs_0_), channel_id=1, source_target_pairs={{0,4},{4,0},{8,12},{12,8},{1,5},{5,1},{9,13},{13,9},{2,6},{6,2},{1... | collective-permute-start | bytes 1572872 | tf_op jit(solution)/shard_map/ppermute | solution.py:556
  10.8 1.9 %collective-permute-start.2 = (f32[2,1,128]{2,1,0:T(1,128)S(1)}, f32[2,1,128]{2,1,0:T(1,128)S(1)}, u32[]{:S(2)}, u32[]{:S(2)}) collective-permute-start(f32[2,1,128]{2,1,0:T(1,128)S(1)} %slice.33), channel_id=1, source_target_pairs={{0,1},{1,0},{2,3},{3,2},{4,5},{5,4},{6,7},{7,6},{8,9},{9,8},{10,11... | collective-permute-start | bytes 3080 | tf_op jit(solution)/shard_map/ppermute | solution.py:574
  20.2 13.0 %collective-permute-start.6 = (f32[2,2,1024]{2,1,0:T(2,128)S(1)}, f32[2,2,1024]{2,1,0:T(2,128)S(1)}, u32[]{:S(2)}, u32[]{:S(2)}) collective-permute-start(f32[2,2,1024]{2,1,0:T(2,128)S(1)} %pad_maximum_fusion.1), channel_id=1, source_target_pairs={{0,8},{4,12},{8,0},{12,4},{1,9},{5,13},{9,1},{13,5},{2,10},{6,14},... | collective-permute-start | bytes 49160 | tf_op jit(solution)/shard_map/ppermute | solution.py:556
  23.3 10.2 %collective-permute-start.5 = (f32[2,2,1024]{2,1,0:T(2,128)S(1)}, f32[2,2,1024]{2,1,0:T(2,128)S(1)}, u32[]{:S(2)}, u32[]{:S(2)}) collective-permute-start(f32[2,2,1024]{2,1,0:T(2,128)S(1)} %pad_maximum_fusion.1), channel_id=1, source_target_pairs={{0,4},{4,0},{8,12},{12,8},{1,5},{5,1},{9,13},{13,9},{2,6},{6,2},{1... | collective-permute-start | bytes 49160 | tf_op jit(solution)/shard_map/ppermute | solution.py:556
  23.6 11.0 %collective-permute-start.4 = (f32[2,2,1024]{2,1,0:T(2,128)S(1)}, f32[2,2,1024]{2,1,0:T(2,128)S(1)}, u32[]{:S(2)}, u32[]{:S(2)}) collective-permute-start(f32[2,2,1024]{2,1,0:T(2,128)S(1)} %pad_maximum_fusion.1), channel_id=1, source_target_pairs={{0,12},{4,8},{8,4},{12,0},{1,13},{5,9},{9,5},{13,1},{2,14},{6,10},... | collective-permute-start | bytes 49160 | tf_op jit(solution)/shard_map/ppermute | solution.py:556
  34.8 13.0 %collective-permute-start.3 = (bf16[2,1024,128]{2,1,0:T(8,128)(2,1)S(1)}, bf16[2,1024,128]{2,1,0:T(8,128)(2,1)S(1)}, u32[]{:S(2)}, u32[]{:S(2)}) collective-permute-start(bf16[2,1024,128]{2,1,0:T(8,128)(2,1)S(1)} %collective-permute-done.1.keys_ref.refs_2_), channel_id=1, source_target_pairs={{0,4},{4,0},{8,12},{12,8},{1,5},{5,1},{9,13},{13,9},{2,6},{6,2},{1... | collective-permute-start | bytes 1572872 | tf_op jit(solution)/shard_map/ppermute | solution.py:556
  40.8 23.7 %collective-permute-start.7 = (bf16[2,544,128]{2,1,0:T(8,128)(2,1)S(1)}, bf16[2,544,128]{2,1,0:T(8,128)(2,1)S(1)}, u32[]{:S(2)}, u32[]{:S(2)}) collective-permute-start(bf16[2,544,128]{2,1,0:T(8,128)(2,1)S(1)} %windows.3), channel_id=1, source_target_pairs={{0,12},{4,8},{8,4},{12,0},{1,13},{5,9},{9,5},{13,1},{2,14},{6,10},... | collective-permute-start | bytes 835592 | tf_op jit(solution)/shard_map/ppermute | solution.py:556
  47.3 22.3 %collective-permute-start.8 = (bf16[2,544,128]{2,1,0:T(8,128)(2,1)S(1)}, bf16[2,544,128]{2,1,0:T(8,128)(2,1)S(1)}, u32[]{:S(2)}, u32[]{:S(2)}) collective-permute-start(bf16[2,544,128]{2,1,0:T(8,128)(2,1)S(1)} %get-tuple-element.69), channel_id=1, source_target_pairs={{0,8},{4,12},{8,0},{12,4},{1,9},{5,13},{9,1},{13,5},{2,10},{6,14},... | collective-permute-start | bytes 835592 | tf_op jit(solution)/shard_map/ppermute | solution.py:556
  56.0 14.7 %collective-permute-start.11 = (f32[2,1,4096]{2,1,0:T(1,128)S(1)}, f32[2,1,4096]{2,1,0:T(1,128)S(1)}, u32[]{:S(2)}, u32[]{:S(2)}) collective-permute-start(f32[2,1,4096]{2,1,0:T(1,128)S(1)} %get-tuple-element.76.refs_0_), channel_id=1, source_target_pairs={{0,12},{4,8},{8,4},{12,0},{1,13},{5,9},{9,5},{13,1},{2,14},{6,10},... | collective-permute-start | bytes 98312 | tf_op jit(solution)/shard_map/ppermute | solution.py:556
  63.9 6.8 %collective-permute-start.10 = (f32[2,1,4096]{2,1,0:T(1,128)S(1)}, f32[2,1,4096]{2,1,0:T(1,128)S(1)}, u32[]{:S(2)}, u32[]{:S(2)}) collective-permute-start(f32[2,1,4096]{2,1,0:T(1,128)S(1)} %get-tuple-element.76.refs_0_), channel_id=1, source_target_pairs={{0,8},{4,12},{8,0},{12,4},{1,9},{5,13},{9,1},{13,5},{2,10},{6,14},... | collective-permute-start | bytes 98312 | tf_op jit(solution)/shard_map/ppermute | solution.py:556
  63.9 6.9 %collective-permute-start.9 = (f32[2,1,4096]{2,1,0:T(1,128)S(1)}, f32[2,1,4096]{2,1,0:T(1,128)S(1)}, u32[]{:S(2)}, u32[]{:S(2)}) collective-permute-start(f32[2,1,4096]{2,1,0:T(1,128)S(1)} %get-tuple-element.76.refs_0_), channel_id=1, source_target_pairs={{0,4},{4,0},{8,12},{12,8},{1,5},{5,1},{9,13},{13,9},{2,6},{6,2},{1... | collective-permute-start | bytes 98312 | tf_op jit(solution)/shard_map/ppermute | solution.py:556
  71.4 7.7 %collective-permute-start.12 = (bf16[2,544,128]{2,1,0:T(8,128)(2,1)S(1)}, bf16[2,544,128]{2,1,0:T(8,128)(2,1)S(1)}, u32[]{:S(2)}, u32[]{:S(2)}) collective-permute-start(bf16[2,544,128]{2,1,0:T(8,128)(2,1)S(1)} %windows.5), channel_id=1, source_target_pairs={{0,4},{4,0},{8,12},{12,8},{1,5},{5,1},{9,13},{13,9},{2,6},{6,2},{1... | collective-permute-start | bytes 835592 | tf_op jit(solution)/shard_map/ppermute | solution.py:556

commit v9 on v7

--- a/solution.py
+++ b/solution.py
@@ -81,7 +81,9 @@
                 total += (other < mine).astype(jnp.int32)
         return total
 
-    total = lax.fori_loop(0, count // wide, step, jnp.zeros((8, tokens), jnp.int32))
+    total = lax.fori_loop(
+        0, count // wide, step, jnp.zeros((8, tokens), jnp.int32), unroll=True
+    )
     return jnp.sum(total, axis=0, keepdims=True)
 
 
@@ -93,44 +95,38 @@
 
 
 def sort_kernel(label_hbm, keys_hbm, *refs):
-    out_keys, out_labels, out_spots, flat_ref, wide_ref, rows_ref, order_ref, label_ref, sems = refs
-    head = pl.program_id(0)
-    _, tokens, width = out_keys.shape
+    out_keys, out_labels, out_spots, flat_ref, wide_ref, order_ref, label_ref, sems = refs
+    heads, tokens, _ = out_keys.shape
+    label_copy = pltpu.make_async_copy(label_hbm, label_ref, sems.at[1])
+    label_copy.start()
     copy = pltpu.make_async_copy(keys_hbm, flat_ref, sems.at[0])
-
-    @pl.when(head == 0)
-    def _():
-        label_copy = pltpu.make_async_copy(label_hbm, label_ref, sems.at[1])
-        label_copy.start()
-        copy.start()
-        label_copy.wait()
-
-    label = label_ref[pl.ds(head, 1), :]
-    order = label * tokens + lax.broadcasted_iota(jnp.int32, label.shape, 1)
-    order_ref[0] = order
-    spot = count_below(order_ref, order, tokens)
-    out_spots[head] = spot
-
-    @pl.when(head == 0)
-    def _():
-        copy.wait()
-        split_heads(flat_ref, wide_ref)
-
-    rows_ref[...] = head_rows(wide_ref, head, wide_ref.shape[0] // tokens).astype(BF16)
-    digits = jnp.concatenate(
-        [
-            jnp.broadcast_to(label >> 6, (8, tokens)),
-            jnp.broadcast_to(label & 63, (8, tokens)),
-        ],
-        axis=0,
-    )
-    digits = digits.astype(F32).astype(BF16)
+    copy.start()
+    label_copy.wait()
+    labels = [label_ref[h : h + 1, :] for h in range(heads)]
+    spots = []
+    for h, label in enumerate(labels):
+        order = label * tokens + lax.broadcasted_iota(jnp.int32, label.shape, 1)
+        order_ref[0] = order
+        spots.append(count_below(order_ref, order, tokens))
+        out_spots[h] = spots[h]
+    copy.wait()
+    split_heads(flat_ref, wide_ref)
     rows = 512
-    for r in range(0, tokens, rows):
-        pick = one_hot_rows(rows, spot - r)
-        out_keys[head, r : r + rows] = dot_nn(pick, rows_ref[...]).astype(BF16)
-        digit = dot_nt(digits, pick)
-        out_labels[head, :, r : r + rows] = digit[0:1] * 64.0 + digit[8:9]
+    for h, label in enumerate(labels):
+        keys = head_rows(wide_ref, h, heads).astype(BF16)
+        digits = jnp.concatenate(
+            [
+                jnp.broadcast_to(label >> 6, (8, tokens)),
+                jnp.broadcast_to(label & 63, (8, tokens)),
+            ],
+            axis=0,
+        )
+        digits = digits.astype(F32).astype(BF16)
+        for r in range(0, tokens, rows):
+            pick = one_hot_rows(rows, spots[h] - r)
+            out_keys[h, r : r + rows] = dot_nn(pick, keys).astype(BF16)
+            digit = dot_nt(digits, pick)
+            out_labels[h, :, r : r + rows] = digit[0:1] * 64.0 + digit[8:9]
 
 
 def sort_keys(labels, keys):
@@ -138,7 +134,6 @@
     flat, width = keys.shape
     return pl.pallas_call(
         sort_kernel,
-        grid=(heads,),
         in_specs=[anywhere()] * 2,
         out_specs=(in_vmem(),) * 3,
         out_shape=(
@@ -149,7 +144,6 @@
         scratch_shapes=[
             pltpu.VMEM((flat, width), BF16),
             pltpu.VMEM((flat, width), F32),
-            pltpu.VMEM((tokens, width), BF16),
             pltpu.VMEM((1, 1, tokens), jnp.int32),
             pltpu.VMEM(labels.shape, jnp.int32),
             pltpu.SemaphoreType.DMA((2,)),
@@ -442,22 +436,23 @@
     )(keep_vmem(raw), *map(keep_vmem, totals), *map(keep_vmem, units))
 
 
-def place_kernel(blocks, size, scalar_ref, label_ref, _, *refs):
-    keys, values, refs = refs[:blocks], refs[blocks : 2 * blocks], refs[2 * blocks :]
-    *out_hbm, rows_ref, near_ref, mixed_ref, done_ref, sems = refs
+def fill_windows(ids, size, scalar_ref, label_ref, keys, values, rows_ref, near_ref):
     heads, tokens, width = keys[0].shape
     digit_rows = tokens // LANES
-    sent = values[0].shape[1] - 2 * digit_rows
-    rows_ref[:, :, width:] = jnp.zeros((heads, blocks * size, width), BF16)
+    sent = values[0][0].shape[1] - 2 * digit_rows
+    rows_ref[:, :, width:] = jnp.zeros((heads, len(ids) * size, width), BF16)
     for h in range(heads):
         low, high, first = (scalar_ref[i, h, 0].astype(F32) for i in range(2, 5))
-        for m in range(blocks):
+        for i, m in enumerate(ids):
             start = pl.multiple_of(scalar_ref[0, h, m], 16)
             gap = pl.multiple_of(scalar_ref[1, h, m], 16)
-            here = m * size
-            rows_ref[h, here : here + size, :width] = keys[m][h, pl.ds(start, size), :]
-            rows_ref[h, pl.ds(here + gap, sent), width:] = values[m][h, :sent, :]
-            digits = values[m][h, sent:, :].astype(F32)
+            here = i * size
+            rows_ref[h, here : here + size, :width] = keys[i][h, pl.ds(start, size), :]
+            value = values[i][0][h]
+            if len(values[i]) == 2:
+                value = jnp.where(scalar_ref[5, 0, 0] > 0, value, values[i][1][h])
+            rows_ref[h, pl.ds(here + gap, sent), width:] = value[:sent]
+            digits = value[sent:].astype(F32)
             rank = digits[:digit_rows] * 128.0 + digits[digit_rows:]
             rank = jnp.concatenate([rank[r : r + 1] for r in range(digit_rows)], axis=1)
             label = label_ref[h, m : m + 1, :]
@@ -466,17 +461,38 @@
             spot = pltpu.roll(spot, lax.rem(tokens - start, tokens), 1)
             near_ref[h, :, here : here + size] = spot[:, :size]
 
-    rows = mixed_ref.shape[1] // heads
+
+def grouped(refs, counts):
+    refs = iter(refs)
+    return [[next(refs) for _ in range(count)] for count in counts]
+
+
+def place_kernel(ids, counts, size, fresh, scalar_ref, label_ref, *refs):
+    keys, refs = refs[: len(ids)], refs[len(ids) :]
+    values, refs = grouped(refs, counts), refs[sum(counts) :]
+    if fresh:
+        so_far_ref, rows_ref, near_ref = refs
+    else:
+        so_far_ref, *out_hbm, rows_ref, near_ref, mixed_ref, done_ref, sems = refs
+    fill_windows(ids, size, scalar_ref, label_ref, keys, values, rows_ref, near_ref)
+    heads, cap, both = so_far_ref.shape
+    width = both // 2
+    rows = 512
     copies = []
-    for step in range(out_hbm[0].shape[0] // (rows * heads)):
+    for r in range(0, cap, rows):
         for h in range(heads):
-            pick = one_hot_rows(rows, near_ref[h] - step * rows)
-            total = dot_nn(pick, rows_ref[h])
+            total = dot_nn(one_hot_rows(rows, near_ref[h] - r), rows_ref[h])
+            if fresh:
+                so_far_ref[h, r : r + rows] = total.astype(BF16)
+                continue
+            total += so_far_ref[h, r : r + rows].astype(F32)
             for side in range(2):
                 mixed_ref[side, pl.Slice(h, rows, heads), :] = total[
                     :, side * width : (side + 1) * width
                 ]
-        here = slice(step * rows * heads, (step + 1) * rows * heads)
+        if fresh:
+            continue
+        here = slice(r * heads, (r + rows) * heads)
         for side in range(2):
             done_ref[side, here] = mixed_ref[side].astype(BF16)
             copies.append(
@@ -489,27 +505,36 @@
         copy.wait()
 
 
-def place(scalars, labels, keys, values, size, cap, after):
-    blocks = len(keys)
+def place(scalars, labels, keys, values, ids, size, cap, so_far):
     heads, _, width = keys[0].shape
-    rows = 512
-    out = jax.ShapeDtypeStruct((heads * cap, width), BF16)
-    return pl.pallas_call(
-        functools.partial(place_kernel, blocks, size),
-        in_specs=[pl.BlockSpec(memory_space=pltpu.SMEM), in_vmem(), anywhere()]
-        + [in_vmem()] * (2 * blocks),
-        out_specs=(anywhere(), anywhere()),
-        out_shape=(out, out),
-        scratch_shapes=[
-            pltpu.VMEM((heads, blocks * size, 2 * width), BF16),
-            pltpu.VMEM((heads, 1, blocks * size), jnp.int32),
-            pltpu.VMEM((2, heads * rows, width), F32),
+    fresh = so_far is None
+    counts = [len(values[m]) for m in ids]
+    moved = [keys[m] for m in ids] + [x for m in ids for x in values[m]]
+    scratch = [
+        pltpu.VMEM((heads, len(ids) * size, 2 * width), BF16),
+        pltpu.VMEM((heads, 1, len(ids) * size), jnp.int32),
+    ]
+    if fresh:
+        out_shape = pltpu.VMEM((heads, cap, 2 * width), BF16)
+        out_specs = in_vmem()
+    else:
+        moved.append(so_far)
+        out_shape = (jax.ShapeDtypeStruct((heads * cap, width), BF16),) * 2
+        out_specs = (anywhere(), anywhere())
+        scratch += [
+            pltpu.VMEM((2, heads * 512, width), F32),
             pltpu.VMEM((2, heads * cap, width), BF16),
-            pltpu.SemaphoreType.DMA((2 * cap // rows,)),
-        ],
+            pltpu.SemaphoreType.DMA((2 * cap // 512,)),
+        ]
+    return pl.pallas_call(
+        functools.partial(place_kernel, ids, counts, size, fresh),
+        in_specs=[pl.BlockSpec(memory_space=pltpu.SMEM)] + [in_vmem()] * (1 + len(moved)),
+        out_specs=out_specs,
+        out_shape=out_shape,
+        scratch_shapes=scratch,
         compiler_params=params(),
         name="place",
-    )(scalars, labels, keep_hbm(after), *(keep_vmem(x) for x in (*keys, *values)))
+    )(scalars, labels, *map(keep_vmem, moved))
 
 
 def body(key_rows, value_rows, cluster_labels, owner_bounds, init_centroids):
@@ -566,28 +591,49 @@
     key_starts = aligned(below, key_size)
     gaps = aligned(below, send_size) - key_starts
     one = jnp.ones((1, n), jnp.int32)
-    scalars = jnp.stack([key_starts, gaps, low * one, high * one, first * one])
+    inner = ((me & 3) == 1) | ((me & 3) == 2)
+    scalars = jnp.stack(
+        [key_starts, gaps, low * one, high * one, first * one, inner * jnp.ones_like(below)]
+    )
 
     starts = aligned(own_below, send_size)
     own_windows = windows(starts, ranks, own_values, send_size, own_labels)
-    middle = [2]
-    far = [d for d in range(1, n) if d & (d - 1)]
-    near = [1] + [d for d in range(3, n) if not d & (d - 1)]
-    values = {0: own_windows[0]}
+    values = {0: [own_windows[0]]}
+
+    def inner_swap(x, wanted):
+        pairs = [(i, i ^ 3 if (i & 3 in (1, 2)) == wanted else i) for i in range(n)]
+        return lax.ppermute(x, "ctx", pairs)
+
+    def leave(m, x):
+        if m == 1 and n > 2:
+            own_windows[3], x = lax.optimization_barrier((own_windows[3], x))
+            values[3] = [inner_swap(own_windows[3], True)]
+        if m == min(2, n - 1):
+            own_windows[1], x = lax.optimization_barrier((own_windows[1], x))
+            values[1] = [swap(own_windows[1], 1)]
+        if m == n - 1:
+            *own_windows[2:], x = lax.optimization_barrier((*own_windows[2:], x))
+            for d in range(2, n):
+                if d == 3:
+                    values[3].append(inner_swap(own_windows[3], False))
+                else:
+                    values[d] = [swap(own_windows[d], d)]
+        return x
+
+    own_windows = list(own_windows)
     for m in range(1, n):
-        group = {1: far, 2: near, 3: middle}.get(m)
-        if group:
-            *leaving, sums = lax.optimization_barrier((*(own_windows[d] for d in group), sums))
-            for d, window in zip(group, leaving):
-                values[d] = swap(window, d)
+        sums = leave(m, sums)
         sums, unit = first_block(me_array, keys[m], totals[m], cents, n, sums)
         units.append(unit)
 
     raw, part = raw_weights(sums, units)
+    values[1][0], values[3][0], scalars, part = lax.optimization_barrier(
+        (values[1][0], values[3][0], scalars, part)
+    )
     parts = spread(part)
+    so_far = place(scalars, labels, keys, values, [0, 1], key_size, cap, None)
     out = weighted_sums(raw, units, parts)
-    values = [values[m] for m in range(n)]
-    placed = place(scalars, labels, keys, values, key_size, cap, out)
+    placed = place(scalars, labels, keys, values, list(range(2, n)), key_size, cap, so_far)
     shape = (cap, heads, width)
     return out, placed[0].reshape(shape), placed[1].reshape(shape)
 

time: 93 us -> 88 us (0.946)
  starting transfers between devices: 30.1 us -> 27.2 us
  waiting for transfers between devices: 9.44 us -> 7.53 us
    ppermute x12 -> x11, starting transfers between devices: 30 us -> 22.1 us  [swap(): return lax.ppermute(x, 'ctx', [(i, i ^ d) for i in range(n)])]
    ppermute x0 -> x2, starting transfers between devices: none -> 5.12 us  [inner_swap(): return lax.ppermute(x, 'ctx', pairs)]
    ppermute x12 -> x11, waiting for transfers between devices: 9.44 us -> 7.53 us  [swap(): return lax.ppermute(x, 'ctx', [(i, i ^ d) for i in range(n)])]
    pallas_call x2 -> x3, Pallas kernels: 12.4 us -> 12.9 us  [the longest x2 8.93 us: place(): pl.pallas_call(functools.partial(place_kernel, ids, counts, size, fresh),...]
  transfers between devices with their start and end apart: 13 -> 14, of which waited for: 7 -> 4; matrix products, arithmetic and copies ran while one was open for 4% -> 3% of each run, Pallas kernels for 39% -> 45%
where the time goes in v9:
time: 88 us; the launch traced here: 87.7 us
  Pallas kernels  49.3 us (56%)
  starting transfers between devices  27.2 us (31%)
  waiting for transfers between devices  7.53 us (9%)
  local copies, waits for them, and re-layouts  1.92 us (2%)
  between operations  1.07 us (1%)
    ppermute x11, starting transfers between devices, swap(): return lax.ppermute(x, 'ctx', [(i, i ^ d) for i in range(n)])  22.1 us
    pallas_call x4, Pallas kernels, first_block(): pl.pallas_call(functools.partial(first_kernel, fresh), grid_spec=pltpu.Pr...  13 us
    pallas_call x2, Pallas kernels, place(): pl.pallas_call(functools.partial(place_kernel, ids, counts, size, fresh),...  8.93 us
    pallas_call x1, Pallas kernels, own_totals(): pl.pallas_call(totals_kernel, grid=(heads, count // rows), in_specs=[in_v...  7.57 us
    ppermute x11, waiting for transfers between devices, swap(): return lax.ppermute(x, 'ctx', [(i, i ^ d) for i in range(n)])  7.53 us
    pallas_call x1, Pallas kernels, weighted_sums(): pl.pallas_call(functools.partial(sums_kernel, len(units)), in_specs=[in_v...  6.06 us
    ppermute x2, starting transfers between devices, inner_swap(): return lax.ppermute(x, 'ctx', pairs)  5.12 us
    pallas_call x1, Pallas kernels, raw_weights(): pl.pallas_call(functools.partial(raw_kernel, len(units)), grid=(heads,),...  5.04 us
  transfers between devices with their start and end apart: 14, of which 4 were waited for; matrix products, arithmetic and copies ran while one was open for 3% of the time, Pallas kernels for 45%

profile of v9, /device:TPU:0, one launch (start us, length us, event | category | flops | bytes accessed | tf_op | source)
XLA Modules:
  0.0 87.7 jit_solution(14640632828236095137)
XLA Ops:
  0.6 0.0 copy-start
  0.6 4.0 %sort_keys.1 = (bf16[2,1024,128]{2,1,0:T(8,128)(2,1)S(1)}, f32[2,1,1024]{2,1,0:T(1,128)S(1)}, s32[2,1,1024]{2,1,0:T(1,128)S(1)}) custom-call(s32[2,1024]{1,0:T(2,128)} %label_hbm.1, bf16[2048,128]{1,0:T(8,128)(2,1)} %bitcast.26), custom_call_target="tpu_custom_call" | custom-call | tf_op jit(solution)/shard_map/sort_keys/pallas_call | solution.py:135
  4.6 4.1 %collective-permute-start.1 = (bf16[2,1024,128]{2,1,0:T(8,128)(2,1)S(1)}, bf16[2,1024,128]{2,1,0:T(8,128)(2,1)S(1)}, u32[]{:S(2)}, u32[]{:S(2)}) collective-permute-start(bf16[2,1024,128]{2,1,0:T(8,128)(2,1)S(1)} %get-tuple-element.68.keys_ref.refs_0_), channel_id=1, source_target_pairs={{0,8},{4,12},{8,0},{12,4},{1,9},{5,13},{9,1},{13,5},{2,10},{6,14},... | collective-permute-start | bytes 1572872 | tf_op jit(solution)/shard_map/ppermute | solution.py:550
  8.8 1.6 %collective-permute-start = (bf16[2,1024,128]{2,1,0:T(8,128)(2,1)S(1)}, bf16[2,1024,128]{2,1,0:T(8,128)(2,1)S(1)}, u32[]{:S(2)}, u32[]{:S(2)}) collective-permute-start(bf16[2,1024,128]{2,1,0:T(8,128)(2,1)S(1)} %get-tuple-element.68.keys_ref.refs_0_), channel_id=1, source_target_pairs={{0,4},{4,0},{8,12},{12,8},{1,5},{5,1},{9,13},{13,9},{2,6},{6,2},{1... | collective-permute-start | bytes 1572872 | tf_op jit(solution)/shard_map/ppermute | solution.py:550
  10.3 0.0 collective-permute-start.2
  10.4 0.8 copy.13
  11.1 0.6 gather_fusion
  11.7 0.1 convert_bitcast_fusion
  11.8 0.1 copy.14
  11.9 0.2 convert_reduce_fusion.2
  12.1 0.0 collective-permute-done.2._
  12.1 7.6 %own_totals.1.tot_ref = f32[2,1,1024]{2,1,0:T(1,128)S(1)} custom-call(bf16[2,1024,128]{2,1,0:T(8,128)(2,1)S(1)} %get-tuple-element.68.keys_ref.refs_0_, f32[2,4096,128]{2,1,0:T(8,128)} %cent_in.1, f32[2,1,128]{2,1,0:T(1,128)S(1)} %collective-permute-done.2._), custom_call_target="tpu_custom_call" | custom-call | tf_op jit(solution)/shard_map/own_totals/pallas_call | solution.py:279
  19.7 0.4 collective-permute-start.6
  20.1 0.0 copy-done
  20.1 0.2 dynamic-slice_reduce_fusion
  20.4 2.3 %sort_values.1.values_ref = bf16[2,1024,128]{2,1,0:T(8,128)(2,1)S(1)} custom-call(s32[2,1,1024]{2,1,0:T(1,128)S(1)} %get-tuple-element.43.spot_ref, bf16[2048,128]{1,0:T(8,128)(2,1)} %bitcast.27), custom_call_target="tpu_custom_call" | custom-call | tf_op jit(solution)/shard_map/sort_values/pallas_call | solution.py:173
  22.7 0.3 collective-permute-start.5
  23.0 3.9 %collective-permute-start.4 = (f32[2,2,1024]{2,1,0:T(2,128)S(1)}, f32[2,2,1024]{2,1,0:T(2,128)S(1)}, u32[]{:S(2)}, u32[]{:S(2)}) collective-permute-start(f32[2,2,1024]{2,1,0:T(2,128)S(1)} %pad_maximum_fusion.1), channel_id=1, source_target_pairs={{0,12},{4,8},{8,4},{12,0},{1,13},{5,9},{9,5},{13,1},{2,14},{6,10},... | collective-permute-start | bytes 49160 | tf_op jit(solution)/shard_map/ppermute | solution.py:550
  26.8 4.1 %first_block.4 = (f32[2,1024,128]{2,1,0:T(8,128)S(1)}, bf16[2,1024,128]{2,1,0:T(8,128)(2,1)S(1)}, bf16[2,1024,128]{2,1,0:T(8,128)(2,1)S(1)}) custom-call(s32[1]{0:T(128)} %bitcast._.me_ref, bf16[2,1024,128]{2,1,0:T(8,128)(2,1)S(1)} %get-tuple-element.68.keys_ref.refs_0_, f32[2,1,1024]{2,1,0:T(1,128)S(1)} %own_totals.1.tot_ref, f32[2,4096,128]{2,1,0:T(8,128)} %cent_in.1), custom_call_target="tpu_custom_call" | custom-call | tf_op jit(solution)/shard_map/first_block/pallas_call | solution.py:349
  31.0 1.8 %collective-permute-done.6 = f32[2,2,1024]{2,1,0:T(2,128)S(1)} collective-permute-done((f32[2,2,1024]{2,1,0:T(2,128)S(1)}, f32[2,2,1024]{2,1,0:T(2,128)S(1)}, u32[]{:S(2)}, u32[]{:S(2)}) %collective-permute-start.6) | collective-permute-done | bytes 16416 | tf_op jit(solution)/shard_map/ppermute | solution.py:550
  32.8 0.3 collective-permute-done.5
  33.1 1.0 %collective-permute-done.4 = f32[2,2,1024]{2,1,0:T(2,128)S(1)} collective-permute-done((f32[2,2,1024]{2,1,0:T(2,128)S(1)}, f32[2,2,1024]{2,1,0:T(2,128)S(1)}, u32[]{:S(2)}, u32[]{:S(2)}) %collective-permute-start.4) | collective-permute-done | bytes 16416 | tf_op jit(solution)/shard_map/ppermute | solution.py:550
  34.1 0.1 broadcast_compare_fusion
  34.2 0.2 convert_reduce_fusion
  34.4 1.8 %own_ranks.1.rank_ref = f32[2,1,1024]{2,1,0:T(1,128)S(1)} custom-call(s32[1]{0:T(128)} %bitcast._.me_ref, f32[2,4,1024]{2,1,0:T(4,128)S(1)} %get-tuple-element.78.label_ref), custom_call_target="tpu_custom_call" | custom-call | tf_op jit(solution)/shard_map/own_ranks/pallas_call | solution.py:239
  36.1 0.6 windows.1
  36.8 0.1 constant_dynamic-update-slice_fusion.3
  36.9 0.0 collective-permute-done.1.keys_ref.refs_0_
  36.9 0.0 collective-permute-done.keys_ref.refs_1_
  36.9 0.6 collective-permute-start.3
  37.4 0.1 constant_dynamic-update-slice_fusion.2
  37.5 0.7 collective-permute-start.8
  38.2 3.0 %first_block.5 = (f32[2,1024,128]{2,1,0:T(8,128)S(1)}, bf16[2,1024,128]{2,1,0:T(8,128)(2,1)S(1)}) custom-call(s32[1]{0:T(128)} %bitcast._.me_ref, bf16[2,1024,128]{2,1,0:T(8,128)(2,1)S(1)} %collective-permute-done.keys_ref.refs_1_, f32[2,1,1024]{2,1,0:T(1,128)S(1)} %get-tuple-element.79.tot_ref, ...), custom_call_target="tpu_custom_call", output_to_operand_aliasing={{0}: (4, {})} | custom-call | tf_op jit(solution)/shard_map/first_block/pallas_call | solution.py:349
  41.2 4.5 %collective-permute-start.7 = (bf16[2,544,128]{2,1,0:T(8,128)(2,1)S(1)}, bf16[2,544,128]{2,1,0:T(8,128)(2,1)S(1)}, u32[]{:S(2)}, u32[]{:S(2)}) collective-permute-start(bf16[2,544,128]{2,1,0:T(8,128)(2,1)S(1)} %get-tuple-element.61), channel_id=1, source_target_pairs={{0,4},{4,0},{8,12},{12,8},{1,5},{5,1},{9,13},{13,9},{2,6},{6,2},{1... | collective-permute-start | bytes 835592 | tf_op jit(solution)/shard_map/ppermute | solution.py:550
  45.7 3.0 %first_block.6 = (f32[2,1024,128]{2,1,0:T(8,128)S(1)}, bf16[2,1024,128]{2,1,0:T(8,128)(2,1)S(1)}) custom-call(s32[1]{0:T(128)} %bitcast._.me_ref, bf16[2,1024,128]{2,1,0:T(8,128)(2,1)S(1)} %collective-permute-done.1.keys_ref.refs_0_, f32[2,1,1024]{2,1,0:T(1,128)S(1)} %get-tuple-element.81.tot_ref, ...), custom_call_target="tpu_custom_call", output_to_operand_aliasing={{0}: (4, {})} | custom-call | tf_op jit(solution)/shard_map/first_block/pallas_call | solution.py:349
  48.7 0.1 collective-permute-start.12
  48.7 4.5 %collective-permute-start.13 = (bf16[2,544,128]{2,1,0:T(8,128)(2,1)S(1)}, bf16[2,544,128]{2,1,0:T(8,128)(2,1)S(1)}, u32[]{:S(2)}, u32[]{:S(2)}) collective-permute-start(bf16[2,544,128]{2,1,0:T(8,128)(2,1)S(1)} %get-tuple-element.67), channel_id=1, source_target_pairs={{0,12},{4,4},{8,8},{12,0},{1,13},{5,5},{9,9},{13,1},{2,14},{6,6},{... | collective-permute-start | bytes 835592 | tf_op jit(solution)/shard_map/ppermute | solution.py:605
  53.2 0.1 constant_dynamic-update-slice_fusion.1
  53.3 4.4 %collective-permute-done.3.keys_ref.refs_1_ = bf16[2,1024,128]{2,1,0:T(8,128)(2,1)S(1)} collective-permute-done((bf16[2,1024,128]{2,1,0:T(8,128)(2,1)S(1)}, bf16[2,1024,128]{2,1,0:T(8,128)(2,1)S(1)}, u32[]{:S(2)}, u32[]{:S(2)}) %collective-permute-start.3) | collective-permute-done | bytes 524320 | tf_op jit(solution)/shard_map/ppermute | solution.py:550
  57.7 3.0 %first_block.7 = (f32[2,1024,128]{2,1,0:T(8,128)S(1)}, bf16[2,1024,128]{2,1,0:T(8,128)(2,1)S(1)}) custom-call(s32[1]{0:T(128)} %bitcast._.me_ref, bf16[2,1024,128]{2,1,0:T(8,128)(2,1)S(1)} %collective-permute-done.3.keys_ref.refs_1_, f32[2,1,1024]{2,1,0:T(1,128)S(1)} %get-tuple-element.84.tot_ref, ...), custom_call_target="tpu_custom_call", output_to_operand_aliasing={{0}: (4, {})} | custom-call | tf_op jit(solution)/shard_map/first_block/pallas_call | solution.py:349
  60.7 5.0 %raw_weights.1 = (bf16[2,1024,4096]{2,1,0:T(8,128)(2,1)S(1)}, f32[2,1,4096]{2,1,0:T(1,128)S(1)}) custom-call(f32[2,1024,128]{2,1,0:T(8,128)S(1)} %get-tuple-element.55.sums_ref, bf16[2,1024,128]{2,1,0:T(8,128)(2,1)S(1)} %get-tuple-element.56.refs_0_.refs_4_, bf16[2,1024,128]{2,1,0:T(8,128)(2,1)S(1)} %get-tuple-element.57.refs_1_.refs_5_, ...), custom_call_target="tpu_custom_call" | custom-call | tf_op jit(solution)/shard_map/raw_weights/pallas_call | solution.py:386
  65.8 0.0 collective-permute-done.8.refs_3_
  65.8 0.0 collective-permute-done.7.refs_3_
  65.8 6.1 %collective-permute-start.11 = (f32[2,1,4096]{2,1,0:T(1,128)S(1)}, f32[2,1,4096]{2,1,0:T(1,128)S(1)}, u32[]{:S(2)}, u32[]{:S(2)}) collective-permute-start(f32[2,1,4096]{2,1,0:T(1,128)S(1)} %get-tuple-element.63.refs_0_), channel_id=1, source_target_pairs={{0,12},{4,8},{8,4},{12,0},{1,13},{5,9},{9,5},{13,1},{2,14},{6,10},... | collective-permute-start | bytes 98312 | tf_op jit(solution)/shard_map/ppermute | solution.py:550
  71.9 0.0 collective-permute-start.10
  71.9 0.6 collective-permute-start.9
  72.5 3.8 %place.2.refs_5_ = bf16[2,2048,256]{2,1,0:T(8,128)(2,1)S(1)} custom-call(s32[6,2,4]{2,1,0:T(2,128)S(1)} %constant_dynamic-update-slice_fusion.scalar_ref, f32[2,4,1024]{2,1,0:T(4,128)S(1)} %get-tuple-element.78.label_ref, bf16[2,1024,128]{2,1,0:T(8,128)(2,1)S(1)} %get-tuple-element.68.keys_ref.refs_0_, ...), custom_call_target="tpu_custom_call" | custom-call | tf_op jit(solution)/shard_map/place/pallas_call | solution.py:529
  76.3 0.0 collective-permute-done.12.refs_2_
  76.3 0.0 collective-permute-done.13.refs_4_
  76.3 5.1 %place.3 = (bf16[4096,128]{1,0:T(8,128)(2,1)}, bf16[4096,128]{1,0:T(8,128)(2,1)}) custom-call(s32[6,2,4]{2,1,0:T(2,128)S(1)} %constant_dynamic-update-slice_fusion.scalar_ref, f32[2,4,1024]{2,1,0:T(4,128)S(1)} %get-tuple-element.78.label_ref, bf16[2,1024,128]{2,1,0:T(8,128)(2,1)S(1)} %collective-permute-done.1.keys_ref.refs_0_, ...), custom_call_target="tpu_custom_call" | custom-call | tf_op jit(solution)/shard_map/place/pallas_call | solution.py:529
  81.4 0.0 collective-permute-done.11.refs_3_
  81.4 0.0 collective-permute-done.10.refs_2_
  81.5 0.0 collective-permute-done.9.refs_1_
  81.5 6.1 %weighted_sums.1 = f32[2,1024,128]{2,1,0:T(8,128)} custom-call(bf16[2,1024,4096]{2,1,0:T(8,128)(2,1)S(1)} %get-tuple-element.60.raw_ref, f32[2,1,4096]{2,1,0:T(1,128)S(1)} %get-tuple-element.63.refs_0_, f32[2,1,4096]{2,1,0:T(1,128)S(1)} %collective-permute-done.9.refs_1_, f32[2,1,4096]{2,1,0:T(1,128)S(1)} %collective-permute-done.10.refs_2_, ...), custom_call_target="tpu_custom_call" | custom-call | tf_op jit(solution)/shard_map/weighted_sums/pallas_call | solution.py:424
  (14 shorter events, 0.1 us)
Async XLA Ops:
  0.6 19.5 %copy-start = (s32[2,5]{1,0:T(2,128)S(1)}, s32[2,5]{1,0:T(2,128)}, u32[]{:S(2)}) copy-start(s32[2,5]{1,0:T(2,128)} %param.8) | copy-start | bytes 124
  4.6 32.2 %collective-permute-start.1 = (bf16[2,1024,128]{2,1,0:T(8,128)(2,1)S(1)}, bf16[2,1024,128]{2,1,0:T(8,128)(2,1)S(1)}, u32[]{:S(2)}, u32[]{:S(2)}) collective-permute-start(bf16[2,1024,128]{2,1,0:T(8,128)(2,1)S(1)} %get-tuple-element.68.keys_ref.refs_0_), channel_id=1, source_target_pairs={{0,8},{4,12},{8,0},{12,4},{1,9},{5,13},{9,1},{13,5},{2,10},{6,14},... | collective-permute-start | bytes 1572872 | tf_op jit(solution)/shard_map/ppermute | solution.py:550
  8.8 28.1 %collective-permute-start = (bf16[2,1024,128]{2,1,0:T(8,128)(2,1)S(1)}, bf16[2,1024,128]{2,1,0:T(8,128)(2,1)S(1)}, u32[]{:S(2)}, u32[]{:S(2)}) collective-permute-start(bf16[2,1024,128]{2,1,0:T(8,128)(2,1)S(1)} %get-tuple-element.68.keys_ref.refs_0_), channel_id=1, source_target_pairs={{0,4},{4,0},{8,12},{12,8},{1,5},{5,1},{9,13},{13,9},{2,6},{6,2},{1... | collective-permute-start | bytes 1572872 | tf_op jit(solution)/shard_map/ppermute | solution.py:550
  10.3 1.8 %collective-permute-start.2 = (f32[2,1,128]{2,1,0:T(1,128)S(1)}, f32[2,1,128]{2,1,0:T(1,128)S(1)}, u32[]{:S(2)}, u32[]{:S(2)}) collective-permute-start(f32[2,1,128]{2,1,0:T(1,128)S(1)} %slice.21), channel_id=1, source_target_pairs={{0,1},{1,0},{2,3},{3,2},{4,5},{5,4},{6,7},{7,6},{8,9},{9,8},{10,11... | collective-permute-start | bytes 3080 | tf_op jit(solution)/shard_map/ppermute | solution.py:568
  19.7 13.0 %collective-permute-start.6 = (f32[2,2,1024]{2,1,0:T(2,128)S(1)}, f32[2,2,1024]{2,1,0:T(2,128)S(1)}, u32[]{:S(2)}, u32[]{:S(2)}) collective-permute-start(f32[2,2,1024]{2,1,0:T(2,128)S(1)} %pad_maximum_fusion.1), channel_id=1, source_target_pairs={{0,8},{4,12},{8,0},{12,4},{1,9},{5,13},{9,1},{13,5},{2,10},{6,14},... | collective-permute-start | bytes 49160 | tf_op jit(solution)/shard_map/ppermute | solution.py:550
  22.7 10.4 %collective-permute-start.5 = (f32[2,2,1024]{2,1,0:T(2,128)S(1)}, f32[2,2,1024]{2,1,0:T(2,128)S(1)}, u32[]{:S(2)}, u32[]{:S(2)}) collective-permute-start(f32[2,2,1024]{2,1,0:T(2,128)S(1)} %pad_maximum_fusion.1), channel_id=1, source_target_pairs={{0,4},{4,0},{8,12},{12,8},{1,5},{5,1},{9,13},{13,9},{2,6},{6,2},{1... | collective-permute-start | bytes 49160 | tf_op jit(solution)/shard_map/ppermute | solution.py:550
  23.0 11.1 %collective-permute-start.4 = (f32[2,2,1024]{2,1,0:T(2,128)S(1)}, f32[2,2,1024]{2,1,0:T(2,128)S(1)}, u32[]{:S(2)}, u32[]{:S(2)}) collective-permute-start(f32[2,2,1024]{2,1,0:T(2,128)S(1)} %pad_maximum_fusion.1), channel_id=1, source_target_pairs={{0,12},{4,8},{8,4},{12,0},{1,13},{5,9},{9,5},{13,1},{2,14},{6,10},... | collective-permute-start | bytes 49160 | tf_op jit(solution)/shard_map/ppermute | solution.py:550
  36.9 20.9 %collective-permute-start.3 = (bf16[2,1024,128]{2,1,0:T(8,128)(2,1)S(1)}, bf16[2,1024,128]{2,1,0:T(8,128)(2,1)S(1)}, u32[]{:S(2)}, u32[]{:S(2)}) collective-permute-start(bf16[2,1024,128]{2,1,0:T(8,128)(2,1)S(1)} %collective-permute-done.1.keys_ref.refs_0_), channel_id=1, source_target_pairs={{0,4},{4,0},{8,12},{12,8},{1,5},{5,1},{9,13},{13,9},{2,6},{6,2},{1... | collective-permute-start | bytes 1572872 | tf_op jit(solution)/shard_map/ppermute | solution.py:550
  37.5 28.2 %collective-permute-start.8 = (bf16[2,544,128]{2,1,0:T(8,128)(2,1)S(1)}, bf16[2,544,128]{2,1,0:T(8,128)(2,1)S(1)}, u32[]{:S(2)}, u32[]{:S(2)}) collective-permute-start(bf16[2,544,128]{2,1,0:T(8,128)(2,1)S(1)} %get-tuple-element.67), channel_id=1, source_target_pairs={{0,0},{4,8},{8,4},{12,12},{1,1},{5,9},{9,5},{13,13},{2,2},{6,10},{... | collective-permute-start | bytes 835592 | tf_op jit(solution)/shard_map/ppermute | solution.py:605
  41.2 24.6 %collective-permute-start.7 = (bf16[2,544,128]{2,1,0:T(8,128)(2,1)S(1)}, bf16[2,544,128]{2,1,0:T(8,128)(2,1)S(1)}, u32[]{:S(2)}, u32[]{:S(2)}) collective-permute-start(bf16[2,544,128]{2,1,0:T(8,128)(2,1)S(1)} %get-tuple-element.61), channel_id=1, source_target_pairs={{0,4},{4,0},{8,12},{12,8},{1,5},{5,1},{9,13},{13,9},{2,6},{6,2},{1... | collective-permute-start | bytes 835592 | tf_op jit(solution)/shard_map/ppermute | solution.py:550
  48.7 27.6 %collective-permute-start.12 = (bf16[2,544,128]{2,1,0:T(8,128)(2,1)S(1)}, bf16[2,544,128]{2,1,0:T(8,128)(2,1)S(1)}, u32[]{:S(2)}, u32[]{:S(2)}) collective-permute-start(bf16[2,544,128]{2,1,0:T(8,128)(2,1)S(1)} %get-tuple-element.65), channel_id=1, source_target_pairs={{0,8},{4,12},{8,0},{12,4},{1,9},{5,13},{9,1},{13,5},{2,10},{6,14},... | collective-permute-start | bytes 835592 | tf_op jit(solution)/shard_map/ppermute | solution.py:550
  48.7 27.6 %collective-permute-start.13 = (bf16[2,544,128]{2,1,0:T(8,128)(2,1)S(1)}, bf16[2,544,128]{2,1,0:T(8,128)(2,1)S(1)}, u32[]{:S(2)}, u32[]{:S(2)}) collective-permute-start(bf16[2,544,128]{2,1,0:T(8,128)(2,1)S(1)} %get-tuple-element.67), channel_id=1, source_target_pairs={{0,12},{4,4},{8,8},{12,0},{1,13},{5,5},{9,9},{13,1},{2,14},{6,6},{... | collective-permute-start | bytes 835592 | tf_op jit(solution)/shard_map/ppermute | solution.py:605
  65.8 15.7 %collective-permute-start.11 = (f32[2,1,4096]{2,1,0:T(1,128)S(1)}, f32[2,1,4096]{2,1,0:T(1,128)S(1)}, u32[]{:S(2)}, u32[]{:S(2)}) collective-permute-start(f32[2,1,4096]{2,1,0:T(1,128)S(1)} %get-tuple-element.63.refs_0_), channel_id=1, source_target_pairs={{0,12},{4,8},{8,4},{12,0},{1,13},{5,9},{9,5},{13,1},{2,14},{6,10},... | collective-permute-start | bytes 98312 | tf_op jit(solution)/shard_map/ppermute | solution.py:550
  71.9 9.5 %collective-permute-start.10 = (f32[2,1,4096]{2,1,0:T(1,128)S(1)}, f32[2,1,4096]{2,1,0:T(1,128)S(1)}, u32[]{:S(2)}, u32[]{:S(2)}) collective-permute-start(f32[2,1,4096]{2,1,0:T(1,128)S(1)} %get-tuple-element.63.refs_0_), channel_id=1, source_target_pairs={{0,8},{4,12},{8,0},{12,4},{1,9},{5,13},{9,1},{13,5},{2,10},{6,14},... | collective-permute-start | bytes 98312 | tf_op jit(solution)/shard_map/ppermute | solution.py:550
  71.9 9.5 %collective-permute-start.9 = (f32[2,1,4096]{2,1,0:T(1,128)S(1)}, f32[2,1,4096]{2,1,0:T(1,128)S(1)}, u32[]{:S(2)}, u32[]{:S(2)}) collective-permute-start(f32[2,1,4096]{2,1,0:T(1,128)S(1)} %get-tuple-element.63.refs_0_), channel_id=1, source_target_pairs={{0,4},{4,0},{8,12},{12,8},{1,5},{5,1},{9,13},{13,9},{2,6},{6,2},{1... | collective-permute-start | bytes 98312 | tf_op jit(solution)/shard_map/ppermute | solution.py:550

commit v10 on v9

--- a/solution.py
+++ b/solution.py
@@ -439,7 +439,7 @@
 def fill_windows(ids, size, scalar_ref, label_ref, keys, values, rows_ref, near_ref):
     heads, tokens, width = keys[0].shape
     digit_rows = tokens // LANES
-    sent = values[0][0].shape[1] - 2 * digit_rows
+    sent = values[0].shape[1] - 2 * digit_rows
     rows_ref[:, :, width:] = jnp.zeros((heads, len(ids) * size, width), BF16)
     for h in range(heads):
         low, high, first = (scalar_ref[i, h, 0].astype(F32) for i in range(2, 5))
@@ -448,11 +448,8 @@
             gap = pl.multiple_of(scalar_ref[1, h, m], 16)
             here = i * size
             rows_ref[h, here : here + size, :width] = keys[i][h, pl.ds(start, size), :]
-            value = values[i][0][h]
-            if len(values[i]) == 2:
-                value = jnp.where(scalar_ref[5, 0, 0] > 0, value, values[i][1][h])
-            rows_ref[h, pl.ds(here + gap, sent), width:] = value[:sent]
-            digits = value[sent:].astype(F32)
+            rows_ref[h, pl.ds(here + gap, sent), width:] = values[i][h, :sent, :]
+            digits = values[i][h, sent:, :].astype(F32)
             rank = digits[:digit_rows] * 128.0 + digits[digit_rows:]
             rank = jnp.concatenate([rank[r : r + 1] for r in range(digit_rows)], axis=1)
             label = label_ref[h, m : m + 1, :]
@@ -462,14 +459,9 @@
             near_ref[h, :, here : here + size] = spot[:, :size]
 
 
-def grouped(refs, counts):
-    refs = iter(refs)
-    return [[next(refs) for _ in range(count)] for count in counts]
-
-
-def place_kernel(ids, counts, size, fresh, scalar_ref, label_ref, *refs):
-    keys, refs = refs[: len(ids)], refs[len(ids) :]
-    values, refs = grouped(refs, counts), refs[sum(counts) :]
+def place_kernel(ids, size, fresh, scalar_ref, label_ref, *refs):
+    count = len(ids)
+    keys, values, refs = refs[:count], refs[count : 2 * count], refs[2 * count :]
     if fresh:
         so_far_ref, rows_ref, near_ref = refs
     else:
@@ -508,8 +500,7 @@
 def place(scalars, labels, keys, values, ids, size, cap, so_far):
     heads, _, width = keys[0].shape
     fresh = so_far is None
-    counts = [len(values[m]) for m in ids]
-    moved = [keys[m] for m in ids] + [x for m in ids for x in values[m]]
+    moved = [x[m] for x in (keys, values) for m in ids]
     scratch = [
         pltpu.VMEM((heads, len(ids) * size, 2 * width), BF16),
         pltpu.VMEM((heads, 1, len(ids) * size), jnp.int32),
@@ -527,7 +518,7 @@
             pltpu.SemaphoreType.DMA((2 * cap // 512,)),
         ]
     return pl.pallas_call(
-        functools.partial(place_kernel, ids, counts, size, fresh),
+        functools.partial(place_kernel, ids, size, fresh),
         in_specs=[pl.BlockSpec(memory_space=pltpu.SMEM)] + [in_vmem()] * (1 + len(moved)),
         out_specs=out_specs,
         out_shape=out_shape,
@@ -582,7 +573,9 @@
     own_below = jnp.sum((own_labels < peer_low[:, :, None]).astype(jnp.int32), axis=2)
     own_values = sort_values(own_spots, value_rows.reshape(heads * tokens, width))
 
-    labels = jnp.concatenate([x[:, -1:] for x in shared], axis=1)
+    labels, sums = lax.optimization_barrier(
+        (jnp.concatenate([x[:, -1:] for x in shared], axis=1), sums)
+    )
     ranks = own_ranks(me_array, labels)
     low = lax.dynamic_slice_in_dim(owner_bounds, me, 1, 1)
     high = lax.dynamic_slice_in_dim(owner_bounds, me + 1, 1, 1)
@@ -591,45 +584,23 @@
     key_starts = aligned(below, key_size)
     gaps = aligned(below, send_size) - key_starts
     one = jnp.ones((1, n), jnp.int32)
-    inner = ((me & 3) == 1) | ((me & 3) == 2)
-    scalars = jnp.stack(
-        [key_starts, gaps, low * one, high * one, first * one, inner * jnp.ones_like(below)]
+    scalars = jnp.stack([key_starts, gaps, low * one, high * one, first * one])
+
+    own_windows = list(
+        windows(aligned(own_below, send_size), ranks, own_values, send_size, own_labels)
     )
-
-    starts = aligned(own_below, send_size)
-    own_windows = windows(starts, ranks, own_values, send_size, own_labels)
-    values = {0: [own_windows[0]]}
-
-    def inner_swap(x, wanted):
-        pairs = [(i, i ^ 3 if (i & 3 in (1, 2)) == wanted else i) for i in range(n)]
-        return lax.ppermute(x, "ctx", pairs)
-
-    def leave(m, x):
-        if m == 1 and n > 2:
-            own_windows[3], x = lax.optimization_barrier((own_windows[3], x))
-            values[3] = [inner_swap(own_windows[3], True)]
-        if m == min(2, n - 1):
-            own_windows[1], x = lax.optimization_barrier((own_windows[1], x))
-            values[1] = [swap(own_windows[1], 1)]
-        if m == n - 1:
-            *own_windows[2:], x = lax.optimization_barrier((*own_windows[2:], x))
-            for d in range(2, n):
-                if d == 3:
-                    values[3].append(inner_swap(own_windows[3], False))
-                else:
-                    values[d] = [swap(own_windows[d], d)]
-        return x
-
-    own_windows = list(own_windows)
+    values = {0: own_windows[0]}
     for m in range(1, n):
-        sums = leave(m, sums)
+        group = {min(2, n - 1): [1], n - 1: list(range(2, n))}.get(m)
+        if group:
+            *leaving, sums = lax.optimization_barrier((*(own_windows[d] for d in group), sums))
+            for d, window in zip(group, leaving):
+                values[d] = swap(window, d)
         sums, unit = first_block(me_array, keys[m], totals[m], cents, n, sums)
         units.append(unit)
 
     raw, part = raw_weights(sums, units)
-    values[1][0], values[3][0], scalars, part = lax.optimization_barrier(
-        (values[1][0], values[3][0], scalars, part)
-    )
+    values[1], scalars, part = lax.optimization_barrier((values[1], scalars, part))
     parts = spread(part)
     so_far = place(scalars, labels, keys, values, [0, 1], key_size, cap, None)
     out = weighted_sums(raw, units, parts)

time: 88 us -> 83.1 us (0.944)
  starting transfers between devices: 27.2 us -> 19.8 us
  waiting for transfers between devices: 7.53 us -> 9.79 us
    ppermute x2 -> x0, starting transfers between devices: 5.12 us -> none  [inner_swap(): return lax.ppermute(x, 'ctx', pairs)]
    ppermute x11 -> x12, starting transfers between devices: 22.1 us -> 19.8 us  [swap(): return lax.ppermute(x, 'ctx', [(i, i ^ d) for i in range(n)])]
    ppermute x11 -> x12, waiting for transfers between devices: 7.53 us -> 9.78 us  [swap(): return lax.ppermute(x, 'ctx', [(i, i ^ d) for i in range(n)])]
  transfers between devices with their start and end apart: 14 -> 13, of which waited for: 4 -> 4; matrix products, arithmetic and copies ran while one was open for 3% -> 3% of each run, Pallas kernels for 45% -> 48%
where the time goes in v10:
time: 83.1 us; the launch traced here: 82.9 us
  Pallas kernels  49.6 us (60%)
  starting transfers between devices  19.8 us (24%)
  waiting for transfers between devices  9.79 us (12%)
  local copies, waits for them, and re-layouts  1.91 us (2%)
  between operations  1.06 us (1%)
    ppermute x12, starting transfers between devices, swap(): return lax.ppermute(x, 'ctx', [(i, i ^ d) for i in range(n)])  19.8 us
    pallas_call x4, Pallas kernels, first_block(): pl.pallas_call(functools.partial(first_kernel, fresh), grid_spec=pltpu.Pr...  13 us
    ppermute x12, waiting for transfers between devices, swap(): return lax.ppermute(x, 'ctx', [(i, i ^ d) for i in range(n)])  9.78 us
    pallas_call x2, Pallas kernels, place(): pl.pallas_call(functools.partial(place_kernel, ids, size, fresh), in_spec...  8.85 us
    pallas_call x1, Pallas kernels, own_totals(): pl.pallas_call(totals_kernel, grid=(heads, count // rows), in_specs=[in_v...  7.74 us
    pallas_call x1, Pallas kernels, weighted_sums(): pl.pallas_call(functools.partial(sums_kernel, len(units)), in_specs=[in_v...  6.06 us
    pallas_call x1, Pallas kernels, raw_weights(): pl.pallas_call(functools.partial(raw_kernel, len(units)), grid=(heads,),...  5.27 us
    pallas_call x1, Pallas kernels, sort_keys(): pl.pallas_call(sort_kernel, in_specs=[anywhere()] * 2, out_specs=(in_vmem...  4 us
  transfers between devices with their start and end apart: 13, of which 4 were waited for; matrix products, arithmetic and copies ran while one was open for 3% of the time, Pallas kernels for 48%

profile of v10, /device:TPU:0, one launch (start us, length us, event | category | flops | bytes accessed | tf_op | source)
XLA Modules:
  0.0 82.9 jit_solution(3394812852373879081)
XLA Ops:
  0.6 0.0 copy-start
  0.6 4.0 %sort_keys.1 = (bf16[2,1024,128]{2,1,0:T(8,128)(2,1)S(1)}, f32[2,1,1024]{2,1,0:T(1,128)S(1)}, s32[2,1,1024]{2,1,0:T(1,128)S(1)}) custom-call(s32[2,1024]{1,0:T(2,128)} %label_hbm.1, bf16[2048,128]{1,0:T(8,128)(2,1)} %bitcast.26), custom_call_target="tpu_custom_call" | custom-call | tf_op jit(solution)/shard_map/sort_keys/pallas_call | solution.py:135
  4.6 4.1 %collective-permute-start.1 = (bf16[2,1024,128]{2,1,0:T(8,128)(2,1)S(1)}, bf16[2,1024,128]{2,1,0:T(8,128)(2,1)S(1)}, u32[]{:S(2)}, u32[]{:S(2)}) collective-permute-start(bf16[2,1024,128]{2,1,0:T(8,128)(2,1)S(1)} %get-tuple-element.66.keys_ref.refs_0_), channel_id=1, source_target_pairs={{0,8},{4,12},{8,0},{12,4},{1,9},{5,13},{9,1},{13,5},{2,10},{6,14},... | collective-permute-start | bytes 1572872 | tf_op jit(solution)/shard_map/ppermute | solution.py:541
  8.8 1.6 %collective-permute-start = (bf16[2,1024,128]{2,1,0:T(8,128)(2,1)S(1)}, bf16[2,1024,128]{2,1,0:T(8,128)(2,1)S(1)}, u32[]{:S(2)}, u32[]{:S(2)}) collective-permute-start(bf16[2,1024,128]{2,1,0:T(8,128)(2,1)S(1)} %get-tuple-element.66.keys_ref.refs_0_), channel_id=1, source_target_pairs={{0,4},{4,0},{8,12},{12,8},{1,5},{5,1},{9,13},{13,9},{2,6},{6,2},{1... | collective-permute-start | bytes 1572872 | tf_op jit(solution)/shard_map/ppermute | solution.py:541
  10.3 0.0 collective-permute-start.2
  10.4 0.8 copy.13
  11.1 0.6 gather_fusion
  11.7 0.1 convert_bitcast_fusion
  11.8 0.1 copy.14
  11.9 0.2 convert_reduce_fusion.2
  12.1 0.0 collective-permute-done.2._
  12.1 7.7 %own_totals.1.tot_ref = f32[2,1,1024]{2,1,0:T(1,128)S(1)} custom-call(bf16[2,1024,128]{2,1,0:T(8,128)(2,1)S(1)} %get-tuple-element.66.keys_ref.refs_0_, f32[2,4096,128]{2,1,0:T(8,128)} %cent_in.1, f32[2,1,128]{2,1,0:T(1,128)S(1)} %collective-permute-done.2._), custom_call_target="tpu_custom_call" | custom-call | tf_op jit(solution)/shard_map/own_totals/pallas_call | solution.py:279
  19.9 0.4 collective-permute-start.6
  20.3 0.0 copy-done
  20.3 0.2 dynamic-slice_reduce_fusion
  20.5 2.4 %sort_values.1.values_ref = bf16[2,1024,128]{2,1,0:T(8,128)(2,1)S(1)} custom-call(s32[2,1,1024]{2,1,0:T(1,128)S(1)} %get-tuple-element.44.spot_ref, bf16[2048,128]{1,0:T(8,128)(2,1)} %bitcast.27), custom_call_target="tpu_custom_call" | custom-call | tf_op jit(solution)/shard_map/sort_values/pallas_call | solution.py:173
  22.9 0.3 collective-permute-start.5
  23.2 3.8 %collective-permute-start.4 = (f32[2,2,1024]{2,1,0:T(2,128)S(1)}, f32[2,2,1024]{2,1,0:T(2,128)S(1)}, u32[]{:S(2)}, u32[]{:S(2)}) collective-permute-start(f32[2,2,1024]{2,1,0:T(2,128)S(1)} %pad_maximum_fusion.1), channel_id=1, source_target_pairs={{0,12},{4,8},{8,4},{12,0},{1,13},{5,9},{9,5},{13,1},{2,14},{6,10},... | collective-permute-start | bytes 49160 | tf_op jit(solution)/shard_map/ppermute | solution.py:541
  27.0 4.1 %first_block.4 = (f32[2,1024,128]{2,1,0:T(8,128)S(1)}, bf16[2,1024,128]{2,1,0:T(8,128)(2,1)S(1)}, bf16[2,1024,128]{2,1,0:T(8,128)(2,1)S(1)}) custom-call(s32[1]{0:T(128)} %bitcast._.me_ref, bf16[2,1024,128]{2,1,0:T(8,128)(2,1)S(1)} %get-tuple-element.66.keys_ref.refs_0_, f32[2,1,1024]{2,1,0:T(1,128)S(1)} %own_totals.1.tot_ref, f32[2,4096,128]{2,1,0:T(8,128)} %cent_in.1), custom_call_target="tpu_custom_call" | custom-call | tf_op jit(solution)/shard_map/first_block/pallas_call | solution.py:349
  31.1 1.6 %collective-permute-done.6 = f32[2,2,1024]{2,1,0:T(2,128)S(1)} collective-permute-done((f32[2,2,1024]{2,1,0:T(2,128)S(1)}, f32[2,2,1024]{2,1,0:T(2,128)S(1)}, u32[]{:S(2)}, u32[]{:S(2)}) %collective-permute-start.6) | collective-permute-done | bytes 16416 | tf_op jit(solution)/shard_map/ppermute | solution.py:541
  32.8 0.3 collective-permute-done.5
  33.1 1.0 %collective-permute-done.4 = f32[2,2,1024]{2,1,0:T(2,128)S(1)} collective-permute-done((f32[2,2,1024]{2,1,0:T(2,128)S(1)}, f32[2,2,1024]{2,1,0:T(2,128)S(1)}, u32[]{:S(2)}, u32[]{:S(2)}) %collective-permute-start.4) | collective-permute-done | bytes 16416 | tf_op jit(solution)/shard_map/ppermute | solution.py:541
  34.1 0.0 collective-permute-done.1.keys_ref.refs_0_
  34.1 0.0 collective-permute-done.keys_ref.refs_1_
  34.2 0.3 convert_reduce_fusion
  34.5 0.6 collective-permute-start.3
  35.1 0.1 constant_dynamic-update-slice_fusion.2
  35.1 1.7 %own_ranks.1.rank_ref = f32[2,1,1024]{2,1,0:T(1,128)S(1)} custom-call(s32[1]{0:T(128)} %bitcast._.me_ref, f32[2,4,1024]{2,1,0:T(4,128)S(1)} %pad_maximum_fusion.label_ref), custom_call_target="tpu_custom_call" | custom-call | tf_op jit(solution)/shard_map/own_ranks/pallas_call | solution.py:239
  36.9 0.6 windows.1
  37.5 3.0 %first_block.5 = (f32[2,1024,128]{2,1,0:T(8,128)S(1)}, bf16[2,1024,128]{2,1,0:T(8,128)(2,1)S(1)}) custom-call(s32[1]{0:T(128)} %bitcast._.me_ref, bf16[2,1024,128]{2,1,0:T(8,128)(2,1)S(1)} %collective-permute-done.keys_ref.refs_1_, f32[2,1,1024]{2,1,0:T(1,128)S(1)} %get-tuple-element.75.tot_ref, ...), custom_call_target="tpu_custom_call", output_to_operand_aliasing={{0}: (4, {})} | custom-call | tf_op jit(solution)/shard_map/first_block/pallas_call | solution.py:349
  40.5 1.6 %collective-permute-start.7 = (bf16[2,544,128]{2,1,0:T(8,128)(2,1)S(1)}, bf16[2,544,128]{2,1,0:T(8,128)(2,1)S(1)}, u32[]{:S(2)}, u32[]{:S(2)}) collective-permute-start(bf16[2,544,128]{2,1,0:T(8,128)(2,1)S(1)} %get-tuple-element.60), channel_id=1, source_target_pairs={{0,4},{4,0},{8,12},{12,8},{1,5},{5,1},{9,13},{13,9},{2,6},{6,2},{1... | collective-permute-start | bytes 835592 | tf_op jit(solution)/shard_map/ppermute | solution.py:541
  42.1 3.0 %first_block.6 = (f32[2,1024,128]{2,1,0:T(8,128)S(1)}, bf16[2,1024,128]{2,1,0:T(8,128)(2,1)S(1)}) custom-call(s32[1]{0:T(128)} %bitcast._.me_ref, bf16[2,1024,128]{2,1,0:T(8,128)(2,1)S(1)} %collective-permute-done.1.keys_ref.refs_0_, f32[2,1,1024]{2,1,0:T(1,128)S(1)} %get-tuple-element.77.tot_ref, ...), custom_call_target="tpu_custom_call", output_to_operand_aliasing={{0}: (4, {})} | custom-call | tf_op jit(solution)/shard_map/first_block/pallas_call | solution.py:349
  45.0 2.0 %collective-permute-start.11 = (bf16[2,544,128]{2,1,0:T(8,128)(2,1)S(1)}, bf16[2,544,128]{2,1,0:T(8,128)(2,1)S(1)}, u32[]{:S(2)}, u32[]{:S(2)}) collective-permute-start(bf16[2,544,128]{2,1,0:T(8,128)(2,1)S(1)} %get-tuple-element.64), channel_id=1, source_target_pairs={{0,8},{4,12},{8,0},{12,4},{1,9},{5,13},{9,1},{13,5},{2,10},{6,14},... | collective-permute-start | bytes 835592 | tf_op jit(solution)/shard_map/ppermute | solution.py:541
  47.0 1.0 %collective-permute-start.12 = (bf16[2,544,128]{2,1,0:T(8,128)(2,1)S(1)}, bf16[2,544,128]{2,1,0:T(8,128)(2,1)S(1)}, u32[]{:S(2)}, u32[]{:S(2)}) collective-permute-start(bf16[2,544,128]{2,1,0:T(8,128)(2,1)S(1)} %get-tuple-element.65), channel_id=1, source_target_pairs={{0,12},{4,8},{8,4},{12,0},{1,13},{5,9},{9,5},{13,1},{2,14},{6,10},... | collective-permute-start | bytes 835592 | tf_op jit(solution)/shard_map/ppermute | solution.py:541
  48.0 0.1 constant_dynamic-update-slice_fusion.1
  48.1 0.1 constant_dynamic-update-slice_fusion.scalar_ref
  48.1 6.9 %collective-permute-done.3.keys_ref.refs_1_ = bf16[2,1024,128]{2,1,0:T(8,128)(2,1)S(1)} collective-permute-done((bf16[2,1024,128]{2,1,0:T(8,128)(2,1)S(1)}, bf16[2,1024,128]{2,1,0:T(8,128)(2,1)S(1)}, u32[]{:S(2)}, u32[]{:S(2)}) %collective-permute-start.3) | collective-permute-done | bytes 524320 | tf_op jit(solution)/shard_map/ppermute | solution.py:541
  55.0 3.0 %first_block.7 = (f32[2,1024,128]{2,1,0:T(8,128)S(1)}, bf16[2,1024,128]{2,1,0:T(8,128)(2,1)S(1)}) custom-call(s32[1]{0:T(128)} %bitcast._.me_ref, bf16[2,1024,128]{2,1,0:T(8,128)(2,1)S(1)} %collective-permute-done.3.keys_ref.refs_1_, f32[2,1,1024]{2,1,0:T(1,128)S(1)} %get-tuple-element.80.tot_ref, ...), custom_call_target="tpu_custom_call", output_to_operand_aliasing={{0}: (4, {})} | custom-call | tf_op jit(solution)/shard_map/first_block/pallas_call | solution.py:349
  58.0 5.3 %raw_weights.1 = (bf16[2,1024,4096]{2,1,0:T(8,128)(2,1)S(1)}, f32[2,1,4096]{2,1,0:T(1,128)S(1)}) custom-call(f32[2,1024,128]{2,1,0:T(8,128)S(1)} %get-tuple-element.54.sums_ref, bf16[2,1024,128]{2,1,0:T(8,128)(2,1)S(1)} %get-tuple-element.55.refs_0_.refs_4_, bf16[2,1024,128]{2,1,0:T(8,128)(2,1)S(1)} %get-tuple-element.56.refs_1_.refs_5_, ...), custom_call_target="tpu_custom_call" | custom-call | tf_op jit(solution)/shard_map/raw_weights/pallas_call | solution.py:386
  63.2 0.0 collective-permute-done.7.refs_3_
  63.2 1.6 %collective-permute-start.10 = (f32[2,1,4096]{2,1,0:T(1,128)S(1)}, f32[2,1,4096]{2,1,0:T(1,128)S(1)}, u32[]{:S(2)}, u32[]{:S(2)}) collective-permute-start(f32[2,1,4096]{2,1,0:T(1,128)S(1)} %get-tuple-element.62.refs_0_), channel_id=1, source_target_pairs={{0,12},{4,8},{8,4},{12,0},{1,13},{5,9},{9,5},{13,1},{2,14},{6,10},... | collective-permute-start | bytes 98312 | tf_op jit(solution)/shard_map/ppermute | solution.py:541
  64.8 0.0 collective-permute-start.9
  64.8 2.9 %collective-permute-start.8 = (f32[2,1,4096]{2,1,0:T(1,128)S(1)}, f32[2,1,4096]{2,1,0:T(1,128)S(1)}, u32[]{:S(2)}, u32[]{:S(2)}) collective-permute-start(f32[2,1,4096]{2,1,0:T(1,128)S(1)} %get-tuple-element.62.refs_0_), channel_id=1, source_target_pairs={{0,4},{4,0},{8,12},{12,8},{1,5},{5,1},{9,13},{13,9},{2,6},{6,2},{1... | collective-permute-start | bytes 98312 | tf_op jit(solution)/shard_map/ppermute | solution.py:541
  67.7 3.8 %place.2.refs_4_ = bf16[2,2048,256]{2,1,0:T(8,128)(2,1)S(1)} custom-call(s32[5,2,4]{2,1,0:T(2,128)S(1)} %constant_dynamic-update-slice_fusion.scalar_ref, f32[2,4,1024]{2,1,0:T(4,128)S(1)} %pad_maximum_fusion.label_ref, bf16[2,1024,128]{2,1,0:T(8,128)(2,1)S(1)} %get-tuple-element.66.keys_ref.refs_0_, ...), custom_call_target="tpu_custom_call" | custom-call | tf_op jit(solution)/shard_map/place/pallas_call | solution.py:520
  71.5 0.0 collective-permute-done.11.refs_2_
  71.5 0.0 collective-permute-done.12.refs_3_
  71.5 5.0 %place.3 = (bf16[4096,128]{1,0:T(8,128)(2,1)}, bf16[4096,128]{1,0:T(8,128)(2,1)}) custom-call(s32[5,2,4]{2,1,0:T(2,128)S(1)} %constant_dynamic-update-slice_fusion.scalar_ref, f32[2,4,1024]{2,1,0:T(4,128)S(1)} %pad_maximum_fusion.label_ref, bf16[2,1024,128]{2,1,0:T(8,128)(2,1)S(1)} %collective-permute-done.1.keys_ref.refs_0_, ...), custom_call_target="tpu_custom_call" | custom-call | tf_op jit(solution)/shard_map/place/pallas_call | solution.py:520
  76.6 0.0 collective-permute-done.10.refs_3_
  76.6 0.0 collective-permute-done.9.refs_2_
  76.6 0.0 collective-permute-done.8.refs_1_
  76.6 6.1 %weighted_sums.1 = f32[2,1024,128]{2,1,0:T(8,128)} custom-call(bf16[2,1024,4096]{2,1,0:T(8,128)(2,1)S(1)} %get-tuple-element.59.raw_ref, f32[2,1,4096]{2,1,0:T(1,128)S(1)} %get-tuple-element.62.refs_0_, f32[2,1,4096]{2,1,0:T(1,128)S(1)} %collective-permute-done.8.refs_1_, f32[2,1,4096]{2,1,0:T(1,128)S(1)} %collective-permute-done.9.refs_2_, ...), custom_call_target="tpu_custom_call" | custom-call | tf_op jit(solution)/shard_map/weighted_sums/pallas_call | solution.py:424
  (14 shorter events, 0.2 us)
Async XLA Ops:
  0.6 19.7 %copy-start = (s32[2,5]{1,0:T(2,128)S(1)}, s32[2,5]{1,0:T(2,128)}, u32[]{:S(2)}) copy-start(s32[2,5]{1,0:T(2,128)} %param.8) | copy-start | bytes 124
  4.6 29.5 %collective-permute-start.1 = (bf16[2,1024,128]{2,1,0:T(8,128)(2,1)S(1)}, bf16[2,1024,128]{2,1,0:T(8,128)(2,1)S(1)}, u32[]{:S(2)}, u32[]{:S(2)}) collective-permute-start(bf16[2,1024,128]{2,1,0:T(8,128)(2,1)S(1)} %get-tuple-element.66.keys_ref.refs_0_), channel_id=1, source_target_pairs={{0,8},{4,12},{8,0},{12,4},{1,9},{5,13},{9,1},{13,5},{2,10},{6,14},... | collective-permute-start | bytes 1572872 | tf_op jit(solution)/shard_map/ppermute | solution.py:541
  8.8 25.4 %collective-permute-start = (bf16[2,1024,128]{2,1,0:T(8,128)(2,1)S(1)}, bf16[2,1024,128]{2,1,0:T(8,128)(2,1)S(1)}, u32[]{:S(2)}, u32[]{:S(2)}) collective-permute-start(bf16[2,1024,128]{2,1,0:T(8,128)(2,1)S(1)} %get-tuple-element.66.keys_ref.refs_0_), channel_id=1, source_target_pairs={{0,4},{4,0},{8,12},{12,8},{1,5},{5,1},{9,13},{13,9},{2,6},{6,2},{1... | collective-permute-start | bytes 1572872 | tf_op jit(solution)/shard_map/ppermute | solution.py:541
  10.3 1.8 %collective-permute-start.2 = (f32[2,1,128]{2,1,0:T(1,128)S(1)}, f32[2,1,128]{2,1,0:T(1,128)S(1)}, u32[]{:S(2)}, u32[]{:S(2)}) collective-permute-start(f32[2,1,128]{2,1,0:T(1,128)S(1)} %slice.21), channel_id=1, source_target_pairs={{0,1},{1,0},{2,3},{3,2},{4,5},{5,4},{6,7},{7,6},{8,9},{9,8},{10,11... | collective-permute-start | bytes 3080 | tf_op jit(solution)/shard_map/ppermute | solution.py:559
  19.9 12.9 %collective-permute-start.6 = (f32[2,2,1024]{2,1,0:T(2,128)S(1)}, f32[2,2,1024]{2,1,0:T(2,128)S(1)}, u32[]{:S(2)}, u32[]{:S(2)}) collective-permute-start(f32[2,2,1024]{2,1,0:T(2,128)S(1)} %pad_maximum_fusion.1), channel_id=1, source_target_pairs={{0,8},{4,12},{8,0},{12,4},{1,9},{5,13},{9,1},{13,5},{2,10},{6,14},... | collective-permute-start | bytes 49160 | tf_op jit(solution)/shard_map/ppermute | solution.py:541
  22.9 10.2 %collective-permute-start.5 = (f32[2,2,1024]{2,1,0:T(2,128)S(1)}, f32[2,2,1024]{2,1,0:T(2,128)S(1)}, u32[]{:S(2)}, u32[]{:S(2)}) collective-permute-start(f32[2,2,1024]{2,1,0:T(2,128)S(1)} %pad_maximum_fusion.1), channel_id=1, source_target_pairs={{0,4},{4,0},{8,12},{12,8},{1,5},{5,1},{9,13},{13,9},{2,6},{6,2},{1... | collective-permute-start | bytes 49160 | tf_op jit(solution)/shard_map/ppermute | solution.py:541
  23.2 10.9 %collective-permute-start.4 = (f32[2,2,1024]{2,1,0:T(2,128)S(1)}, f32[2,2,1024]{2,1,0:T(2,128)S(1)}, u32[]{:S(2)}, u32[]{:S(2)}) collective-permute-start(f32[2,2,1024]{2,1,0:T(2,128)S(1)} %pad_maximum_fusion.1), channel_id=1, source_target_pairs={{0,12},{4,8},{8,4},{12,0},{1,13},{5,9},{9,5},{13,1},{2,14},{6,10},... | collective-permute-start | bytes 49160 | tf_op jit(solution)/shard_map/ppermute | solution.py:541
  34.5 20.5 %collective-permute-start.3 = (bf16[2,1024,128]{2,1,0:T(8,128)(2,1)S(1)}, bf16[2,1024,128]{2,1,0:T(8,128)(2,1)S(1)}, u32[]{:S(2)}, u32[]{:S(2)}) collective-permute-start(bf16[2,1024,128]{2,1,0:T(8,128)(2,1)S(1)} %collective-permute-done.1.keys_ref.refs_0_), channel_id=1, source_target_pairs={{0,4},{4,0},{8,12},{12,8},{1,5},{5,1},{9,13},{13,9},{2,6},{6,2},{1... | collective-permute-start | bytes 1572872 | tf_op jit(solution)/shard_map/ppermute | solution.py:541
  40.5 22.7 %collective-permute-start.7 = (bf16[2,544,128]{2,1,0:T(8,128)(2,1)S(1)}, bf16[2,544,128]{2,1,0:T(8,128)(2,1)S(1)}, u32[]{:S(2)}, u32[]{:S(2)}) collective-permute-start(bf16[2,544,128]{2,1,0:T(8,128)(2,1)S(1)} %get-tuple-element.60), channel_id=1, source_target_pairs={{0,4},{4,0},{8,12},{12,8},{1,5},{5,1},{9,13},{13,9},{2,6},{6,2},{1... | collective-permute-start | bytes 835592 | tf_op jit(solution)/shard_map/ppermute | solution.py:541
  45.0 26.5 %collective-permute-start.11 = (bf16[2,544,128]{2,1,0:T(8,128)(2,1)S(1)}, bf16[2,544,128]{2,1,0:T(8,128)(2,1)S(1)}, u32[]{:S(2)}, u32[]{:S(2)}) collective-permute-start(bf16[2,544,128]{2,1,0:T(8,128)(2,1)S(1)} %get-tuple-element.64), channel_id=1, source_target_pairs={{0,8},{4,12},{8,0},{12,4},{1,9},{5,13},{9,1},{13,5},{2,10},{6,14},... | collective-permute-start | bytes 835592 | tf_op jit(solution)/shard_map/ppermute | solution.py:541
  47.0 24.5 %collective-permute-start.12 = (bf16[2,544,128]{2,1,0:T(8,128)(2,1)S(1)}, bf16[2,544,128]{2,1,0:T(8,128)(2,1)S(1)}, u32[]{:S(2)}, u32[]{:S(2)}) collective-permute-start(bf16[2,544,128]{2,1,0:T(8,128)(2,1)S(1)} %get-tuple-element.65), channel_id=1, source_target_pairs={{0,12},{4,8},{8,4},{12,0},{1,13},{5,9},{9,5},{13,1},{2,14},{6,10},... | collective-permute-start | bytes 835592 | tf_op jit(solution)/shard_map/ppermute | solution.py:541
  63.2 13.3 %collective-permute-start.10 = (f32[2,1,4096]{2,1,0:T(1,128)S(1)}, f32[2,1,4096]{2,1,0:T(1,128)S(1)}, u32[]{:S(2)}, u32[]{:S(2)}) collective-permute-start(f32[2,1,4096]{2,1,0:T(1,128)S(1)} %get-tuple-element.62.refs_0_), channel_id=1, source_target_pairs={{0,12},{4,8},{8,4},{12,0},{1,13},{5,9},{9,5},{13,1},{2,14},{6,10},... | collective-permute-start | bytes 98312 | tf_op jit(solution)/shard_map/ppermute | solution.py:541
  64.8 11.8 %collective-permute-start.9 = (f32[2,1,4096]{2,1,0:T(1,128)S(1)}, f32[2,1,4096]{2,1,0:T(1,128)S(1)}, u32[]{:S(2)}, u32[]{:S(2)}) collective-permute-start(f32[2,1,4096]{2,1,0:T(1,128)S(1)} %get-tuple-element.62.refs_0_), channel_id=1, source_target_pairs={{0,8},{4,12},{8,0},{12,4},{1,9},{5,13},{9,1},{13,5},{2,10},{6,14},... | collective-permute-start | bytes 98312 | tf_op jit(solution)/shard_map/ppermute | solution.py:541
  64.8 11.8 %collective-permute-start.8 = (f32[2,1,4096]{2,1,0:T(1,128)S(1)}, f32[2,1,4096]{2,1,0:T(1,128)S(1)}, u32[]{:S(2)}, u32[]{:S(2)}) collective-permute-start(f32[2,1,4096]{2,1,0:T(1,128)S(1)} %get-tuple-element.62.refs_0_), channel_id=1, source_target_pairs={{0,4},{4,0},{8,12},{12,8},{1,5},{5,1},{9,13},{13,9},{2,6},{6,2},{1... | collective-permute-start | bytes 98312 | tf_op jit(solution)/shard_map/ppermute | solution.py:541

commit v11 on v10

--- a/solution.py
+++ b/solution.py
@@ -589,22 +589,29 @@
     own_windows = list(
         windows(aligned(own_below, send_size), ranks, own_values, send_size, own_labels)
     )
+    late = [2]
+    early = [d for d in range(1, n) if d not in late]
     values = {0: own_windows[0]}
+
+    def leave(group, x):
+        *leaving, x = lax.optimization_barrier((*(own_windows[d] for d in group), x))
+        for d, window in zip(group, leaving):
+            values[d] = swap(window, d)
+        return x
+
     for m in range(1, n):
-        group = {min(2, n - 1): [1], n - 1: list(range(2, n))}.get(m)
-        if group:
-            *leaving, sums = lax.optimization_barrier((*(own_windows[d] for d in group), sums))
-            for d, window in zip(group, leaving):
-                values[d] = swap(window, d)
+        if m == min(2, n - 1):
+            sums = leave(early, sums)
         sums, unit = first_block(me_array, keys[m], totals[m], cents, n, sums)
         units.append(unit)
+    sums = leave(late, sums)
 
     raw, part = raw_weights(sums, units)
-    values[1], scalars, part = lax.optimization_barrier((values[1], scalars, part))
+    scalars, part = lax.optimization_barrier((scalars, part))
     parts = spread(part)
-    so_far = place(scalars, labels, keys, values, [0, 1], key_size, cap, None)
+    so_far = place(scalars, labels, keys, values, [0, *early], key_size, cap, None)
     out = weighted_sums(raw, units, parts)
-    placed = place(scalars, labels, keys, values, list(range(2, n)), key_size, cap, so_far)
+    placed = place(scalars, labels, keys, values, late, key_size, cap, so_far)
     shape = (cap, heads, width)
     return out, placed[0].reshape(shape), placed[1].reshape(shape)
 

time: 83.1 us -> 83.4 us (level)
  waiting for transfers between devices: 9.79 us -> 8.84 us
    ppermute x12, waiting for transfers between devices: 9.78 us -> 8.84 us  [swap(): return lax.ppermute(x, 'ctx', [(i, i ^ d) for i in range(n)])]
    ppermute x12, starting transfers between devices: 19.8 us -> 20.6 us  [swap(): return lax.ppermute(x, 'ctx', [(i, i ^ d) for i in range(n)])]
  transfers between devices with their start and end apart: 13 -> 13, of which waited for: 4 -> 5; matrix products, arithmetic and copies ran while one was open for 3% -> 3% of each run, Pallas kernels for 48% -> 51%
where the time goes in v11:
time: 83.4 us; the launch traced here: 83.2 us
  Pallas kernels  50.1 us (60%)
  starting transfers between devices  20.6 us (25%)
  waiting for transfers between devices  8.84 us (11%)
  local copies, waits for them, and re-layouts  1.92 us (2%)
  between operations  1.05 us (1%)
    ppermute x12, starting transfers between devices, swap(): return lax.ppermute(x, 'ctx', [(i, i ^ d) for i in range(n)])  20.6 us
    pallas_call x4, Pallas kernels, first_block(): pl.pallas_call(functools.partial(first_kernel, fresh), grid_spec=pltpu.Pr...  13 us
    pallas_call x2, Pallas kernels, place(): pl.pallas_call(functools.partial(place_kernel, ids, size, fresh), in_spec...  9.39 us
    ppermute x12, waiting for transfers between devices, swap(): return lax.ppermute(x, 'ctx', [(i, i ^ d) for i in range(n)])  8.84 us
    pallas_call x1, Pallas kernels, own_totals(): pl.pallas_call(totals_kernel, grid=(heads, count // rows), in_specs=[in_v...  7.74 us
    pallas_call x1, Pallas kernels, weighted_sums(): pl.pallas_call(functools.partial(sums_kernel, len(units)), in_specs=[in_v...  6.06 us
    pallas_call x1, Pallas kernels, raw_weights(): pl.pallas_call(functools.partial(raw_kernel, len(units)), grid=(heads,),...  5.13 us
    pallas_call x1, Pallas kernels, sort_keys(): pl.pallas_call(sort_kernel, in_specs=[anywhere()] * 2, out_specs=(in_vmem...  4 us
  transfers between devices with their start and end apart: 13, of which 5 were waited for; matrix products, arithmetic and copies ran while one was open for 3% of the time, Pallas kernels for 51%

profile of v11, /device:TPU:0, one launch (start us, length us, event | category | flops | bytes accessed | tf_op | source)
XLA Modules:
  0.0 83.2 jit_solution(6847828309927487645)
XLA Ops:
  0.6 0.0 copy-start
  0.6 4.0 %sort_keys.1 = (bf16[2,1024,128]{2,1,0:T(8,128)(2,1)S(1)}, f32[2,1,1024]{2,1,0:T(1,128)S(1)}, s32[2,1,1024]{2,1,0:T(1,128)S(1)}) custom-call(s32[2,1024]{1,0:T(2,128)} %label_hbm.1, bf16[2048,128]{1,0:T(8,128)(2,1)} %bitcast.26), custom_call_target="tpu_custom_call" | custom-call | tf_op jit(solution)/shard_map/sort_keys/pallas_call | solution.py:135
  4.6 3.1 %collective-permute-start.4 = (bf16[2,1024,128]{2,1,0:T(8,128)(2,1)S(1)}, bf16[2,1024,128]{2,1,0:T(8,128)(2,1)S(1)}, u32[]{:S(2)}, u32[]{:S(2)}) collective-permute-start(bf16[2,1024,128]{2,1,0:T(8,128)(2,1)S(1)} %get-tuple-element.63.keys_ref.refs_0_), channel_id=1, source_target_pairs={{0,4},{4,0},{8,12},{12,8},{1,5},{5,1},{9,13},{13,9},{2,6},{6,2},{1... | collective-permute-start | bytes 1572872 | tf_op jit(solution)/shard_map/ppermute | solution.py:541
  7.7 2.6 %collective-permute-start.5 = (bf16[2,1024,128]{2,1,0:T(8,128)(2,1)S(1)}, bf16[2,1024,128]{2,1,0:T(8,128)(2,1)S(1)}, u32[]{:S(2)}, u32[]{:S(2)}) collective-permute-start(bf16[2,1024,128]{2,1,0:T(8,128)(2,1)S(1)} %get-tuple-element.63.keys_ref.refs_0_), channel_id=1, source_target_pairs={{0,8},{4,12},{8,0},{12,4},{1,9},{5,13},{9,1},{13,5},{2,10},{6,14},... | collective-permute-start | bytes 1572872 | tf_op jit(solution)/shard_map/ppermute | solution.py:541
  10.3 0.0 collective-permute-start
  10.4 0.8 copy.13
  11.1 0.6 gather_fusion
  11.7 0.1 convert_bitcast_fusion
  11.8 0.1 copy.14
  11.9 0.2 convert_reduce_fusion.2
  12.1 0.0 collective-permute-done._
  12.1 7.7 %own_totals.1.tot_ref = f32[2,1,1024]{2,1,0:T(1,128)S(1)} custom-call(bf16[2,1024,128]{2,1,0:T(8,128)(2,1)S(1)} %get-tuple-element.63.keys_ref.refs_0_, f32[2,4096,128]{2,1,0:T(8,128)} %cent_in.1, f32[2,1,128]{2,1,0:T(1,128)S(1)} %collective-permute-done._), custom_call_target="tpu_custom_call" | custom-call | tf_op jit(solution)/shard_map/own_totals/pallas_call | solution.py:279
  19.9 0.1 collective-permute-start.3
  20.0 0.0 copy-done
  20.0 0.2 dynamic-slice_reduce_fusion
  20.2 2.4 %sort_values.1.values_ref = bf16[2,1024,128]{2,1,0:T(8,128)(2,1)S(1)} custom-call(s32[2,1,1024]{2,1,0:T(1,128)S(1)} %get-tuple-element.41.spot_ref, bf16[2048,128]{1,0:T(8,128)(2,1)} %bitcast.27), custom_call_target="tpu_custom_call" | custom-call | tf_op jit(solution)/shard_map/sort_values/pallas_call | solution.py:173
  22.6 2.0 %collective-permute-start.2 = (f32[2,2,1024]{2,1,0:T(2,128)S(1)}, f32[2,2,1024]{2,1,0:T(2,128)S(1)}, u32[]{:S(2)}, u32[]{:S(2)}) collective-permute-start(f32[2,2,1024]{2,1,0:T(2,128)S(1)} %pad_maximum_fusion.1), channel_id=1, source_target_pairs={{0,8},{4,12},{8,0},{12,4},{1,9},{5,13},{9,1},{13,5},{2,10},{6,14},... | collective-permute-start | bytes 49160 | tf_op jit(solution)/shard_map/ppermute | solution.py:541
  24.5 2.5 %collective-permute-start.1 = (f32[2,2,1024]{2,1,0:T(2,128)S(1)}, f32[2,2,1024]{2,1,0:T(2,128)S(1)}, u32[]{:S(2)}, u32[]{:S(2)}) collective-permute-start(f32[2,2,1024]{2,1,0:T(2,128)S(1)} %pad_maximum_fusion.1), channel_id=1, source_target_pairs={{0,4},{4,0},{8,12},{12,8},{1,5},{5,1},{9,13},{13,9},{2,6},{6,2},{1... | collective-permute-start | bytes 49160 | tf_op jit(solution)/shard_map/ppermute | solution.py:541
  27.0 4.1 %first_block.4 = (f32[2,1024,128]{2,1,0:T(8,128)S(1)}, bf16[2,1024,128]{2,1,0:T(8,128)(2,1)S(1)}, bf16[2,1024,128]{2,1,0:T(8,128)(2,1)S(1)}) custom-call(s32[1]{0:T(128)} %bitcast.3._.me_ref, bf16[2,1024,128]{2,1,0:T(8,128)(2,1)S(1)} %get-tuple-element.63.keys_ref.refs_0_, f32[2,1,1024]{2,1,0:T(1,128)S(1)} %own_totals.1.tot_ref, f32[2,4096,128]{2,1,0:T(8,128)} %cent_in.1), custom_call_target="tpu_custom_call" | custom-call | tf_op jit(solution)/shard_map/first_block/pallas_call | solution.py:349
  31.1 2.7 %collective-permute-done.3 = f32[2,2,1024]{2,1,0:T(2,128)S(1)} collective-permute-done((f32[2,2,1024]{2,1,0:T(2,128)S(1)}, f32[2,2,1024]{2,1,0:T(2,128)S(1)}, u32[]{:S(2)}, u32[]{:S(2)}) %collective-permute-start.3) | collective-permute-done | bytes 16416 | tf_op jit(solution)/shard_map/ppermute | solution.py:541
  33.9 0.9 %collective-permute-done.2 = f32[2,2,1024]{2,1,0:T(2,128)S(1)} collective-permute-done((f32[2,2,1024]{2,1,0:T(2,128)S(1)}, f32[2,2,1024]{2,1,0:T(2,128)S(1)}, u32[]{:S(2)}, u32[]{:S(2)}) %collective-permute-start.2) | collective-permute-done | bytes 16416 | tf_op jit(solution)/shard_map/ppermute | solution.py:541
  34.7 0.0 collective-permute-done.1
  34.8 0.0 collective-permute-done.4.keys_ref.refs_1_
  34.8 0.0 collective-permute-done.5.keys_ref.refs_0_
  34.8 0.5 collective-permute-start.6
  35.3 0.3 convert_reduce_fusion
  35.6 1.8 %own_ranks.1.rank_ref = f32[2,1,1024]{2,1,0:T(1,128)S(1)} custom-call(s32[1]{0:T(128)} %bitcast.3._.me_ref, f32[2,4,1024]{2,1,0:T(4,128)S(1)} %pad_maximum_fusion.label_ref), custom_call_target="tpu_custom_call" | custom-call | tf_op jit(solution)/shard_map/own_ranks/pallas_call | solution.py:239
  37.4 0.6 windows.1
  38.0 3.0 %first_block.5 = (f32[2,1024,128]{2,1,0:T(8,128)S(1)}, bf16[2,1024,128]{2,1,0:T(8,128)(2,1)S(1)}) custom-call(s32[1]{0:T(128)} %bitcast.3._.me_ref, bf16[2,1024,128]{2,1,0:T(8,128)(2,1)S(1)} %collective-permute-done.4.keys_ref.refs_1_, f32[2,1,1024]{2,1,0:T(1,128)S(1)} %get-tuple-element.73.tot_ref, ...), custom_call_target="tpu_custom_call", output_to_operand_aliasing={{0}: (4, {})} | custom-call | tf_op jit(solution)/shard_map/first_block/pallas_call | solution.py:349
  41.0 1.7 %collective-permute-start.11 = (bf16[2,544,128]{2,1,0:T(8,128)(2,1)S(1)}, bf16[2,544,128]{2,1,0:T(8,128)(2,1)S(1)}, u32[]{:S(2)}, u32[]{:S(2)}) collective-permute-start(bf16[2,544,128]{2,1,0:T(8,128)(2,1)S(1)} %get-tuple-element.65), channel_id=1, source_target_pairs={{0,4},{4,0},{8,12},{12,8},{1,5},{5,1},{9,13},{13,9},{2,6},{6,2},{1... | collective-permute-start | bytes 835592 | tf_op jit(solution)/shard_map/ppermute | solution.py:541
  42.7 2.5 %collective-permute-start.12 = (bf16[2,544,128]{2,1,0:T(8,128)(2,1)S(1)}, bf16[2,544,128]{2,1,0:T(8,128)(2,1)S(1)}, u32[]{:S(2)}, u32[]{:S(2)}) collective-permute-start(bf16[2,544,128]{2,1,0:T(8,128)(2,1)S(1)} %get-tuple-element.66), channel_id=1, source_target_pairs={{0,12},{4,8},{8,4},{12,0},{1,13},{5,9},{9,5},{13,1},{2,14},{6,10},... | collective-permute-start | bytes 835592 | tf_op jit(solution)/shard_map/ppermute | solution.py:541
  45.1 3.0 %first_block.6 = (f32[2,1024,128]{2,1,0:T(8,128)S(1)}, bf16[2,1024,128]{2,1,0:T(8,128)(2,1)S(1)}) custom-call(s32[1]{0:T(128)} %bitcast.3._.me_ref, bf16[2,1024,128]{2,1,0:T(8,128)(2,1)S(1)} %collective-permute-done.5.keys_ref.refs_0_, f32[2,1,1024]{2,1,0:T(1,128)S(1)} %get-tuple-element.75.tot_ref, ...), custom_call_target="tpu_custom_call", output_to_operand_aliasing={{0}: (4, {})} | custom-call | tf_op jit(solution)/shard_map/first_block/pallas_call | solution.py:349
  48.1 0.1 constant_dynamic-update-slice_fusion.2
  48.2 1.5 %collective-permute-done.6.keys_ref.refs_2_ = bf16[2,1024,128]{2,1,0:T(8,128)(2,1)S(1)} collective-permute-done((bf16[2,1024,128]{2,1,0:T(8,128)(2,1)S(1)}, bf16[2,1024,128]{2,1,0:T(8,128)(2,1)S(1)}, u32[]{:S(2)}, u32[]{:S(2)}) %collective-permute-start.6) | collective-permute-done | bytes 524320 | tf_op jit(solution)/shard_map/ppermute | solution.py:541
  49.7 3.0 %first_block.7 = (f32[2,1024,128]{2,1,0:T(8,128)S(1)}, bf16[2,1024,128]{2,1,0:T(8,128)(2,1)S(1)}) custom-call(s32[1]{0:T(128)} %bitcast.3._.me_ref, bf16[2,1024,128]{2,1,0:T(8,128)(2,1)S(1)} %collective-permute-done.6.keys_ref.refs_2_, f32[2,1,1024]{2,1,0:T(1,128)S(1)} %get-tuple-element.77.tot_ref, ...), custom_call_target="tpu_custom_call", output_to_operand_aliasing={{0}: (4, {})} | custom-call | tf_op jit(solution)/shard_map/first_block/pallas_call | solution.py:349
  52.7 1.5 %collective-permute-start.10 = (bf16[2,544,128]{2,1,0:T(8,128)(2,1)S(1)}, bf16[2,544,128]{2,1,0:T(8,128)(2,1)S(1)}, u32[]{:S(2)}, u32[]{:S(2)}) collective-permute-start(bf16[2,544,128]{2,1,0:T(8,128)(2,1)S(1)} %get-tuple-element.62), channel_id=1, source_target_pairs={{0,8},{4,12},{8,0},{12,4},{1,9},{5,13},{9,1},{13,5},{2,10},{6,14},... | collective-permute-start | bytes 835592 | tf_op jit(solution)/shard_map/ppermute | solution.py:541
  54.2 0.1 constant_dynamic-update-slice_fusion.1
  54.3 0.1 constant_dynamic-update-slice_fusion.scalar_ref
  54.4 5.1 %raw_weights.1 = (bf16[2,1024,4096]{2,1,0:T(8,128)(2,1)S(1)}, f32[2,1,4096]{2,1,0:T(1,128)S(1)}) custom-call(f32[2,1024,128]{2,1,0:T(8,128)S(1)} %get-tuple-element.53.sums_ref, bf16[2,1024,128]{2,1,0:T(8,128)(2,1)S(1)} %get-tuple-element.54.refs_0_.refs_4_, bf16[2,1024,128]{2,1,0:T(8,128)(2,1)S(1)} %get-tuple-element.55.refs_1_.refs_5_, ...), custom_call_target="tpu_custom_call" | custom-call | tf_op jit(solution)/shard_map/raw_weights/pallas_call | solution.py:386
  59.5 1.7 %collective-permute-start.7 = (f32[2,1,4096]{2,1,0:T(1,128)S(1)}, f32[2,1,4096]{2,1,0:T(1,128)S(1)}, u32[]{:S(2)}, u32[]{:S(2)}) collective-permute-start(f32[2,1,4096]{2,1,0:T(1,128)S(1)} %get-tuple-element.60.refs_0_), channel_id=1, source_target_pairs={{0,4},{4,0},{8,12},{12,8},{1,5},{5,1},{9,13},{13,9},{2,6},{6,2},{1... | collective-permute-start | bytes 98312 | tf_op jit(solution)/shard_map/ppermute | solution.py:541
  61.2 0.3 collective-permute-start.8
  61.5 0.2 collective-permute-done.11.refs_4_
  61.6 2.3 %collective-permute-start.9 = (f32[2,1,4096]{2,1,0:T(1,128)S(1)}, f32[2,1,4096]{2,1,0:T(1,128)S(1)}, u32[]{:S(2)}, u32[]{:S(2)}) collective-permute-start(f32[2,1,4096]{2,1,0:T(1,128)S(1)} %get-tuple-element.60.refs_0_), channel_id=1, source_target_pairs={{0,12},{4,8},{8,4},{12,0},{1,13},{5,9},{9,5},{13,1},{2,14},{6,10},... | collective-permute-start | bytes 98312 | tf_op jit(solution)/shard_map/ppermute | solution.py:541
  64.0 0.0 collective-permute-done.12.refs_5_
  64.0 5.6 %place.2.refs_2_ = bf16[2,2048,256]{2,1,0:T(8,128)(2,1)S(1)} custom-call(s32[5,2,4]{2,1,0:T(2,128)S(1)} %constant_dynamic-update-slice_fusion.scalar_ref, f32[2,4,1024]{2,1,0:T(4,128)S(1)} %pad_maximum_fusion.label_ref, bf16[2,1024,128]{2,1,0:T(8,128)(2,1)S(1)} %get-tuple-element.63.keys_ref.refs_0_, ...), custom_call_target="tpu_custom_call" | custom-call | tf_op jit(solution)/shard_map/place/pallas_call | solution.py:520
  69.6 0.0 collective-permute-done.7.refs_1_
  69.6 3.6 %collective-permute-done.8.refs_2_ = f32[2,1,4096]{2,1,0:T(1,128)S(1)} collective-permute-done((f32[2,1,4096]{2,1,0:T(1,128)S(1)}, f32[2,1,4096]{2,1,0:T(1,128)S(1)}, u32[]{:S(2)}, u32[]{:S(2)}) %collective-permute-start.8) | collective-permute-done | bytes 32800 | tf_op jit(solution)/shard_map/ppermute | solution.py:541
  73.1 0.0 collective-permute-done.9.refs_3_
  73.1 6.1 %weighted_sums.1 = f32[2,1024,128]{2,1,0:T(8,128)} custom-call(bf16[2,1024,4096]{2,1,0:T(8,128)(2,1)S(1)} %get-tuple-element.58.raw_ref, f32[2,1,4096]{2,1,0:T(1,128)S(1)} %get-tuple-element.60.refs_0_, f32[2,1,4096]{2,1,0:T(1,128)S(1)} %collective-permute-done.7.refs_1_, f32[2,1,4096]{2,1,0:T(1,128)S(1)} %collective-permute-done.8.refs_2_, ...), custom_call_target="tpu_custom_call" | custom-call | tf_op jit(solution)/shard_map/weighted_sums/pallas_call | solution.py:424
  79.2 0.0 collective-permute-done.10.refs_1_
  79.2 3.8 %place.3 = (bf16[4096,128]{1,0:T(8,128)(2,1)}, bf16[4096,128]{1,0:T(8,128)(2,1)}) custom-call(s32[5,2,4]{2,1,0:T(2,128)S(1)} %constant_dynamic-update-slice_fusion.scalar_ref, f32[2,4,1024]{2,1,0:T(4,128)S(1)} %pad_maximum_fusion.label_ref, bf16[2,1024,128]{2,1,0:T(8,128)(2,1)S(1)} %collective-permute-done.5.keys_ref.refs_0_, ...), custom_call_target="tpu_custom_call" | custom-call | tf_op jit(solution)/shard_map/place/pallas_call | solution.py:520
  (14 shorter events, 0.2 us)
Async XLA Ops:
  0.6 19.3 %copy-start = (s32[2,5]{1,0:T(2,128)S(1)}, s32[2,5]{1,0:T(2,128)}, u32[]{:S(2)}) copy-start(s32[2,5]{1,0:T(2,128)} %param.8) | copy-start | bytes 124
  4.6 30.2 %collective-permute-start.4 = (bf16[2,1024,128]{2,1,0:T(8,128)(2,1)S(1)}, bf16[2,1024,128]{2,1,0:T(8,128)(2,1)S(1)}, u32[]{:S(2)}, u32[]{:S(2)}) collective-permute-start(bf16[2,1024,128]{2,1,0:T(8,128)(2,1)S(1)} %get-tuple-element.63.keys_ref.refs_0_), channel_id=1, source_target_pairs={{0,4},{4,0},{8,12},{12,8},{1,5},{5,1},{9,13},{13,9},{2,6},{6,2},{1... | collective-permute-start | bytes 1572872 | tf_op jit(solution)/shard_map/ppermute | solution.py:541
  7.7 27.1 %collective-permute-start.5 = (bf16[2,1024,128]{2,1,0:T(8,128)(2,1)S(1)}, bf16[2,1024,128]{2,1,0:T(8,128)(2,1)S(1)}, u32[]{:S(2)}, u32[]{:S(2)}) collective-permute-start(bf16[2,1024,128]{2,1,0:T(8,128)(2,1)S(1)} %get-tuple-element.63.keys_ref.refs_0_), channel_id=1, source_target_pairs={{0,8},{4,12},{8,0},{12,4},{1,9},{5,13},{9,1},{13,5},{2,10},{6,14},... | collective-permute-start | bytes 1572872 | tf_op jit(solution)/shard_map/ppermute | solution.py:541
  10.3 1.8 %collective-permute-start = (f32[2,1,128]{2,1,0:T(1,128)S(1)}, f32[2,1,128]{2,1,0:T(1,128)S(1)}, u32[]{:S(2)}, u32[]{:S(2)}) collective-permute-start(f32[2,1,128]{2,1,0:T(1,128)S(1)} %slice.21), channel_id=1, source_target_pairs={{0,1},{1,0},{2,3},{3,2},{4,5},{5,4},{6,7},{7,6},{8,9},{9,8},{10,11... | collective-permute-start | bytes 3080 | tf_op jit(solution)/shard_map/ppermute | solution.py:559
  19.9 14.0 %collective-permute-start.3 = (f32[2,2,1024]{2,1,0:T(2,128)S(1)}, f32[2,2,1024]{2,1,0:T(2,128)S(1)}, u32[]{:S(2)}, u32[]{:S(2)}) collective-permute-start(f32[2,2,1024]{2,1,0:T(2,128)S(1)} %pad_maximum_fusion.1), channel_id=1, source_target_pairs={{0,12},{4,8},{8,4},{12,0},{1,13},{5,9},{9,5},{13,1},{2,14},{6,10},... | collective-permute-start | bytes 49160 | tf_op jit(solution)/shard_map/ppermute | solution.py:541
  22.6 12.1 %collective-permute-start.2 = (f32[2,2,1024]{2,1,0:T(2,128)S(1)}, f32[2,2,1024]{2,1,0:T(2,128)S(1)}, u32[]{:S(2)}, u32[]{:S(2)}) collective-permute-start(f32[2,2,1024]{2,1,0:T(2,128)S(1)} %pad_maximum_fusion.1), channel_id=1, source_target_pairs={{0,8},{4,12},{8,0},{12,4},{1,9},{5,13},{9,1},{13,5},{2,10},{6,14},... | collective-permute-start | bytes 49160 | tf_op jit(solution)/shard_map/ppermute | solution.py:541
  24.5 10.2 %collective-permute-start.1 = (f32[2,2,1024]{2,1,0:T(2,128)S(1)}, f32[2,2,1024]{2,1,0:T(2,128)S(1)}, u32[]{:S(2)}, u32[]{:S(2)}) collective-permute-start(f32[2,2,1024]{2,1,0:T(2,128)S(1)} %pad_maximum_fusion.1), channel_id=1, source_target_pairs={{0,4},{4,0},{8,12},{12,8},{1,5},{5,1},{9,13},{13,9},{2,6},{6,2},{1... | collective-permute-start | bytes 49160 | tf_op jit(solution)/shard_map/ppermute | solution.py:541
  34.8 14.9 %collective-permute-start.6 = (bf16[2,1024,128]{2,1,0:T(8,128)(2,1)S(1)}, bf16[2,1024,128]{2,1,0:T(8,128)(2,1)S(1)}, u32[]{:S(2)}, u32[]{:S(2)}) collective-permute-start(bf16[2,1024,128]{2,1,0:T(8,128)(2,1)S(1)} %collective-permute-done.5.keys_ref.refs_0_), channel_id=1, source_target_pairs={{0,4},{4,0},{8,12},{12,8},{1,5},{5,1},{9,13},{13,9},{2,6},{6,2},{1... | collective-permute-start | bytes 1572872 | tf_op jit(solution)/shard_map/ppermute | solution.py:541
  41.0 20.6 %collective-permute-start.11 = (bf16[2,544,128]{2,1,0:T(8,128)(2,1)S(1)}, bf16[2,544,128]{2,1,0:T(8,128)(2,1)S(1)}, u32[]{:S(2)}, u32[]{:S(2)}) collective-permute-start(bf16[2,544,128]{2,1,0:T(8,128)(2,1)S(1)} %get-tuple-element.65), channel_id=1, source_target_pairs={{0,4},{4,0},{8,12},{12,8},{1,5},{5,1},{9,13},{13,9},{2,6},{6,2},{1... | collective-permute-start | bytes 835592 | tf_op jit(solution)/shard_map/ppermute | solution.py:541
  42.7 21.3 %collective-permute-start.12 = (bf16[2,544,128]{2,1,0:T(8,128)(2,1)S(1)}, bf16[2,544,128]{2,1,0:T(8,128)(2,1)S(1)}, u32[]{:S(2)}, u32[]{:S(2)}) collective-permute-start(bf16[2,544,128]{2,1,0:T(8,128)(2,1)S(1)} %get-tuple-element.66), channel_id=1, source_target_pairs={{0,12},{4,8},{8,4},{12,0},{1,13},{5,9},{9,5},{13,1},{2,14},{6,10},... | collective-permute-start | bytes 835592 | tf_op jit(solution)/shard_map/ppermute | solution.py:541
  52.7 26.5 %collective-permute-start.10 = (bf16[2,544,128]{2,1,0:T(8,128)(2,1)S(1)}, bf16[2,544,128]{2,1,0:T(8,128)(2,1)S(1)}, u32[]{:S(2)}, u32[]{:S(2)}) collective-permute-start(bf16[2,544,128]{2,1,0:T(8,128)(2,1)S(1)} %get-tuple-element.62), channel_id=1, source_target_pairs={{0,8},{4,12},{8,0},{12,4},{1,9},{5,13},{9,1},{13,5},{2,10},{6,14},... | collective-permute-start | bytes 835592 | tf_op jit(solution)/shard_map/ppermute | solution.py:541
  59.5 10.0 %collective-permute-start.7 = (f32[2,1,4096]{2,1,0:T(1,128)S(1)}, f32[2,1,4096]{2,1,0:T(1,128)S(1)}, u32[]{:S(2)}, u32[]{:S(2)}) collective-permute-start(f32[2,1,4096]{2,1,0:T(1,128)S(1)} %get-tuple-element.60.refs_0_), channel_id=1, source_target_pairs={{0,4},{4,0},{8,12},{12,8},{1,5},{5,1},{9,13},{13,9},{2,6},{6,2},{1... | collective-permute-start | bytes 98312 | tf_op jit(solution)/shard_map/ppermute | solution.py:541
  61.2 11.9 %collective-permute-start.8 = (f32[2,1,4096]{2,1,0:T(1,128)S(1)}, f32[2,1,4096]{2,1,0:T(1,128)S(1)}, u32[]{:S(2)}, u32[]{:S(2)}) collective-permute-start(f32[2,1,4096]{2,1,0:T(1,128)S(1)} %get-tuple-element.60.refs_0_), channel_id=1, source_target_pairs={{0,8},{4,12},{8,0},{12,4},{1,9},{5,13},{9,1},{13,5},{2,10},{6,14},... | collective-permute-start | bytes 98312 | tf_op jit(solution)/shard_map/ppermute | solution.py:541
  61.6 11.5 %collective-permute-start.9 = (f32[2,1,4096]{2,1,0:T(1,128)S(1)}, f32[2,1,4096]{2,1,0:T(1,128)S(1)}, u32[]{:S(2)}, u32[]{:S(2)}) collective-permute-start(f32[2,1,4096]{2,1,0:T(1,128)S(1)} %get-tuple-element.60.refs_0_), channel_id=1, source_target_pairs={{0,12},{4,8},{8,4},{12,0},{1,13},{5,9},{9,5},{13,1},{2,14},{6,10},... | collective-permute-start | bytes 98312 | tf_op jit(solution)/shard_map/ppermute | solution.py:541

commit v12 on v11

--- a/solution.py
+++ b/solution.py
@@ -439,7 +439,8 @@
 def fill_windows(ids, size, scalar_ref, label_ref, keys, values, rows_ref, near_ref):
     heads, tokens, width = keys[0].shape
     digit_rows = tokens // LANES
-    sent = values[0].shape[1] - 2 * digit_rows
+    one = values[0][0] if isinstance(values[0], list) else values[0]
+    sent = one.shape[1] - 2 * digit_rows
     rows_ref[:, :, width:] = jnp.zeros((heads, len(ids) * size, width), BF16)
     for h in range(heads):
         low, high, first = (scalar_ref[i, h, 0].astype(F32) for i in range(2, 5))
@@ -448,8 +449,9 @@
             gap = pl.multiple_of(scalar_ref[1, h, m], 16)
             here = i * size
             rows_ref[h, here : here + size, :width] = keys[i][h, pl.ds(start, size), :]
-            rows_ref[h, pl.ds(here + gap, sent), width:] = values[i][h, :sent, :]
-            digits = values[i][h, sent:, :].astype(F32)
+            value = values[i][h][0] if isinstance(values[i], list) else values[i][h]
+            rows_ref[h, pl.ds(here + gap, sent), width:] = value[:sent]
+            digits = value[sent:].astype(F32)
             rank = digits[:digit_rows] * 128.0 + digits[digit_rows:]
             rank = jnp.concatenate([rank[r : r + 1] for r in range(digit_rows)], axis=1)
             label = label_ref[h, m : m + 1, :]
@@ -461,7 +463,12 @@
 
 def place_kernel(ids, size, fresh, scalar_ref, label_ref, *refs):
     count = len(ids)
-    keys, values, refs = refs[:count], refs[count : 2 * count], refs[2 * count :]
+    keys, refs = refs[:count], refs[count:]
+    if fresh:
+        values, refs = refs[:count], refs[count:]
+    else:
+        heads = keys[0].shape[0]
+        values, refs = [list(refs[:heads])], refs[heads:]
     if fresh:
         so_far_ref, rows_ref, near_ref = refs
     else:
@@ -469,7 +476,7 @@
     fill_windows(ids, size, scalar_ref, label_ref, keys, values, rows_ref, near_ref)
     heads, cap, both = so_far_ref.shape
     width = both // 2
-    rows = 512
+    rows = 1024 if fresh else 512
     copies = []
     for r in range(0, cap, rows):
         for h in range(heads):
@@ -500,7 +507,7 @@
 def place(scalars, labels, keys, values, ids, size, cap, so_far):
     heads, _, width = keys[0].shape
     fresh = so_far is None
-    moved = [x[m] for x in (keys, values) for m in ids]
+    moved = [keys[m] for m in ids] + ([values[m] for m in ids] if fresh else values[ids[0]])
     scratch = [
         pltpu.VMEM((heads, len(ids) * size, 2 * width), BF16),
         pltpu.VMEM((heads, 1, len(ids) * size), jnp.int32),
@@ -604,11 +611,15 @@
             sums = leave(early, sums)
         sums, unit = first_block(me_array, keys[m], totals[m], cents, n, sums)
         units.append(unit)
-    sums = leave(late, sums)
+    pieces = [own_windows[late[0]][h : h + 1] for h in range(heads)]
+    pieces[0], sums = lax.optimization_barrier((pieces[0], sums))
+    values[late[0]] = [swap(pieces[0], late[0])]
 
     raw, part = raw_weights(sums, units)
     scalars, part = lax.optimization_barrier((scalars, part))
     parts = spread(part)
+    *parts, pieces[-1] = lax.optimization_barrier((*parts, pieces[-1]))
+    values[late[0]] += [swap(piece, late[0]) for piece in pieces[1:]]
     so_far = place(scalars, labels, keys, values, [0, *early], key_size, cap, None)
     out = weighted_sums(raw, units, parts)
     placed = place(scalars, labels, keys, values, late, key_size, cap, so_far)

time: 83.4 us -> 88.5 us (1.061)
  starting transfers between devices: 20.6 us -> 23.9 us
  waiting for transfers between devices: 8.84 us -> 10.5 us
    ppermute x12 -> x13, starting transfers between devices: 20.6 us -> 23.9 us  [swap(): return lax.ppermute(x, 'ctx', [(i, i ^ d) for i in range(n)])]
    ppermute x12 -> x13, waiting for transfers between devices: 8.84 us -> 10.5 us  [swap(): return lax.ppermute(x, 'ctx', [(i, i ^ d) for i in range(n)])]
  transfers between devices with their start and end apart: 13 -> 14, of which waited for: 5 -> 4; matrix products, arithmetic and copies ran while one was open for 3% -> 3% of each run, Pallas kernels for 51% -> 46%
where the time goes in v12:
time: 88.5 us; the launch traced here: 88.3 us
  Pallas kernels  50.2 us (57%)
  starting transfers between devices  23.9 us (27%)
  waiting for transfers between devices  10.5 us (12%)
  local copies, waits for them, and re-layouts  1.94 us (2%)
  between operations  1.06 us (1%)
    ppermute x13, starting transfers between devices, swap(): return lax.ppermute(x, 'ctx', [(i, i ^ d) for i in range(n)])  23.9 us
    pallas_call x4, Pallas kernels, first_block(): pl.pallas_call(functools.partial(first_kernel, fresh), grid_spec=pltpu.Pr...  13 us
    ppermute x13, waiting for transfers between devices, swap(): return lax.ppermute(x, 'ctx', [(i, i ^ d) for i in range(n)])  10.5 us
    pallas_call x2, Pallas kernels, place(): pl.pallas_call(functools.partial(place_kernel, ids, size, fresh), in_spec...  9.39 us
    pallas_call x1, Pallas kernels, own_totals(): pl.pallas_call(totals_kernel, grid=(heads, count // rows), in_specs=[in_v...  7.74 us
    pallas_call x1, Pallas kernels, weighted_sums(): pl.pallas_call(functools.partial(sums_kernel, len(units)), in_specs=[in_v...  6.06 us
    pallas_call x1, Pallas kernels, raw_weights(): pl.pallas_call(functools.partial(raw_kernel, len(units)), grid=(heads,),...  5.26 us
    pallas_call x1, Pallas kernels, sort_keys(): pl.pallas_call(sort_kernel, in_specs=[anywhere()] * 2, out_specs=(in_vmem...  4 us
  transfers between devices with their start and end apart: 14, of which 4 were waited for; matrix products, arithmetic and copies ran while one was open for 3% of the time, Pallas kernels for 46%

profile of v12, /device:TPU:0, one launch (start us, length us, event | category | flops | bytes accessed | tf_op | source)
XLA Modules:
  0.0 88.3 jit_solution(13718225597831951908)
XLA Ops:
  0.6 0.0 copy-start
  0.6 4.0 %sort_keys.1 = (bf16[2,1024,128]{2,1,0:T(8,128)(2,1)S(1)}, f32[2,1,1024]{2,1,0:T(1,128)S(1)}, s32[2,1,1024]{2,1,0:T(1,128)S(1)}) custom-call(s32[2,1024]{1,0:T(2,128)} %label_hbm.1, bf16[2048,128]{1,0:T(8,128)(2,1)} %bitcast.26), custom_call_target="tpu_custom_call" | custom-call | tf_op jit(solution)/shard_map/sort_keys/pallas_call | solution.py:135
  4.6 3.1 %collective-permute-start.4 = (bf16[2,1024,128]{2,1,0:T(8,128)(2,1)S(1)}, bf16[2,1024,128]{2,1,0:T(8,128)(2,1)S(1)}, u32[]{:S(2)}, u32[]{:S(2)}) collective-permute-start(bf16[2,1024,128]{2,1,0:T(8,128)(2,1)S(1)} %get-tuple-element.73.keys_ref.refs_0_), channel_id=1, source_target_pairs={{0,4},{4,0},{8,12},{12,8},{1,5},{5,1},{9,13},{13,9},{2,6},{6,2},{1... | collective-permute-start | bytes 1572872 | tf_op jit(solution)/shard_map/ppermute | solution.py:548
  7.7 2.6 %collective-permute-start.5 = (bf16[2,1024,128]{2,1,0:T(8,128)(2,1)S(1)}, bf16[2,1024,128]{2,1,0:T(8,128)(2,1)S(1)}, u32[]{:S(2)}, u32[]{:S(2)}) collective-permute-start(bf16[2,1024,128]{2,1,0:T(8,128)(2,1)S(1)} %get-tuple-element.73.keys_ref.refs_0_), channel_id=1, source_target_pairs={{0,8},{4,12},{8,0},{12,4},{1,9},{5,13},{9,1},{13,5},{2,10},{6,14},... | collective-permute-start | bytes 1572872 | tf_op jit(solution)/shard_map/ppermute | solution.py:548
  10.3 0.0 collective-permute-start
  10.4 0.8 copy.13
  11.1 0.6 gather_fusion
  11.7 0.1 convert_bitcast_fusion
  11.8 0.1 copy.14
  11.9 0.2 convert_reduce_fusion.2
  12.1 0.0 collective-permute-done._
  12.1 7.7 %own_totals.1.tot_ref = f32[2,1,1024]{2,1,0:T(1,128)S(1)} custom-call(bf16[2,1024,128]{2,1,0:T(8,128)(2,1)S(1)} %get-tuple-element.73.keys_ref.refs_0_, f32[2,4096,128]{2,1,0:T(8,128)} %cent_in.1, f32[2,1,128]{2,1,0:T(1,128)S(1)} %collective-permute-done._), custom_call_target="tpu_custom_call" | custom-call | tf_op jit(solution)/shard_map/own_totals/pallas_call | solution.py:279
  19.9 0.1 collective-permute-start.3
  20.0 0.0 copy-done
  20.0 0.2 dynamic-slice_reduce_fusion
  20.2 2.4 %sort_values.1.values_ref = bf16[2,1024,128]{2,1,0:T(8,128)(2,1)S(1)} custom-call(s32[2,1,1024]{2,1,0:T(1,128)S(1)} %get-tuple-element.46.spot_ref, bf16[2048,128]{1,0:T(8,128)(2,1)} %bitcast.27), custom_call_target="tpu_custom_call" | custom-call | tf_op jit(solution)/shard_map/sort_values/pallas_call | solution.py:173
  22.6 2.0 %collective-permute-start.2 = (f32[2,2,1024]{2,1,0:T(2,128)S(1)}, f32[2,2,1024]{2,1,0:T(2,128)S(1)}, u32[]{:S(2)}, u32[]{:S(2)}) collective-permute-start(f32[2,2,1024]{2,1,0:T(2,128)S(1)} %pad_maximum_fusion.1), channel_id=1, source_target_pairs={{0,8},{4,12},{8,0},{12,4},{1,9},{5,13},{9,1},{13,5},{2,10},{6,14},... | collective-permute-start | bytes 49160 | tf_op jit(solution)/shard_map/ppermute | solution.py:548
  24.5 2.5 %collective-permute-start.1 = (f32[2,2,1024]{2,1,0:T(2,128)S(1)}, f32[2,2,1024]{2,1,0:T(2,128)S(1)}, u32[]{:S(2)}, u32[]{:S(2)}) collective-permute-start(f32[2,2,1024]{2,1,0:T(2,128)S(1)} %pad_maximum_fusion.1), channel_id=1, source_target_pairs={{0,4},{4,0},{8,12},{12,8},{1,5},{5,1},{9,13},{13,9},{2,6},{6,2},{1... | collective-permute-start | bytes 49160 | tf_op jit(solution)/shard_map/ppermute | solution.py:548
  27.0 4.1 %first_block.4 = (f32[2,1024,128]{2,1,0:T(8,128)S(1)}, bf16[2,1024,128]{2,1,0:T(8,128)(2,1)S(1)}, bf16[2,1024,128]{2,1,0:T(8,128)(2,1)S(1)}) custom-call(s32[1]{0:T(128)} %bitcast.3._.me_ref, bf16[2,1024,128]{2,1,0:T(8,128)(2,1)S(1)} %get-tuple-element.73.keys_ref.refs_0_, f32[2,1,1024]{2,1,0:T(1,128)S(1)} %own_totals.1.tot_ref, f32[2,4096,128]{2,1,0:T(8,128)} %cent_in.1), custom_call_target="tpu_custom_call" | custom-call | tf_op jit(solution)/shard_map/first_block/pallas_call | solution.py:349
  31.1 2.7 %collective-permute-done.3 = f32[2,2,1024]{2,1,0:T(2,128)S(1)} collective-permute-done((f32[2,2,1024]{2,1,0:T(2,128)S(1)}, f32[2,2,1024]{2,1,0:T(2,128)S(1)}, u32[]{:S(2)}, u32[]{:S(2)}) %collective-permute-start.3) | collective-permute-done | bytes 16416 | tf_op jit(solution)/shard_map/ppermute | solution.py:548
  33.9 0.9 collective-permute-done.2
  34.7 0.0 collective-permute-done.1
  34.8 0.0 collective-permute-done.4.keys_ref.refs_1_
  34.8 0.0 collective-permute-done.5.keys_ref.refs_0_
  34.8 1.8 %own_ranks.1.rank_ref = f32[2,1,1024]{2,1,0:T(1,128)S(1)} custom-call(s32[1]{0:T(128)} %bitcast.3._.me_ref, f32[2,4,1024]{2,1,0:T(4,128)S(1)} %pad_maximum_fusion.label_ref), custom_call_target="tpu_custom_call" | custom-call | tf_op jit(solution)/shard_map/own_ranks/pallas_call | solution.py:239
  36.6 0.5 collective-permute-start.6
  37.1 0.6 windows.1
  37.7 3.0 %first_block.5 = (f32[2,1024,128]{2,1,0:T(8,128)S(1)}, bf16[2,1024,128]{2,1,0:T(8,128)(2,1)S(1)}) custom-call(s32[1]{0:T(128)} %bitcast.3._.me_ref, bf16[2,1024,128]{2,1,0:T(8,128)(2,1)S(1)} %collective-permute-done.4.keys_ref.refs_1_, f32[2,1,1024]{2,1,0:T(1,128)S(1)} %get-tuple-element.85.tot_ref, ...), custom_call_target="tpu_custom_call", output_to_operand_aliasing={{0}: (4, {})} | custom-call | tf_op jit(solution)/shard_map/first_block/pallas_call | solution.py:349
  40.7 0.3 convert_reduce_fusion
  41.0 0.1 constant_dynamic-update-slice_fusion.2
  41.1 1.6 %collective-permute-start.12 = (bf16[2,544,128]{2,1,0:T(8,128)(2,1)S(1)}, bf16[2,544,128]{2,1,0:T(8,128)(2,1)S(1)}, u32[]{:S(2)}, u32[]{:S(2)}) collective-permute-start(bf16[2,544,128]{2,1,0:T(8,128)(2,1)S(1)} %get-tuple-element.75), channel_id=1, source_target_pairs={{0,4},{4,0},{8,12},{12,8},{1,5},{5,1},{9,13},{13,9},{2,6},{6,2},{1... | collective-permute-start | bytes 835592 | tf_op jit(solution)/shard_map/ppermute | solution.py:548
  42.7 2.5 %collective-permute-start.13 = (bf16[2,544,128]{2,1,0:T(8,128)(2,1)S(1)}, bf16[2,544,128]{2,1,0:T(8,128)(2,1)S(1)}, u32[]{:S(2)}, u32[]{:S(2)}) collective-permute-start(bf16[2,544,128]{2,1,0:T(8,128)(2,1)S(1)} %get-tuple-element.76), channel_id=1, source_target_pairs={{0,12},{4,8},{8,4},{12,0},{1,13},{5,9},{9,5},{13,1},{2,14},{6,10},... | collective-permute-start | bytes 835592 | tf_op jit(solution)/shard_map/ppermute | solution.py:548
  45.2 0.1 constant_dynamic-update-slice_fusion.1
  45.3 0.1 constant_dynamic-update-slice_fusion.scalar_ref
  45.3 3.0 %first_block.6 = (f32[2,1024,128]{2,1,0:T(8,128)S(1)}, bf16[2,1024,128]{2,1,0:T(8,128)(2,1)S(1)}) custom-call(s32[1]{0:T(128)} %bitcast.3._.me_ref, bf16[2,1024,128]{2,1,0:T(8,128)(2,1)S(1)} %collective-permute-done.5.keys_ref.refs_0_, f32[2,1,1024]{2,1,0:T(1,128)S(1)} %get-tuple-element.87.tot_ref, ...), custom_call_target="tpu_custom_call", output_to_operand_aliasing={{0}: (4, {})} | custom-call | tf_op jit(solution)/shard_map/first_block/pallas_call | solution.py:349
  48.3 3.2 %collective-permute-done.6.keys_ref.refs_2_ = bf16[2,1024,128]{2,1,0:T(8,128)(2,1)S(1)} collective-permute-done((bf16[2,1024,128]{2,1,0:T(8,128)(2,1)S(1)}, bf16[2,1024,128]{2,1,0:T(8,128)(2,1)S(1)}, u32[]{:S(2)}, u32[]{:S(2)}) %collective-permute-start.6) | collective-permute-done | bytes 524320 | tf_op jit(solution)/shard_map/ppermute | solution.py:548
  51.5 3.0 %first_block.7 = (f32[2,1024,128]{2,1,0:T(8,128)S(1)}, bf16[2,1024,128]{2,1,0:T(8,128)(2,1)S(1)}) custom-call(s32[1]{0:T(128)} %bitcast.3._.me_ref, bf16[2,1024,128]{2,1,0:T(8,128)(2,1)S(1)} %collective-permute-done.6.keys_ref.refs_2_, f32[2,1,1024]{2,1,0:T(1,128)S(1)} %get-tuple-element.89.tot_ref, ...), custom_call_target="tpu_custom_call", output_to_operand_aliasing={{0}: (4, {})} | custom-call | tf_op jit(solution)/shard_map/first_block/pallas_call | solution.py:349
  54.5 5.3 %raw_weights.1 = (bf16[2,1024,4096]{2,1,0:T(8,128)(2,1)S(1)}, f32[2,1,4096]{2,1,0:T(1,128)S(1)}) custom-call(f32[2,1024,128]{2,1,0:T(8,128)S(1)} %get-tuple-element.58.sums_ref, bf16[2,1024,128]{2,1,0:T(8,128)(2,1)S(1)} %get-tuple-element.59.refs_0_.refs_4_, bf16[2,1024,128]{2,1,0:T(8,128)(2,1)S(1)} %get-tuple-element.60.refs_1_.refs_5_, ...), custom_call_target="tpu_custom_call" | custom-call | tf_op jit(solution)/shard_map/raw_weights/pallas_call | solution.py:386
  59.7 0.5 collective-permute-start.7
  60.2 2.6 %collective-permute-start.8 = (f32[2,1,4096]{2,1,0:T(1,128)S(1)}, f32[2,1,4096]{2,1,0:T(1,128)S(1)}, u32[]{:S(2)}, u32[]{:S(2)}) collective-permute-start(f32[2,1,4096]{2,1,0:T(1,128)S(1)} %get-tuple-element.66.refs_0_), channel_id=1, source_target_pairs={{0,8},{4,12},{8,0},{12,4},{1,9},{5,13},{9,1},{13,5},{2,10},{6,14},... | collective-permute-start | bytes 98312 | tf_op jit(solution)/shard_map/ppermute | solution.py:548
  62.9 1.3 %collective-permute-start.9 = (f32[2,1,4096]{2,1,0:T(1,128)S(1)}, f32[2,1,4096]{2,1,0:T(1,128)S(1)}, u32[]{:S(2)}, u32[]{:S(2)}) collective-permute-start(f32[2,1,4096]{2,1,0:T(1,128)S(1)} %get-tuple-element.66.refs_0_), channel_id=1, source_target_pairs={{0,12},{4,8},{8,4},{12,0},{1,13},{5,9},{9,5},{13,1},{2,14},{6,10},... | collective-permute-start | bytes 98312 | tf_op jit(solution)/shard_map/ppermute | solution.py:548
  64.2 0.0 collective-permute-done.7.refs_1_
  64.2 1.0 %collective-permute-start.10 = (bf16[1,544,128]{2,1,0:T(8,128)(2,1)S(1)}, bf16[1,544,128]{2,1,0:T(8,128)(2,1)S(1)}, u32[]{:S(2)}, u32[]{:S(2)}) collective-permute-start(bf16[1,544,128]{2,1,0:T(8,128)(2,1)S(1)} %get-tuple-element.71), channel_id=1, source_target_pairs={{0,8},{4,12},{8,0},{12,4},{1,9},{5,13},{9,1},{13,5},{2,10},{6,14},... | collective-permute-start | bytes 417800 | tf_op jit(solution)/shard_map/ppermute | solution.py:548
  65.2 0.0 collective-permute-done.8.refs_2_
  65.2 3.7 %collective-permute-done.9.refs_3_ = f32[2,1,4096]{2,1,0:T(1,128)S(1)} collective-permute-done((f32[2,1,4096]{2,1,0:T(1,128)S(1)}, f32[2,1,4096]{2,1,0:T(1,128)S(1)}, u32[]{:S(2)}, u32[]{:S(2)}) %collective-permute-start.9) | collective-permute-done | bytes 32800 | tf_op jit(solution)/shard_map/ppermute | solution.py:548
  68.9 3.7 %collective-permute-start.11 = (bf16[1,544,128]{2,1,0:T(8,128)(2,1)S(1)}, bf16[1,544,128]{2,1,0:T(8,128)(2,1)S(1)}, u32[]{:S(2)}, u32[]{:S(2)}) collective-permute-start(bf16[1,544,128]{2,1,0:T(8,128)(2,1)S(1)} %get-tuple-element.72), channel_id=1, source_target_pairs={{0,8},{4,12},{8,0},{12,4},{1,9},{5,13},{9,1},{13,5},{2,10},{6,14},... | collective-permute-start | bytes 417800 | tf_op jit(solution)/shard_map/ppermute | solution.py:548
  72.6 0.0 collective-permute-done.12.refs_4_
  72.6 0.0 collective-permute-done.13.refs_5_
  72.6 5.6 %place.2.refs_3_ = bf16[2,2048,256]{2,1,0:T(8,128)(2,1)S(1)} custom-call(s32[5,2,4]{2,1,0:T(2,128)S(1)} %constant_dynamic-update-slice_fusion.scalar_ref, f32[2,4,1024]{2,1,0:T(4,128)S(1)} %pad_maximum_fusion.label_ref, bf16[2,1024,128]{2,1,0:T(8,128)(2,1)S(1)} %get-tuple-element.73.keys_ref.refs_0_, ...), custom_call_target="tpu_custom_call" | custom-call | tf_op jit(solution)/shard_map/place/pallas_call | solution.py:527
  78.2 6.1 %weighted_sums.1 = f32[2,1024,128]{2,1,0:T(8,128)} custom-call(bf16[2,1024,4096]{2,1,0:T(8,128)(2,1)S(1)} %get-tuple-element.63.raw_ref, f32[2,1,4096]{2,1,0:T(1,128)S(1)} %get-tuple-element.66.refs_0_, f32[2,1,4096]{2,1,0:T(1,128)S(1)} %collective-permute-done.7.refs_1_, f32[2,1,4096]{2,1,0:T(1,128)S(1)} %collective-permute-done.8.refs_2_, ...), custom_call_target="tpu_custom_call" | custom-call | tf_op jit(solution)/shard_map/weighted_sums/pallas_call | solution.py:424
  84.3 0.0 collective-permute-done.10.refs_1_
  84.3 0.0 collective-permute-done.11.refs_2_
  84.3 3.8 %place.3 = (bf16[4096,128]{1,0:T(8,128)(2,1)}, bf16[4096,128]{1,0:T(8,128)(2,1)}) custom-call(s32[5,2,4]{2,1,0:T(2,128)S(1)} %constant_dynamic-update-slice_fusion.scalar_ref, f32[2,4,1024]{2,1,0:T(4,128)S(1)} %pad_maximum_fusion.label_ref, bf16[2,1024,128]{2,1,0:T(8,128)(2,1)S(1)} %collective-permute-done.5.keys_ref.refs_0_, ...), custom_call_target="tpu_custom_call" | custom-call | tf_op jit(solution)/shard_map/place/pallas_call | solution.py:527
  (15 shorter events, 0.2 us)
Async XLA Ops:
  0.6 19.3 %copy-start = (s32[2,5]{1,0:T(2,128)S(1)}, s32[2,5]{1,0:T(2,128)}, u32[]{:S(2)}) copy-start(s32[2,5]{1,0:T(2,128)} %param.8) | copy-start | bytes 124
  4.6 30.2 %collective-permute-start.4 = (bf16[2,1024,128]{2,1,0:T(8,128)(2,1)S(1)}, bf16[2,1024,128]{2,1,0:T(8,128)(2,1)S(1)}, u32[]{:S(2)}, u32[]{:S(2)}) collective-permute-start(bf16[2,1024,128]{2,1,0:T(8,128)(2,1)S(1)} %get-tuple-element.73.keys_ref.refs_0_), channel_id=1, source_target_pairs={{0,4},{4,0},{8,12},{12,8},{1,5},{5,1},{9,13},{13,9},{2,6},{6,2},{1... | collective-permute-start | bytes 1572872 | tf_op jit(solution)/shard_map/ppermute | solution.py:548
  7.7 27.1 %collective-permute-start.5 = (bf16[2,1024,128]{2,1,0:T(8,128)(2,1)S(1)}, bf16[2,1024,128]{2,1,0:T(8,128)(2,1)S(1)}, u32[]{:S(2)}, u32[]{:S(2)}) collective-permute-start(bf16[2,1024,128]{2,1,0:T(8,128)(2,1)S(1)} %get-tuple-element.73.keys_ref.refs_0_), channel_id=1, source_target_pairs={{0,8},{4,12},{8,0},{12,4},{1,9},{5,13},{9,1},{13,5},{2,10},{6,14},... | collective-permute-start | bytes 1572872 | tf_op jit(solution)/shard_map/ppermute | solution.py:548
  10.3 1.8 %collective-permute-start = (f32[2,1,128]{2,1,0:T(1,128)S(1)}, f32[2,1,128]{2,1,0:T(1,128)S(1)}, u32[]{:S(2)}, u32[]{:S(2)}) collective-permute-start(f32[2,1,128]{2,1,0:T(1,128)S(1)} %slice.27), channel_id=1, source_target_pairs={{0,1},{1,0},{2,3},{3,2},{4,5},{5,4},{6,7},{7,6},{8,9},{9,8},{10,11... | collective-permute-start | bytes 3080 | tf_op jit(solution)/shard_map/ppermute | solution.py:566
  19.9 14.0 %collective-permute-start.3 = (f32[2,2,1024]{2,1,0:T(2,128)S(1)}, f32[2,2,1024]{2,1,0:T(2,128)S(1)}, u32[]{:S(2)}, u32[]{:S(2)}) collective-permute-start(f32[2,2,1024]{2,1,0:T(2,128)S(1)} %pad_maximum_fusion.1), channel_id=1, source_target_pairs={{0,12},{4,8},{8,4},{12,0},{1,13},{5,9},{9,5},{13,1},{2,14},{6,10},... | collective-permute-start | bytes 49160 | tf_op jit(solution)/shard_map/ppermute | solution.py:548
  22.6 12.1 %collective-permute-start.2 = (f32[2,2,1024]{2,1,0:T(2,128)S(1)}, f32[2,2,1024]{2,1,0:T(2,128)S(1)}, u32[]{:S(2)}, u32[]{:S(2)}) collective-permute-start(f32[2,2,1024]{2,1,0:T(2,128)S(1)} %pad_maximum_fusion.1), channel_id=1, source_target_pairs={{0,8},{4,12},{8,0},{12,4},{1,9},{5,13},{9,1},{13,5},{2,10},{6,14},... | collective-permute-start | bytes 49160 | tf_op jit(solution)/shard_map/ppermute | solution.py:548
  24.5 10.2 %collective-permute-start.1 = (f32[2,2,1024]{2,1,0:T(2,128)S(1)}, f32[2,2,1024]{2,1,0:T(2,128)S(1)}, u32[]{:S(2)}, u32[]{:S(2)}) collective-permute-start(f32[2,2,1024]{2,1,0:T(2,128)S(1)} %pad_maximum_fusion.1), channel_id=1, source_target_pairs={{0,4},{4,0},{8,12},{12,8},{1,5},{5,1},{9,13},{13,9},{2,6},{6,2},{1... | collective-permute-start | bytes 49160 | tf_op jit(solution)/shard_map/ppermute | solution.py:548
  36.6 14.9 %collective-permute-start.6 = (bf16[2,1024,128]{2,1,0:T(8,128)(2,1)S(1)}, bf16[2,1024,128]{2,1,0:T(8,128)(2,1)S(1)}, u32[]{:S(2)}, u32[]{:S(2)}) collective-permute-start(bf16[2,1024,128]{2,1,0:T(8,128)(2,1)S(1)} %collective-permute-done.5.keys_ref.refs_0_), channel_id=1, source_target_pairs={{0,4},{4,0},{8,12},{12,8},{1,5},{5,1},{9,13},{13,9},{2,6},{6,2},{1... | collective-permute-start | bytes 1572872 | tf_op jit(solution)/shard_map/ppermute | solution.py:548
  41.1 31.5 %collective-permute-start.12 = (bf16[2,544,128]{2,1,0:T(8,128)(2,1)S(1)}, bf16[2,544,128]{2,1,0:T(8,128)(2,1)S(1)}, u32[]{:S(2)}, u32[]{:S(2)}) collective-permute-start(bf16[2,544,128]{2,1,0:T(8,128)(2,1)S(1)} %get-tuple-element.75), channel_id=1, source_target_pairs={{0,4},{4,0},{8,12},{12,8},{1,5},{5,1},{9,13},{13,9},{2,6},{6,2},{1... | collective-permute-start | bytes 835592 | tf_op jit(solution)/shard_map/ppermute | solution.py:548
  42.7 29.9 %collective-permute-start.13 = (bf16[2,544,128]{2,1,0:T(8,128)(2,1)S(1)}, bf16[2,544,128]{2,1,0:T(8,128)(2,1)S(1)}, u32[]{:S(2)}, u32[]{:S(2)}) collective-permute-start(bf16[2,544,128]{2,1,0:T(8,128)(2,1)S(1)} %get-tuple-element.76), channel_id=1, source_target_pairs={{0,12},{4,8},{8,4},{12,0},{1,13},{5,9},{9,5},{13,1},{2,14},{6,10},... | collective-permute-start | bytes 835592 | tf_op jit(solution)/shard_map/ppermute | solution.py:548
  59.7 4.5 %collective-permute-start.7 = (f32[2,1,4096]{2,1,0:T(1,128)S(1)}, f32[2,1,4096]{2,1,0:T(1,128)S(1)}, u32[]{:S(2)}, u32[]{:S(2)}) collective-permute-start(f32[2,1,4096]{2,1,0:T(1,128)S(1)} %get-tuple-element.66.refs_0_), channel_id=1, source_target_pairs={{0,4},{4,0},{8,12},{12,8},{1,5},{5,1},{9,13},{13,9},{2,6},{6,2},{1... | collective-permute-start | bytes 98312 | tf_op jit(solution)/shard_map/ppermute | solution.py:548
  60.2 5.0 %collective-permute-start.8 = (f32[2,1,4096]{2,1,0:T(1,128)S(1)}, f32[2,1,4096]{2,1,0:T(1,128)S(1)}, u32[]{:S(2)}, u32[]{:S(2)}) collective-permute-start(f32[2,1,4096]{2,1,0:T(1,128)S(1)} %get-tuple-element.66.refs_0_), channel_id=1, source_target_pairs={{0,8},{4,12},{8,0},{12,4},{1,9},{5,13},{9,1},{13,5},{2,10},{6,14},... | collective-permute-start | bytes 98312 | tf_op jit(solution)/shard_map/ppermute | solution.py:548
  62.9 6.0 %collective-permute-start.9 = (f32[2,1,4096]{2,1,0:T(1,128)S(1)}, f32[2,1,4096]{2,1,0:T(1,128)S(1)}, u32[]{:S(2)}, u32[]{:S(2)}) collective-permute-start(f32[2,1,4096]{2,1,0:T(1,128)S(1)} %get-tuple-element.66.refs_0_), channel_id=1, source_target_pairs={{0,12},{4,8},{8,4},{12,0},{1,13},{5,9},{9,5},{13,1},{2,14},{6,10},... | collective-permute-start | bytes 98312 | tf_op jit(solution)/shard_map/ppermute | solution.py:548
  64.2 20.1 %collective-permute-start.10 = (bf16[1,544,128]{2,1,0:T(8,128)(2,1)S(1)}, bf16[1,544,128]{2,1,0:T(8,128)(2,1)S(1)}, u32[]{:S(2)}, u32[]{:S(2)}) collective-permute-start(bf16[1,544,128]{2,1,0:T(8,128)(2,1)S(1)} %get-tuple-element.71), channel_id=1, source_target_pairs={{0,8},{4,12},{8,0},{12,4},{1,9},{5,13},{9,1},{13,5},{2,10},{6,14},... | collective-permute-start | bytes 417800 | tf_op jit(solution)/shard_map/ppermute | solution.py:548
  68.9 15.4 %collective-permute-start.11 = (bf16[1,544,128]{2,1,0:T(8,128)(2,1)S(1)}, bf16[1,544,128]{2,1,0:T(8,128)(2,1)S(1)}, u32[]{:S(2)}, u32[]{:S(2)}) collective-permute-start(bf16[1,544,128]{2,1,0:T(8,128)(2,1)S(1)} %get-tuple-element.72), channel_id=1, source_target_pairs={{0,8},{4,12},{8,0},{12,4},{1,9},{5,13},{9,1},{13,5},{2,10},{6,14},... | collective-permute-start | bytes 417800 | tf_op jit(solution)/shard_map/ppermute | solution.py:548

commit v13 on v11

--- a/solution.py
+++ b/solution.py
@@ -27,6 +27,12 @@
 
 def unit_rows(x):
     return x * lax.rsqrt(jnp.sum(x * x, axis=-1, keepdims=True) + 1e-06)
+
+
+def two_terms(cent):
+    scaled = cent.astype(F32) * EXP2_SCALE
+    high = scaled.astype(BF16)
+    return jnp.concatenate([high, (scaled - high.astype(F32)).astype(BF16)], axis=1)
 
 
 def params(**kwargs):
@@ -256,15 +262,16 @@
 
     @pl.when(step == 0)
     def _():
-        unit_ref[...] = unit_rows(keys_ref[pl.program_id(0)].astype(F32)).astype(BF16)
+        unit = unit_rows(keys_ref[pl.program_id(0)].astype(F32)).astype(BF16)
+        unit_ref[...] = jnp.concatenate([unit, unit], axis=1)
         sum_ref[...] = jnp.zeros_like(sum_ref)
 
     part = 256
     rows = min(1024, cent_ref.shape[1])
     for c in range(0, cent_ref.shape[1], rows):
-        cent = unit_rows(cent_ref[0, c : c + rows]).astype(BF16)
+        cent = two_terms(unit_rows(cent_ref[0, c : c + rows]).astype(BF16))
         for t in range(0, tokens, part):
-            raw = jnp.exp2(dot_nt(cent, unit_ref[t : t + part, :]) * EXP2_SCALE)
+            raw = jnp.exp2(dot_nt(cent, unit_ref[t : t + part, :]))
             sum_ref[:, t : t + part] += jnp.sum(raw.reshape(-1, 8, part), axis=0)
 
     @pl.when(step == pl.num_programs(1) - 1)
@@ -287,7 +294,7 @@
         out_specs=pl.BlockSpec((1, 1, tokens), lambda h, c: (h, 0, 0)),
         out_shape=jax.ShapeDtypeStruct((heads, 1, tokens), F32),
         scratch_shapes=[
-            pltpu.VMEM((tokens, width), BF16),
+            pltpu.VMEM((tokens, 2 * width), BF16),
             pltpu.VMEM((8, tokens), F32),
         ],
         compiler_params=params(),
@@ -573,9 +580,7 @@
     own_below = jnp.sum((own_labels < peer_low[:, :, None]).astype(jnp.int32), axis=2)
     own_values = sort_values(own_spots, value_rows.reshape(heads * tokens, width))
 
-    labels, sums = lax.optimization_barrier(
-        (jnp.concatenate([x[:, -1:] for x in shared], axis=1), sums)
-    )
+    labels = jnp.concatenate([x[:, -1:] for x in shared], axis=1)
     ranks = own_ranks(me_array, labels)
     low = lax.dynamic_slice_in_dim(owner_bounds, me, 1, 1)
     high = lax.dynamic_slice_in_dim(owner_bounds, me + 1, 1, 1)
@@ -586,28 +591,20 @@
     one = jnp.ones((1, n), jnp.int32)
     scalars = jnp.stack([key_starts, gaps, low * one, high * one, first * one])
 
-    own_windows = list(
-        windows(aligned(own_below, send_size), ranks, own_values, send_size, own_labels)
-    )
+    starts = aligned(own_below, send_size)
     late = [2]
     early = [d for d in range(1, n) if d not in late]
-    values = {0: own_windows[0]}
-
-    def leave(group, x):
-        *leaving, x = lax.optimization_barrier((*(own_windows[d] for d in group), x))
-        for d, window in zip(group, leaving):
-            values[d] = swap(window, d)
-        return x
-
+    values = {}
     for m in range(1, n):
-        if m == min(2, n - 1):
-            sums = leave(early, sums)
         sums, unit = first_block(me_array, keys[m], totals[m], cents, n, sums)
         units.append(unit)
-    sums = leave(late, sums)
+        group = {1: early, 2: [0, *late]}.get(m)
+        if group:
+            some = jnp.stack([starts[:, d] for d in group], axis=1)
+            for d, window in zip(group, windows(some, ranks, own_values, send_size, unit)):
+                values[d] = swap(window, d) if d else window
 
     raw, part = raw_weights(sums, units)
-    scalars, part = lax.optimization_barrier((scalars, part))
     parts = spread(part)
     so_far = place(scalars, labels, keys, values, [0, *early], key_size, cap, None)
     out = weighted_sums(raw, units, parts)

time: 83.4 us -> 80.7 us (0.968)
  starting transfers between devices: 20.6 us -> 18.3 us
  waiting for transfers between devices: 8.84 us -> 7.64 us
    ppermute x12, starting transfers between devices: 20.6 us -> 18.3 us  [swap(): return lax.ppermute(x, 'ctx', [(i, i ^ d) for i in range(n)])]
    ppermute x12, waiting for transfers between devices: 8.84 us -> 7.64 us  [swap(): return lax.ppermute(x, 'ctx', [(i, i ^ d) for i in range(n)])]
where the time goes in v13:
time: 80.7 us; the launch traced here: 80.5 us
  Pallas kernels  50.8 us (63%)
  starting transfers between devices  18.3 us (23%)
  waiting for transfers between devices  7.64 us (9%)
  local copies, waits for them, and re-layouts  1.99 us (2%)
  between operations  1.06 us (1%)
    ppermute x12, starting transfers between devices, swap(): return lax.ppermute(x, 'ctx', [(i, i ^ d) for i in range(n)])  18.3 us
    pallas_call x4, Pallas kernels, first_block(): pl.pallas_call(functools.partial(first_kernel, fresh), grid_spec=pltpu.Pr...  13 us
    pallas_call x2, Pallas kernels, place(): pl.pallas_call(functools.partial(place_kernel, ids, size, fresh), in_spec...  9.37 us
    pallas_call x1, Pallas kernels, own_totals(): pl.pallas_call(totals_kernel, grid=(heads, count // rows), in_specs=[in_v...  7.79 us
    ppermute x12, waiting for transfers between devices, swap(): return lax.ppermute(x, 'ctx', [(i, i ^ d) for i in range(n)])  7.64 us
    pallas_call x1, Pallas kernels, weighted_sums(): pl.pallas_call(functools.partial(sums_kernel, len(units)), in_specs=[in_v...  6.06 us
    pallas_call x1, Pallas kernels, raw_weights(): pl.pallas_call(functools.partial(raw_kernel, len(units)), grid=(heads,),...  5.27 us
    pallas_call x1, Pallas kernels, sort_keys(): pl.pallas_call(sort_kernel, in_specs=[anywhere()] * 2, out_specs=(in_vmem...  4 us
  transfers between devices with their start and end apart: 13, of which 5 were waited for; matrix products, arithmetic and copies ran while one was open for 3% of the time, Pallas kernels for 51%

profile of v13, /device:TPU:0, one launch (start us, length us, event | category | flops | bytes accessed | tf_op | source)
XLA Modules:
  0.0 80.5 jit_solution(3855552161299090871)
XLA Ops:
  0.6 0.0 copy-start
  0.6 4.0 %sort_keys.1 = (bf16[2,1024,128]{2,1,0:T(8,128)(2,1)S(1)}, f32[2,1,1024]{2,1,0:T(1,128)S(1)}, s32[2,1,1024]{2,1,0:T(1,128)S(1)}) custom-call(s32[2,1024]{1,0:T(2,128)} %label_hbm.1, bf16[2048,128]{1,0:T(8,128)(2,1)} %bitcast.26), custom_call_target="tpu_custom_call" | custom-call | tf_op jit(solution)/shard_map/sort_keys/pallas_call | solution.py:141
  4.6 4.1 %collective-permute-start.1 = (bf16[2,1024,128]{2,1,0:T(8,128)(2,1)S(1)}, bf16[2,1024,128]{2,1,0:T(8,128)(2,1)S(1)}, u32[]{:S(2)}, u32[]{:S(2)}) collective-permute-start(bf16[2,1024,128]{2,1,0:T(8,128)(2,1)S(1)} %get-tuple-element.45.keys_ref.refs_0_), channel_id=1, source_target_pairs={{0,8},{4,12},{8,0},{12,4},{1,9},{5,13},{9,1},{13,5},{2,10},{6,14},... | collective-permute-start | bytes 1572872 | tf_op jit(solution)/shard_map/ppermute | solution.py:548
  8.8 1.6 %collective-permute-start = (bf16[2,1024,128]{2,1,0:T(8,128)(2,1)S(1)}, bf16[2,1024,128]{2,1,0:T(8,128)(2,1)S(1)}, u32[]{:S(2)}, u32[]{:S(2)}) collective-permute-start(bf16[2,1024,128]{2,1,0:T(8,128)(2,1)S(1)} %get-tuple-element.45.keys_ref.refs_0_), channel_id=1, source_target_pairs={{0,4},{4,0},{8,12},{12,8},{1,5},{5,1},{9,13},{13,9},{2,6},{6,2},{1... | collective-permute-start | bytes 1572872 | tf_op jit(solution)/shard_map/ppermute | solution.py:548
  10.3 0.0 collective-permute-start.2
  10.4 0.8 copy.13
  11.1 0.6 gather_fusion
  11.7 0.1 convert_bitcast_fusion
  11.8 0.1 copy.14
  11.9 0.2 convert_reduce_fusion.2
  12.1 0.1 fusion.5
  12.2 0.0 collective-permute-done.2._
  12.2 7.8 %own_totals.1.tot_ref = f32[2,1,1024]{2,1,0:T(1,128)S(1)} custom-call(bf16[2,1024,128]{2,1,0:T(8,128)(2,1)S(1)} %get-tuple-element.45.keys_ref.refs_0_, f32[2,4096,128]{2,1,0:T(8,128)} %cent_in.1, f32[2,1,128]{2,1,0:T(1,128)S(1)} %collective-permute-done.2._), custom_call_target="tpu_custom_call" | custom-call | tf_op jit(solution)/shard_map/own_totals/pallas_call | solution.py:286
  20.0 0.5 collective-permute-start.6
  20.5 0.1 pad_add_fusion
  20.6 0.0 copy-done
  20.6 0.2 dynamic-slice_reduce_fusion
  20.8 2.4 %sort_values.1.values_ref = bf16[2,1024,128]{2,1,0:T(8,128)(2,1)S(1)} custom-call(s32[2,1,1024]{2,1,0:T(1,128)S(1)} %get-tuple-element.43.spot_ref, bf16[2048,128]{1,0:T(8,128)(2,1)} %bitcast.27), custom_call_target="tpu_custom_call" | custom-call | tf_op jit(solution)/shard_map/sort_values/pallas_call | solution.py:179
  23.2 0.1 collective-permute-start.5
  23.4 3.9 %collective-permute-start.4 = (f32[2,2,1024]{2,1,0:T(2,128)S(1)}, f32[2,2,1024]{2,1,0:T(2,128)S(1)}, u32[]{:S(2)}, u32[]{:S(2)}) collective-permute-start(f32[2,2,1024]{2,1,0:T(2,128)S(1)} %pad_maximum_fusion.1), channel_id=1, source_target_pairs={{0,12},{4,8},{8,4},{12,0},{1,13},{5,9},{9,5},{13,1},{2,14},{6,10},... | collective-permute-start | bytes 49160 | tf_op jit(solution)/shard_map/ppermute | solution.py:548
  27.2 4.1 %first_block.4 = (f32[2,1024,128]{2,1,0:T(8,128)S(1)}, bf16[2,1024,128]{2,1,0:T(8,128)(2,1)S(1)}, bf16[2,1024,128]{2,1,0:T(8,128)(2,1)S(1)}) custom-call(s32[1]{0:T(128)} %bitcast._.me_ref, bf16[2,1024,128]{2,1,0:T(8,128)(2,1)S(1)} %get-tuple-element.45.keys_ref.refs_0_, f32[2,1,1024]{2,1,0:T(1,128)S(1)} %own_totals.1.tot_ref, f32[2,4096,128]{2,1,0:T(8,128)} %cent_in.1), custom_call_target="tpu_custom_call" | custom-call | tf_op jit(solution)/shard_map/first_block/pallas_call | solution.py:356
  31.3 1.8 %collective-permute-done.6 = f32[2,2,1024]{2,1,0:T(2,128)S(1)} collective-permute-done((f32[2,2,1024]{2,1,0:T(2,128)S(1)}, f32[2,2,1024]{2,1,0:T(2,128)S(1)}, u32[]{:S(2)}, u32[]{:S(2)}) %collective-permute-start.6) | collective-permute-done | bytes 16416 | tf_op jit(solution)/shard_map/ppermute | solution.py:548
  33.1 0.0 collective-permute-done.5
  33.1 0.9 %collective-permute-done.4 = f32[2,2,1024]{2,1,0:T(2,128)S(1)} collective-permute-done((f32[2,2,1024]{2,1,0:T(2,128)S(1)}, f32[2,2,1024]{2,1,0:T(2,128)S(1)}, u32[]{:S(2)}, u32[]{:S(2)}) %collective-permute-start.4) | collective-permute-done | bytes 16416 | tf_op jit(solution)/shard_map/ppermute | solution.py:548
  34.1 0.1 broadcast_compare_fusion
  34.2 0.2 convert_reduce_fusion
  34.4 0.0 collective-permute-done.1.keys_ref.refs_0_
  34.4 0.0 collective-permute-done.keys_ref.refs_1_
  34.4 0.5 collective-permute-start.3
  34.9 1.8 %own_ranks.1.rank_ref = f32[2,1,1024]{2,1,0:T(1,128)S(1)} custom-call(s32[1]{0:T(128)} %bitcast._.me_ref, f32[2,4,1024]{2,1,0:T(4,128)S(1)} %get-tuple-element.56.label_ref), custom_call_target="tpu_custom_call" | custom-call | tf_op jit(solution)/shard_map/own_ranks/pallas_call | solution.py:245
  36.6 3.0 %first_block.5 = (f32[2,1024,128]{2,1,0:T(8,128)S(1)}, bf16[2,1024,128]{2,1,0:T(8,128)(2,1)S(1)}) custom-call(s32[1]{0:T(128)} %bitcast._.me_ref, bf16[2,1024,128]{2,1,0:T(8,128)(2,1)S(1)} %collective-permute-done.keys_ref.refs_1_, f32[2,1,1024]{2,1,0:T(1,128)S(1)} %get-tuple-element.58.tot_ref, ...), custom_call_target="tpu_custom_call", output_to_operand_aliasing={{0}: (4, {})} | custom-call | tf_op jit(solution)/shard_map/first_block/pallas_call | solution.py:356
  39.6 0.6 windows.3
  40.2 1.7 %collective-permute-start.11 = (bf16[2,544,128]{2,1,0:T(8,128)(2,1)S(1)}, bf16[2,544,128]{2,1,0:T(8,128)(2,1)S(1)}, u32[]{:S(2)}, u32[]{:S(2)}) collective-permute-start(bf16[2,544,128]{2,1,0:T(8,128)(2,1)S(1)} %get-tuple-element.47), channel_id=1, source_target_pairs={{0,4},{4,0},{8,12},{12,8},{1,5},{5,1},{9,13},{13,9},{2,6},{6,2},{1... | collective-permute-start | bytes 835592 | tf_op jit(solution)/shard_map/ppermute | solution.py:548
  41.9 0.1 constant_dynamic-update-slice_fusion.2
  42.0 2.6 %collective-permute-start.12 = (bf16[2,544,128]{2,1,0:T(8,128)(2,1)S(1)}, bf16[2,544,128]{2,1,0:T(8,128)(2,1)S(1)}, u32[]{:S(2)}, u32[]{:S(2)}) collective-permute-start(bf16[2,544,128]{2,1,0:T(8,128)(2,1)S(1)} %get-tuple-element.48), channel_id=1, source_target_pairs={{0,12},{4,8},{8,4},{12,0},{1,13},{5,9},{9,5},{13,1},{2,14},{6,10},... | collective-permute-start | bytes 835592 | tf_op jit(solution)/shard_map/ppermute | solution.py:548
  44.6 3.0 %first_block.6 = (f32[2,1024,128]{2,1,0:T(8,128)S(1)}, bf16[2,1024,128]{2,1,0:T(8,128)(2,1)S(1)}) custom-call(s32[1]{0:T(128)} %bitcast._.me_ref, bf16[2,1024,128]{2,1,0:T(8,128)(2,1)S(1)} %collective-permute-done.1.keys_ref.refs_0_, f32[2,1,1024]{2,1,0:T(1,128)S(1)} %get-tuple-element.60.tot_ref, ...), custom_call_target="tpu_custom_call", output_to_operand_aliasing={{0}: (4, {})} | custom-call | tf_op jit(solution)/shard_map/first_block/pallas_call | solution.py:356
  47.5 0.6 windows.2
  48.1 0.1 collective-permute-start.10
  48.2 0.1 constant_dynamic-update-slice_fusion.1
  48.3 1.0 %collective-permute-done.3.keys_ref.refs_2_ = bf16[2,1024,128]{2,1,0:T(8,128)(2,1)S(1)} collective-permute-done((bf16[2,1024,128]{2,1,0:T(8,128)(2,1)S(1)}, bf16[2,1024,128]{2,1,0:T(8,128)(2,1)S(1)}, u32[]{:S(2)}, u32[]{:S(2)}) %collective-permute-start.3) | collective-permute-done | bytes 524320 | tf_op jit(solution)/shard_map/ppermute | solution.py:548
  49.3 3.0 %first_block.7 = (f32[2,1024,128]{2,1,0:T(8,128)S(1)}, bf16[2,1024,128]{2,1,0:T(8,128)(2,1)S(1)}) custom-call(s32[1]{0:T(128)} %bitcast._.me_ref, bf16[2,1024,128]{2,1,0:T(8,128)(2,1)S(1)} %collective-permute-done.3.keys_ref.refs_2_, f32[2,1,1024]{2,1,0:T(1,128)S(1)} %get-tuple-element.62.tot_ref, ...), custom_call_target="tpu_custom_call", output_to_operand_aliasing={{0}: (4, {})} | custom-call | tf_op jit(solution)/shard_map/first_block/pallas_call | solution.py:356
  52.3 5.3 %raw_weights.1 = (bf16[2,1024,4096]{2,1,0:T(8,128)(2,1)S(1)}, f32[2,1,4096]{2,1,0:T(1,128)S(1)}) custom-call(f32[2,1024,128]{2,1,0:T(8,128)S(1)} %get-tuple-element.36.sums_ref, bf16[2,1024,128]{2,1,0:T(8,128)(2,1)S(1)} %get-tuple-element.37.refs_0_.refs_4_, bf16[2,1024,128]{2,1,0:T(8,128)(2,1)S(1)} %get-tuple-element.38.refs_1_.refs_5_._, ...), custom_call_target="tpu_custom_call" | custom-call | tf_op jit(solution)/shard_map/raw_weights/pallas_call | solution.py:393
  57.6 3.3 %collective-permute-start.9 = (f32[2,1,4096]{2,1,0:T(1,128)S(1)}, f32[2,1,4096]{2,1,0:T(1,128)S(1)}, u32[]{:S(2)}, u32[]{:S(2)}) collective-permute-start(f32[2,1,4096]{2,1,0:T(1,128)S(1)} %get-tuple-element.42.refs_0_), channel_id=1, source_target_pairs={{0,12},{4,8},{8,4},{12,0},{1,13},{5,9},{9,5},{13,1},{2,14},{6,10},... | collective-permute-start | bytes 98312 | tf_op jit(solution)/shard_map/ppermute | solution.py:548
  60.8 0.0 collective-permute-start.8
  60.8 3.6 %collective-permute-done.11.refs_4_ = bf16[2,544,128]{2,1,0:T(8,128)(2,1)S(1)} collective-permute-done((bf16[2,544,128]{2,1,0:T(8,128)(2,1)S(1)}, bf16[2,544,128]{2,1,0:T(8,128)(2,1)S(1)}, u32[]{:S(2)}, u32[]{:S(2)}) %collective-permute-start.11) | collective-permute-done | bytes 278560 | tf_op jit(solution)/shard_map/ppermute | solution.py:548
  64.5 0.0 collective-permute-start.7
  64.5 0.1 constant_dynamic-update-slice_fusion.scalar_ref
  64.6 0.0 collective-permute-done.12.refs_5_
  64.6 5.6 %place.2.refs_2_ = bf16[2,2048,256]{2,1,0:T(8,128)(2,1)S(1)} custom-call(s32[5,2,4]{2,1,0:T(2,128)S(1)} %constant_dynamic-update-slice_fusion.scalar_ref, f32[2,4,1024]{2,1,0:T(4,128)S(1)} %get-tuple-element.56.label_ref, bf16[2,1024,128]{2,1,0:T(8,128)(2,1)S(1)} %get-tuple-element.45.keys_ref.refs_0_, ...), custom_call_target="tpu_custom_call" | custom-call | tf_op jit(solution)/shard_map/place/pallas_call | solution.py:527
  70.2 0.3 collective-permute-done.10.refs_1_
  70.4 3.8 %place.3 = (bf16[4096,128]{1,0:T(8,128)(2,1)}, bf16[4096,128]{1,0:T(8,128)(2,1)}) custom-call(s32[5,2,4]{2,1,0:T(2,128)S(1)} %constant_dynamic-update-slice_fusion.scalar_ref, f32[2,4,1024]{2,1,0:T(4,128)S(1)} %get-tuple-element.56.label_ref, bf16[2,1024,128]{2,1,0:T(8,128)(2,1)S(1)} %collective-permute-done.1.keys_ref.refs_0_, ...), custom_call_target="tpu_custom_call" | custom-call | tf_op jit(solution)/shard_map/place/pallas_call | solution.py:527
  74.2 0.0 collective-permute-done.9.refs_3_
  74.2 0.0 collective-permute-done.8.refs_2_
  74.2 0.0 collective-permute-done.7.refs_1_
  74.2 6.1 %weighted_sums.1 = f32[2,1024,128]{2,1,0:T(8,128)} custom-call(bf16[2,1024,4096]{2,1,0:T(8,128)(2,1)S(1)} %get-tuple-element.41.raw_ref, f32[2,1,4096]{2,1,0:T(1,128)S(1)} %get-tuple-element.42.refs_0_, f32[2,1,4096]{2,1,0:T(1,128)S(1)} %collective-permute-done.7.refs_1_, f32[2,1,4096]{2,1,0:T(1,128)S(1)} %collective-permute-done.8.refs_2_, ...), custom_call_target="tpu_custom_call" | custom-call | tf_op jit(solution)/shard_map/weighted_sums/pallas_call | solution.py:431
  (13 shorter events, 0.1 us)
Async XLA Ops:
  0.6 20.0 %copy-start = (s32[2,5]{1,0:T(2,128)S(1)}, s32[2,5]{1,0:T(2,128)}, u32[]{:S(2)}) copy-start(s32[2,5]{1,0:T(2,128)} %param.8) | copy-start | bytes 124
  4.6 29.7 %collective-permute-start.1 = (bf16[2,1024,128]{2,1,0:T(8,128)(2,1)S(1)}, bf16[2,1024,128]{2,1,0:T(8,128)(2,1)S(1)}, u32[]{:S(2)}, u32[]{:S(2)}) collective-permute-start(bf16[2,1024,128]{2,1,0:T(8,128)(2,1)S(1)} %get-tuple-element.45.keys_ref.refs_0_), channel_id=1, source_target_pairs={{0,8},{4,12},{8,0},{12,4},{1,9},{5,13},{9,1},{13,5},{2,10},{6,14},... | collective-permute-start | bytes 1572872 | tf_op jit(solution)/shard_map/ppermute | solution.py:548
  8.8 25.6 %collective-permute-start = (bf16[2,1024,128]{2,1,0:T(8,128)(2,1)S(1)}, bf16[2,1024,128]{2,1,0:T(8,128)(2,1)S(1)}, u32[]{:S(2)}, u32[]{:S(2)}) collective-permute-start(bf16[2,1024,128]{2,1,0:T(8,128)(2,1)S(1)} %get-tuple-element.45.keys_ref.refs_0_), channel_id=1, source_target_pairs={{0,4},{4,0},{8,12},{12,8},{1,5},{5,1},{9,13},{13,9},{2,6},{6,2},{1... | collective-permute-start | bytes 1572872 | tf_op jit(solution)/shard_map/ppermute | solution.py:548
  10.3 1.9 %collective-permute-start.2 = (f32[2,1,128]{2,1,0:T(1,128)S(1)}, f32[2,1,128]{2,1,0:T(1,128)S(1)}, u32[]{:S(2)}, u32[]{:S(2)}) collective-permute-start(f32[2,1,128]{2,1,0:T(1,128)S(1)} %slice.33), channel_id=1, source_target_pairs={{0,1},{1,0},{2,3},{3,2},{4,5},{5,4},{6,7},{7,6},{8,9},{9,8},{10,11... | collective-permute-start | bytes 3080 | tf_op jit(solution)/shard_map/ppermute | solution.py:566
  20.0 13.1 %collective-permute-start.6 = (f32[2,2,1024]{2,1,0:T(2,128)S(1)}, f32[2,2,1024]{2,1,0:T(2,128)S(1)}, u32[]{:S(2)}, u32[]{:S(2)}) collective-permute-start(f32[2,2,1024]{2,1,0:T(2,128)S(1)} %pad_maximum_fusion.1), channel_id=1, source_target_pairs={{0,4},{4,0},{8,12},{12,8},{1,5},{5,1},{9,13},{13,9},{2,6},{6,2},{1... | collective-permute-start | bytes 49160 | tf_op jit(solution)/shard_map/ppermute | solution.py:548
  23.2 9.9 %collective-permute-start.5 = (f32[2,2,1024]{2,1,0:T(2,128)S(1)}, f32[2,2,1024]{2,1,0:T(2,128)S(1)}, u32[]{:S(2)}, u32[]{:S(2)}) collective-permute-start(f32[2,2,1024]{2,1,0:T(2,128)S(1)} %pad_maximum_fusion.1), channel_id=1, source_target_pairs={{0,8},{4,12},{8,0},{12,4},{1,9},{5,13},{9,1},{13,5},{2,10},{6,14},... | collective-permute-start | bytes 49160 | tf_op jit(solution)/shard_map/ppermute | solution.py:548
  23.4 10.7 %collective-permute-start.4 = (f32[2,2,1024]{2,1,0:T(2,128)S(1)}, f32[2,2,1024]{2,1,0:T(2,128)S(1)}, u32[]{:S(2)}, u32[]{:S(2)}) collective-permute-start(f32[2,2,1024]{2,1,0:T(2,128)S(1)} %pad_maximum_fusion.1), channel_id=1, source_target_pairs={{0,12},{4,8},{8,4},{12,0},{1,13},{5,9},{9,5},{13,1},{2,14},{6,10},... | collective-permute-start | bytes 49160 | tf_op jit(solution)/shard_map/ppermute | solution.py:548
  34.4 14.9 %collective-permute-start.3 = (bf16[2,1024,128]{2,1,0:T(8,128)(2,1)S(1)}, bf16[2,1024,128]{2,1,0:T(8,128)(2,1)S(1)}, u32[]{:S(2)}, u32[]{:S(2)}) collective-permute-start(bf16[2,1024,128]{2,1,0:T(8,128)(2,1)S(1)} %collective-permute-done.1.keys_ref.refs_0_), channel_id=1, source_target_pairs={{0,4},{4,0},{8,12},{12,8},{1,5},{5,1},{9,13},{13,9},{2,6},{6,2},{1... | collective-permute-start | bytes 1572872 | tf_op jit(solution)/shard_map/ppermute | solution.py:548
  40.2 24.3 %collective-permute-start.11 = (bf16[2,544,128]{2,1,0:T(8,128)(2,1)S(1)}, bf16[2,544,128]{2,1,0:T(8,128)(2,1)S(1)}, u32[]{:S(2)}, u32[]{:S(2)}) collective-permute-start(bf16[2,544,128]{2,1,0:T(8,128)(2,1)S(1)} %get-tuple-element.47), channel_id=1, source_target_pairs={{0,4},{4,0},{8,12},{12,8},{1,5},{5,1},{9,13},{13,9},{2,6},{6,2},{1... | collective-permute-start | bytes 835592 | tf_op jit(solution)/shard_map/ppermute | solution.py:548
  42.0 22.6 %collective-permute-start.12 = (bf16[2,544,128]{2,1,0:T(8,128)(2,1)S(1)}, bf16[2,544,128]{2,1,0:T(8,128)(2,1)S(1)}, u32[]{:S(2)}, u32[]{:S(2)}) collective-permute-start(bf16[2,544,128]{2,1,0:T(8,128)(2,1)S(1)} %get-tuple-element.48), channel_id=1, source_target_pairs={{0,12},{4,8},{8,4},{12,0},{1,13},{5,9},{9,5},{13,1},{2,14},{6,10},... | collective-permute-start | bytes 835592 | tf_op jit(solution)/shard_map/ppermute | solution.py:548
  48.1 22.3 %collective-permute-start.10 = (bf16[2,544,128]{2,1,0:T(8,128)(2,1)S(1)}, bf16[2,544,128]{2,1,0:T(8,128)(2,1)S(1)}, u32[]{:S(2)}, u32[]{:S(2)}) collective-permute-start(bf16[2,544,128]{2,1,0:T(8,128)(2,1)S(1)} %get-tuple-element.44), channel_id=1, source_target_pairs={{0,8},{4,12},{8,0},{12,4},{1,9},{5,13},{9,1},{13,5},{2,10},{6,14},... | collective-permute-start | bytes 835592 | tf_op jit(solution)/shard_map/ppermute | solution.py:548
  57.6 16.7 %collective-permute-start.9 = (f32[2,1,4096]{2,1,0:T(1,128)S(1)}, f32[2,1,4096]{2,1,0:T(1,128)S(1)}, u32[]{:S(2)}, u32[]{:S(2)}) collective-permute-start(f32[2,1,4096]{2,1,0:T(1,128)S(1)} %get-tuple-element.42.refs_0_), channel_id=1, source_target_pairs={{0,12},{4,8},{8,4},{12,0},{1,13},{5,9},{9,5},{13,1},{2,14},{6,10},... | collective-permute-start | bytes 98312 | tf_op jit(solution)/shard_map/ppermute | solution.py:548
  60.8 13.4 %collective-permute-start.8 = (f32[2,1,4096]{2,1,0:T(1,128)S(1)}, f32[2,1,4096]{2,1,0:T(1,128)S(1)}, u32[]{:S(2)}, u32[]{:S(2)}) collective-permute-start(f32[2,1,4096]{2,1,0:T(1,128)S(1)} %get-tuple-element.42.refs_0_), channel_id=1, source_target_pairs={{0,8},{4,12},{8,0},{12,4},{1,9},{5,13},{9,1},{13,5},{2,10},{6,14},... | collective-permute-start | bytes 98312 | tf_op jit(solution)/shard_map/ppermute | solution.py:548
  64.5 9.8 %collective-permute-start.7 = (f32[2,1,4096]{2,1,0:T(1,128)S(1)}, f32[2,1,4096]{2,1,0:T(1,128)S(1)}, u32[]{:S(2)}, u32[]{:S(2)}) collective-permute-start(f32[2,1,4096]{2,1,0:T(1,128)S(1)} %get-tuple-element.42.refs_0_), channel_id=1, source_target_pairs={{0,4},{4,0},{8,12},{12,8},{1,5},{5,1},{9,13},{13,9},{2,6},{6,2},{1... | collective-permute-start | bytes 98312 | tf_op jit(solution)/shard_map/ppermute | solution.py:548

commit v14 on v13

--- a/solution.py
+++ b/solution.py
@@ -27,12 +27,6 @@
 
 def unit_rows(x):
     return x * lax.rsqrt(jnp.sum(x * x, axis=-1, keepdims=True) + 1e-06)
-
-
-def two_terms(cent):
-    scaled = cent.astype(F32) * EXP2_SCALE
-    high = scaled.astype(BF16)
-    return jnp.concatenate([high, (scaled - high.astype(F32)).astype(BF16)], axis=1)
 
 
 def params(**kwargs):
@@ -222,34 +216,31 @@
 
 
 def rank_kernel(me_ref, label_ref, rank_ref):
-    n, tokens = label_ref.shape[1:]
+    heads, n, tokens = label_ref.shape
     me = me_ref[0]
-    own = label_ref[0, 0:1, :].astype(jnp.int32)
-    rank = lax.broadcasted_iota(jnp.int32, own.shape, 1)
-    for m in range(1, n):
-        bar = own + ((me ^ m) < me).astype(jnp.int32)
-        bar = jnp.broadcast_to(bar, (16, tokens)).astype(jnp.int16)
-        count = jnp.zeros((16, tokens), BF16)
-        for s in range(0, tokens, LANES):
-            column = row_to_lanes(label_ref[0, m : m + 1, s : s + LANES])
-            column = column.astype(jnp.int32).astype(jnp.int16)
-            for r in range(0, LANES, 16):
-                other = jnp.tile(column[r : r + 16], (1, tokens // LANES))
-                count += jnp.where(other < bar, jnp.ones((), BF16), jnp.zeros((), BF16))
-        rank += jnp.sum(count.astype(F32), axis=0, keepdims=True).astype(jnp.int32)
-    rank_ref[0] = rank.astype(F32)
+    for h in range(heads):
+        own = label_ref[h, 0:1, :].astype(jnp.int32)
+        rank = lax.broadcasted_iota(jnp.int32, own.shape, 1)
+        for m in range(1, n):
+            bar = own + ((me ^ m) < me).astype(jnp.int32)
+            bar = jnp.broadcast_to(bar, (16, tokens)).astype(jnp.int16)
+            count = jnp.zeros((16, tokens), BF16)
+            for s in range(0, tokens, LANES):
+                column = row_to_lanes(label_ref[h, m : m + 1, s : s + LANES])
+                column = column.astype(jnp.int32).astype(jnp.int16)
+                for r in range(0, LANES, 16):
+                    other = jnp.tile(column[r : r + 16], (1, tokens // LANES))
+                    count += jnp.where(other < bar, jnp.ones((), BF16), jnp.zeros((), BF16))
+            rank += jnp.sum(count.astype(F32), axis=0, keepdims=True).astype(jnp.int32)
+        rank_ref[h] = rank.astype(F32)
 
 
 def own_ranks(me, labels):
-    heads, n, tokens = labels.shape
+    heads, _, tokens = labels.shape
     return pl.pallas_call(
         rank_kernel,
-        grid=(heads,),
-        in_specs=[
-            pl.BlockSpec(memory_space=pltpu.SMEM),
-            pl.BlockSpec((1, n, tokens), lambda h: (h, 0, 0)),
-        ],
-        out_specs=pl.BlockSpec((1, 1, tokens), lambda h: (h, 0, 0)),
+        in_specs=[pl.BlockSpec(memory_space=pltpu.SMEM), in_vmem()],
+        out_specs=in_vmem(),
         out_shape=jax.ShapeDtypeStruct((heads, 1, tokens), F32),
         compiler_params=params(),
         name="own_ranks",
@@ -262,16 +253,15 @@
 
     @pl.when(step == 0)
     def _():
-        unit = unit_rows(keys_ref[pl.program_id(0)].astype(F32)).astype(BF16)
-        unit_ref[...] = jnp.concatenate([unit, unit], axis=1)
+        unit_ref[...] = unit_rows(keys_ref[pl.program_id(0)].astype(F32)).astype(BF16)
         sum_ref[...] = jnp.zeros_like(sum_ref)
 
-    part = 256
+    part = 512
     rows = min(1024, cent_ref.shape[1])
     for c in range(0, cent_ref.shape[1], rows):
-        cent = two_terms(unit_rows(cent_ref[0, c : c + rows]).astype(BF16))
+        cent = unit_rows(cent_ref[0, c : c + rows]).astype(BF16)
         for t in range(0, tokens, part):
-            raw = jnp.exp2(dot_nt(cent, unit_ref[t : t + part, :]))
+            raw = jnp.exp2(dot_nt(cent, unit_ref[t : t + part, :]) * EXP2_SCALE)
             sum_ref[:, t : t + part] += jnp.sum(raw.reshape(-1, 8, part), axis=0)
 
     @pl.when(step == pl.num_programs(1) - 1)
@@ -294,7 +284,7 @@
         out_specs=pl.BlockSpec((1, 1, tokens), lambda h, c: (h, 0, 0)),
         out_shape=jax.ShapeDtypeStruct((heads, 1, tokens), F32),
         scratch_shapes=[
-            pltpu.VMEM((tokens, 2 * width), BF16),
+            pltpu.VMEM((tokens, width), BF16),
             pltpu.VMEM((8, tokens), F32),
         ],
         compiler_params=params(),
@@ -321,7 +311,7 @@
     unit = unit_rows(keys_ref[head].astype(F32)).astype(BF16)
     unit_ref[head] = unit
     scale_rows(unit, 1.0 / tot_ref[0], scaled_ref)
-    part = 256
+    part = 512
     for t in range(0, unit.shape[0], part):
         raw = jnp.exp2(dot_nt(cent, unit[t : t + part, :]) * EXP2_SCALE)
         more = dot_nn(raw.astype(BF16), scaled_ref[t : t + part])
@@ -374,7 +364,7 @@
     raw_ref, total_ref, cent_ref = refs[blocks:]
     head = pl.program_id(0)
     cent_ref[...] = unit_rows(sums_ref[head]).astype(BF16)
-    part = 256
+    part = 512
     start = 0
     for unit_ref in units:
         for t in range(0, unit_ref.shape[1], part):

time: 80.7 us -> 80.6 us (level)
  transfers between devices with their start and end apart: 13 -> 13, of which waited for: 5 -> 4; matrix products, arithmetic and copies ran while one was open for 3% -> 3% of each run, Pallas kernels for 51% -> 50%
where the time goes in v14:
time: 80.6 us; the launch traced here: 80.4 us
  Pallas kernels  50.6 us (63%)
  starting transfers between devices  18.4 us (23%)
  waiting for transfers between devices  7.58 us (9%)
  local copies, waits for them, and re-layouts  1.99 us (2%)
  between operations  1.07 us (1%)
    ppermute x12, starting transfers between devices, swap(): return lax.ppermute(x, 'ctx', [(i, i ^ d) for i in range(n)])  18.4 us
    pallas_call x4, Pallas kernels, first_block(): pl.pallas_call(functools.partial(first_kernel, fresh), grid_spec=pltpu.Pr...  13 us
    pallas_call x2, Pallas kernels, place(): pl.pallas_call(functools.partial(place_kernel, ids, size, fresh), in_spec...  9.38 us
    pallas_call x1, Pallas kernels, own_totals(): pl.pallas_call(totals_kernel, grid=(heads, count // rows), in_specs=[in_v...  7.7 us
    ppermute x12, waiting for transfers between devices, swap(): return lax.ppermute(x, 'ctx', [(i, i ^ d) for i in range(n)])  7.57 us
    pallas_call x1, Pallas kernels, weighted_sums(): pl.pallas_call(functools.partial(sums_kernel, len(units)), in_specs=[in_v...  6.06 us
    pallas_call x1, Pallas kernels, raw_weights(): pl.pallas_call(functools.partial(raw_kernel, len(units)), grid=(heads,),...  5.28 us
    pallas_call x1, Pallas kernels, sort_keys(): pl.pallas_call(sort_kernel, in_specs=[anywhere()] * 2, out_specs=(in_vmem...  4 us
  transfers between devices with their start and end apart: 13, of which 4 were waited for; matrix products, arithmetic and copies ran while one was open for 3% of the time, Pallas kernels for 50%

profile of v14, /device:TPU:0, one launch (start us, length us, event | category | flops | bytes accessed | tf_op | source)
XLA Modules:
  0.0 80.4 jit_solution(17143439825064103960)
XLA Ops:
  0.6 0.0 copy-start
  0.6 4.0 %sort_keys.1 = (bf16[2,1024,128]{2,1,0:T(8,128)(2,1)S(1)}, f32[2,1,1024]{2,1,0:T(1,128)S(1)}, s32[2,1,1024]{2,1,0:T(1,128)S(1)}) custom-call(s32[2,1024]{1,0:T(2,128)} %label_hbm.1, bf16[2048,128]{1,0:T(8,128)(2,1)} %bitcast.26), custom_call_target="tpu_custom_call" | custom-call | tf_op jit(solution)/shard_map/sort_keys/pallas_call | solution.py:135
  4.6 4.1 %collective-permute-start.1 = (bf16[2,1024,128]{2,1,0:T(8,128)(2,1)S(1)}, bf16[2,1024,128]{2,1,0:T(8,128)(2,1)S(1)}, u32[]{:S(2)}, u32[]{:S(2)}) collective-permute-start(bf16[2,1024,128]{2,1,0:T(8,128)(2,1)S(1)} %get-tuple-element.45.keys_ref.refs_0_), channel_id=1, source_target_pairs={{0,8},{4,12},{8,0},{12,4},{1,9},{5,13},{9,1},{13,5},{2,10},{6,14},... | collective-permute-start | bytes 1572872 | tf_op jit(solution)/shard_map/ppermute | solution.py:538
  8.8 1.6 %collective-permute-start = (bf16[2,1024,128]{2,1,0:T(8,128)(2,1)S(1)}, bf16[2,1024,128]{2,1,0:T(8,128)(2,1)S(1)}, u32[]{:S(2)}, u32[]{:S(2)}) collective-permute-start(bf16[2,1024,128]{2,1,0:T(8,128)(2,1)S(1)} %get-tuple-element.45.keys_ref.refs_0_), channel_id=1, source_target_pairs={{0,4},{4,0},{8,12},{12,8},{1,5},{5,1},{9,13},{13,9},{2,6},{6,2},{1... | collective-permute-start | bytes 1572872 | tf_op jit(solution)/shard_map/ppermute | solution.py:538
  10.3 0.0 collective-permute-start.2
  10.4 0.8 copy.13
  11.1 0.6 gather_fusion
  11.7 0.1 convert_bitcast_fusion
  11.8 0.1 copy.14
  11.9 0.2 convert_reduce_fusion.2
  12.1 0.1 fusion.5
  12.2 0.0 collective-permute-done.2._
  12.2 7.7 %own_totals.1.tot_ref = f32[2,1,1024]{2,1,0:T(1,128)S(1)} custom-call(bf16[2,1024,128]{2,1,0:T(8,128)(2,1)S(1)} %get-tuple-element.45.keys_ref.refs_0_, f32[2,4096,128]{2,1,0:T(8,128)} %cent_in.1, f32[2,1,128]{2,1,0:T(1,128)S(1)} %collective-permute-done.2._), custom_call_target="tpu_custom_call" | custom-call | tf_op jit(solution)/shard_map/own_totals/pallas_call | solution.py:276
  19.9 0.5 collective-permute-start.6
  20.4 0.1 pad_add_fusion
  20.5 0.0 copy-done
  20.5 0.2 dynamic-slice_reduce_fusion
  20.7 2.4 %sort_values.1.values_ref = bf16[2,1024,128]{2,1,0:T(8,128)(2,1)S(1)} custom-call(s32[2,1,1024]{2,1,0:T(1,128)S(1)} %get-tuple-element.43.spot_ref, bf16[2048,128]{1,0:T(8,128)(2,1)} %bitcast.27), custom_call_target="tpu_custom_call" | custom-call | tf_op jit(solution)/shard_map/sort_values/pallas_call | solution.py:173
  23.1 0.1 collective-permute-start.5
  23.2 3.9 %collective-permute-start.4 = (f32[2,2,1024]{2,1,0:T(2,128)S(1)}, f32[2,2,1024]{2,1,0:T(2,128)S(1)}, u32[]{:S(2)}, u32[]{:S(2)}) collective-permute-start(f32[2,2,1024]{2,1,0:T(2,128)S(1)} %pad_maximum_fusion.1), channel_id=1, source_target_pairs={{0,12},{4,8},{8,4},{12,0},{1,13},{5,9},{9,5},{13,1},{2,14},{6,10},... | collective-permute-start | bytes 49160 | tf_op jit(solution)/shard_map/ppermute | solution.py:538
  27.1 4.1 %first_block.4 = (f32[2,1024,128]{2,1,0:T(8,128)S(1)}, bf16[2,1024,128]{2,1,0:T(8,128)(2,1)S(1)}, bf16[2,1024,128]{2,1,0:T(8,128)(2,1)S(1)}) custom-call(s32[1]{0:T(128)} %bitcast._.me_ref, bf16[2,1024,128]{2,1,0:T(8,128)(2,1)S(1)} %get-tuple-element.45.keys_ref.refs_0_, f32[2,1,1024]{2,1,0:T(1,128)S(1)} %own_totals.1.tot_ref, f32[2,4096,128]{2,1,0:T(8,128)} %cent_in.1), custom_call_target="tpu_custom_call" | custom-call | tf_op jit(solution)/shard_map/first_block/pallas_call | solution.py:346
  31.2 1.9 %collective-permute-done.6 = f32[2,2,1024]{2,1,0:T(2,128)S(1)} collective-permute-done((f32[2,2,1024]{2,1,0:T(2,128)S(1)}, f32[2,2,1024]{2,1,0:T(2,128)S(1)}, u32[]{:S(2)}, u32[]{:S(2)}) %collective-permute-start.6) | collective-permute-done | bytes 16416 | tf_op jit(solution)/shard_map/ppermute | solution.py:538
  33.1 0.0 collective-permute-done.5
  33.1 0.9 %collective-permute-done.4 = f32[2,2,1024]{2,1,0:T(2,128)S(1)} collective-permute-done((f32[2,2,1024]{2,1,0:T(2,128)S(1)}, f32[2,2,1024]{2,1,0:T(2,128)S(1)}, u32[]{:S(2)}, u32[]{:S(2)}) %collective-permute-start.4) | collective-permute-done | bytes 16416 | tf_op jit(solution)/shard_map/ppermute | solution.py:538
  34.1 0.1 broadcast_compare_fusion
  34.2 0.2 convert_reduce_fusion
  34.4 0.0 collective-permute-done.1.keys_ref.refs_0_
  34.4 0.0 collective-permute-done.keys_ref.refs_1_
  34.4 0.5 collective-permute-start.3
  34.9 1.6 %own_ranks.1.rank_ref = f32[2,1,1024]{2,1,0:T(1,128)S(1)} custom-call(s32[1]{0:T(128)} %bitcast._.me_ref, f32[2,4,1024]{2,1,0:T(4,128)S(1)} %get-tuple-element.56.label_ref), custom_call_target="tpu_custom_call" | custom-call | tf_op jit(solution)/shard_map/own_ranks/pallas_call | solution.py:240
  36.5 3.0 %first_block.5 = (f32[2,1024,128]{2,1,0:T(8,128)S(1)}, bf16[2,1024,128]{2,1,0:T(8,128)(2,1)S(1)}) custom-call(s32[1]{0:T(128)} %bitcast._.me_ref, bf16[2,1024,128]{2,1,0:T(8,128)(2,1)S(1)} %collective-permute-done.keys_ref.refs_1_, f32[2,1,1024]{2,1,0:T(1,128)S(1)} %get-tuple-element.58.tot_ref, ...), custom_call_target="tpu_custom_call", output_to_operand_aliasing={{0}: (4, {})} | custom-call | tf_op jit(solution)/shard_map/first_block/pallas_call | solution.py:346
  39.5 0.6 windows.3
  40.1 1.7 %collective-permute-start.11 = (bf16[2,544,128]{2,1,0:T(8,128)(2,1)S(1)}, bf16[2,544,128]{2,1,0:T(8,128)(2,1)S(1)}, u32[]{:S(2)}, u32[]{:S(2)}) collective-permute-start(bf16[2,544,128]{2,1,0:T(8,128)(2,1)S(1)} %get-tuple-element.47), channel_id=1, source_target_pairs={{0,4},{4,0},{8,12},{12,8},{1,5},{5,1},{9,13},{13,9},{2,6},{6,2},{1... | collective-permute-start | bytes 835592 | tf_op jit(solution)/shard_map/ppermute | solution.py:538
  41.8 0.1 constant_dynamic-update-slice_fusion.2
  41.9 2.6 %collective-permute-start.12 = (bf16[2,544,128]{2,1,0:T(8,128)(2,1)S(1)}, bf16[2,544,128]{2,1,0:T(8,128)(2,1)S(1)}, u32[]{:S(2)}, u32[]{:S(2)}) collective-permute-start(bf16[2,544,128]{2,1,0:T(8,128)(2,1)S(1)} %get-tuple-element.48), channel_id=1, source_target_pairs={{0,12},{4,8},{8,4},{12,0},{1,13},{5,9},{9,5},{13,1},{2,14},{6,10},... | collective-permute-start | bytes 835592 | tf_op jit(solution)/shard_map/ppermute | solution.py:538
  44.4 3.0 %first_block.6 = (f32[2,1024,128]{2,1,0:T(8,128)S(1)}, bf16[2,1024,128]{2,1,0:T(8,128)(2,1)S(1)}) custom-call(s32[1]{0:T(128)} %bitcast._.me_ref, bf16[2,1024,128]{2,1,0:T(8,128)(2,1)S(1)} %collective-permute-done.1.keys_ref.refs_0_, f32[2,1,1024]{2,1,0:T(1,128)S(1)} %get-tuple-element.60.tot_ref, ...), custom_call_target="tpu_custom_call", output_to_operand_aliasing={{0}: (4, {})} | custom-call | tf_op jit(solution)/shard_map/first_block/pallas_call | solution.py:346
  47.4 0.6 windows.2
  48.0 0.1 collective-permute-start.10
  48.1 0.1 constant_dynamic-update-slice_fusion.1
  48.2 1.1 %collective-permute-done.3.keys_ref.refs_2_ = bf16[2,1024,128]{2,1,0:T(8,128)(2,1)S(1)} collective-permute-done((bf16[2,1024,128]{2,1,0:T(8,128)(2,1)S(1)}, bf16[2,1024,128]{2,1,0:T(8,128)(2,1)S(1)}, u32[]{:S(2)}, u32[]{:S(2)}) %collective-permute-start.3) | collective-permute-done | bytes 524320 | tf_op jit(solution)/shard_map/ppermute | solution.py:538
  49.3 3.0 %first_block.7 = (f32[2,1024,128]{2,1,0:T(8,128)S(1)}, bf16[2,1024,128]{2,1,0:T(8,128)(2,1)S(1)}) custom-call(s32[1]{0:T(128)} %bitcast._.me_ref, bf16[2,1024,128]{2,1,0:T(8,128)(2,1)S(1)} %collective-permute-done.3.keys_ref.refs_2_, f32[2,1,1024]{2,1,0:T(1,128)S(1)} %get-tuple-element.62.tot_ref, ...), custom_call_target="tpu_custom_call", output_to_operand_aliasing={{0}: (4, {})} | custom-call | tf_op jit(solution)/shard_map/first_block/pallas_call | solution.py:346
  52.3 5.3 %raw_weights.1 = (bf16[2,1024,4096]{2,1,0:T(8,128)(2,1)S(1)}, f32[2,1,4096]{2,1,0:T(1,128)S(1)}) custom-call(f32[2,1024,128]{2,1,0:T(8,128)S(1)} %get-tuple-element.36.sums_ref, bf16[2,1024,128]{2,1,0:T(8,128)(2,1)S(1)} %get-tuple-element.37.refs_0_.refs_4_, bf16[2,1024,128]{2,1,0:T(8,128)(2,1)S(1)} %get-tuple-element.38.refs_1_.refs_5_._, ...), custom_call_target="tpu_custom_call" | custom-call | tf_op jit(solution)/shard_map/raw_weights/pallas_call | solution.py:383
  57.6 3.4 %collective-permute-start.9 = (f32[2,1,4096]{2,1,0:T(1,128)S(1)}, f32[2,1,4096]{2,1,0:T(1,128)S(1)}, u32[]{:S(2)}, u32[]{:S(2)}) collective-permute-start(f32[2,1,4096]{2,1,0:T(1,128)S(1)} %get-tuple-element.42.refs_0_), channel_id=1, source_target_pairs={{0,12},{4,8},{8,4},{12,0},{1,13},{5,9},{9,5},{13,1},{2,14},{6,10},... | collective-permute-start | bytes 98312 | tf_op jit(solution)/shard_map/ppermute | solution.py:538
  61.0 0.0 collective-permute-start.8
  61.0 3.6 %collective-permute-done.11.refs_4_ = bf16[2,544,128]{2,1,0:T(8,128)(2,1)S(1)} collective-permute-done((bf16[2,544,128]{2,1,0:T(8,128)(2,1)S(1)}, bf16[2,544,128]{2,1,0:T(8,128)(2,1)S(1)}, u32[]{:S(2)}, u32[]{:S(2)}) %collective-permute-start.11) | collective-permute-done | bytes 278560 | tf_op jit(solution)/shard_map/ppermute | solution.py:538
  64.6 0.0 collective-permute-start.7
  64.6 0.1 constant_dynamic-update-slice_fusion.scalar_ref
  64.7 0.0 collective-permute-done.12.refs_5_
  64.7 5.6 %place.2.refs_2_ = bf16[2,2048,256]{2,1,0:T(8,128)(2,1)S(1)} custom-call(s32[5,2,4]{2,1,0:T(2,128)S(1)} %constant_dynamic-update-slice_fusion.scalar_ref, f32[2,4,1024]{2,1,0:T(4,128)S(1)} %get-tuple-element.56.label_ref, bf16[2,1024,128]{2,1,0:T(8,128)(2,1)S(1)} %get-tuple-element.45.keys_ref.refs_0_, ...), custom_call_target="tpu_custom_call" | custom-call | tf_op jit(solution)/shard_map/place/pallas_call | solution.py:517
  70.3 0.0 collective-permute-done.10.refs_1_
  70.3 3.8 %place.3 = (bf16[4096,128]{1,0:T(8,128)(2,1)}, bf16[4096,128]{1,0:T(8,128)(2,1)}) custom-call(s32[5,2,4]{2,1,0:T(2,128)S(1)} %constant_dynamic-update-slice_fusion.scalar_ref, f32[2,4,1024]{2,1,0:T(4,128)S(1)} %get-tuple-element.56.label_ref, bf16[2,1024,128]{2,1,0:T(8,128)(2,1)S(1)} %collective-permute-done.1.keys_ref.refs_0_, ...), custom_call_target="tpu_custom_call" | custom-call | tf_op jit(solution)/shard_map/place/pallas_call | solution.py:517
  74.1 0.0 collective-permute-done.9.refs_3_
  74.1 0.0 collective-permute-done.8.refs_2_
  74.1 0.0 collective-permute-done.7.refs_1_
  74.1 6.1 %weighted_sums.1 = f32[2,1024,128]{2,1,0:T(8,128)} custom-call(bf16[2,1024,4096]{2,1,0:T(8,128)(2,1)S(1)} %get-tuple-element.41.raw_ref, f32[2,1,4096]{2,1,0:T(1,128)S(1)} %get-tuple-element.42.refs_0_, f32[2,1,4096]{2,1,0:T(1,128)S(1)} %collective-permute-done.7.refs_1_, f32[2,1,4096]{2,1,0:T(1,128)S(1)} %collective-permute-done.8.refs_2_, ...), custom_call_target="tpu_custom_call" | custom-call | tf_op jit(solution)/shard_map/weighted_sums/pallas_call | solution.py:421
  (13 shorter events, 0.1 us)
Async XLA Ops:
  0.6 19.9 %copy-start = (s32[2,5]{1,0:T(2,128)S(1)}, s32[2,5]{1,0:T(2,128)}, u32[]{:S(2)}) copy-start(s32[2,5]{1,0:T(2,128)} %param.8) | copy-start | bytes 124
  4.6 29.7 %collective-permute-start.1 = (bf16[2,1024,128]{2,1,0:T(8,128)(2,1)S(1)}, bf16[2,1024,128]{2,1,0:T(8,128)(2,1)S(1)}, u32[]{:S(2)}, u32[]{:S(2)}) collective-permute-start(bf16[2,1024,128]{2,1,0:T(8,128)(2,1)S(1)} %get-tuple-element.45.keys_ref.refs_0_), channel_id=1, source_target_pairs={{0,8},{4,12},{8,0},{12,4},{1,9},{5,13},{9,1},{13,5},{2,10},{6,14},... | collective-permute-start | bytes 1572872 | tf_op jit(solution)/shard_map/ppermute | solution.py:538
  8.8 25.6 %collective-permute-start = (bf16[2,1024,128]{2,1,0:T(8,128)(2,1)S(1)}, bf16[2,1024,128]{2,1,0:T(8,128)(2,1)S(1)}, u32[]{:S(2)}, u32[]{:S(2)}) collective-permute-start(bf16[2,1024,128]{2,1,0:T(8,128)(2,1)S(1)} %get-tuple-element.45.keys_ref.refs_0_), channel_id=1, source_target_pairs={{0,4},{4,0},{8,12},{12,8},{1,5},{5,1},{9,13},{13,9},{2,6},{6,2},{1... | collective-permute-start | bytes 1572872 | tf_op jit(solution)/shard_map/ppermute | solution.py:538
  10.3 1.9 %collective-permute-start.2 = (f32[2,1,128]{2,1,0:T(1,128)S(1)}, f32[2,1,128]{2,1,0:T(1,128)S(1)}, u32[]{:S(2)}, u32[]{:S(2)}) collective-permute-start(f32[2,1,128]{2,1,0:T(1,128)S(1)} %slice.33), channel_id=1, source_target_pairs={{0,1},{1,0},{2,3},{3,2},{4,5},{5,4},{6,7},{7,6},{8,9},{9,8},{10,11... | collective-permute-start | bytes 3080 | tf_op jit(solution)/shard_map/ppermute | solution.py:556
  19.9 13.2 %collective-permute-start.6 = (f32[2,2,1024]{2,1,0:T(2,128)S(1)}, f32[2,2,1024]{2,1,0:T(2,128)S(1)}, u32[]{:S(2)}, u32[]{:S(2)}) collective-permute-start(f32[2,2,1024]{2,1,0:T(2,128)S(1)} %pad_maximum_fusion.1), channel_id=1, source_target_pairs={{0,4},{4,0},{8,12},{12,8},{1,5},{5,1},{9,13},{13,9},{2,6},{6,2},{1... | collective-permute-start | bytes 49160 | tf_op jit(solution)/shard_map/ppermute | solution.py:538
  23.1 10.0 %collective-permute-start.5 = (f32[2,2,1024]{2,1,0:T(2,128)S(1)}, f32[2,2,1024]{2,1,0:T(2,128)S(1)}, u32[]{:S(2)}, u32[]{:S(2)}) collective-permute-start(f32[2,2,1024]{2,1,0:T(2,128)S(1)} %pad_maximum_fusion.1), channel_id=1, source_target_pairs={{0,8},{4,12},{8,0},{12,4},{1,9},{5,13},{9,1},{13,5},{2,10},{6,14},... | collective-permute-start | bytes 49160 | tf_op jit(solution)/shard_map/ppermute | solution.py:538
  23.2 10.8 %collective-permute-start.4 = (f32[2,2,1024]{2,1,0:T(2,128)S(1)}, f32[2,2,1024]{2,1,0:T(2,128)S(1)}, u32[]{:S(2)}, u32[]{:S(2)}) collective-permute-start(f32[2,2,1024]{2,1,0:T(2,128)S(1)} %pad_maximum_fusion.1), channel_id=1, source_target_pairs={{0,12},{4,8},{8,4},{12,0},{1,13},{5,9},{9,5},{13,1},{2,14},{6,10},... | collective-permute-start | bytes 49160 | tf_op jit(solution)/shard_map/ppermute | solution.py:538
  34.4 14.9 %collective-permute-start.3 = (bf16[2,1024,128]{2,1,0:T(8,128)(2,1)S(1)}, bf16[2,1024,128]{2,1,0:T(8,128)(2,1)S(1)}, u32[]{:S(2)}, u32[]{:S(2)}) collective-permute-start(bf16[2,1024,128]{2,1,0:T(8,128)(2,1)S(1)} %collective-permute-done.1.keys_ref.refs_0_), channel_id=1, source_target_pairs={{0,4},{4,0},{8,12},{12,8},{1,5},{5,1},{9,13},{13,9},{2,6},{6,2},{1... | collective-permute-start | bytes 1572872 | tf_op jit(solution)/shard_map/ppermute | solution.py:538
  40.1 24.5 %collective-permute-start.11 = (bf16[2,544,128]{2,1,0:T(8,128)(2,1)S(1)}, bf16[2,544,128]{2,1,0:T(8,128)(2,1)S(1)}, u32[]{:S(2)}, u32[]{:S(2)}) collective-permute-start(bf16[2,544,128]{2,1,0:T(8,128)(2,1)S(1)} %get-tuple-element.47), channel_id=1, source_target_pairs={{0,4},{4,0},{8,12},{12,8},{1,5},{5,1},{9,13},{13,9},{2,6},{6,2},{1... | collective-permute-start | bytes 835592 | tf_op jit(solution)/shard_map/ppermute | solution.py:538
  41.9 22.8 %collective-permute-start.12 = (bf16[2,544,128]{2,1,0:T(8,128)(2,1)S(1)}, bf16[2,544,128]{2,1,0:T(8,128)(2,1)S(1)}, u32[]{:S(2)}, u32[]{:S(2)}) collective-permute-start(bf16[2,544,128]{2,1,0:T(8,128)(2,1)S(1)} %get-tuple-element.48), channel_id=1, source_target_pairs={{0,12},{4,8},{8,4},{12,0},{1,13},{5,9},{9,5},{13,1},{2,14},{6,10},... | collective-permute-start | bytes 835592 | tf_op jit(solution)/shard_map/ppermute | solution.py:538
  48.0 22.3 %collective-permute-start.10 = (bf16[2,544,128]{2,1,0:T(8,128)(2,1)S(1)}, bf16[2,544,128]{2,1,0:T(8,128)(2,1)S(1)}, u32[]{:S(2)}, u32[]{:S(2)}) collective-permute-start(bf16[2,544,128]{2,1,0:T(8,128)(2,1)S(1)} %get-tuple-element.44), channel_id=1, source_target_pairs={{0,8},{4,12},{8,0},{12,4},{1,9},{5,13},{9,1},{13,5},{2,10},{6,14},... | collective-permute-start | bytes 835592 | tf_op jit(solution)/shard_map/ppermute | solution.py:538
  57.6 16.5 %collective-permute-start.9 = (f32[2,1,4096]{2,1,0:T(1,128)S(1)}, f32[2,1,4096]{2,1,0:T(1,128)S(1)}, u32[]{:S(2)}, u32[]{:S(2)}) collective-permute-start(f32[2,1,4096]{2,1,0:T(1,128)S(1)} %get-tuple-element.42.refs_0_), channel_id=1, source_target_pairs={{0,12},{4,8},{8,4},{12,0},{1,13},{5,9},{9,5},{13,1},{2,14},{6,10},... | collective-permute-start | bytes 98312 | tf_op jit(solution)/shard_map/ppermute | solution.py:538
  61.0 13.1 %collective-permute-start.8 = (f32[2,1,4096]{2,1,0:T(1,128)S(1)}, f32[2,1,4096]{2,1,0:T(1,128)S(1)}, u32[]{:S(2)}, u32[]{:S(2)}) collective-permute-start(f32[2,1,4096]{2,1,0:T(1,128)S(1)} %get-tuple-element.42.refs_0_), channel_id=1, source_target_pairs={{0,8},{4,12},{8,0},{12,4},{1,9},{5,13},{9,1},{13,5},{2,10},{6,14},... | collective-permute-start | bytes 98312 | tf_op jit(solution)/shard_map/ppermute | solution.py:538
  64.6 9.5 %collective-permute-start.7 = (f32[2,1,4096]{2,1,0:T(1,128)S(1)}, f32[2,1,4096]{2,1,0:T(1,128)S(1)}, u32[]{:S(2)}, u32[]{:S(2)}) collective-permute-start(f32[2,1,4096]{2,1,0:T(1,128)S(1)} %get-tuple-element.42.refs_0_), channel_id=1, source_target_pairs={{0,4},{4,0},{8,12},{12,8},{1,5},{5,1},{9,13},{13,9},{2,6},{6,2},{1... | collective-permute-start | bytes 98312 | tf_op jit(solution)/shard_map/ppermute | solution.py:538

commit v15 on v13

--- a/solution.py
+++ b/solution.py
@@ -27,12 +27,6 @@
 
 def unit_rows(x):
     return x * lax.rsqrt(jnp.sum(x * x, axis=-1, keepdims=True) + 1e-06)
-
-
-def two_terms(cent):
-    scaled = cent.astype(F32) * EXP2_SCALE
-    high = scaled.astype(BF16)
-    return jnp.concatenate([high, (scaled - high.astype(F32)).astype(BF16)], axis=1)
 
 
 def params(**kwargs):
@@ -262,16 +256,15 @@
 
     @pl.when(step == 0)
     def _():
-        unit = unit_rows(keys_ref[pl.program_id(0)].astype(F32)).astype(BF16)
-        unit_ref[...] = jnp.concatenate([unit, unit], axis=1)
+        unit_ref[...] = unit_rows(keys_ref[pl.program_id(0)].astype(F32)).astype(BF16)
         sum_ref[...] = jnp.zeros_like(sum_ref)
 
     part = 256
     rows = min(1024, cent_ref.shape[1])
     for c in range(0, cent_ref.shape[1], rows):
-        cent = two_terms(unit_rows(cent_ref[0, c : c + rows]).astype(BF16))
+        cent = unit_rows(cent_ref[0, c : c + rows]).astype(BF16)
         for t in range(0, tokens, part):
-            raw = jnp.exp2(dot_nt(cent, unit_ref[t : t + part, :]))
+            raw = jnp.exp2(dot_nt(cent, unit_ref[t : t + part, :]) * EXP2_SCALE)
             sum_ref[:, t : t + part] += jnp.sum(raw.reshape(-1, 8, part), axis=0)
 
     @pl.when(step == pl.num_programs(1) - 1)
@@ -294,7 +287,7 @@
         out_specs=pl.BlockSpec((1, 1, tokens), lambda h, c: (h, 0, 0)),
         out_shape=jax.ShapeDtypeStruct((heads, 1, tokens), F32),
         scratch_shapes=[
-            pltpu.VMEM((tokens, 2 * width), BF16),
+            pltpu.VMEM((tokens, width), BF16),
             pltpu.VMEM((8, tokens), F32),
         ],
         compiler_params=params(),
@@ -369,10 +362,18 @@
     )(*args)
 
 
-def raw_kernel(blocks, sums_ref, *refs):
-    units = refs[:blocks]
-    raw_ref, total_ref, cent_ref = refs[blocks:]
+def raw_kernel(blocks, size, sums_ref, *refs):
+    units, refs = refs[:blocks], refs[blocks:]
+    scalar_ref, label_ref, key_ref, value_ref, *refs = refs
+    raw_ref, total_ref, so_far_ref, cent_ref, rows_ref, near_ref = refs
     head = pl.program_id(0)
+
+    @pl.when(head == 0)
+    def _():
+        fill_windows(
+            [0], size, scalar_ref, label_ref, [key_ref], [value_ref], rows_ref, near_ref
+        )
+
     cent_ref[...] = unit_rows(sums_ref[head]).astype(BF16)
     part = 256
     start = 0
@@ -384,25 +385,40 @@
             total = jnp.sum(raw.reshape(-1, 8, part), axis=0)
             total_ref[0, :, here] = jnp.sum(total, axis=0, keepdims=True)
         start += unit_ref.shape[1]
-
-
-def raw_weights(sums, units):
+    rows = 512
+    for r in range(0, so_far_ref.shape[1], rows):
+        pick = one_hot_rows(rows, near_ref[head] - r)
+        so_far_ref[head, r : r + rows] = dot_nn(pick, rows_ref[head]).astype(BF16)
+
+
+def raw_weights(sums, units, scalars, labels, keys, values, size, cap):
     heads, rows, width = sums.shape
     tokens = units[0].shape[1]
     count = tokens * len(units)
     return pl.pallas_call(
-        functools.partial(raw_kernel, len(units)),
+        functools.partial(raw_kernel, len(units), size),
         grid=(heads,),
-        in_specs=[in_vmem()] * (1 + len(units)),
-        out_specs=(in_vmem(), pl.BlockSpec((1, 1, count), lambda h: (h, 0, 0))),
+        in_specs=[in_vmem()] * (1 + len(units))
+        + [pl.BlockSpec(memory_space=pltpu.SMEM)]
+        + [in_vmem()] * 3,
+        out_specs=(
+            in_vmem(),
+            pl.BlockSpec((1, 1, count), lambda h: (h, 0, 0)),
+            in_vmem(),
+        ),
         out_shape=(
             pltpu.VMEM((heads, rows, count), BF16),
             jax.ShapeDtypeStruct((heads, 1, count), F32),
+            pltpu.VMEM((heads, cap, 2 * width), BF16),
         ),
-        scratch_shapes=[pltpu.VMEM((rows, width), BF16)],
+        scratch_shapes=[
+            pltpu.VMEM((rows, width), BF16),
+            pltpu.VMEM((heads, size, 2 * width), BF16),
+            pltpu.VMEM((heads, 1, size), jnp.int32),
+        ],
         compiler_params=params(),
         name="raw_weights",
-    )(keep_vmem(sums), *map(keep_vmem, units))
+    )(keep_vmem(sums), *map(keep_vmem, units), scalars, labels, *map(keep_vmem, (keys, values)))
 
 
 def sums_kernel(blocks, raw_ref, *refs):
@@ -466,30 +482,33 @@
             near_ref[h, :, here : here + size] = spot[:, :size]
 
 
-def place_kernel(ids, size, fresh, scalar_ref, label_ref, *refs):
+def place_kernel(ids, size, last, scalar_ref, label_ref, *refs):
     count = len(ids)
     keys, values, refs = refs[:count], refs[count : 2 * count], refs[2 * count :]
-    if fresh:
-        so_far_ref, rows_ref, near_ref = refs
+    so_far_ref, *refs = refs
+    if last:
+        *out_hbm, rows_ref, near_ref, mixed_ref, done_ref, sems = refs
+        width = done_ref.shape[2]
+        cap = done_ref.shape[1] // rows_ref.shape[0]
     else:
-        so_far_ref, *out_hbm, rows_ref, near_ref, mixed_ref, done_ref, sems = refs
+        out_ref, rows_ref, near_ref = refs
+        cap = out_ref.shape[1]
+    heads = rows_ref.shape[0]
     fill_windows(ids, size, scalar_ref, label_ref, keys, values, rows_ref, near_ref)
-    heads, cap, both = so_far_ref.shape
-    width = both // 2
     rows = 512
     copies = []
     for r in range(0, cap, rows):
         for h in range(heads):
             total = dot_nn(one_hot_rows(rows, near_ref[h] - r), rows_ref[h])
-            if fresh:
-                so_far_ref[h, r : r + rows] = total.astype(BF16)
+            total += so_far_ref[h, r : r + rows].astype(F32)
+            if not last:
+                out_ref[h, r : r + rows] = total.astype(BF16)
                 continue
-            total += so_far_ref[h, r : r + rows].astype(F32)
             for side in range(2):
                 mixed_ref[side, pl.Slice(h, rows, heads), :] = total[
                     :, side * width : (side + 1) * width
                 ]
-        if fresh:
+        if not last:
             continue
         here = slice(r * heads, (r + rows) * heads)
         for side in range(2):
@@ -504,19 +523,14 @@
         copy.wait()
 
 
-def place(scalars, labels, keys, values, ids, size, cap, so_far):
+def place(scalars, labels, keys, values, ids, size, cap, so_far, last=False):
     heads, _, width = keys[0].shape
-    fresh = so_far is None
-    moved = [x[m] for x in (keys, values) for m in ids]
+    moved = [x[m] for x in (keys, values) for m in ids] + [so_far]
     scratch = [
         pltpu.VMEM((heads, len(ids) * size, 2 * width), BF16),
         pltpu.VMEM((heads, 1, len(ids) * size), jnp.int32),
     ]
-    if fresh:
-        out_shape = pltpu.VMEM((heads, cap, 2 * width), BF16)
-        out_specs = in_vmem()
-    else:
-        moved.append(so_far)
+    if last:
         out_shape = (jax.ShapeDtypeStruct((heads * cap, width), BF16),) * 2
         out_specs = (anywhere(), anywhere())
         scratch += [
@@ -524,8 +538,11 @@
             pltpu.VMEM((2, heads * cap, width), BF16),
             pltpu.SemaphoreType.DMA((2 * cap // 512,)),
         ]
-    return pl.pallas_call(
-        functools.partial(place_kernel, ids, size, fresh),
+    else:
+        out_shape = pltpu.VMEM((heads, cap, 2 * width), BF16)
+        out_specs = in_vmem()
+    return pl.pallas_call(
+        functools.partial(place_kernel, ids, size, last),
         in_specs=[pl.BlockSpec(memory_space=pltpu.SMEM)] + [in_vmem()] * (1 + len(moved)),
         out_specs=out_specs,
         out_shape=out_shape,
@@ -604,11 +621,14 @@
             for d, window in zip(group, windows(some, ranks, own_values, send_size, unit)):
                 values[d] = swap(window, d) if d else window
 
-    raw, part = raw_weights(sums, units)
+    raw, part, so_far = raw_weights(
+        sums, units, scalars, labels, own_keys, values[0], key_size, cap
+    )
     parts = spread(part)
-    so_far = place(scalars, labels, keys, values, [0, *early], key_size, cap, None)
+    so_far = place(scalars, labels, keys, values, early, key_size, cap, so_far)
+    so_far, units[0] = lax.optimization_barrier((so_far, units[0]))
     out = weighted_sums(raw, units, parts)
-    placed = place(scalars, labels, keys, values, late, key_size, cap, so_far)
+    placed = place(scalars, labels, keys, values, late, key_size, cap, so_far, last=True)
     shape = (cap, heads, width)
     return out, placed[0].reshape(shape), placed[1].reshape(shape)
 

time: 80.7 us -> 81.4 us (level)
  starting transfers between devices: 18.3 us -> 20.4 us
  waiting for transfers between devices: 7.64 us -> 5.55 us
    ppermute x12, starting transfers between devices: 18.3 us -> 20.4 us  [swap(): return lax.ppermute(x, 'ctx', [(i, i ^ d) for i in range(n)])]
    ppermute x12, waiting for transfers between devices: 7.64 us -> 5.55 us  [swap(): return lax.ppermute(x, 'ctx', [(i, i ^ d) for i in range(n)])]
  transfers between devices with their start and end apart: 13 -> 13, of which waited for: 5 -> 3; matrix products, arithmetic and copies ran while one was open for 3% -> 3% of each run, Pallas kernels for 51% -> 51%
where the time goes in v15:
time: 81.4 us; the launch traced here: 81.2 us
  Pallas kernels  51.5 us (63%)
  starting transfers between devices  20.4 us (25%)
  waiting for transfers between devices  5.55 us (7%)
  local copies, waits for them, and re-layouts  1.99 us (2%)
  between operations  1.08 us (1%)
    ppermute x12, starting transfers between devices, swap(): return lax.ppermute(x, 'ctx', [(i, i ^ d) for i in range(n)])  20.4 us
    pallas_call x4, Pallas kernels, first_block(): pl.pallas_call(functools.partial(first_kernel, fresh), grid_spec=pltpu.Pr...  13 us
    pallas_call x1, Pallas kernels, raw_weights(): pl.pallas_call(functools.partial(raw_kernel, len(units), size), grid=(hea...  7.78 us
    pallas_call x1, Pallas kernels, own_totals(): pl.pallas_call(totals_kernel, grid=(heads, count // rows), in_specs=[in_v...  7.7 us
    pallas_call x2, Pallas kernels, place(): pl.pallas_call(functools.partial(place_kernel, ids, size, last), in_specs...  7.62 us
    pallas_call x1, Pallas kernels, weighted_sums(): pl.pallas_call(functools.partial(sums_kernel, len(units)), in_specs=[in_v...  6.09 us
    ppermute x12, waiting for transfers between devices, swap(): return lax.ppermute(x, 'ctx', [(i, i ^ d) for i in range(n)])  5.55 us
    pallas_call x1, Pallas kernels, sort_keys(): pl.pallas_call(sort_kernel, in_specs=[anywhere()] * 2, out_specs=(in_vmem...  4 us
  transfers between devices with their start and end apart: 13, of which 3 were waited for; matrix products, arithmetic and copies ran while one was open for 3% of the time, Pallas kernels for 51%

profile of v15, /device:TPU:0, one launch (start us, length us, event | category | flops | bytes accessed | tf_op | source)
XLA Modules:
  0.0 81.2 jit_solution(14737299768652601325)
XLA Ops:
  0.6 0.0 copy-start
  0.6 4.0 %sort_keys.1 = (bf16[2,1024,128]{2,1,0:T(8,128)(2,1)S(1)}, f32[2,1,1024]{2,1,0:T(1,128)S(1)}, s32[2,1,1024]{2,1,0:T(1,128)S(1)}) custom-call(s32[2,1024]{1,0:T(2,128)} %label_hbm.1, bf16[2048,128]{1,0:T(8,128)(2,1)} %bitcast.26), custom_call_target="tpu_custom_call" | custom-call | tf_op jit(solution)/shard_map/sort_keys/pallas_call | solution.py:135
  4.6 3.1 %collective-permute-start = (bf16[2,1024,128]{2,1,0:T(8,128)(2,1)S(1)}, bf16[2,1024,128]{2,1,0:T(8,128)(2,1)S(1)}, u32[]{:S(2)}, u32[]{:S(2)}) collective-permute-start(bf16[2,1024,128]{2,1,0:T(8,128)(2,1)S(1)} %get-tuple-element.29.keys_ref.refs_6_), channel_id=1, source_target_pairs={{0,4},{4,0},{8,12},{12,8},{1,5},{5,1},{9,13},{13,9},{2,6},{6,2},{1... | collective-permute-start | bytes 1572872 | tf_op jit(solution)/shard_map/ppermute | solution.py:565
  7.7 2.6 %collective-permute-start.1 = (bf16[2,1024,128]{2,1,0:T(8,128)(2,1)S(1)}, bf16[2,1024,128]{2,1,0:T(8,128)(2,1)S(1)}, u32[]{:S(2)}, u32[]{:S(2)}) collective-permute-start(bf16[2,1024,128]{2,1,0:T(8,128)(2,1)S(1)} %get-tuple-element.29.keys_ref.refs_6_), channel_id=1, source_target_pairs={{0,8},{4,12},{8,0},{12,4},{1,9},{5,13},{9,1},{13,5},{2,10},{6,14},... | collective-permute-start | bytes 1572872 | tf_op jit(solution)/shard_map/ppermute | solution.py:565
  10.3 0.0 collective-permute-start.2
  10.4 0.8 copy.13
  11.1 0.6 gather_fusion
  11.7 0.1 convert_bitcast_fusion
  11.8 0.1 copy.14
  11.9 0.2 convert_reduce_fusion.2
  12.1 0.1 fusion.5
  12.2 0.0 collective-permute-done.2._
  12.2 7.7 %own_totals.1.tot_ref = f32[2,1,1024]{2,1,0:T(1,128)S(1)} custom-call(bf16[2,1024,128]{2,1,0:T(8,128)(2,1)S(1)} %get-tuple-element.29.keys_ref.refs_6_, f32[2,4096,128]{2,1,0:T(8,128)} %cent_in.1, f32[2,1,128]{2,1,0:T(1,128)S(1)} %collective-permute-done.2._), custom_call_target="tpu_custom_call" | custom-call | tf_op jit(solution)/shard_map/own_totals/pallas_call | solution.py:279
  19.9 0.5 collective-permute-start.6
  20.4 0.1 pad_add_fusion
  20.5 0.0 copy-done
  20.5 0.2 dynamic-slice_reduce_fusion
  20.7 2.4 %sort_values.1.values_ref = bf16[2,1024,128]{2,1,0:T(8,128)(2,1)S(1)} custom-call(s32[2,1,1024]{2,1,0:T(1,128)S(1)} %get-tuple-element.43.spot_ref, bf16[2048,128]{1,0:T(8,128)(2,1)} %bitcast.27), custom_call_target="tpu_custom_call" | custom-call | tf_op jit(solution)/shard_map/sort_values/pallas_call | solution.py:173
  23.1 0.1 collective-permute-start.5
  23.2 3.9 %collective-permute-start.4 = (f32[2,2,1024]{2,1,0:T(2,128)S(1)}, f32[2,2,1024]{2,1,0:T(2,128)S(1)}, u32[]{:S(2)}, u32[]{:S(2)}) collective-permute-start(f32[2,2,1024]{2,1,0:T(2,128)S(1)} %pad_maximum_fusion.1), channel_id=1, source_target_pairs={{0,12},{4,8},{8,4},{12,0},{1,13},{5,9},{9,5},{13,1},{2,14},{6,10},... | collective-permute-start | bytes 49160 | tf_op jit(solution)/shard_map/ppermute | solution.py:565
  27.1 4.1 %first_block.4 = (f32[2,1024,128]{2,1,0:T(8,128)S(1)}, bf16[2,1024,128]{2,1,0:T(8,128)(2,1)S(1)}, bf16[2,1024,128]{2,1,0:T(8,128)(2,1)S(1)}) custom-call(s32[1]{0:T(128)} %bitcast._.me_ref, bf16[2,1024,128]{2,1,0:T(8,128)(2,1)S(1)} %get-tuple-element.29.keys_ref.refs_6_, f32[2,1,1024]{2,1,0:T(1,128)S(1)} %own_totals.1.tot_ref, f32[2,4096,128]{2,1,0:T(8,128)} %cent_in.1), custom_call_target="tpu_custom_call" | custom-call | tf_op jit(solution)/shard_map/first_block/pallas_call | solution.py:349
  31.2 0.0 collective-permute-done.6
  31.3 3.1 %collective-permute-done.5 = f32[2,2,1024]{2,1,0:T(2,128)S(1)} collective-permute-done((f32[2,2,1024]{2,1,0:T(2,128)S(1)}, f32[2,2,1024]{2,1,0:T(2,128)S(1)}, u32[]{:S(2)}, u32[]{:S(2)}) %collective-permute-start.5) | collective-permute-done | bytes 16416 | tf_op jit(solution)/shard_map/ppermute | solution.py:565
  34.4 0.0 collective-permute-done.4
  34.5 0.1 broadcast_compare_fusion
  34.5 0.2 convert_reduce_fusion
  34.7 0.0 collective-permute-done.keys_ref.refs_0_
  34.8 0.0 collective-permute-done.1.keys_ref.refs_0_
  34.8 0.9 %collective-permute-start.3 = (bf16[2,1024,128]{2,1,0:T(8,128)(2,1)S(1)}, bf16[2,1024,128]{2,1,0:T(8,128)(2,1)S(1)}, u32[]{:S(2)}, u32[]{:S(2)}) collective-permute-start(bf16[2,1024,128]{2,1,0:T(8,128)(2,1)S(1)} %collective-permute-done.1.keys_ref.refs_0_), channel_id=1, source_target_pairs={{0,4},{4,0},{8,12},{12,8},{1,5},{5,1},{9,13},{13,9},{2,6},{6,2},{1... | collective-permute-start | bytes 1572872 | tf_op jit(solution)/shard_map/ppermute | solution.py:565
  35.7 0.1 constant_dynamic-update-slice_fusion.2
  35.7 1.7 %own_ranks.1.rank_ref = f32[2,1,1024]{2,1,0:T(1,128)S(1)} custom-call(s32[1]{0:T(128)} %bitcast._.me_ref, f32[2,4,1024]{2,1,0:T(4,128)S(1)} %get-tuple-element.60.label_ref.refs_5_), custom_call_target="tpu_custom_call" | custom-call | tf_op jit(solution)/shard_map/own_ranks/pallas_call | solution.py:239
  37.5 3.0 %first_block.5 = (f32[2,1024,128]{2,1,0:T(8,128)S(1)}, bf16[2,1024,128]{2,1,0:T(8,128)(2,1)S(1)}) custom-call(s32[1]{0:T(128)} %bitcast._.me_ref, bf16[2,1024,128]{2,1,0:T(8,128)(2,1)S(1)} %collective-permute-done.keys_ref.refs_0_, f32[2,1,1024]{2,1,0:T(1,128)S(1)} %get-tuple-element.62.tot_ref, ...), custom_call_target="tpu_custom_call", output_to_operand_aliasing={{0}: (4, {})} | custom-call | tf_op jit(solution)/shard_map/first_block/pallas_call | solution.py:349
  40.5 0.6 windows.3
  41.1 1.3 %collective-permute-start.10 = (bf16[2,544,128]{2,1,0:T(8,128)(2,1)S(1)}, bf16[2,544,128]{2,1,0:T(8,128)(2,1)S(1)}, u32[]{:S(2)}, u32[]{:S(2)}) collective-permute-start(bf16[2,544,128]{2,1,0:T(8,128)(2,1)S(1)} %get-tuple-element.47), channel_id=1, source_target_pairs={{0,4},{4,0},{8,12},{12,8},{1,5},{5,1},{9,13},{13,9},{2,6},{6,2},{1... | collective-permute-start | bytes 835592 | tf_op jit(solution)/shard_map/ppermute | solution.py:565
  42.3 2.6 %collective-permute-start.11 = (bf16[2,544,128]{2,1,0:T(8,128)(2,1)S(1)}, bf16[2,544,128]{2,1,0:T(8,128)(2,1)S(1)}, u32[]{:S(2)}, u32[]{:S(2)}) collective-permute-start(bf16[2,544,128]{2,1,0:T(8,128)(2,1)S(1)} %get-tuple-element.48), channel_id=1, source_target_pairs={{0,12},{4,8},{8,4},{12,0},{1,13},{5,9},{9,5},{13,1},{2,14},{6,10},... | collective-permute-start | bytes 835592 | tf_op jit(solution)/shard_map/ppermute | solution.py:565
  44.9 3.0 %first_block.6 = (f32[2,1024,128]{2,1,0:T(8,128)S(1)}, bf16[2,1024,128]{2,1,0:T(8,128)(2,1)S(1)}) custom-call(s32[1]{0:T(128)} %bitcast._.me_ref, bf16[2,1024,128]{2,1,0:T(8,128)(2,1)S(1)} %collective-permute-done.1.keys_ref.refs_0_, f32[2,1,1024]{2,1,0:T(1,128)S(1)} %get-tuple-element.64.tot_ref, ...), custom_call_target="tpu_custom_call", output_to_operand_aliasing={{0}: (4, {})} | custom-call | tf_op jit(solution)/shard_map/first_block/pallas_call | solution.py:349
  47.9 0.6 windows.2
  48.5 0.1 collective-permute-start.12
  48.6 0.1 constant_dynamic-update-slice_fusion.1
  48.7 0.1 constant_dynamic-update-slice_fusion.refs_4_.scalar_ref
  48.7 0.9 %collective-permute-done.3.keys_ref.refs_1_ = bf16[2,1024,128]{2,1,0:T(8,128)(2,1)S(1)} collective-permute-done((bf16[2,1024,128]{2,1,0:T(8,128)(2,1)S(1)}, bf16[2,1024,128]{2,1,0:T(8,128)(2,1)S(1)}, u32[]{:S(2)}, u32[]{:S(2)}) %collective-permute-start.3) | collective-permute-done | bytes 524320 | tf_op jit(solution)/shard_map/ppermute | solution.py:565
  49.6 3.0 %first_block.7 = (f32[2,1024,128]{2,1,0:T(8,128)S(1)}, bf16[2,1024,128]{2,1,0:T(8,128)(2,1)S(1)}) custom-call(s32[1]{0:T(128)} %bitcast._.me_ref, bf16[2,1024,128]{2,1,0:T(8,128)(2,1)S(1)} %collective-permute-done.3.keys_ref.refs_1_, f32[2,1,1024]{2,1,0:T(1,128)S(1)} %get-tuple-element.66.tot_ref, ...), custom_call_target="tpu_custom_call", output_to_operand_aliasing={{0}: (4, {})} | custom-call | tf_op jit(solution)/shard_map/first_block/pallas_call | solution.py:349
  52.6 7.8 %raw_weights.1 = (bf16[2,1024,4096]{2,1,0:T(8,128)(2,1)S(1)}, f32[2,1,4096]{2,1,0:T(1,128)S(1)}, bf16[2,2048,256]{2,1,0:T(8,128)(2,1)S(1)}) custom-call(f32[2,1024,128]{2,1,0:T(8,128)S(1)} %get-tuple-element.38.sums_ref, bf16[2,1024,128]{2,1,0:T(8,128)(2,1)S(1)} %get-tuple-element.50.refs_0_.refs_4_, ...), custom_call_target="tpu_custom_call" | custom-call | tf_op jit(solution)/shard_map/raw_weights/pallas_call | solution.py:398
  60.4 0.9 %collective-permute-start.7 = (f32[2,1,4096]{2,1,0:T(1,128)S(1)}, f32[2,1,4096]{2,1,0:T(1,128)S(1)}, u32[]{:S(2)}, u32[]{:S(2)}) collective-permute-start(f32[2,1,4096]{2,1,0:T(1,128)S(1)} %get-tuple-element.46.refs_0_), channel_id=1, source_target_pairs={{0,4},{4,0},{8,12},{12,8},{1,5},{5,1},{9,13},{13,9},{2,6},{6,2},{1... | collective-permute-start | bytes 98312 | tf_op jit(solution)/shard_map/ppermute | solution.py:565
  61.3 2.3 %collective-permute-start.8 = (f32[2,1,4096]{2,1,0:T(1,128)S(1)}, f32[2,1,4096]{2,1,0:T(1,128)S(1)}, u32[]{:S(2)}, u32[]{:S(2)}) collective-permute-start(f32[2,1,4096]{2,1,0:T(1,128)S(1)} %get-tuple-element.46.refs_0_), channel_id=1, source_target_pairs={{0,8},{4,12},{8,0},{12,4},{1,9},{5,13},{9,1},{13,5},{2,10},{6,14},... | collective-permute-start | bytes 98312 | tf_op jit(solution)/shard_map/ppermute | solution.py:565
  63.7 1.5 %collective-permute-done.10.refs_2_ = bf16[2,544,128]{2,1,0:T(8,128)(2,1)S(1)} collective-permute-done((bf16[2,544,128]{2,1,0:T(8,128)(2,1)S(1)}, bf16[2,544,128]{2,1,0:T(8,128)(2,1)S(1)}, u32[]{:S(2)}, u32[]{:S(2)}) %collective-permute-start.10) | collective-permute-done | bytes 278560 | tf_op jit(solution)/shard_map/ppermute | solution.py:565
  65.2 2.1 %collective-permute-start.9 = (f32[2,1,4096]{2,1,0:T(1,128)S(1)}, f32[2,1,4096]{2,1,0:T(1,128)S(1)}, u32[]{:S(2)}, u32[]{:S(2)}) collective-permute-start(f32[2,1,4096]{2,1,0:T(1,128)S(1)} %get-tuple-element.46.refs_0_), channel_id=1, source_target_pairs={{0,12},{4,8},{8,4},{12,0},{1,13},{5,9},{9,5},{13,1},{2,14},{6,10},... | collective-permute-start | bytes 98312 | tf_op jit(solution)/shard_map/ppermute | solution.py:565
  67.2 0.0 collective-permute-done.11.refs_3_
  67.2 3.8 %place.2.refs_2_ = bf16[2,2048,256]{2,1,0:T(8,128)(2,1)S(1)} custom-call(s32[5,2,4]{2,1,0:T(2,128)S(1)} %constant_dynamic-update-slice_fusion.refs_4_.scalar_ref, f32[2,4,1024]{2,1,0:T(4,128)S(1)} %get-tuple-element.60.label_ref.refs_5_, bf16[2,1024,128]{2,1,0:T(8,128)(2,1)S(1)} %collective-permute-done.keys_ref.refs_0_, ...), custom_call_target="tpu_custom_call" | custom-call | tf_op jit(solution)/shard_map/place/pallas_call | solution.py:544
  71.1 0.0 collective-permute-done.12.refs_1_
  71.1 3.8 %place.3 = (bf16[4096,128]{1,0:T(8,128)(2,1)}, bf16[4096,128]{1,0:T(8,128)(2,1)}) custom-call(s32[5,2,4]{2,1,0:T(2,128)S(1)} %constant_dynamic-update-slice_fusion.refs_4_.scalar_ref, f32[2,4,1024]{2,1,0:T(4,128)S(1)} %get-tuple-element.60.label_ref.refs_5_, bf16[2,1024,128]{2,1,0:T(8,128)(2,1)S(1)} %collective-permute-done.1.keys_ref.refs_0_, ...), custom_call_target="tpu_custom_call" | custom-call | tf_op jit(solution)/shard_map/place/pallas_call | solution.py:544
  74.9 0.0 collective-permute-done.7.refs_1_
  74.9 0.0 collective-permute-done.8.refs_2_
  74.9 0.0 collective-permute-done.9.refs_3_
  74.9 6.1 %weighted_sums.1 = f32[2,1024,128]{2,1,0:T(8,128)} custom-call(bf16[2,1024,4096]{2,1,0:T(8,128)(2,1)S(1)} %get-tuple-element.45.raw_ref, f32[2,1,4096]{2,1,0:T(1,128)S(1)} %get-tuple-element.46.refs_0_, f32[2,1,4096]{2,1,0:T(1,128)S(1)} %collective-permute-done.7.refs_1_, f32[2,1,4096]{2,1,0:T(1,128)S(1)} %collective-permute-done.8.refs_2_, ...), custom_call_target="tpu_custom_call" | custom-call | tf_op jit(solution)/shard_map/weighted_sums/pallas_call | solution.py:447
  (13 shorter events, 0.1 us)
Async XLA Ops:
  0.6 19.9 %copy-start = (s32[2,5]{1,0:T(2,128)S(1)}, s32[2,5]{1,0:T(2,128)}, u32[]{:S(2)}) copy-start(s32[2,5]{1,0:T(2,128)} %param.8) | copy-start | bytes 124
  4.6 30.1 %collective-permute-start = (bf16[2,1024,128]{2,1,0:T(8,128)(2,1)S(1)}, bf16[2,1024,128]{2,1,0:T(8,128)(2,1)S(1)}, u32[]{:S(2)}, u32[]{:S(2)}) collective-permute-start(bf16[2,1024,128]{2,1,0:T(8,128)(2,1)S(1)} %get-tuple-element.29.keys_ref.refs_6_), channel_id=1, source_target_pairs={{0,4},{4,0},{8,12},{12,8},{1,5},{5,1},{9,13},{13,9},{2,6},{6,2},{1... | collective-permute-start | bytes 1572872 | tf_op jit(solution)/shard_map/ppermute | solution.py:565
  7.7 27.0 %collective-permute-start.1 = (bf16[2,1024,128]{2,1,0:T(8,128)(2,1)S(1)}, bf16[2,1024,128]{2,1,0:T(8,128)(2,1)S(1)}, u32[]{:S(2)}, u32[]{:S(2)}) collective-permute-start(bf16[2,1024,128]{2,1,0:T(8,128)(2,1)S(1)} %get-tuple-element.29.keys_ref.refs_6_), channel_id=1, source_target_pairs={{0,8},{4,12},{8,0},{12,4},{1,9},{5,13},{9,1},{13,5},{2,10},{6,14},... | collective-permute-start | bytes 1572872 | tf_op jit(solution)/shard_map/ppermute | solution.py:565
  10.3 1.9 %collective-permute-start.2 = (f32[2,1,128]{2,1,0:T(1,128)S(1)}, f32[2,1,128]{2,1,0:T(1,128)S(1)}, u32[]{:S(2)}, u32[]{:S(2)}) collective-permute-start(f32[2,1,128]{2,1,0:T(1,128)S(1)} %slice.33), channel_id=1, source_target_pairs={{0,1},{1,0},{2,3},{3,2},{4,5},{5,4},{6,7},{7,6},{8,9},{9,8},{10,11... | collective-permute-start | bytes 3080 | tf_op jit(solution)/shard_map/ppermute | solution.py:583
  19.9 11.3 %collective-permute-start.6 = (f32[2,2,1024]{2,1,0:T(2,128)S(1)}, f32[2,2,1024]{2,1,0:T(2,128)S(1)}, u32[]{:S(2)}, u32[]{:S(2)}) collective-permute-start(f32[2,2,1024]{2,1,0:T(2,128)S(1)} %pad_maximum_fusion.1), channel_id=1, source_target_pairs={{0,4},{4,0},{8,12},{12,8},{1,5},{5,1},{9,13},{13,9},{2,6},{6,2},{1... | collective-permute-start | bytes 49160 | tf_op jit(solution)/shard_map/ppermute | solution.py:565
  23.1 11.3 %collective-permute-start.5 = (f32[2,2,1024]{2,1,0:T(2,128)S(1)}, f32[2,2,1024]{2,1,0:T(2,128)S(1)}, u32[]{:S(2)}, u32[]{:S(2)}) collective-permute-start(f32[2,2,1024]{2,1,0:T(2,128)S(1)} %pad_maximum_fusion.1), channel_id=1, source_target_pairs={{0,8},{4,12},{8,0},{12,4},{1,9},{5,13},{9,1},{13,5},{2,10},{6,14},... | collective-permute-start | bytes 49160 | tf_op jit(solution)/shard_map/ppermute | solution.py:565
  23.2 11.2 %collective-permute-start.4 = (f32[2,2,1024]{2,1,0:T(2,128)S(1)}, f32[2,2,1024]{2,1,0:T(2,128)S(1)}, u32[]{:S(2)}, u32[]{:S(2)}) collective-permute-start(f32[2,2,1024]{2,1,0:T(2,128)S(1)} %pad_maximum_fusion.1), channel_id=1, source_target_pairs={{0,12},{4,8},{8,4},{12,0},{1,13},{5,9},{9,5},{13,1},{2,14},{6,10},... | collective-permute-start | bytes 49160 | tf_op jit(solution)/shard_map/ppermute | solution.py:565
  34.8 14.9 %collective-permute-start.3 = (bf16[2,1024,128]{2,1,0:T(8,128)(2,1)S(1)}, bf16[2,1024,128]{2,1,0:T(8,128)(2,1)S(1)}, u32[]{:S(2)}, u32[]{:S(2)}) collective-permute-start(bf16[2,1024,128]{2,1,0:T(8,128)(2,1)S(1)} %collective-permute-done.1.keys_ref.refs_0_), channel_id=1, source_target_pairs={{0,4},{4,0},{8,12},{12,8},{1,5},{5,1},{9,13},{13,9},{2,6},{6,2},{1... | collective-permute-start | bytes 1572872 | tf_op jit(solution)/shard_map/ppermute | solution.py:565
  41.1 24.1 %collective-permute-start.10 = (bf16[2,544,128]{2,1,0:T(8,128)(2,1)S(1)}, bf16[2,544,128]{2,1,0:T(8,128)(2,1)S(1)}, u32[]{:S(2)}, u32[]{:S(2)}) collective-permute-start(bf16[2,544,128]{2,1,0:T(8,128)(2,1)S(1)} %get-tuple-element.47), channel_id=1, source_target_pairs={{0,4},{4,0},{8,12},{12,8},{1,5},{5,1},{9,13},{13,9},{2,6},{6,2},{1... | collective-permute-start | bytes 835592 | tf_op jit(solution)/shard_map/ppermute | solution.py:565
  42.3 24.9 %collective-permute-start.11 = (bf16[2,544,128]{2,1,0:T(8,128)(2,1)S(1)}, bf16[2,544,128]{2,1,0:T(8,128)(2,1)S(1)}, u32[]{:S(2)}, u32[]{:S(2)}) collective-permute-start(bf16[2,544,128]{2,1,0:T(8,128)(2,1)S(1)} %get-tuple-element.48), channel_id=1, source_target_pairs={{0,12},{4,8},{8,4},{12,0},{1,13},{5,9},{9,5},{13,1},{2,14},{6,10},... | collective-permute-start | bytes 835592 | tf_op jit(solution)/shard_map/ppermute | solution.py:565
  48.5 22.6 %collective-permute-start.12 = (bf16[2,544,128]{2,1,0:T(8,128)(2,1)S(1)}, bf16[2,544,128]{2,1,0:T(8,128)(2,1)S(1)}, u32[]{:S(2)}, u32[]{:S(2)}) collective-permute-start(bf16[2,544,128]{2,1,0:T(8,128)(2,1)S(1)} %get-tuple-element.51), channel_id=1, source_target_pairs={{0,8},{4,12},{8,0},{12,4},{1,9},{5,13},{9,1},{13,5},{2,10},{6,14},... | collective-permute-start | bytes 835592 | tf_op jit(solution)/shard_map/ppermute | solution.py:565
  60.4 14.5 %collective-permute-start.7 = (f32[2,1,4096]{2,1,0:T(1,128)S(1)}, f32[2,1,4096]{2,1,0:T(1,128)S(1)}, u32[]{:S(2)}, u32[]{:S(2)}) collective-permute-start(f32[2,1,4096]{2,1,0:T(1,128)S(1)} %get-tuple-element.46.refs_0_), channel_id=1, source_target_pairs={{0,4},{4,0},{8,12},{12,8},{1,5},{5,1},{9,13},{13,9},{2,6},{6,2},{1... | collective-permute-start | bytes 98312 | tf_op jit(solution)/shard_map/ppermute | solution.py:565
  61.3 13.6 %collective-permute-start.8 = (f32[2,1,4096]{2,1,0:T(1,128)S(1)}, f32[2,1,4096]{2,1,0:T(1,128)S(1)}, u32[]{:S(2)}, u32[]{:S(2)}) collective-permute-start(f32[2,1,4096]{2,1,0:T(1,128)S(1)} %get-tuple-element.46.refs_0_), channel_id=1, source_target_pairs={{0,8},{4,12},{8,0},{12,4},{1,9},{5,13},{9,1},{13,5},{2,10},{6,14},... | collective-permute-start | bytes 98312 | tf_op jit(solution)/shard_map/ppermute | solution.py:565
  65.2 9.8 %collective-permute-start.9 = (f32[2,1,4096]{2,1,0:T(1,128)S(1)}, f32[2,1,4096]{2,1,0:T(1,128)S(1)}, u32[]{:S(2)}, u32[]{:S(2)}) collective-permute-start(f32[2,1,4096]{2,1,0:T(1,128)S(1)} %get-tuple-element.46.refs_0_), channel_id=1, source_target_pairs={{0,12},{4,8},{8,4},{12,0},{1,13},{5,9},{9,5},{13,1},{2,14},{6,10},... | collective-permute-start | bytes 98312 | tf_op jit(solution)/shard_map/ppermute | solution.py:565

commit v16 on v14

--- a/solution.py
+++ b/solution.py
@@ -408,7 +408,10 @@
                 row_total += totals[d][h, :, peer * tokens : (peer + 1) * tokens]
             here = slice(m * tokens, (m + 1) * tokens)
             scale_rows(unit_ref[h], 1.0 / row_total, scaled_ref.at[h, here])
-        result_ref[h] = unit_rows(dot_nn(raw_ref[h], scaled_ref[h]))
+        turned = lax.dot_general(
+            scaled_ref[h], raw_ref[h], (((0,), (1,)), ((), ())), preferred_element_type=F32
+        )
+        result_ref[h] = unit_rows(jnp.transpose(turned))
         copies.append(pltpu.make_async_copy(result_ref.at[h], out_hbm.at[h], sems.at[h]))
         copies[-1].start()
     for copy in copies:

time: 80.6 us -> 82.3 us (1.021)
  Pallas kernels: 50.6 us -> 52.4 us
    pallas_call x1, Pallas kernels: 6.06 us -> 7.81 us  [weighted_sums(): pl.pallas_call(functools.partial(sums_kernel, len(units)), in_specs=[in_v...]
  transfers between devices with their start and end apart: 13 -> 13, of which waited for: 4 -> 4; matrix products, arithmetic and copies ran while one was open for 3% -> 3% of each run, Pallas kernels for 50% -> 49%
where the time goes in v16:
time: 82.3 us; the launch traced here: 82.1 us
  Pallas kernels  52.4 us (64%)
  starting transfers between devices  18.4 us (22%)
  waiting for transfers between devices  7.58 us (9%)
  local copies, waits for them, and re-layouts  1.99 us (2%)
  between operations  1.07 us (1%)
    ppermute x12, starting transfers between devices, swap(): return lax.ppermute(x, 'ctx', [(i, i ^ d) for i in range(n)])  18.4 us
    pallas_call x4, Pallas kernels, first_block(): pl.pallas_call(functools.partial(first_kernel, fresh), grid_spec=pltpu.Pr...  13 us
    pallas_call x2, Pallas kernels, place(): pl.pallas_call(functools.partial(place_kernel, ids, size, fresh), in_spec...  9.38 us
    pallas_call x1, Pallas kernels, weighted_sums(): pl.pallas_call(functools.partial(sums_kernel, len(units)), in_specs=[in_v...  7.81 us
    pallas_call x1, Pallas kernels, own_totals(): pl.pallas_call(totals_kernel, grid=(heads, count // rows), in_specs=[in_v...  7.7 us
    ppermute x12, waiting for transfers between devices, swap(): return lax.ppermute(x, 'ctx', [(i, i ^ d) for i in range(n)])  7.57 us
    pallas_call x1, Pallas kernels, raw_weights(): pl.pallas_call(functools.partial(raw_kernel, len(units)), grid=(heads,),...  5.28 us
    pallas_call x1, Pallas kernels, sort_keys(): pl.pallas_call(sort_kernel, in_specs=[anywhere()] * 2, out_specs=(in_vmem...  4 us
  transfers between devices with their start and end apart: 13, of which 4 were waited for; matrix products, arithmetic and copies ran while one was open for 3% of the time, Pallas kernels for 49%

profile of v16, /device:TPU:0, one launch (start us, length us, event | category | flops | bytes accessed | tf_op | source)
XLA Modules:
  0.0 82.1 jit_solution(6884311140679857835)
XLA Ops:
  0.6 0.0 copy-start
  0.6 4.0 %sort_keys.1 = (bf16[2,1024,128]{2,1,0:T(8,128)(2,1)S(1)}, f32[2,1,1024]{2,1,0:T(1,128)S(1)}, s32[2,1,1024]{2,1,0:T(1,128)S(1)}) custom-call(s32[2,1024]{1,0:T(2,128)} %label_hbm.1, bf16[2048,128]{1,0:T(8,128)(2,1)} %bitcast.26), custom_call_target="tpu_custom_call" | custom-call | tf_op jit(solution)/shard_map/sort_keys/pallas_call | solution.py:135
  4.6 4.1 %collective-permute-start.1 = (bf16[2,1024,128]{2,1,0:T(8,128)(2,1)S(1)}, bf16[2,1024,128]{2,1,0:T(8,128)(2,1)S(1)}, u32[]{:S(2)}, u32[]{:S(2)}) collective-permute-start(bf16[2,1024,128]{2,1,0:T(8,128)(2,1)S(1)} %get-tuple-element.45.keys_ref.refs_0_), channel_id=1, source_target_pairs={{0,8},{4,12},{8,0},{12,4},{1,9},{5,13},{9,1},{13,5},{2,10},{6,14},... | collective-permute-start | bytes 1572872 | tf_op jit(solution)/shard_map/ppermute | solution.py:541
  8.8 1.6 %collective-permute-start = (bf16[2,1024,128]{2,1,0:T(8,128)(2,1)S(1)}, bf16[2,1024,128]{2,1,0:T(8,128)(2,1)S(1)}, u32[]{:S(2)}, u32[]{:S(2)}) collective-permute-start(bf16[2,1024,128]{2,1,0:T(8,128)(2,1)S(1)} %get-tuple-element.45.keys_ref.refs_0_), channel_id=1, source_target_pairs={{0,4},{4,0},{8,12},{12,8},{1,5},{5,1},{9,13},{13,9},{2,6},{6,2},{1... | collective-permute-start | bytes 1572872 | tf_op jit(solution)/shard_map/ppermute | solution.py:541
  10.3 0.0 collective-permute-start.2
  10.4 0.8 copy.13
  11.1 0.6 gather_fusion
  11.7 0.1 convert_bitcast_fusion
  11.8 0.1 copy.14
  11.9 0.2 convert_reduce_fusion.2
  12.1 0.1 fusion.5
  12.2 0.0 collective-permute-done.2._
  12.2 7.7 %own_totals.1.tot_ref = f32[2,1,1024]{2,1,0:T(1,128)S(1)} custom-call(bf16[2,1024,128]{2,1,0:T(8,128)(2,1)S(1)} %get-tuple-element.45.keys_ref.refs_0_, f32[2,4096,128]{2,1,0:T(8,128)} %cent_in.1, f32[2,1,128]{2,1,0:T(1,128)S(1)} %collective-permute-done.2._), custom_call_target="tpu_custom_call" | custom-call | tf_op jit(solution)/shard_map/own_totals/pallas_call | solution.py:276
  19.9 0.5 collective-permute-start.6
  20.4 0.1 pad_add_fusion
  20.5 0.0 copy-done
  20.5 0.2 dynamic-slice_reduce_fusion
  20.7 2.4 %sort_values.1.values_ref = bf16[2,1024,128]{2,1,0:T(8,128)(2,1)S(1)} custom-call(s32[2,1,1024]{2,1,0:T(1,128)S(1)} %get-tuple-element.43.spot_ref, bf16[2048,128]{1,0:T(8,128)(2,1)} %bitcast.27), custom_call_target="tpu_custom_call" | custom-call | tf_op jit(solution)/shard_map/sort_values/pallas_call | solution.py:173
  23.1 0.1 collective-permute-start.5
  23.2 3.9 %collective-permute-start.4 = (f32[2,2,1024]{2,1,0:T(2,128)S(1)}, f32[2,2,1024]{2,1,0:T(2,128)S(1)}, u32[]{:S(2)}, u32[]{:S(2)}) collective-permute-start(f32[2,2,1024]{2,1,0:T(2,128)S(1)} %pad_maximum_fusion.1), channel_id=1, source_target_pairs={{0,12},{4,8},{8,4},{12,0},{1,13},{5,9},{9,5},{13,1},{2,14},{6,10},... | collective-permute-start | bytes 49160 | tf_op jit(solution)/shard_map/ppermute | solution.py:541
  27.1 4.1 %first_block.4 = (f32[2,1024,128]{2,1,0:T(8,128)S(1)}, bf16[2,1024,128]{2,1,0:T(8,128)(2,1)S(1)}, bf16[2,1024,128]{2,1,0:T(8,128)(2,1)S(1)}) custom-call(s32[1]{0:T(128)} %bitcast._.me_ref, bf16[2,1024,128]{2,1,0:T(8,128)(2,1)S(1)} %get-tuple-element.45.keys_ref.refs_0_, f32[2,1,1024]{2,1,0:T(1,128)S(1)} %own_totals.1.tot_ref, f32[2,4096,128]{2,1,0:T(8,128)} %cent_in.1), custom_call_target="tpu_custom_call" | custom-call | tf_op jit(solution)/shard_map/first_block/pallas_call | solution.py:346
  31.2 1.9 %collective-permute-done.6 = f32[2,2,1024]{2,1,0:T(2,128)S(1)} collective-permute-done((f32[2,2,1024]{2,1,0:T(2,128)S(1)}, f32[2,2,1024]{2,1,0:T(2,128)S(1)}, u32[]{:S(2)}, u32[]{:S(2)}) %collective-permute-start.6) | collective-permute-done | bytes 16416 | tf_op jit(solution)/shard_map/ppermute | solution.py:541
  33.1 0.0 collective-permute-done.5
  33.1 0.9 %collective-permute-done.4 = f32[2,2,1024]{2,1,0:T(2,128)S(1)} collective-permute-done((f32[2,2,1024]{2,1,0:T(2,128)S(1)}, f32[2,2,1024]{2,1,0:T(2,128)S(1)}, u32[]{:S(2)}, u32[]{:S(2)}) %collective-permute-start.4) | collective-permute-done | bytes 16416 | tf_op jit(solution)/shard_map/ppermute | solution.py:541
  34.1 0.1 broadcast_compare_fusion
  34.2 0.2 convert_reduce_fusion
  34.4 0.0 collective-permute-done.1.keys_ref.refs_0_
  34.4 0.0 collective-permute-done.keys_ref.refs_1_
  34.4 0.5 collective-permute-start.3
  34.9 1.6 %own_ranks.1.rank_ref = f32[2,1,1024]{2,1,0:T(1,128)S(1)} custom-call(s32[1]{0:T(128)} %bitcast._.me_ref, f32[2,4,1024]{2,1,0:T(4,128)S(1)} %get-tuple-element.56.label_ref), custom_call_target="tpu_custom_call" | custom-call | tf_op jit(solution)/shard_map/own_ranks/pallas_call | solution.py:240
  36.5 3.0 %first_block.5 = (f32[2,1024,128]{2,1,0:T(8,128)S(1)}, bf16[2,1024,128]{2,1,0:T(8,128)(2,1)S(1)}) custom-call(s32[1]{0:T(128)} %bitcast._.me_ref, bf16[2,1024,128]{2,1,0:T(8,128)(2,1)S(1)} %collective-permute-done.keys_ref.refs_1_, f32[2,1,1024]{2,1,0:T(1,128)S(1)} %get-tuple-element.58.tot_ref, ...), custom_call_target="tpu_custom_call", output_to_operand_aliasing={{0}: (4, {})} | custom-call | tf_op jit(solution)/shard_map/first_block/pallas_call | solution.py:346
  39.5 0.6 windows.3
  40.1 1.7 %collective-permute-start.11 = (bf16[2,544,128]{2,1,0:T(8,128)(2,1)S(1)}, bf16[2,544,128]{2,1,0:T(8,128)(2,1)S(1)}, u32[]{:S(2)}, u32[]{:S(2)}) collective-permute-start(bf16[2,544,128]{2,1,0:T(8,128)(2,1)S(1)} %get-tuple-element.47), channel_id=1, source_target_pairs={{0,4},{4,0},{8,12},{12,8},{1,5},{5,1},{9,13},{13,9},{2,6},{6,2},{1... | collective-permute-start | bytes 835592 | tf_op jit(solution)/shard_map/ppermute | solution.py:541
  41.8 0.1 constant_dynamic-update-slice_fusion.2
  41.9 2.6 %collective-permute-start.12 = (bf16[2,544,128]{2,1,0:T(8,128)(2,1)S(1)}, bf16[2,544,128]{2,1,0:T(8,128)(2,1)S(1)}, u32[]{:S(2)}, u32[]{:S(2)}) collective-permute-start(bf16[2,544,128]{2,1,0:T(8,128)(2,1)S(1)} %get-tuple-element.48), channel_id=1, source_target_pairs={{0,12},{4,8},{8,4},{12,0},{1,13},{5,9},{9,5},{13,1},{2,14},{6,10},... | collective-permute-start | bytes 835592 | tf_op jit(solution)/shard_map/ppermute | solution.py:541
  44.4 3.0 %first_block.6 = (f32[2,1024,128]{2,1,0:T(8,128)S(1)}, bf16[2,1024,128]{2,1,0:T(8,128)(2,1)S(1)}) custom-call(s32[1]{0:T(128)} %bitcast._.me_ref, bf16[2,1024,128]{2,1,0:T(8,128)(2,1)S(1)} %collective-permute-done.1.keys_ref.refs_0_, f32[2,1,1024]{2,1,0:T(1,128)S(1)} %get-tuple-element.60.tot_ref, ...), custom_call_target="tpu_custom_call", output_to_operand_aliasing={{0}: (4, {})} | custom-call | tf_op jit(solution)/shard_map/first_block/pallas_call | solution.py:346
  47.4 0.6 windows.2
  48.0 0.1 collective-permute-start.10
  48.1 0.1 constant_dynamic-update-slice_fusion.1
  48.2 1.1 %collective-permute-done.3.keys_ref.refs_2_ = bf16[2,1024,128]{2,1,0:T(8,128)(2,1)S(1)} collective-permute-done((bf16[2,1024,128]{2,1,0:T(8,128)(2,1)S(1)}, bf16[2,1024,128]{2,1,0:T(8,128)(2,1)S(1)}, u32[]{:S(2)}, u32[]{:S(2)}) %collective-permute-start.3) | collective-permute-done | bytes 524320 | tf_op jit(solution)/shard_map/ppermute | solution.py:541
  49.3 3.0 %first_block.7 = (f32[2,1024,128]{2,1,0:T(8,128)S(1)}, bf16[2,1024,128]{2,1,0:T(8,128)(2,1)S(1)}) custom-call(s32[1]{0:T(128)} %bitcast._.me_ref, bf16[2,1024,128]{2,1,0:T(8,128)(2,1)S(1)} %collective-permute-done.3.keys_ref.refs_2_, f32[2,1,1024]{2,1,0:T(1,128)S(1)} %get-tuple-element.62.tot_ref, ...), custom_call_target="tpu_custom_call", output_to_operand_aliasing={{0}: (4, {})} | custom-call | tf_op jit(solution)/shard_map/first_block/pallas_call | solution.py:346
  52.3 5.3 %raw_weights.1 = (bf16[2,1024,4096]{2,1,0:T(8,128)(2,1)S(1)}, f32[2,1,4096]{2,1,0:T(1,128)S(1)}) custom-call(f32[2,1024,128]{2,1,0:T(8,128)S(1)} %get-tuple-element.36.sums_ref, bf16[2,1024,128]{2,1,0:T(8,128)(2,1)S(1)} %get-tuple-element.37.refs_0_.refs_4_, bf16[2,1024,128]{2,1,0:T(8,128)(2,1)S(1)} %get-tuple-element.38.refs_1_.refs_5_._, ...), custom_call_target="tpu_custom_call" | custom-call | tf_op jit(solution)/shard_map/raw_weights/pallas_call | solution.py:383
  57.6 3.4 %collective-permute-start.9 = (f32[2,1,4096]{2,1,0:T(1,128)S(1)}, f32[2,1,4096]{2,1,0:T(1,128)S(1)}, u32[]{:S(2)}, u32[]{:S(2)}) collective-permute-start(f32[2,1,4096]{2,1,0:T(1,128)S(1)} %get-tuple-element.42.refs_0_), channel_id=1, source_target_pairs={{0,12},{4,8},{8,4},{12,0},{1,13},{5,9},{9,5},{13,1},{2,14},{6,10},... | collective-permute-start | bytes 98312 | tf_op jit(solution)/shard_map/ppermute | solution.py:541
  61.0 0.0 collective-permute-start.8
  61.0 3.6 %collective-permute-done.11.refs_4_ = bf16[2,544,128]{2,1,0:T(8,128)(2,1)S(1)} collective-permute-done((bf16[2,544,128]{2,1,0:T(8,128)(2,1)S(1)}, bf16[2,544,128]{2,1,0:T(8,128)(2,1)S(1)}, u32[]{:S(2)}, u32[]{:S(2)}) %collective-permute-start.11) | collective-permute-done | bytes 278560 | tf_op jit(solution)/shard_map/ppermute | solution.py:541
  64.6 0.0 collective-permute-start.7
  64.6 0.1 constant_dynamic-update-slice_fusion.scalar_ref
  64.7 0.0 collective-permute-done.12.refs_5_
  64.7 5.6 %place.2.refs_2_ = bf16[2,2048,256]{2,1,0:T(8,128)(2,1)S(1)} custom-call(s32[5,2,4]{2,1,0:T(2,128)S(1)} %constant_dynamic-update-slice_fusion.scalar_ref, f32[2,4,1024]{2,1,0:T(4,128)S(1)} %get-tuple-element.56.label_ref, bf16[2,1024,128]{2,1,0:T(8,128)(2,1)S(1)} %get-tuple-element.45.keys_ref.refs_0_, ...), custom_call_target="tpu_custom_call" | custom-call | tf_op jit(solution)/shard_map/place/pallas_call | solution.py:520
  70.3 0.0 collective-permute-done.10.refs_1_
  70.3 3.8 %place.3 = (bf16[4096,128]{1,0:T(8,128)(2,1)}, bf16[4096,128]{1,0:T(8,128)(2,1)}) custom-call(s32[5,2,4]{2,1,0:T(2,128)S(1)} %constant_dynamic-update-slice_fusion.scalar_ref, f32[2,4,1024]{2,1,0:T(4,128)S(1)} %get-tuple-element.56.label_ref, bf16[2,1024,128]{2,1,0:T(8,128)(2,1)S(1)} %collective-permute-done.1.keys_ref.refs_0_, ...), custom_call_target="tpu_custom_call" | custom-call | tf_op jit(solution)/shard_map/place/pallas_call | solution.py:520
  74.1 0.0 collective-permute-done.9.refs_3_
  74.1 0.0 collective-permute-done.8.refs_2_
  74.1 0.0 collective-permute-done.7.refs_1_
  74.1 7.8 %weighted_sums.1 = f32[2,1024,128]{2,1,0:T(8,128)} custom-call(bf16[2,1024,4096]{2,1,0:T(8,128)(2,1)S(1)} %get-tuple-element.41.raw_ref, f32[2,1,4096]{2,1,0:T(1,128)S(1)} %get-tuple-element.42.refs_0_, f32[2,1,4096]{2,1,0:T(1,128)S(1)} %collective-permute-done.7.refs_1_, f32[2,1,4096]{2,1,0:T(1,128)S(1)} %collective-permute-done.8.refs_2_, ...), custom_call_target="tpu_custom_call" | custom-call | tf_op jit(solution)/shard_map/weighted_sums/pallas_call | solution.py:424
  (13 shorter events, 0.1 us)
Async XLA Ops:
  0.6 19.9 %copy-start = (s32[2,5]{1,0:T(2,128)S(1)}, s32[2,5]{1,0:T(2,128)}, u32[]{:S(2)}) copy-start(s32[2,5]{1,0:T(2,128)} %param.8) | copy-start | bytes 124
  4.6 29.7 %collective-permute-start.1 = (bf16[2,1024,128]{2,1,0:T(8,128)(2,1)S(1)}, bf16[2,1024,128]{2,1,0:T(8,128)(2,1)S(1)}, u32[]{:S(2)}, u32[]{:S(2)}) collective-permute-start(bf16[2,1024,128]{2,1,0:T(8,128)(2,1)S(1)} %get-tuple-element.45.keys_ref.refs_0_), channel_id=1, source_target_pairs={{0,8},{4,12},{8,0},{12,4},{1,9},{5,13},{9,1},{13,5},{2,10},{6,14},... | collective-permute-start | bytes 1572872 | tf_op jit(solution)/shard_map/ppermute | solution.py:541
  8.8 25.6 %collective-permute-start = (bf16[2,1024,128]{2,1,0:T(8,128)(2,1)S(1)}, bf16[2,1024,128]{2,1,0:T(8,128)(2,1)S(1)}, u32[]{:S(2)}, u32[]{:S(2)}) collective-permute-start(bf16[2,1024,128]{2,1,0:T(8,128)(2,1)S(1)} %get-tuple-element.45.keys_ref.refs_0_), channel_id=1, source_target_pairs={{0,4},{4,0},{8,12},{12,8},{1,5},{5,1},{9,13},{13,9},{2,6},{6,2},{1... | collective-permute-start | bytes 1572872 | tf_op jit(solution)/shard_map/ppermute | solution.py:541
  10.3 1.9 %collective-permute-start.2 = (f32[2,1,128]{2,1,0:T(1,128)S(1)}, f32[2,1,128]{2,1,0:T(1,128)S(1)}, u32[]{:S(2)}, u32[]{:S(2)}) collective-permute-start(f32[2,1,128]{2,1,0:T(1,128)S(1)} %slice.33), channel_id=1, source_target_pairs={{0,1},{1,0},{2,3},{3,2},{4,5},{5,4},{6,7},{7,6},{8,9},{9,8},{10,11... | collective-permute-start | bytes 3080 | tf_op jit(solution)/shard_map/ppermute | solution.py:559
  19.9 13.2 %collective-permute-start.6 = (f32[2,2,1024]{2,1,0:T(2,128)S(1)}, f32[2,2,1024]{2,1,0:T(2,128)S(1)}, u32[]{:S(2)}, u32[]{:S(2)}) collective-permute-start(f32[2,2,1024]{2,1,0:T(2,128)S(1)} %pad_maximum_fusion.1), channel_id=1, source_target_pairs={{0,4},{4,0},{8,12},{12,8},{1,5},{5,1},{9,13},{13,9},{2,6},{6,2},{1... | collective-permute-start | bytes 49160 | tf_op jit(solution)/shard_map/ppermute | solution.py:541
  23.1 10.0 %collective-permute-start.5 = (f32[2,2,1024]{2,1,0:T(2,128)S(1)}, f32[2,2,1024]{2,1,0:T(2,128)S(1)}, u32[]{:S(2)}, u32[]{:S(2)}) collective-permute-start(f32[2,2,1024]{2,1,0:T(2,128)S(1)} %pad_maximum_fusion.1), channel_id=1, source_target_pairs={{0,8},{4,12},{8,0},{12,4},{1,9},{5,13},{9,1},{13,5},{2,10},{6,14},... | collective-permute-start | bytes 49160 | tf_op jit(solution)/shard_map/ppermute | solution.py:541
  23.2 10.8 %collective-permute-start.4 = (f32[2,2,1024]{2,1,0:T(2,128)S(1)}, f32[2,2,1024]{2,1,0:T(2,128)S(1)}, u32[]{:S(2)}, u32[]{:S(2)}) collective-permute-start(f32[2,2,1024]{2,1,0:T(2,128)S(1)} %pad_maximum_fusion.1), channel_id=1, source_target_pairs={{0,12},{4,8},{8,4},{12,0},{1,13},{5,9},{9,5},{13,1},{2,14},{6,10},... | collective-permute-start | bytes 49160 | tf_op jit(solution)/shard_map/ppermute | solution.py:541
  34.4 14.9 %collective-permute-start.3 = (bf16[2,1024,128]{2,1,0:T(8,128)(2,1)S(1)}, bf16[2,1024,128]{2,1,0:T(8,128)(2,1)S(1)}, u32[]{:S(2)}, u32[]{:S(2)}) collective-permute-start(bf16[2,1024,128]{2,1,0:T(8,128)(2,1)S(1)} %collective-permute-done.1.keys_ref.refs_0_), channel_id=1, source_target_pairs={{0,4},{4,0},{8,12},{12,8},{1,5},{5,1},{9,13},{13,9},{2,6},{6,2},{1... | collective-permute-start | bytes 1572872 | tf_op jit(solution)/shard_map/ppermute | solution.py:541
  40.1 24.5 %collective-permute-start.11 = (bf16[2,544,128]{2,1,0:T(8,128)(2,1)S(1)}, bf16[2,544,128]{2,1,0:T(8,128)(2,1)S(1)}, u32[]{:S(2)}, u32[]{:S(2)}) collective-permute-start(bf16[2,544,128]{2,1,0:T(8,128)(2,1)S(1)} %get-tuple-element.47), channel_id=1, source_target_pairs={{0,4},{4,0},{8,12},{12,8},{1,5},{5,1},{9,13},{13,9},{2,6},{6,2},{1... | collective-permute-start | bytes 835592 | tf_op jit(solution)/shard_map/ppermute | solution.py:541
  41.9 22.8 %collective-permute-start.12 = (bf16[2,544,128]{2,1,0:T(8,128)(2,1)S(1)}, bf16[2,544,128]{2,1,0:T(8,128)(2,1)S(1)}, u32[]{:S(2)}, u32[]{:S(2)}) collective-permute-start(bf16[2,544,128]{2,1,0:T(8,128)(2,1)S(1)} %get-tuple-element.48), channel_id=1, source_target_pairs={{0,12},{4,8},{8,4},{12,0},{1,13},{5,9},{9,5},{13,1},{2,14},{6,10},... | collective-permute-start | bytes 835592 | tf_op jit(solution)/shard_map/ppermute | solution.py:541
  48.0 22.3 %collective-permute-start.10 = (bf16[2,544,128]{2,1,0:T(8,128)(2,1)S(1)}, bf16[2,544,128]{2,1,0:T(8,128)(2,1)S(1)}, u32[]{:S(2)}, u32[]{:S(2)}) collective-permute-start(bf16[2,544,128]{2,1,0:T(8,128)(2,1)S(1)} %get-tuple-element.44), channel_id=1, source_target_pairs={{0,8},{4,12},{8,0},{12,4},{1,9},{5,13},{9,1},{13,5},{2,10},{6,14},... | collective-permute-start | bytes 835592 | tf_op jit(solution)/shard_map/ppermute | solution.py:541
  57.6 16.5 %collective-permute-start.9 = (f32[2,1,4096]{2,1,0:T(1,128)S(1)}, f32[2,1,4096]{2,1,0:T(1,128)S(1)}, u32[]{:S(2)}, u32[]{:S(2)}) collective-permute-start(f32[2,1,4096]{2,1,0:T(1,128)S(1)} %get-tuple-element.42.refs_0_), channel_id=1, source_target_pairs={{0,12},{4,8},{8,4},{12,0},{1,13},{5,9},{9,5},{13,1},{2,14},{6,10},... | collective-permute-start | bytes 98312 | tf_op jit(solution)/shard_map/ppermute | solution.py:541
  61.0 13.1 %collective-permute-start.8 = (f32[2,1,4096]{2,1,0:T(1,128)S(1)}, f32[2,1,4096]{2,1,0:T(1,128)S(1)}, u32[]{:S(2)}, u32[]{:S(2)}) collective-permute-start(f32[2,1,4096]{2,1,0:T(1,128)S(1)} %get-tuple-element.42.refs_0_), channel_id=1, source_target_pairs={{0,8},{4,12},{8,0},{12,4},{1,9},{5,13},{9,1},{13,5},{2,10},{6,14},... | collective-permute-start | bytes 98312 | tf_op jit(solution)/shard_map/ppermute | solution.py:541
  64.6 9.5 %collective-permute-start.7 = (f32[2,1,4096]{2,1,0:T(1,128)S(1)}, f32[2,1,4096]{2,1,0:T(1,128)S(1)}, u32[]{:S(2)}, u32[]{:S(2)}) collective-permute-start(f32[2,1,4096]{2,1,0:T(1,128)S(1)} %get-tuple-element.42.refs_0_), channel_id=1, source_target_pairs={{0,4},{4,0},{8,12},{12,8},{1,5},{5,1},{9,13},{13,9},{2,6},{6,2},{1... | collective-permute-start | bytes 98312 | tf_op jit(solution)/shard_map/ppermute | solution.py:541
